TPU v7x, 32 devices: a whole 2x2x4 slice. The times are simulated.
32 devices in a mesh: grp: 4 (over z), blk: 8 (over y, x, core).
Axes of the slice: x: 2, y: 2, z: 4, core: 2. Of those that a mesh axis runs over, the one named last changes fastest.
Arguments:
- tile_values: bfloat16 [256, 320, 128], P(('grp', 'blk'))
- tile_paper: int32 [256], P(('grp', 'blk')), may hold values from 0 to 1
- tile_author: int32 [256], P(('grp', 'blk')), may hold values from 0 to 1
- tile_count: int32 [32], P(('grp', 'blk')), may hold values from 2 to 8, as said below
- seed_class: int32 [20480], P(('grp', 'blk')), may hold values from 0 to 152
- train_mask: int32 [20480], P(('grp', 'blk')), may hold values from 0 to 1
- class_prior: float32 [256], replicated, may hold values from 0.02 to 0.2
- class_target: float32 [256], replicated, may hold values from 0.5 to 2
Outputs:
- paper_scores: float32 [20480, 256], P(('grp', 'blk'))
- author_scores: float32 [8192, 256], P(('grp', 'blk'))
Inputs may be any that keep to these rules, and one draw needn't show every extreme that they name: The first tile_count[d] slots of device d are live, the others empty; some device has all 8 live.
All inputs are finite; a program needn't handle non-finite values.
Results may differ from a plain program's by a relative error of at most 0.0012.
Values may be sent and summed in bfloat16 or wider, within the bound.
No kernel may reach another device: no remote copies, remote signals or barrier semaphores. Data moves between devices by JAX's collectives and lax.ppermute only.
A program may use at most 64 MiB of HBM per device.

v0:
```python
import jax
import jax.numpy as jnp
from jax import lax
from jax.sharding import PartitionSpec as P

AT_DEV = 2
ITERS = 4
ROUNDS = 2


keep_share = 0.8


def class_balancer(label_masses, class_prior, class_target):
    kernel = label_masses + class_prior[None, :]
    scale_rows = None
    scale_cols = None
    for iteration in range(ITERS):
        if scale_rows is None:
            local_mass = jnp.sum(kernel, axis=0)
        else:
            local_mass = jnp.sum(scale_rows[:, None] * kernel, axis=0)
        column = lax.psum(local_mass, ("grp", "blk"))
        scale_cols = class_target / column
        scale_rows = 1.0 / jnp.sum(kernel * scale_cols[None, :], axis=1)
    return scale_rows[:, None] * kernel * scale_cols[None, :]


def on_device(
    tile_values,
    tile_paper,
    tile_author,
    tile_count,
    seed_class,
    train_mask,
    class_prior,
    class_target,
):
    high = lax.Precision.HIGHEST
    slot_count = tile_values.shape[0]
    tile_rows = tile_values.shape[1]
    tile_cols = tile_values.shape[2]
    classes = class_prior.shape[0]
    paper_rows = seed_class.shape[0]
    paper_tiles = paper_rows // tile_rows
    author_tiles = AT_DEV
    live_slots = (jnp.arange(slot_count) < tile_count[0]).astype(jnp.float32)
    seed_rows = (
        (seed_class[:, None] == jnp.arange(classes)[None, :]) & (train_mask[:, None] == 1)
    ).astype(jnp.float32)
    labels = seed_rows.astype(jnp.bfloat16).reshape(paper_tiles, tile_rows, classes)
    paper_pick = (tile_paper[:, None] == jnp.arange(paper_tiles)[None, :]).astype(
        jnp.float32
    ) * live_slots[:, None]
    author_pick = (tile_author[:, None] == jnp.arange(author_tiles)[None, :]).astype(jnp.bfloat16)
    updated = seed_rows
    author_share = jnp.zeros((author_tiles * tile_cols, classes), jnp.float32)
    for repeat in range(ROUNDS):
        chosen = labels[tile_paper]
        partial_value = jnp.einsum(
            "spa,spc->sac", tile_values, chosen, preferred_element_type=jnp.float32
        )
        parcel = (partial_value * live_slots[:, None, None]).astype(jnp.bfloat16)
        received_mass, received_selection = (
            lax.all_to_all(parcel, "blk", split_axis=0, concat_axis=0, tiled=True),
            lax.all_to_all(author_pick, "blk", split_axis=0, concat_axis=0, tiled=True),
        )
        author_mass = jnp.einsum(
            "ib,iey->bey", received_selection, received_mass, preferred_element_type=jnp.float32
        )
        author_mass = author_mass.reshape(author_tiles * tile_cols, classes)
        author_share = class_balancer(author_mass, class_prior, class_target)
        author_class_labels = author_share.astype(jnp.bfloat16).reshape(
            author_tiles, tile_cols, classes
        )
        picked = jnp.einsum(
            "ih,hlp->ilp",
            received_selection,
            author_class_labels,
            preferred_element_type=jnp.float32,
        ).astype(jnp.bfloat16)
        returned = lax.all_to_all(picked, "blk", split_axis=0, concat_axis=0, tiled=True)
        products = jnp.einsum(
            "spa,sac->spc", tile_values, returned, preferred_element_type=jnp.float32
        )
        paper_mass = jnp.einsum("sq,spc->qpc", paper_pick, products, precision=high)
        paper_mass = paper_mass.reshape(paper_rows, classes)
        paper_share = class_balancer(paper_mass, class_prior, class_target)
        updated = keep_share * paper_share + (1.0 - keep_share) * seed_rows
        labels = updated.astype(jnp.bfloat16).reshape(paper_tiles, tile_rows, classes)
    return (classes * updated, classes * author_share)


def solution(mesh):
    placed = (
        P(("grp", "blk"), None, None),
        P(("grp", "blk")),
        P(("grp", "blk")),
        P(("grp", "blk")),
        P(("grp", "blk")),
        P(("grp", "blk")),
        P(),
        P(),
    )
    return jax.shard_map(
        on_device,
        mesh=mesh,
        in_specs=placed,
        out_specs=(P(("grp", "blk"), None), P(("grp", "blk"), None)),
        check_vma=False,
    )
```

profile of v0, /device:TPU:0, one launch (start us, length us, event | category | flops | bytes accessed | tf_op | source)
XLA Modules:
  0.0 731.0 jit_solution(895558337367446098)
XLA Ops:
  2.0 5.2 all-to-all-start
  13.9 4.2 all-to-all-start.1
  18.2 9.6 %all-to-all-done.1 = bf16[8,128,256]{2,1,0:T(8,128)(2,1)S(1)} async-done(((bf16[8,128,256]{2,1,0:T(8,128)(2,1)}), bf16[8,128,256]{2,1,0:T(8,128)(2,1)S(1)}, u32[]{:S(2)}, u32[]{:S(2)}) %all-to-all-start.1) | async-done | bytes 524320 | tf_op jit(solution)/shard_map/all_to_all | solution.py:65
  28.3 39.5 %psum.112 = f32[256]{0:T(256)S(1)} all-reduce(f32[256]{0:T(256)S(1)} %get-tuple-element.2), channel_id=1, replica_groups=mesh['grp'=4,'blk'=8] {'grp','blk'}, use_global_device_ids=true, to_apply=%region_1.0 | all-reduce | flops 256 | bytes 2048 | tf_op jit(solution)/shard_map/psum | solution.py:23
  68.3 40.3 %psum.113 = f32[256]{0:T(256)S(1)} all-reduce(f32[256]{0:T(256)S(1)} %multiply_reduce_fusion.26), channel_id=1, replica_groups=mesh['grp'=4,'blk'=8] {'grp','blk'}, use_global_device_ids=true, to_apply=%region_4.0 | all-reduce | flops 256 | bytes 2048 | tf_op jit(solution)/shard_map/psum | solution.py:23
  109.0 39.8 %psum.114 = f32[256]{0:T(256)S(1)} all-reduce(f32[256]{0:T(256)S(1)} %multiply_reduce_fusion.24), channel_id=1, replica_groups=mesh['grp'=4,'blk'=8] {'grp','blk'}, use_global_device_ids=true, to_apply=%region_7.0 | all-reduce | flops 256 | bytes 2048 | tf_op jit(solution)/shard_map/psum | solution.py:23
  149.2 40.4 %psum.115 = f32[256]{0:T(256)S(1)} all-reduce(f32[256]{0:T(256)S(1)} %multiply_reduce_fusion.22), channel_id=1, replica_groups=mesh['grp'=4,'blk'=8] {'grp','blk'}, use_global_device_ids=true, to_apply=%region_10.0 | all-reduce | flops 256 | bytes 2048 | tf_op jit(solution)/shard_map/psum | solution.py:23
  190.4 13.9 %all_to_all.30 = bf16[8,128,256]{2,1,0:T(8,128)(2,1)S(1)} all-to-all(bf16[8,128,256]{2,1,0:T(8,128)(2,1)S(1)} %copy.54), channel_id=1, replica_groups=mesh['grp'=4,'blk'=8] {'blk'}, dimensions={0} | all-to-all | bytes 1048576 | tf_op jit(solution)/shard_map/all_to_all | solution.py:82
  205.0 3.8 fusion.45
  208.8 38.2 %psum.116 = f32[256]{0:T(256)S(1)} all-reduce(f32[256]{0:T(256)S(1)} %get-tuple-element.4), channel_id=1, replica_groups=mesh['grp'=4,'blk'=8] {'grp','blk'}, use_global_device_ids=true, to_apply=%region_13.0 | all-reduce | flops 256 | bytes 2048 | tf_op jit(solution)/shard_map/psum | solution.py:23
  247.9 40.4 %psum.117 = f32[256]{0:T(256)S(1)} all-reduce(f32[256]{0:T(256)S(1)} %multiply_reduce_fusion.12), channel_id=1, replica_groups=mesh['grp'=4,'blk'=8] {'grp','blk'}, use_global_device_ids=true, to_apply=%region_16.0 | all-reduce | flops 256 | bytes 2048 | tf_op jit(solution)/shard_map/psum | solution.py:23
  289.2 39.6 %psum.118 = f32[256]{0:T(256)S(1)} all-reduce(f32[256]{0:T(256)S(1)} %multiply_reduce_fusion.10), channel_id=1, replica_groups=mesh['grp'=4,'blk'=8] {'grp','blk'}, use_global_device_ids=true, to_apply=%region_19.0 | all-reduce | flops 256 | bytes 2048 | tf_op jit(solution)/shard_map/psum | solution.py:23
  329.7 40.4 %psum.119 = f32[256]{0:T(256)S(1)} all-reduce(f32[256]{0:T(256)S(1)} %multiply_reduce_fusion.8), channel_id=1, replica_groups=mesh['grp'=4,'blk'=8] {'grp','blk'}, use_global_device_ids=true, to_apply=%region_22.0 | all-reduce | flops 256 | bytes 2048 | tf_op jit(solution)/shard_map/psum | solution.py:23
  373.6 14.0 %all_to_all.31 = bf16[8,128,256]{2,1,0:T(8,128)(2,1)S(1)} all-to-all(bf16[8,128,256]{2,1,0:T(8,128)(2,1)S(1)} %copy.57), channel_id=1, replica_groups=mesh['grp'=4,'blk'=8] {'blk'}, dimensions={0} | all-to-all | bytes 1048576 | tf_op jit(solution)/shard_map/all_to_all | solution.py:65
  388.0 37.9 %psum.120 = f32[256]{0:T(256)S(1)} all-reduce(f32[256]{0:T(256)S(1)} %get-tuple-element.6), channel_id=1, replica_groups=mesh['grp'=4,'blk'=8] {'grp','blk'}, use_global_device_ids=true, to_apply=%region_25.0 | all-reduce | flops 256 | bytes 2048 | tf_op jit(solution)/shard_map/psum | solution.py:23
  426.4 40.4 %psum.121 = f32[256]{0:T(256)S(1)} all-reduce(f32[256]{0:T(256)S(1)} %multiply_reduce_fusion.19), channel_id=1, replica_groups=mesh['grp'=4,'blk'=8] {'grp','blk'}, use_global_device_ids=true, to_apply=%region_28.0 | all-reduce | flops 256 | bytes 2048 | tf_op jit(solution)/shard_map/psum | solution.py:23
  467.3 39.6 %psum.122 = f32[256]{0:T(256)S(1)} all-reduce(f32[256]{0:T(256)S(1)} %multiply_reduce_fusion.17), channel_id=1, replica_groups=mesh['grp'=4,'blk'=8] {'grp','blk'}, use_global_device_ids=true, to_apply=%region_31.0 | all-reduce | flops 256 | bytes 2048 | tf_op jit(solution)/shard_map/psum | solution.py:23
  507.4 40.6 %psum.123 = f32[256]{0:T(256)S(1)} all-reduce(f32[256]{0:T(256)S(1)} %multiply_reduce_fusion.15), channel_id=1, replica_groups=mesh['grp'=4,'blk'=8] {'grp','blk'}, use_global_device_ids=true, to_apply=%region_34.0 | all-reduce | flops 256 | bytes 2048 | tf_op jit(solution)/shard_map/psum | solution.py:23
  549.6 4.4 all-to-all-start.4
  555.0 8.8 %all-to-all-done.4 = bf16[8,128,256]{2,1,0:T(8,128)(2,1)S(1)} async-done(((bf16[8,128,256]{2,1,0:T(8,128)(2,1)}), bf16[8,128,256]{2,1,0:T(8,128)(2,1)S(1)}, u32[]{:S(2)}, u32[]{:S(2)}) %all-to-all-start.4) | async-done | bytes 524320 | tf_op jit(solution)/shard_map/all_to_all | solution.py:82
  568.1 37.9 %psum.124 = f32[256]{0:T(256)S(1)} all-reduce(f32[256]{0:T(256)S(1)} %get-tuple-element.8), channel_id=1, replica_groups=mesh['grp'=4,'blk'=8] {'grp','blk'}, use_global_device_ids=true, to_apply=%region_37.0 | all-reduce | flops 256 | bytes 2048 | tf_op jit(solution)/shard_map/psum | solution.py:23
  607.0 40.4 %psum.125 = f32[256]{0:T(256)S(1)} all-reduce(f32[256]{0:T(256)S(1)} %multiply_reduce_fusion.5), channel_id=1, replica_groups=mesh['grp'=4,'blk'=8] {'grp','blk'}, use_global_device_ids=true, to_apply=%region_40.0 | all-reduce | flops 256 | bytes 2048 | tf_op jit(solution)/shard_map/psum | solution.py:23
  648.3 39.6 %psum.126 = f32[256]{0:T(256)S(1)} all-reduce(f32[256]{0:T(256)S(1)} %multiply_reduce_fusion.3), channel_id=1, replica_groups=mesh['grp'=4,'blk'=8] {'grp','blk'}, use_global_device_ids=true, to_apply=%region_43.0 | all-reduce | flops 256 | bytes 2048 | tf_op jit(solution)/shard_map/psum | solution.py:23
  688.8 40.4 %psum.127 = f32[256]{0:T(256)S(1)} all-reduce(f32[256]{0:T(256)S(1)} %multiply_reduce_fusion.1), channel_id=1, replica_groups=mesh['grp'=4,'blk'=8] {'grp','blk'}, use_global_device_ids=true, to_apply=%region_46.0 | all-reduce | flops 256 | bytes 2048 | tf_op jit(solution)/shard_map/psum | solution.py:23
  (107 shorter events, 29.9 us)
Async XLA Ops:
  0.6 11.5 %copy-start = (bf16[8,320,128]{2,1,0:T(8,128)(2,1)S(1)}, bf16[8,320,128]{2,1,0:T(8,128)(2,1)}, u32[]{:S(2)}) copy-start(bf16[8,320,128]{2,1,0:T(8,128)(2,1)} %param.8) | copy-start | bytes 1966084
  2.0 11.9 %all-to-all-start = ((bf16[8,1,2]{2,1,0:T(2,128)(2,1)}), bf16[8,1,2]{2,1,0:T(2,128)(2,1)S(1)}, u32[]{:S(2)}, u32[]{:S(2)}) async-start(bf16[8,1,2]{2,1,0:T(2,128)(2,1)} %compare_convert_fusion), calls=%async_computation | async-start | bytes 8192 | tf_op jit(solution)/shard_map/all_to_all | solution.py:66
  12.9 15.0 %copy-start.1 = (f32[256]{0:T(256)S(1)}, f32[256]{0:T(256)}, u32[]{:S(2)}) copy-start(f32[256]{0:T(256)} %param.14) | copy-start | bytes 3076
  12.9 54.9 %copy-start.2 = (f32[256]{0:T(256)S(1)}, f32[256]{0:T(256)}, u32[]{:S(2)}) copy-start(f32[256]{0:T(256)} %param.15) | copy-start | bytes 3076
  13.9 13.9 %all-to-all-start.1 = ((bf16[8,128,256]{2,1,0:T(8,128)(2,1)}), bf16[8,128,256]{2,1,0:T(8,128)(2,1)S(1)}, u32[]{:S(2)}, u32[]{:S(2)}) async-start(bf16[8,128,256]{2,1,0:T(8,128)(2,1)} %copy.52), calls=%async_computation.1 | async-start | bytes 1048576 | tf_op jit(solution)/shard_map/all_to_all | solution.py:65
  204.4 0.7 copy-start.4
  549.6 14.2 %all-to-all-start.4 = ((bf16[8,128,256]{2,1,0:T(8,128)(2,1)}), bf16[8,128,256]{2,1,0:T(8,128)(2,1)S(1)}, u32[]{:S(2)}, u32[]{:S(2)}) async-start(bf16[8,128,256]{2,1,0:T(8,128)(2,1)} %copy.59), calls=%async_computation.4 | async-start | bytes 1048576 | tf_op jit(solution)/shard_map/all_to_all | solution.py:82
  688.3 41.5 %copy-start.3 = (s32[640]{0:T(1024)S(1)}, s32[640]{0:T(1024)}, u32[]{:S(2)}) copy-start(s32[640]{0:T(1024)} %param.12) | copy-start | bytes 7684
where the time goes:
time: 734 us; the launch traced here: 731 us
  blocking collectives  663 us (90%)
  waiting for transfers between devices  18.5 us (3%)
  other arithmetic  16.6 us (2%)
  starting transfers between devices  13.8 us (2%)
  matrix products  11.8 us (2%)
    psum x16, blocking collectives, class_balancer(): column = lax.psum(local_mass, ('grp', 'blk'))  635 us
  transfers between devices with their start and end apart: 3, of which 2 were waited for; matrix products, arithmetic and copies ran while one was open for 1% of the time, Pallas kernels for 0%

commit v1 on v0

--- a/solution.py
+++ b/solution.py
@@ -11,6 +11,13 @@
 keep_share = 0.8
 
 
+def total(local_mass):
+    devices = lax.axis_size(("grp", "blk"))
+    sent = jnp.broadcast_to(local_mass[None, :], (devices, local_mass.shape[0]))
+    parts = lax.all_to_all(sent, ("grp", "blk"), split_axis=0, concat_axis=0, tiled=True)
+    return jnp.sum(parts, axis=0)
+
+
 def class_balancer(label_masses, class_prior, class_target):
     kernel = label_masses + class_prior[None, :]
     scale_rows = None
@@ -20,7 +27,7 @@
             local_mass = jnp.sum(kernel, axis=0)
         else:
             local_mass = jnp.sum(scale_rows[:, None] * kernel, axis=0)
-        column = lax.psum(local_mass, ("grp", "blk"))
+        column = total(local_mass)
         scale_cols = class_target / column
         scale_rows = 1.0 / jnp.sum(kernel * scale_cols[None, :], axis=1)
     return scale_rows[:, None] * kernel * scale_cols[None, :]

time: 734 us -> 240 us (0.33)
  blocking collectives: 663 us -> 164 us
    psum x16 -> x0, blocking collectives: 635 us -> none  [class_balancer(): column = lax.psum(local_mass, ('grp', 'blk'))]
    all_to_all x0 -> x14, blocking collectives: none -> 127 us  [total(): lax.all_to_all(sent, ('grp', 'blk'), split_axis=0, concat_axis=0, tiled=T...]
    all_to_all x1 -> x2, blocking collectives: 13.9 us -> 24.3 us  [on_device(): lax.all_to_all(picked, 'blk', split_axis=0, concat_axis=0, tiled=True)]
  transfers between devices with their start and end apart: 3 -> 4, of which waited for: 2 -> 3; matrix products, arithmetic and copies ran while one was open for 1% -> 3% of each run, Pallas kernels for 0% -> 0%
where the time goes in v1:
time: 240 us; the launch traced here: 239 us
  blocking collectives  164 us (68%)
  waiting for transfers between devices  23.2 us (10%)
  other arithmetic  17.5 us (7%)
  starting transfers between devices  14.6 us (6%)
  matrix products  11.8 us (5%)
  local copies, waits for them, and re-layouts  6.08 us (3%)
    all_to_all x14, blocking collectives, total(): lax.all_to_all(sent, ('grp', 'blk'), split_axis=0, concat_axis=0, tiled=T...  127 us
    all_to_all x2, blocking collectives, on_device(): lax.all_to_all(picked, 'blk', split_axis=0, concat_axis=0, tiled=True)  24.3 us
    all_to_all x2, waiting for transfers between devices, total(): lax.all_to_all(sent, ('grp', 'blk'), split_axis=0, concat_axis=0, tiled=T...  13.6 us
    all_to_all x1, blocking collectives, on_device(): lax.all_to_all(parcel, 'blk', split_axis=0, concat_axis=0, tiled=True)  12.2 us
    all_to_all x1, waiting for transfers between devices, on_device(): lax.all_to_all(parcel, 'blk', split_axis=0, concat_axis=0, tiled=True)  9.65 us
    dot_general x2, matrix products, on_device(): paper_mass = jnp.einsum('sq,spc->qpc', paper_pick, products, precision=high)  7.59 us
    all_to_all x1, starting transfers between devices, on_device(): lax.all_to_all(author_pick, 'blk', split_axis=0, concat_axis=0, tiled=True)  5.17 us
    all_to_all x2, starting transfers between devices, total(): lax.all_to_all(sent, ('grp', 'blk'), split_axis=0, concat_axis=0, tiled=T...  5.13 us
  transfers between devices with their start and end apart: 4, of which 3 were waited for; matrix products, arithmetic and copies ran while one was open for 3% of the time, Pallas kernels for 0%

profile of v1, /device:TPU:0, one launch (start us, length us, event | category | flops | bytes accessed | tf_op | source)
XLA Modules:
  0.0 238.8 jit_solution(3056398550972807683)
XLA Ops:
  2.0 5.2 %all-to-all-start = ((bf16[8,1,2]{2,1,0:T(2,128)(2,1)}), bf16[8,1,2]{2,1,0:T(2,128)(2,1)S(1)}, u32[]{:S(2)}, u32[]{:S(2)}) async-start(bf16[8,1,2]{2,1,0:T(2,128)(2,1)} %compare_convert_fusion), calls=%async_computation | async-start | bytes 8192 | tf_op jit(solution)/shard_map/all_to_all | solution.py:73
  13.9 4.3 %all-to-all-start.1 = ((bf16[8,128,256]{2,1,0:T(8,128)(2,1)}), bf16[8,128,256]{2,1,0:T(8,128)(2,1)S(1)}, u32[]{:S(2)}, u32[]{:S(2)}) async-start(bf16[8,128,256]{2,1,0:T(8,128)(2,1)} %copy.86), calls=%async_computation.1 | async-start | bytes 1048576 | tf_op jit(solution)/shard_map/all_to_all | solution.py:72
  18.3 9.6 %all-to-all-done.1 = bf16[8,128,256]{2,1,0:T(8,128)(2,1)S(1)} async-done(((bf16[8,128,256]{2,1,0:T(8,128)(2,1)}), bf16[8,128,256]{2,1,0:T(8,128)(2,1)S(1)}, u32[]{:S(2)}, u32[]{:S(2)}) %all-to-all-start.1) | async-done | bytes 524320 | tf_op jit(solution)/shard_map/all_to_all | solution.py:72
  28.4 11.0 %all_to_all.126 = f32[32,1,256]{2,1,0:T(1,128)S(1)} all-to-all(f32[32,1,256]{2,1,0:T(1,128)S(1)} %broadcast_in_dim.35), channel_id=1, replica_groups=mesh['grp'=4,'blk'=8] {'grp','blk'}, dimensions={0} | all-to-all | bytes 65536 | tf_op jit(solution)/shard_map/all_to_all | solution.py:17
  40.0 8.9 %all_to_all.127 = f32[32,1,256]{2,1,0:T(1,128)S(1)} all-to-all(f32[32,1,256]{2,1,0:T(1,128)S(1)} %broadcast_in_dim.36), channel_id=1, replica_groups=mesh['grp'=4,'blk'=8] {'grp','blk'}, dimensions={0} | all-to-all | bytes 65536 | tf_op jit(solution)/shard_map/all_to_all | solution.py:17
  49.5 8.9 %all_to_all.128 = f32[32,1,256]{2,1,0:T(1,128)S(1)} all-to-all(f32[32,1,256]{2,1,0:T(1,128)S(1)} %broadcast_in_dim.37), channel_id=1, replica_groups=mesh['grp'=4,'blk'=8] {'grp','blk'}, dimensions={0} | all-to-all | bytes 65536 | tf_op jit(solution)/shard_map/all_to_all | solution.py:17
  59.0 8.9 %all_to_all.129 = f32[32,1,256]{2,1,0:T(1,128)S(1)} all-to-all(f32[32,1,256]{2,1,0:T(1,128)S(1)} %broadcast_in_dim.38), channel_id=1, replica_groups=mesh['grp'=4,'blk'=8] {'grp','blk'}, dimensions={0} | all-to-all | bytes 65536 | tf_op jit(solution)/shard_map/all_to_all | solution.py:17
  68.8 12.2 %all_to_all.130 = bf16[8,128,256]{2,1,0:T(8,128)(2,1)S(1)} all-to-all(bf16[8,128,256]{2,1,0:T(8,128)(2,1)S(1)} %copy.92), channel_id=1, replica_groups=mesh['grp'=4,'blk'=8] {'blk'}, dimensions={0} | all-to-all | bytes 1048576 | tf_op jit(solution)/shard_map/all_to_all | solution.py:89
  81.7 3.8 %fusion.45 = (f32[256]{0:T(256)S(1)}, f32[2,320,256]{2,0,1:T(2,128)S(1)}) fusion(f32[256]{0:T(256)S(1)} %copy-done.1, f32[8,320,256]{2,1,0:T(8,128)S(1)} %convolution_bitcast_fusion.1, f32[8]{0:T(128)S(1)} %compare_convert_fusion.1, s32[8]{0:T(128)S(1)} %copy-done.4), kind=kOutput, calls=%fused_computation.110 | convolution fusion | flops 16056096 | bytes 3278912 | tf_op jit(solution)/shard_map/sq,spc->qpc/dot_general | solution.py:93
  85.5 8.9 %all_to_all.131 = f32[32,1,256]{2,1,0:T(1,128)S(1)} all-to-all(f32[32,1,256]{2,1,0:T(1,128)S(1)} %broadcast_in_dim.39), channel_id=1, replica_groups=mesh['grp'=4,'blk'=8] {'grp','blk'}, dimensions={0} | all-to-all | bytes 65536 | tf_op jit(solution)/shard_map/all_to_all | solution.py:17
  95.4 8.9 %all_to_all.132 = f32[32,1,256]{2,1,0:T(1,128)S(1)} all-to-all(f32[32,1,256]{2,1,0:T(1,128)S(1)} %broadcast_in_dim.40), channel_id=1, replica_groups=mesh['grp'=4,'blk'=8] {'grp','blk'}, dimensions={0} | all-to-all | bytes 65536 | tf_op jit(solution)/shard_map/all_to_all | solution.py:17
  105.3 8.9 %all_to_all.133 = f32[32,1,256]{2,1,0:T(1,128)S(1)} all-to-all(f32[32,1,256]{2,1,0:T(1,128)S(1)} %broadcast_in_dim.41), channel_id=1, replica_groups=mesh['grp'=4,'blk'=8] {'grp','blk'}, dimensions={0} | all-to-all | bytes 65536 | tf_op jit(solution)/shard_map/all_to_all | solution.py:17
  115.3 8.9 %all_to_all.134 = f32[32,1,256]{2,1,0:T(1,128)S(1)} all-to-all(f32[32,1,256]{2,1,0:T(1,128)S(1)} %broadcast_in_dim.42), channel_id=1, replica_groups=mesh['grp'=4,'blk'=8] {'grp','blk'}, dimensions={0} | all-to-all | bytes 65536 | tf_op jit(solution)/shard_map/all_to_all | solution.py:17
  127.8 12.2 %all_to_all.135 = bf16[8,128,256]{2,1,0:T(8,128)(2,1)S(1)} all-to-all(bf16[8,128,256]{2,1,0:T(8,128)(2,1)S(1)} %copy.99), channel_id=1, replica_groups=mesh['grp'=4,'blk'=8] {'blk'}, dimensions={0} | all-to-all | bytes 1048576 | tf_op jit(solution)/shard_map/all_to_all | solution.py:72
  140.4 8.9 %all_to_all.136 = f32[32,1,256]{2,1,0:T(1,128)S(1)} all-to-all(f32[32,1,256]{2,1,0:T(1,128)S(1)} %broadcast_in_dim.43), channel_id=1, replica_groups=mesh['grp'=4,'blk'=8] {'grp','blk'}, dimensions={0} | all-to-all | bytes 65536 | tf_op jit(solution)/shard_map/all_to_all | solution.py:17
  149.9 8.9 %all_to_all.137 = f32[32,1,256]{2,1,0:T(1,128)S(1)} all-to-all(f32[32,1,256]{2,1,0:T(1,128)S(1)} %broadcast_in_dim.44), channel_id=1, replica_groups=mesh['grp'=4,'blk'=8] {'grp','blk'}, dimensions={0} | all-to-all | bytes 65536 | tf_op jit(solution)/shard_map/all_to_all | solution.py:17
  159.4 8.9 %all_to_all.138 = f32[32,1,256]{2,1,0:T(1,128)S(1)} all-to-all(f32[32,1,256]{2,1,0:T(1,128)S(1)} %broadcast_in_dim.45), channel_id=1, replica_groups=mesh['grp'=4,'blk'=8] {'grp','blk'}, dimensions={0} | all-to-all | bytes 65536 | tf_op jit(solution)/shard_map/all_to_all | solution.py:17
  168.9 8.9 %all_to_all.139 = f32[32,1,256]{2,1,0:T(1,128)S(1)} all-to-all(f32[32,1,256]{2,1,0:T(1,128)S(1)} %broadcast_in_dim.46), channel_id=1, replica_groups=mesh['grp'=4,'blk'=8] {'grp','blk'}, dimensions={0} | all-to-all | bytes 65536 | tf_op jit(solution)/shard_map/all_to_all | solution.py:17
  178.8 12.2 %all_to_all.140 = bf16[8,128,256]{2,1,0:T(8,128)(2,1)S(1)} all-to-all(bf16[8,128,256]{2,1,0:T(8,128)(2,1)S(1)} %copy.105), channel_id=1, replica_groups=mesh['grp'=4,'blk'=8] {'blk'}, dimensions={0} | all-to-all | bytes 1048576 | tf_op jit(solution)/shard_map/all_to_all | solution.py:89
  191.4 3.8 %fusion.43 = (f32[256]{0:T(256)S(1)}, f32[2,320,256]{2,0,1:T(2,128)S(1)}) fusion(f32[256]{0:T(256)S(1)} %copy-done.1, f32[8,320,256]{2,1,0:T(8,128)S(1)} %convolution_bitcast_fusion, f32[8]{0:T(128)S(1)} %compare_convert_fusion.1, s32[8]{0:T(128)S(1)} %copy-done.4), kind=kOutput, calls=%fused_computation.108 | convolution fusion | flops 16056096 | bytes 3278912 | tf_op jit(solution)/shard_map/sq,spc->qpc/dot_general | solution.py:93
  195.2 8.9 %all_to_all.141 = f32[32,1,256]{2,1,0:T(1,128)S(1)} all-to-all(f32[32,1,256]{2,1,0:T(1,128)S(1)} %broadcast_in_dim.47), channel_id=1, replica_groups=mesh['grp'=4,'blk'=8] {'grp','blk'}, dimensions={0} | all-to-all | bytes 65536 | tf_op jit(solution)/shard_map/all_to_all | solution.py:17
  205.2 8.9 %all_to_all.142 = f32[32,1,256]{2,1,0:T(1,128)S(1)} all-to-all(f32[32,1,256]{2,1,0:T(1,128)S(1)} %broadcast_in_dim.48), channel_id=1, replica_groups=mesh['grp'=4,'blk'=8] {'grp','blk'}, dimensions={0} | all-to-all | bytes 65536 | tf_op jit(solution)/shard_map/all_to_all | solution.py:17
  218.4 7.2 %all-to-all-done.19 = f32[32,1,256]{2,1,0:T(1,128)S(1)} async-done(((f32[32,1,256]{2,1,0:T(1,128)}), f32[32,1,256]{2,1,0:T(1,128)S(1)}, u32[]{:S(2)}, u32[]{:S(2)}) %all-to-all-start.19) | async-done | bytes 32800 | tf_op jit(solution)/shard_map/all_to_all | solution.py:17
  230.6 6.4 %all-to-all-done.20 = f32[32,1,256]{2,1,0:T(1,128)S(1)} async-done(((f32[32,1,256]{2,1,0:T(1,128)}), f32[32,1,256]{2,1,0:T(1,128)S(1)}, u32[]{:S(2)}, u32[]{:S(2)}) %all-to-all-start.20) | async-done | bytes 32800 | tf_op jit(solution)/shard_map/all_to_all | solution.py:17
  (140 shorter events, 32.9 us)
Async XLA Ops:
  0.6 11.5 %copy-start = (bf16[8,320,128]{2,1,0:T(8,128)(2,1)S(1)}, bf16[8,320,128]{2,1,0:T(8,128)(2,1)}, u32[]{:S(2)}) copy-start(bf16[8,320,128]{2,1,0:T(8,128)(2,1)} %param.8) | copy-start | bytes 1966084
  2.0 11.9 %all-to-all-start = ((bf16[8,1,2]{2,1,0:T(2,128)(2,1)}), bf16[8,1,2]{2,1,0:T(2,128)(2,1)S(1)}, u32[]{:S(2)}, u32[]{:S(2)}) async-start(bf16[8,1,2]{2,1,0:T(2,128)(2,1)} %compare_convert_fusion), calls=%async_computation | async-start | bytes 8192 | tf_op jit(solution)/shard_map/all_to_all | solution.py:73
  12.9 15.1 %copy-start.1 = (f32[256]{0:T(256)S(1)}, f32[256]{0:T(256)}, u32[]{:S(2)}) copy-start(f32[256]{0:T(256)} %param.14) | copy-start | bytes 3076
  13.9 25.6 %copy-start.2 = (f32[256]{0:T(256)S(1)}, f32[256]{0:T(256)}, u32[]{:S(2)}) copy-start(f32[256]{0:T(256)} %param.15) | copy-start | bytes 3076
  13.9 14.1 %all-to-all-start.1 = ((bf16[8,128,256]{2,1,0:T(8,128)(2,1)}), bf16[8,128,256]{2,1,0:T(8,128)(2,1)S(1)}, u32[]{:S(2)}, u32[]{:S(2)}) async-start(bf16[8,128,256]{2,1,0:T(8,128)(2,1)} %copy.86), calls=%async_computation.1 | async-start | bytes 1048576 | tf_op jit(solution)/shard_map/all_to_all | solution.py:72
  81.0 0.7 copy-start.4
  215.7 9.8 %all-to-all-start.19 = ((f32[32,1,256]{2,1,0:T(1,128)}), f32[32,1,256]{2,1,0:T(1,128)S(1)}, u32[]{:S(2)}, u32[]{:S(2)}) async-start(f32[32,1,256]{2,1,0:T(1,128)} %broadcast_in_dim.49), calls=%async_computation.19 | async-start | bytes 65536 | tf_op jit(solution)/shard_map/all_to_all | solution.py:17
  227.1 9.8 %all-to-all-start.20 = ((f32[32,1,256]{2,1,0:T(1,128)}), f32[32,1,256]{2,1,0:T(1,128)S(1)}, u32[]{:S(2)}, u32[]{:S(2)}) async-start(f32[32,1,256]{2,1,0:T(1,128)} %broadcast_in_dim.50), calls=%async_computation.20 | async-start | bytes 65536 | tf_op jit(solution)/shard_map/all_to_all | solution.py:17
  230.5 7.1 %copy-start.3 = (s32[640]{0:T(1024)S(1)}, s32[640]{0:T(1024)}, u32[]{:S(2)}) copy-start(s32[640]{0:T(1024)} %param.12) | copy-start | bytes 7684

commit v2 on v0

--- a/solution.py
+++ b/solution.py
@@ -11,6 +11,22 @@
 keep_share = 0.8
 
 
+def axis_total(value, axis):
+    size = lax.axis_size(axis)
+    parts = [value]
+    for shift in range(1, size):
+        pairs = [(i, (i + shift) % size) for i in range(size)]
+        parts.append(lax.ppermute(value, axis, pairs))
+    while len(parts) > 1:
+        half = len(parts) // 2
+        parts = [parts[i] + parts[i + half] for i in range(half)] + parts[2 * half :]
+    return parts[0]
+
+
+def total(local_mass):
+    return axis_total(axis_total(local_mass, "blk"), "grp")
+
+
 def class_balancer(label_masses, class_prior, class_target):
     kernel = label_masses + class_prior[None, :]
     scale_rows = None
@@ -20,7 +36,7 @@
             local_mass = jnp.sum(kernel, axis=0)
         else:
             local_mass = jnp.sum(scale_rows[:, None] * kernel, axis=0)
-        column = lax.psum(local_mass, ("grp", "blk"))
+        column = total(local_mass)
         scale_cols = class_target / column
         scale_rows = 1.0 / jnp.sum(kernel * scale_cols[None, :], axis=1)
     return scale_rows[:, None] * kernel * scale_cols[None, :]

time: 734 us -> 372 us (0.51)
  blocking collectives: 663 us -> 36.9 us
  starting transfers between devices: 13.8 us -> 161 us
  waiting for transfers between devices: 18.5 us -> 132 us
    psum x16 -> x0, blocking collectives: 635 us -> none  [class_balancer(): column = lax.psum(local_mass, ('grp', 'blk'))]
    ppermute x0 -> x160, starting transfers between devices: none -> 151 us  [axis_total(): parts.append(lax.ppermute(value, axis, pairs))]
    ppermute x0 -> x160, waiting for transfers between devices: none -> 123 us  [axis_total(): parts.append(lax.ppermute(value, axis, pairs))]
    all_to_all x1 -> x2, blocking collectives: 13.9 us -> 24.8 us  [on_device(): lax.all_to_all(picked, 'blk', split_axis=0, concat_axis=0, tiled=True)]
    all_to_all x1 -> x0, waiting for transfers between devices: 8.83 us -> none  [on_device(): lax.all_to_all(picked, 'blk', split_axis=0, concat_axis=0, tiled=True)]
  transfers between devices with their start and end apart: 3 -> 162, of which waited for: 2 -> 80; matrix products, arithmetic and copies ran while one was open for 1% -> 2% of each run, Pallas kernels for 0% -> 0%
where the time goes in v2:
time: 372 us; the launch traced here: 366 us
  starting transfers between devices  161 us (43%)
  waiting for transfers between devices  132 us (35%)
  blocking collectives  36.9 us (10%)
  other arithmetic  16.8 us (5%)
  matrix products  11.8 us (3%)
  local copies, waits for them, and re-layouts  4.51 us (1%)
    ppermute x160, starting transfers between devices, axis_total(): parts.append(lax.ppermute(value, axis, pairs))  151 us
    ppermute x160, waiting for transfers between devices, axis_total(): parts.append(lax.ppermute(value, axis, pairs))  123 us
    all_to_all x2, blocking collectives, on_device(): lax.all_to_all(picked, 'blk', split_axis=0, concat_axis=0, tiled=True)  24.8 us
    all_to_all x1, blocking collectives, on_device(): lax.all_to_all(parcel, 'blk', split_axis=0, concat_axis=0, tiled=True)  12.2 us
    all_to_all x1, waiting for transfers between devices, on_device(): lax.all_to_all(parcel, 'blk', split_axis=0, concat_axis=0, tiled=True)  9.65 us
    dot_general x2, matrix products, on_device(): paper_mass = jnp.einsum('sq,spc->qpc', paper_pick, products, precision=high)  7.59 us
  transfers between devices with their start and end apart: 162, of which 80 were waited for; matrix products, arithmetic and copies ran while one was open for 2% of the time, Pallas kernels for 0%

profile of v2, /device:TPU:0, one launch (start us, length us, event | category | flops | bytes accessed | tf_op | source)
XLA Modules:
  0.0 365.5 jit_solution(6700881376784621166)
XLA Ops:
  2.0 5.2 %all-to-all-start = ((bf16[8,1,2]{2,1,0:T(2,128)(2,1)}), bf16[8,1,2]{2,1,0:T(2,128)(2,1)S(1)}, u32[]{:S(2)}, u32[]{:S(2)}) async-start(bf16[8,1,2]{2,1,0:T(2,128)(2,1)} %compare_convert_fusion), calls=%async_computation | async-start | bytes 8192 | tf_op jit(solution)/shard_map/all_to_all | solution.py:82
  13.9 4.2 %all-to-all-start.1 = ((bf16[8,128,256]{2,1,0:T(8,128)(2,1)}), bf16[8,128,256]{2,1,0:T(8,128)(2,1)S(1)}, u32[]{:S(2)}, u32[]{:S(2)}) async-start(bf16[8,128,256]{2,1,0:T(8,128)(2,1)} %copy.52), calls=%async_computation.1 | async-start | bytes 1048576 | tf_op jit(solution)/shard_map/all_to_all | solution.py:81
  18.2 9.6 %all-to-all-done.1 = bf16[8,128,256]{2,1,0:T(8,128)(2,1)S(1)} async-done(((bf16[8,128,256]{2,1,0:T(8,128)(2,1)}), bf16[8,128,256]{2,1,0:T(8,128)(2,1)S(1)}, u32[]{:S(2)}, u32[]{:S(2)}) %all-to-all-start.1) | async-done | bytes 524320 | tf_op jit(solution)/shard_map/all_to_all | solution.py:81
  42.0 4.1 %collective-permute-done.8 = f32[256]{0:T(256)S(1)} collective-permute-done((f32[256]{0:T(256)S(1)}, f32[256]{0:T(256)S(1)}, u32[]{:S(2)}, u32[]{:S(2)}) %collective-permute-start.8) | collective-permute-done | bytes 1056 | tf_op jit(solution)/shard_map/ppermute | solution.py:19
  59.7 4.1 %collective-permute-done.18 = f32[256]{0:T(256)S(1)} collective-permute-done((f32[256]{0:T(256)S(1)}, f32[256]{0:T(256)S(1)}, u32[]{:S(2)}, u32[]{:S(2)}) %collective-permute-start.18) | collective-permute-done | bytes 1056 | tf_op jit(solution)/shard_map/ppermute | solution.py:19
  77.3 4.1 %collective-permute-done.28 = f32[256]{0:T(256)S(1)} collective-permute-done((f32[256]{0:T(256)S(1)}, f32[256]{0:T(256)S(1)}, u32[]{:S(2)}, u32[]{:S(2)}) %collective-permute-start.28) | collective-permute-done | bytes 1056 | tf_op jit(solution)/shard_map/ppermute | solution.py:19
  95.0 4.1 %collective-permute-done.38 = f32[256]{0:T(256)S(1)} collective-permute-done((f32[256]{0:T(256)S(1)}, f32[256]{0:T(256)S(1)}, u32[]{:S(2)}, u32[]{:S(2)}) %collective-permute-start.38) | collective-permute-done | bytes 1056 | tf_op jit(solution)/shard_map/ppermute | solution.py:19
  99.9 12.3 %all_to_all.30 = bf16[8,128,256]{2,1,0:T(8,128)(2,1)S(1)} all-to-all(bf16[8,128,256]{2,1,0:T(8,128)(2,1)S(1)} %copy.54), channel_id=1, replica_groups=mesh['grp'=4,'blk'=8] {'blk'}, dimensions={0} | all-to-all | bytes 1048576 | tf_op jit(solution)/shard_map/all_to_all | solution.py:98
  112.8 3.8 %fusion.45 = (f32[256]{0:T(256)S(1)}, f32[2,320,256]{2,0,1:T(2,128)S(1)}) fusion(f32[256]{0:T(256)S(1)} %copy-done.1, f32[8,320,256]{2,1,0:T(8,128)S(1)} %convolution_bitcast_fusion.1, f32[8]{0:T(128)S(1)} %compare_convert_fusion.1, s32[8]{0:T(128)S(1)} %copy-done.4), kind=kOutput, calls=%fused_computation.142 | convolution fusion | flops 16056096 | bytes 3278912 | tf_op jit(solution)/shard_map/sq,spc->qpc/dot_general | solution.py:102
  129.7 4.1 %collective-permute-done.48 = f32[256]{0:T(256)S(1)} collective-permute-done((f32[256]{0:T(256)S(1)}, f32[256]{0:T(256)S(1)}, u32[]{:S(2)}, u32[]{:S(2)}) %collective-permute-start.48) | collective-permute-done | bytes 1056 | tf_op jit(solution)/shard_map/ppermute | solution.py:19
  147.8 4.1 %collective-permute-done.58 = f32[256]{0:T(256)S(1)} collective-permute-done((f32[256]{0:T(256)S(1)}, f32[256]{0:T(256)S(1)}, u32[]{:S(2)}, u32[]{:S(2)}) %collective-permute-start.58) | collective-permute-done | bytes 1056 | tf_op jit(solution)/shard_map/ppermute | solution.py:19
  165.9 4.1 %collective-permute-done.68 = f32[256]{0:T(256)S(1)} collective-permute-done((f32[256]{0:T(256)S(1)}, f32[256]{0:T(256)S(1)}, u32[]{:S(2)}, u32[]{:S(2)}) %collective-permute-start.68) | collective-permute-done | bytes 1056 | tf_op jit(solution)/shard_map/ppermute | solution.py:19
  183.9 4.3 %collective-permute-done.78 = f32[256]{0:T(256)S(1)} collective-permute-done((f32[256]{0:T(256)S(1)}, f32[256]{0:T(256)S(1)}, u32[]{:S(2)}, u32[]{:S(2)}) %collective-permute-start.78) | collective-permute-done | bytes 1056 | tf_op jit(solution)/shard_map/ppermute | solution.py:19
  191.8 12.2 %all_to_all.31 = bf16[8,128,256]{2,1,0:T(8,128)(2,1)S(1)} all-to-all(bf16[8,128,256]{2,1,0:T(8,128)(2,1)S(1)} %copy.57), channel_id=1, replica_groups=mesh['grp'=4,'blk'=8] {'blk'}, dimensions={0} | all-to-all | bytes 1048576 | tf_op jit(solution)/shard_map/all_to_all | solution.py:81
  217.4 4.1 %collective-permute-done.88 = f32[256]{0:T(256)S(1)} collective-permute-done((f32[256]{0:T(256)S(1)}, f32[256]{0:T(256)S(1)}, u32[]{:S(2)}, u32[]{:S(2)}) %collective-permute-start.88) | collective-permute-done | bytes 1056 | tf_op jit(solution)/shard_map/ppermute | solution.py:19
  235.1 4.1 %collective-permute-done.98 = f32[256]{0:T(256)S(1)} collective-permute-done((f32[256]{0:T(256)S(1)}, f32[256]{0:T(256)S(1)}, u32[]{:S(2)}, u32[]{:S(2)}) %collective-permute-start.98) | collective-permute-done | bytes 1056 | tf_op jit(solution)/shard_map/ppermute | solution.py:19
  252.7 4.1 %collective-permute-done.108 = f32[256]{0:T(256)S(1)} collective-permute-done((f32[256]{0:T(256)S(1)}, f32[256]{0:T(256)S(1)}, u32[]{:S(2)}, u32[]{:S(2)}) %collective-permute-start.108) | collective-permute-done | bytes 1056 | tf_op jit(solution)/shard_map/ppermute | solution.py:19
  270.3 4.1 %collective-permute-done.118 = f32[256]{0:T(256)S(1)} collective-permute-done((f32[256]{0:T(256)S(1)}, f32[256]{0:T(256)S(1)}, u32[]{:S(2)}, u32[]{:S(2)}) %collective-permute-start.118) | collective-permute-done | bytes 1056 | tf_op jit(solution)/shard_map/ppermute | solution.py:19
  275.2 12.4 %all_to_all.32 = bf16[8,128,256]{2,1,0:T(8,128)(2,1)S(1)} all-to-all(bf16[8,128,256]{2,1,0:T(8,128)(2,1)S(1)} %copy.59), channel_id=1, replica_groups=mesh['grp'=4,'blk'=8] {'blk'}, dimensions={0} | all-to-all | bytes 1048576 | tf_op jit(solution)/shard_map/all_to_all | solution.py:98
  288.1 3.8 %fusion.43 = (f32[256]{0:T(256)S(1)}, f32[2,320,256]{2,0,1:T(2,128)S(1)}) fusion(f32[256]{0:T(256)S(1)} %copy-done.1, f32[8,320,256]{2,1,0:T(8,128)S(1)} %convolution_bitcast_fusion, f32[8]{0:T(128)S(1)} %compare_convert_fusion.1, s32[8]{0:T(128)S(1)} %copy-done.4), kind=kOutput, calls=%fused_computation.140 | convolution fusion | flops 16056096 | bytes 3278912 | tf_op jit(solution)/shard_map/sq,spc->qpc/dot_general | solution.py:102
  305.0 4.1 %collective-permute-done.128 = f32[256]{0:T(256)S(1)} collective-permute-done((f32[256]{0:T(256)S(1)}, f32[256]{0:T(256)S(1)}, u32[]{:S(2)}, u32[]{:S(2)}) %collective-permute-start.128) | collective-permute-done | bytes 1056 | tf_op jit(solution)/shard_map/ppermute | solution.py:19
  323.1 4.1 %collective-permute-done.138 = f32[256]{0:T(256)S(1)} collective-permute-done((f32[256]{0:T(256)S(1)}, f32[256]{0:T(256)S(1)}, u32[]{:S(2)}, u32[]{:S(2)}) %collective-permute-start.138) | collective-permute-done | bytes 1056 | tf_op jit(solution)/shard_map/ppermute | solution.py:19
  341.1 4.1 %collective-permute-done.148 = f32[256]{0:T(256)S(1)} collective-permute-done((f32[256]{0:T(256)S(1)}, f32[256]{0:T(256)S(1)}, u32[]{:S(2)}, u32[]{:S(2)}) %collective-permute-start.148) | collective-permute-done | bytes 1056 | tf_op jit(solution)/shard_map/ppermute | solution.py:19
  359.4 3.9 %collective-permute-done.158 = f32[256]{0:T(256)S(1)} collective-permute-done((f32[256]{0:T(256)S(1)}, f32[256]{0:T(256)S(1)}, u32[]{:S(2)}, u32[]{:S(2)}) %collective-permute-start.158) | collective-permute-done | bytes 1056 | tf_op jit(solution)/shard_map/ppermute | solution.py:19
  (426 shorter events, 234.5 us)
Async XLA Ops:
  2.0 11.9 %all-to-all-start = ((bf16[8,1,2]{2,1,0:T(2,128)(2,1)}), bf16[8,1,2]{2,1,0:T(2,128)(2,1)S(1)}, u32[]{:S(2)}, u32[]{:S(2)}) async-start(bf16[8,1,2]{2,1,0:T(2,128)(2,1)} %compare_convert_fusion), calls=%async_computation | async-start | bytes 8192 | tf_op jit(solution)/shard_map/all_to_all | solution.py:82
  13.9 13.9 %all-to-all-start.1 = ((bf16[8,128,256]{2,1,0:T(8,128)(2,1)}), bf16[8,128,256]{2,1,0:T(8,128)(2,1)S(1)}, u32[]{:S(2)}, u32[]{:S(2)}) async-start(bf16[8,128,256]{2,1,0:T(8,128)(2,1)} %copy.52), calls=%async_computation.1 | async-start | bytes 1048576 | tf_op jit(solution)/shard_map/all_to_all | solution.py:81
  40.7 5.4 %collective-permute-start.8 = (f32[256]{0:T(256)S(1)}, f32[256]{0:T(256)S(1)}, u32[]{:S(2)}, u32[]{:S(2)}) collective-permute-start(f32[256]{0:T(256)S(1)} %add_add_fusion.15), channel_id=1, source_target_pairs={{0,8},{8,16},{16,24},{24,0},{1,9},{9,17},{17,25},{25,1},{2,10},{10... | collective-permute-start | bytes 3080 | tf_op jit(solution)/shard_map/ppermute | solution.py:19
  40.7 5.4 %collective-permute-start.7 = (f32[256]{0:T(256)S(1)}, f32[256]{0:T(256)S(1)}, u32[]{:S(2)}, u32[]{:S(2)}) collective-permute-start(f32[256]{0:T(256)S(1)} %add_add_fusion.15), channel_id=1, source_target_pairs={{0,16},{8,24},{16,0},{24,8},{1,17},{9,25},{17,1},{25,9},{2,18},{10... | collective-permute-start | bytes 3080 | tf_op jit(solution)/shard_map/ppermute | solution.py:19
  58.4 5.4 %collective-permute-start.18 = (f32[256]{0:T(256)S(1)}, f32[256]{0:T(256)S(1)}, u32[]{:S(2)}, u32[]{:S(2)}) collective-permute-start(f32[256]{0:T(256)S(1)} %add_add_fusion.14), channel_id=1, source_target_pairs={{0,8},{8,16},{16,24},{24,0},{1,9},{9,17},{17,25},{25,1},{2,10},{10... | collective-permute-start | bytes 3080 | tf_op jit(solution)/shard_map/ppermute | solution.py:19
  58.4 5.4 %collective-permute-start.17 = (f32[256]{0:T(256)S(1)}, f32[256]{0:T(256)S(1)}, u32[]{:S(2)}, u32[]{:S(2)}) collective-permute-start(f32[256]{0:T(256)S(1)} %add_add_fusion.14), channel_id=1, source_target_pairs={{0,16},{8,24},{16,0},{24,8},{1,17},{9,25},{17,1},{25,9},{2,18},{10... | collective-permute-start | bytes 3080 | tf_op jit(solution)/shard_map/ppermute | solution.py:19
  76.0 5.4 %collective-permute-start.28 = (f32[256]{0:T(256)S(1)}, f32[256]{0:T(256)S(1)}, u32[]{:S(2)}, u32[]{:S(2)}) collective-permute-start(f32[256]{0:T(256)S(1)} %add_add_fusion.13), channel_id=1, source_target_pairs={{0,8},{8,16},{16,24},{24,0},{1,9},{9,17},{17,25},{25,1},{2,10},{10... | collective-permute-start | bytes 3080 | tf_op jit(solution)/shard_map/ppermute | solution.py:19
  76.0 5.4 %collective-permute-start.27 = (f32[256]{0:T(256)S(1)}, f32[256]{0:T(256)S(1)}, u32[]{:S(2)}, u32[]{:S(2)}) collective-permute-start(f32[256]{0:T(256)S(1)} %add_add_fusion.13), channel_id=1, source_target_pairs={{0,16},{8,24},{16,0},{24,8},{1,17},{9,25},{17,1},{25,9},{2,18},{10... | collective-permute-start | bytes 3080 | tf_op jit(solution)/shard_map/ppermute | solution.py:19
  93.7 5.4 %collective-permute-start.38 = (f32[256]{0:T(256)S(1)}, f32[256]{0:T(256)S(1)}, u32[]{:S(2)}, u32[]{:S(2)}) collective-permute-start(f32[256]{0:T(256)S(1)} %add_add_fusion.12), channel_id=1, source_target_pairs={{0,8},{8,16},{16,24},{24,0},{1,9},{9,17},{17,25},{25,1},{2,10},{10... | collective-permute-start | bytes 3080 | tf_op jit(solution)/shard_map/ppermute | solution.py:19
  93.7 5.4 %collective-permute-start.37 = (f32[256]{0:T(256)S(1)}, f32[256]{0:T(256)S(1)}, u32[]{:S(2)}, u32[]{:S(2)}) collective-permute-start(f32[256]{0:T(256)S(1)} %add_add_fusion.12), channel_id=1, source_target_pairs={{0,16},{8,24},{16,0},{24,8},{1,17},{9,25},{17,1},{25,9},{2,18},{10... | collective-permute-start | bytes 3080 | tf_op jit(solution)/shard_map/ppermute | solution.py:19
  128.4 5.4 %collective-permute-start.48 = (f32[256]{0:T(256)S(1)}, f32[256]{0:T(256)S(1)}, u32[]{:S(2)}, u32[]{:S(2)}) collective-permute-start(f32[256]{0:T(256)S(1)} %add_add_fusion.11), channel_id=1, source_target_pairs={{0,8},{8,16},{16,24},{24,0},{1,9},{9,17},{17,25},{25,1},{2,10},{10... | collective-permute-start | bytes 3080 | tf_op jit(solution)/shard_map/ppermute | solution.py:19
  128.4 5.4 %collective-permute-start.47 = (f32[256]{0:T(256)S(1)}, f32[256]{0:T(256)S(1)}, u32[]{:S(2)}, u32[]{:S(2)}) collective-permute-start(f32[256]{0:T(256)S(1)} %add_add_fusion.11), channel_id=1, source_target_pairs={{0,16},{8,24},{16,0},{24,8},{1,17},{9,25},{17,1},{25,9},{2,18},{10... | collective-permute-start | bytes 3080 | tf_op jit(solution)/shard_map/ppermute | solution.py:19
  146.5 5.4 %collective-permute-start.58 = (f32[256]{0:T(256)S(1)}, f32[256]{0:T(256)S(1)}, u32[]{:S(2)}, u32[]{:S(2)}) collective-permute-start(f32[256]{0:T(256)S(1)} %add_add_fusion.10), channel_id=1, source_target_pairs={{0,8},{8,16},{16,24},{24,0},{1,9},{9,17},{17,25},{25,1},{2,10},{10... | collective-permute-start | bytes 3080 | tf_op jit(solution)/shard_map/ppermute | solution.py:19
  146.5 5.4 %collective-permute-start.57 = (f32[256]{0:T(256)S(1)}, f32[256]{0:T(256)S(1)}, u32[]{:S(2)}, u32[]{:S(2)}) collective-permute-start(f32[256]{0:T(256)S(1)} %add_add_fusion.10), channel_id=1, source_target_pairs={{0,16},{8,24},{16,0},{24,8},{1,17},{9,25},{17,1},{25,9},{2,18},{10... | collective-permute-start | bytes 3080 | tf_op jit(solution)/shard_map/ppermute | solution.py:19
  164.6 5.4 %collective-permute-start.68 = (f32[256]{0:T(256)S(1)}, f32[256]{0:T(256)S(1)}, u32[]{:S(2)}, u32[]{:S(2)}) collective-permute-start(f32[256]{0:T(256)S(1)} %add_add_fusion.9), channel_id=1, source_target_pairs={{0,8},{8,16},{16,24},{24,0},{1,9},{9,17},{17,25},{25,1},{2,10},{10... | collective-permute-start | bytes 3080 | tf_op jit(solution)/shard_map/ppermute | solution.py:19
  164.6 5.4 %collective-permute-start.67 = (f32[256]{0:T(256)S(1)}, f32[256]{0:T(256)S(1)}, u32[]{:S(2)}, u32[]{:S(2)}) collective-permute-start(f32[256]{0:T(256)S(1)} %add_add_fusion.9), channel_id=1, source_target_pairs={{0,16},{8,24},{16,0},{24,8},{1,17},{9,25},{17,1},{25,9},{2,18},{10... | collective-permute-start | bytes 3080 | tf_op jit(solution)/shard_map/ppermute | solution.py:19
  182.6 5.6 %collective-permute-start.78 = (f32[256]{0:T(256)S(1)}, f32[256]{0:T(256)S(1)}, u32[]{:S(2)}, u32[]{:S(2)}) collective-permute-start(f32[256]{0:T(256)S(1)} %add_add_fusion.8), channel_id=1, source_target_pairs={{0,8},{8,16},{16,24},{24,0},{1,9},{9,17},{17,25},{25,1},{2,10},{10... | collective-permute-start | bytes 3080 | tf_op jit(solution)/shard_map/ppermute | solution.py:19
  216.1 5.4 %collective-permute-start.88 = (f32[256]{0:T(256)S(1)}, f32[256]{0:T(256)S(1)}, u32[]{:S(2)}, u32[]{:S(2)}) collective-permute-start(f32[256]{0:T(256)S(1)} %add_add_fusion.7), channel_id=1, source_target_pairs={{0,8},{8,16},{16,24},{24,0},{1,9},{9,17},{17,25},{25,1},{2,10},{10... | collective-permute-start | bytes 3080 | tf_op jit(solution)/shard_map/ppermute | solution.py:19
  216.1 5.4 %collective-permute-start.87 = (f32[256]{0:T(256)S(1)}, f32[256]{0:T(256)S(1)}, u32[]{:S(2)}, u32[]{:S(2)}) collective-permute-start(f32[256]{0:T(256)S(1)} %add_add_fusion.7), channel_id=1, source_target_pairs={{0,16},{8,24},{16,0},{24,8},{1,17},{9,25},{17,1},{25,9},{2,18},{10... | collective-permute-start | bytes 3080 | tf_op jit(solution)/shard_map/ppermute | solution.py:19
  233.8 5.4 %collective-permute-start.98 = (f32[256]{0:T(256)S(1)}, f32[256]{0:T(256)S(1)}, u32[]{:S(2)}, u32[]{:S(2)}) collective-permute-start(f32[256]{0:T(256)S(1)} %add_add_fusion.6), channel_id=1, source_target_pairs={{0,8},{8,16},{16,24},{24,0},{1,9},{9,17},{17,25},{25,1},{2,10},{10... | collective-permute-start | bytes 3080 | tf_op jit(solution)/shard_map/ppermute | solution.py:19
  233.8 5.4 %collective-permute-start.97 = (f32[256]{0:T(256)S(1)}, f32[256]{0:T(256)S(1)}, u32[]{:S(2)}, u32[]{:S(2)}) collective-permute-start(f32[256]{0:T(256)S(1)} %add_add_fusion.6), channel_id=1, source_target_pairs={{0,16},{8,24},{16,0},{24,8},{1,17},{9,25},{17,1},{25,9},{2,18},{10... | collective-permute-start | bytes 3080 | tf_op jit(solution)/shard_map/ppermute | solution.py:19
  251.4 5.4 %collective-permute-start.108 = (f32[256]{0:T(256)S(1)}, f32[256]{0:T(256)S(1)}, u32[]{:S(2)}, u32[]{:S(2)}) collective-permute-start(f32[256]{0:T(256)S(1)} %add_add_fusion.5), channel_id=1, source_target_pairs={{0,8},{8,16},{16,24},{24,0},{1,9},{9,17},{17,25},{25,1},{2,10},{10... | collective-permute-start | bytes 3080 | tf_op jit(solution)/shard_map/ppermute | solution.py:19
  251.4 5.4 %collective-permute-start.107 = (f32[256]{0:T(256)S(1)}, f32[256]{0:T(256)S(1)}, u32[]{:S(2)}, u32[]{:S(2)}) collective-permute-start(f32[256]{0:T(256)S(1)} %add_add_fusion.5), channel_id=1, source_target_pairs={{0,16},{8,24},{16,0},{24,8},{1,17},{9,25},{17,1},{25,9},{2,18},{10... | collective-permute-start | bytes 3080 | tf_op jit(solution)/shard_map/ppermute | solution.py:19
  303.7 5.4 %collective-permute-start.127 = (f32[256]{0:T(256)S(1)}, f32[256]{0:T(256)S(1)}, u32[]{:S(2)}, u32[]{:S(2)}) collective-permute-start(f32[256]{0:T(256)S(1)} %add_add_fusion.3), channel_id=1, source_target_pairs={{0,16},{8,24},{16,0},{24,8},{1,17},{9,25},{17,1},{25,9},{2,18},{10... | collective-permute-start | bytes 3080 | tf_op jit(solution)/shard_map/ppermute | solution.py:19
  (143 other events, 652.7 us)

commit v3 on v0

--- a/solution.py
+++ b/solution.py
@@ -11,6 +11,17 @@
 keep_share = 0.8
 
 
+def total(value):
+    for axis in ("blk", "grp"):
+        size = lax.axis_size(axis)
+        step = 1
+        while step < size:
+            pairs = [(i, i ^ step) for i in range(size)]
+            value = value + lax.ppermute(value, axis, pairs)
+            step *= 2
+    return value
+
+
 def class_balancer(label_masses, class_prior, class_target):
     kernel = label_masses + class_prior[None, :]
     scale_rows = None
@@ -20,7 +31,7 @@
             local_mass = jnp.sum(kernel, axis=0)
         else:
             local_mass = jnp.sum(scale_rows[:, None] * kernel, axis=0)
-        column = lax.psum(local_mass, ("grp", "blk"))
+        column = total(local_mass)
         scale_cols = class_target / column
         scale_rows = 1.0 / jnp.sum(kernel * scale_cols[None, :], axis=1)
     return scale_rows[:, None] * kernel * scale_cols[None, :]

time: 734 us -> 352 us (0.48)
  blocking collectives: 663 us -> 36.5 us
  waiting for transfers between devices: 18.5 us -> 185 us
  starting transfers between devices: 13.8 us -> 94.9 us
    psum x16 -> x0, blocking collectives: 635 us -> none  [class_balancer(): column = lax.psum(local_mass, ('grp', 'blk'))]
    ppermute x0 -> x80, waiting for transfers between devices: none -> 175 us  [total(): value = value + lax.ppermute(value, axis, pairs)]
    ppermute x0 -> x80, starting transfers between devices: none -> 85.5 us  [total(): value = value + lax.ppermute(value, axis, pairs)]
    all_to_all x1 -> x2, blocking collectives: 13.9 us -> 24.3 us  [on_device(): lax.all_to_all(picked, 'blk', split_axis=0, concat_axis=0, tiled=True)]
    all_to_all x1 -> x0, waiting for transfers between devices: 8.83 us -> none  [on_device(): lax.all_to_all(picked, 'blk', split_axis=0, concat_axis=0, tiled=True)]
  transfers between devices with their start and end apart: 3 -> 82, of which waited for: 2 -> 81; matrix products, arithmetic and copies ran while one was open for 1% -> 2% of each run, Pallas kernels for 0% -> 0%
where the time goes in v3:
time: 352 us
  waiting for transfers between devices  185 us (53%)
  starting transfers between devices  94.9 us (27%)
  blocking collectives  36.5 us (10%)
  other arithmetic  16.8 us (5%)
  matrix products  11.8 us (3%)
  local copies, waits for them, and re-layouts  4.51 us (1%)
    ppermute x80, waiting for transfers between devices, total(): value = value + lax.ppermute(value, axis, pairs)  175 us
    ppermute x80, starting transfers between devices, total(): value = value + lax.ppermute(value, axis, pairs)  85.5 us
    all_to_all x2, blocking collectives, on_device(): lax.all_to_all(picked, 'blk', split_axis=0, concat_axis=0, tiled=True)  24.3 us
    all_to_all x1, blocking collectives, on_device(): lax.all_to_all(parcel, 'blk', split_axis=0, concat_axis=0, tiled=True)  12.2 us
    all_to_all x1, waiting for transfers between devices, on_device(): lax.all_to_all(parcel, 'blk', split_axis=0, concat_axis=0, tiled=True)  9.65 us
    dot_general x2, matrix products, on_device(): paper_mass = jnp.einsum('sq,spc->qpc', paper_pick, products, precision=high)  7.59 us
  transfers between devices with their start and end apart: 82, of which 81 were waited for; matrix products, arithmetic and copies ran while one was open for 2% of the time, Pallas kernels for 0%

profile of v3, /device:TPU:0, one launch (start us, length us, event | category | flops | bytes accessed | tf_op | source)
XLA Modules:
  0.0 351.5 jit_solution(13915570431819459862)
XLA Ops:
  2.0 5.2 %all-to-all-start = ((bf16[8,1,2]{2,1,0:T(2,128)(2,1)}), bf16[8,1,2]{2,1,0:T(2,128)(2,1)S(1)}, u32[]{:S(2)}, u32[]{:S(2)}) async-start(bf16[8,1,2]{2,1,0:T(2,128)(2,1)} %compare_convert_fusion), calls=%async_computation | async-start | bytes 8192 | tf_op jit(solution)/shard_map/all_to_all | solution.py:77
  13.9 4.2 %all-to-all-start.1 = ((bf16[8,128,256]{2,1,0:T(8,128)(2,1)}), bf16[8,128,256]{2,1,0:T(8,128)(2,1)S(1)}, u32[]{:S(2)}, u32[]{:S(2)}) async-start(bf16[8,128,256]{2,1,0:T(8,128)(2,1)} %copy.52), calls=%async_computation.1 | async-start | bytes 1048576 | tf_op jit(solution)/shard_map/all_to_all | solution.py:76
  18.2 9.6 %all-to-all-done.1 = bf16[8,128,256]{2,1,0:T(8,128)(2,1)S(1)} async-done(((bf16[8,128,256]{2,1,0:T(8,128)(2,1)}), bf16[8,128,256]{2,1,0:T(8,128)(2,1)S(1)}, u32[]{:S(2)}, u32[]{:S(2)}) %all-to-all-start.1) | async-done | bytes 524320 | tf_op jit(solution)/shard_map/all_to_all | solution.py:76
  96.1 12.2 %all_to_all.30 = bf16[8,128,256]{2,1,0:T(8,128)(2,1)S(1)} all-to-all(bf16[8,128,256]{2,1,0:T(8,128)(2,1)S(1)} %copy.54), channel_id=1, replica_groups=mesh['grp'=4,'blk'=8] {'blk'}, dimensions={0} | all-to-all | bytes 1048576 | tf_op jit(solution)/shard_map/all_to_all | solution.py:93
  108.9 3.8 %fusion.45 = (f32[256]{0:T(256)S(1)}, f32[2,320,256]{2,0,1:T(2,128)S(1)}) fusion(f32[256]{0:T(256)S(1)} %copy-done.1, f32[8,320,256]{2,1,0:T(8,128)S(1)} %convolution_bitcast_fusion.1, f32[8]{0:T(128)S(1)} %compare_convert_fusion.1, s32[8]{0:T(128)S(1)} %copy-done.4), kind=kOutput, calls=%fused_computation.126 | convolution fusion | flops 16056096 | bytes 3278912 | tf_op jit(solution)/shard_map/sq,spc->qpc/dot_general | solution.py:97
  118.1 3.0 collective-permute-done.22
  135.3 3.0 collective-permute-done.27
  152.6 3.0 collective-permute-done.32
  169.9 3.0 collective-permute-done.37
  184.6 12.2 %all_to_all.31 = bf16[8,128,256]{2,1,0:T(8,128)(2,1)S(1)} all-to-all(bf16[8,128,256]{2,1,0:T(8,128)(2,1)S(1)} %copy.57), channel_id=1, replica_groups=mesh['grp'=4,'blk'=8] {'blk'}, dimensions={0} | all-to-all | bytes 1048576 | tf_op jit(solution)/shard_map/all_to_all | solution.py:76
  202.5 3.0 collective-permute-done.42
  219.4 3.0 collective-permute-done.47
  236.2 3.0 collective-permute-done.52
  253.1 3.0 collective-permute-done.57
  265.0 12.2 %all_to_all.32 = bf16[8,128,256]{2,1,0:T(8,128)(2,1)S(1)} all-to-all(bf16[8,128,256]{2,1,0:T(8,128)(2,1)S(1)} %copy.59), channel_id=1, replica_groups=mesh['grp'=4,'blk'=8] {'blk'}, dimensions={0} | all-to-all | bytes 1048576 | tf_op jit(solution)/shard_map/all_to_all | solution.py:93
  277.6 3.8 %fusion.43 = (f32[256]{0:T(256)S(1)}, f32[2,320,256]{2,0,1:T(2,128)S(1)}) fusion(f32[256]{0:T(256)S(1)} %copy-done.1, f32[8,320,256]{2,1,0:T(8,128)S(1)} %convolution_bitcast_fusion, f32[8]{0:T(128)S(1)} %compare_convert_fusion.1, s32[8]{0:T(128)S(1)} %copy-done.4), kind=kOutput, calls=%fused_computation.124 | convolution fusion | flops 16056096 | bytes 3278912 | tf_op jit(solution)/shard_map/sq,spc->qpc/dot_general | solution.py:97
  283.2 3.0 collective-permute-done.61
  286.8 3.0 collective-permute-done.62
  300.5 3.0 collective-permute-done.66
  304.0 3.0 collective-permute-done.67
  317.8 3.0 collective-permute-done.71
  321.3 3.0 collective-permute-done.72
  335.0 3.0 collective-permute-done.76
  338.6 3.0 collective-permute-done.77
  (314 shorter events, 238.2 us)
Async XLA Ops:
  2.0 11.9 %all-to-all-start = ((bf16[8,1,2]{2,1,0:T(2,128)(2,1)}), bf16[8,1,2]{2,1,0:T(2,128)(2,1)S(1)}, u32[]{:S(2)}, u32[]{:S(2)}) async-start(bf16[8,1,2]{2,1,0:T(2,128)(2,1)} %compare_convert_fusion), calls=%async_computation | async-start | bytes 8192 | tf_op jit(solution)/shard_map/all_to_all | solution.py:77
  13.9 13.9 %all-to-all-start.1 = ((bf16[8,128,256]{2,1,0:T(8,128)(2,1)}), bf16[8,128,256]{2,1,0:T(8,128)(2,1)S(1)}, u32[]{:S(2)}, u32[]{:S(2)}) async-start(bf16[8,128,256]{2,1,0:T(8,128)(2,1)} %copy.52), calls=%async_computation.1 | async-start | bytes 1048576 | tf_op jit(solution)/shard_map/all_to_all | solution.py:76
  36.6 3.6 %collective-permute-start.3 = (f32[256]{0:T(256)S(1)}, f32[256]{0:T(256)S(1)}, u32[]{:S(2)}, u32[]{:S(2)}) collective-permute-start(f32[256]{0:T(256)S(1)} %add.327), channel_id=1, source_target_pairs={{0,8},{8,0},{16,24},{24,16},{1,9},{9,1},{17,25},{25,17},{2,10},{10... | collective-permute-start | bytes 3080 | tf_op jit(solution)/shard_map/ppermute | solution.py:20
  40.2 4.5 %collective-permute-start.4 = (f32[256]{0:T(256)S(1)}, f32[256]{0:T(256)S(1)}, u32[]{:S(2)}, u32[]{:S(2)}) collective-permute-start(f32[256]{0:T(256)S(1)} %add.328), channel_id=1, source_target_pairs={{0,16},{8,24},{16,0},{24,8},{1,17},{9,25},{17,1},{25,9},{2,18},{10... | collective-permute-start | bytes 3080 | tf_op jit(solution)/shard_map/ppermute | solution.py:20
  46.4 3.6 %collective-permute-start.6 = (f32[256]{0:T(256)S(1)}, f32[256]{0:T(256)S(1)}, u32[]{:S(2)}, u32[]{:S(2)}) collective-permute-start(f32[256]{0:T(256)S(1)} %add.330), channel_id=1, source_target_pairs={{0,2},{1,3},{2,0},{3,1},{4,6},{5,7},{6,4},{7,5},{8,10},{9,11},{10,... | collective-permute-start | bytes 3080 | tf_op jit(solution)/shard_map/ppermute | solution.py:20
  57.1 4.5 %collective-permute-start.9 = (f32[256]{0:T(256)S(1)}, f32[256]{0:T(256)S(1)}, u32[]{:S(2)}, u32[]{:S(2)}) collective-permute-start(f32[256]{0:T(256)S(1)} %add.333), channel_id=1, source_target_pairs={{0,16},{8,24},{16,0},{24,8},{1,17},{9,25},{17,1},{25,9},{2,18},{10... | collective-permute-start | bytes 3080 | tf_op jit(solution)/shard_map/ppermute | solution.py:20
  73.9 4.5 %collective-permute-start.14 = (f32[256]{0:T(256)S(1)}, f32[256]{0:T(256)S(1)}, u32[]{:S(2)}, u32[]{:S(2)}) collective-permute-start(f32[256]{0:T(256)S(1)} %add.338), channel_id=1, source_target_pairs={{0,16},{8,24},{16,0},{24,8},{1,17},{9,25},{17,1},{25,9},{2,18},{10... | collective-permute-start | bytes 3080 | tf_op jit(solution)/shard_map/ppermute | solution.py:20
  80.1 3.6 %collective-permute-start.16 = (f32[256]{0:T(256)S(1)}, f32[256]{0:T(256)S(1)}, u32[]{:S(2)}, u32[]{:S(2)}) collective-permute-start(f32[256]{0:T(256)S(1)} %add.340), channel_id=1, source_target_pairs={{0,2},{1,3},{2,0},{3,1},{4,6},{5,7},{6,4},{7,5},{8,10},{9,11},{10,... | collective-permute-start | bytes 3080 | tf_op jit(solution)/shard_map/ppermute | solution.py:20
  83.7 3.6 %collective-permute-start.17 = (f32[256]{0:T(256)S(1)}, f32[256]{0:T(256)S(1)}, u32[]{:S(2)}, u32[]{:S(2)}) collective-permute-start(f32[256]{0:T(256)S(1)} %add.341), channel_id=1, source_target_pairs={{0,4},{1,5},{2,6},{3,7},{4,0},{5,1},{6,2},{7,3},{8,12},{9,13},{10,... | collective-permute-start | bytes 3080 | tf_op jit(solution)/shard_map/ppermute | solution.py:20
  87.2 3.6 %collective-permute-start.18 = (f32[256]{0:T(256)S(1)}, f32[256]{0:T(256)S(1)}, u32[]{:S(2)}, u32[]{:S(2)}) collective-permute-start(f32[256]{0:T(256)S(1)} %add.342), channel_id=1, source_target_pairs={{0,8},{8,0},{16,24},{24,16},{1,9},{9,1},{17,25},{25,17},{2,10},{10... | collective-permute-start | bytes 3080 | tf_op jit(solution)/shard_map/ppermute | solution.py:20
  90.8 4.5 %collective-permute-start.19 = (f32[256]{0:T(256)S(1)}, f32[256]{0:T(256)S(1)}, u32[]{:S(2)}, u32[]{:S(2)}) collective-permute-start(f32[256]{0:T(256)S(1)} %add.343), channel_id=1, source_target_pairs={{0,16},{8,24},{16,0},{24,8},{1,17},{9,25},{17,1},{25,9},{2,18},{10... | collective-permute-start | bytes 3080 | tf_op jit(solution)/shard_map/ppermute | solution.py:20
  113.9 3.6 %collective-permute-start.21 = (f32[256]{0:T(256)S(1)}, f32[256]{0:T(256)S(1)}, u32[]{:S(2)}, u32[]{:S(2)}) collective-permute-start(f32[256]{0:T(256)S(1)} %add.347), channel_id=1, source_target_pairs={{0,2},{1,3},{2,0},{3,1},{4,6},{5,7},{6,4},{7,5},{8,10},{9,11},{10,... | collective-permute-start | bytes 3080 | tf_op jit(solution)/shard_map/ppermute | solution.py:20
  124.6 4.5 %collective-permute-start.24 = (f32[256]{0:T(256)S(1)}, f32[256]{0:T(256)S(1)}, u32[]{:S(2)}, u32[]{:S(2)}) collective-permute-start(f32[256]{0:T(256)S(1)} %add.350), channel_id=1, source_target_pairs={{0,16},{8,24},{16,0},{24,8},{1,17},{9,25},{17,1},{25,9},{2,18},{10... | collective-permute-start | bytes 3080 | tf_op jit(solution)/shard_map/ppermute | solution.py:20
  141.9 4.5 %collective-permute-start.29 = (f32[256]{0:T(256)S(1)}, f32[256]{0:T(256)S(1)}, u32[]{:S(2)}, u32[]{:S(2)}) collective-permute-start(f32[256]{0:T(256)S(1)} %add.355), channel_id=1, source_target_pairs={{0,16},{8,24},{16,0},{24,8},{1,17},{9,25},{17,1},{25,9},{2,18},{10... | collective-permute-start | bytes 3080 | tf_op jit(solution)/shard_map/ppermute | solution.py:20
  159.2 4.5 %collective-permute-start.34 = (f32[256]{0:T(256)S(1)}, f32[256]{0:T(256)S(1)}, u32[]{:S(2)}, u32[]{:S(2)}) collective-permute-start(f32[256]{0:T(256)S(1)} %add.360), channel_id=1, source_target_pairs={{0,16},{8,24},{16,0},{24,8},{1,17},{9,25},{17,1},{25,9},{2,18},{10... | collective-permute-start | bytes 3080 | tf_op jit(solution)/shard_map/ppermute | solution.py:20
  176.5 4.5 %collective-permute-start.39 = (f32[256]{0:T(256)S(1)}, f32[256]{0:T(256)S(1)}, u32[]{:S(2)}, u32[]{:S(2)}) collective-permute-start(f32[256]{0:T(256)S(1)} %add.365), channel_id=1, source_target_pairs={{0,16},{8,24},{16,0},{24,8},{1,17},{9,25},{17,1},{25,9},{2,18},{10... | collective-permute-start | bytes 3080 | tf_op jit(solution)/shard_map/ppermute | solution.py:20
  209.1 4.5 %collective-permute-start.44 = (f32[256]{0:T(256)S(1)}, f32[256]{0:T(256)S(1)}, u32[]{:S(2)}, u32[]{:S(2)}) collective-permute-start(f32[256]{0:T(256)S(1)} %add.372), channel_id=1, source_target_pairs={{0,16},{8,24},{16,0},{24,8},{1,17},{9,25},{17,1},{25,9},{2,18},{10... | collective-permute-start | bytes 3080 | tf_op jit(solution)/shard_map/ppermute | solution.py:20
  226.0 4.5 %collective-permute-start.49 = (f32[256]{0:T(256)S(1)}, f32[256]{0:T(256)S(1)}, u32[]{:S(2)}, u32[]{:S(2)}) collective-permute-start(f32[256]{0:T(256)S(1)} %add.377), channel_id=1, source_target_pairs={{0,16},{8,24},{16,0},{24,8},{1,17},{9,25},{17,1},{25,9},{2,18},{10... | collective-permute-start | bytes 3080 | tf_op jit(solution)/shard_map/ppermute | solution.py:20
  242.8 4.5 %collective-permute-start.54 = (f32[256]{0:T(256)S(1)}, f32[256]{0:T(256)S(1)}, u32[]{:S(2)}, u32[]{:S(2)}) collective-permute-start(f32[256]{0:T(256)S(1)} %add.382), channel_id=1, source_target_pairs={{0,16},{8,24},{16,0},{24,8},{1,17},{9,25},{17,1},{25,9},{2,18},{10... | collective-permute-start | bytes 3080 | tf_op jit(solution)/shard_map/ppermute | solution.py:20
  259.7 4.5 %collective-permute-start.59 = (f32[256]{0:T(256)S(1)}, f32[256]{0:T(256)S(1)}, u32[]{:S(2)}, u32[]{:S(2)}) collective-permute-start(f32[256]{0:T(256)S(1)} %add.387), channel_id=1, source_target_pairs={{0,16},{8,24},{16,0},{24,8},{1,17},{9,25},{17,1},{25,9},{2,18},{10... | collective-permute-start | bytes 3080 | tf_op jit(solution)/shard_map/ppermute | solution.py:20
  293.4 4.5 %collective-permute-start.64 = (f32[256]{0:T(256)S(1)}, f32[256]{0:T(256)S(1)}, u32[]{:S(2)}, u32[]{:S(2)}) collective-permute-start(f32[256]{0:T(256)S(1)} %add.393), channel_id=1, source_target_pairs={{0,16},{8,24},{16,0},{24,8},{1,17},{9,25},{17,1},{25,9},{2,18},{10... | collective-permute-start | bytes 3080 | tf_op jit(solution)/shard_map/ppermute | solution.py:20
  310.6 4.5 %collective-permute-start.69 = (f32[256]{0:T(256)S(1)}, f32[256]{0:T(256)S(1)}, u32[]{:S(2)}, u32[]{:S(2)}) collective-permute-start(f32[256]{0:T(256)S(1)} %add.398), channel_id=1, source_target_pairs={{0,16},{8,24},{16,0},{24,8},{1,17},{9,25},{17,1},{25,9},{2,18},{10... | collective-permute-start | bytes 3080 | tf_op jit(solution)/shard_map/ppermute | solution.py:20
  327.9 4.5 %collective-permute-start.74 = (f32[256]{0:T(256)S(1)}, f32[256]{0:T(256)S(1)}, u32[]{:S(2)}, u32[]{:S(2)}) collective-permute-start(f32[256]{0:T(256)S(1)} %add.403), channel_id=1, source_target_pairs={{0,16},{8,24},{16,0},{24,8},{1,17},{9,25},{17,1},{25,9},{2,18},{10... | collective-permute-start | bytes 3080 | tf_op jit(solution)/shard_map/ppermute | solution.py:20
  345.2 4.5 %collective-permute-start.79 = (f32[256]{0:T(256)S(1)}, f32[256]{0:T(256)S(1)}, u32[]{:S(2)}, u32[]{:S(2)}) collective-permute-start(f32[256]{0:T(256)S(1)} %add.408), channel_id=1, source_target_pairs={{0,16},{8,24},{16,0},{24,8},{1,17},{9,25},{17,1},{25,9},{2,18},{10... | collective-permute-start | bytes 3080 | tf_op jit(solution)/shard_map/ppermute | solution.py:20
  (63 other events, 229.8 us)

commit v4 on v1

--- a/solution.py
+++ b/solution.py
@@ -12,9 +12,7 @@
 
 
 def total(local_mass):
-    devices = lax.axis_size(("grp", "blk"))
-    sent = jnp.broadcast_to(local_mass[None, :], (devices, local_mass.shape[0]))
-    parts = lax.all_to_all(sent, ("grp", "blk"), split_axis=0, concat_axis=0, tiled=True)
+    parts = lax.all_gather(local_mass, ("grp", "blk"))
     return jnp.sum(parts, axis=0)
 
 

time: 240 us -> 693 us (2.89)
  blocking collectives: 164 us -> 624 us
    all_gather x0 -> x16, blocking collectives: none -> 600 us  [total(): parts = lax.all_gather(local_mass, ('grp', 'blk'))]
    all_to_all x14 -> x0, blocking collectives: 127 us -> none  [total(): lax.all_to_all(sent, ('grp', 'blk'), split_axis=0, concat_axis=0, tiled=T...]
    all_to_all x2 -> x1, blocking collectives: 24.3 us -> 12.5 us  [on_device(): lax.all_to_all(picked, 'blk', split_axis=0, concat_axis=0, tiled=True)]
  transfers between devices with their start and end apart: 4 -> 3, of which waited for: 3 -> 2; matrix products, arithmetic and copies ran while one was open for 3% -> 1% of each run, Pallas kernels for 0% -> 0%
where the time goes in v4:
time: 693 us; the launch traced here: 692 us
  blocking collectives  624 us (90%)
  waiting for transfers between devices  18.2 us (3%)
  other arithmetic  17.5 us (3%)
  starting transfers between devices  13.2 us (2%)
  matrix products  11.8 us (2%)
    all_gather x16, blocking collectives, total(): parts = lax.all_gather(local_mass, ('grp', 'blk'))  600 us
  transfers between devices with their start and end apart: 3, of which 2 were waited for; matrix products, arithmetic and copies ran while one was open for 1% of the time, Pallas kernels for 0%

profile of v4, /device:TPU:0, one launch (start us, length us, event | category | flops | bytes accessed | tf_op | source)
XLA Modules:
  0.0 692.1 jit_solution(4032777363241848818)
XLA Ops:
  2.0 5.2 all-to-all-start
  13.9 4.3 all-to-all-start.1
  18.3 9.6 %all-to-all-done.1 = bf16[8,128,256]{2,1,0:T(8,128)(2,1)S(1)} async-done(((bf16[8,128,256]{2,1,0:T(8,128)(2,1)}), bf16[8,128,256]{2,1,0:T(8,128)(2,1)S(1)}, u32[]{:S(2)}, u32[]{:S(2)}) %all-to-all-start.1) | async-done | bytes 524320 | tf_op jit(solution)/shard_map/all_to_all | solution.py:70
  28.4 39.9 %all-gather.16 = f32[32,1,256]{2,1,0:T(1,128)S(1)} all-gather(f32[1,1,256]{2,1,0:T(1,128)S(1)} %bitcast.92), channel_id=2, replica_groups=mesh['grp'=4,'blk'=8] {'grp','blk'}, dimensions={0}, use_global_device_ids=true | all-gather | bytes 33792 | tf_op jit(solution)/shard_map/all_gather | solution.py:15
  68.9 36.7 %all-gather.17 = f32[32,1,256]{2,1,0:T(1,128)S(1)} all-gather(f32[1,1,256]{2,1,0:T(1,128)S(1)} %bitcast.80), channel_id=3, replica_groups=mesh['grp'=4,'blk'=8] {'grp','blk'}, dimensions={0}, use_global_device_ids=true | all-gather | bytes 33792 | tf_op jit(solution)/shard_map/all_gather | solution.py:15
  106.1 38.0 %all-gather.18 = f32[32,1,256]{2,1,0:T(1,128)S(1)} all-gather(f32[1,1,256]{2,1,0:T(1,128)S(1)} %bitcast.81), channel_id=4, replica_groups=mesh['grp'=4,'blk'=8] {'grp','blk'}, dimensions={0}, use_global_device_ids=true | all-gather | bytes 33792 | tf_op jit(solution)/shard_map/all_gather | solution.py:15
  144.6 36.7 %all-gather.19 = f32[32,1,256]{2,1,0:T(1,128)S(1)} all-gather(f32[1,1,256]{2,1,0:T(1,128)S(1)} %bitcast.82), channel_id=5, replica_groups=mesh['grp'=4,'blk'=8] {'grp','blk'}, dimensions={0}, use_global_device_ids=true | all-gather | bytes 33792 | tf_op jit(solution)/shard_map/all_gather | solution.py:15
  182.2 12.5 %all_to_all.30 = bf16[8,128,256]{2,1,0:T(8,128)(2,1)S(1)} all-to-all(bf16[8,128,256]{2,1,0:T(8,128)(2,1)S(1)} %copy.54), channel_id=1, replica_groups=mesh['grp'=4,'blk'=8] {'blk'}, dimensions={0} | all-to-all | bytes 1048576 | tf_op jit(solution)/shard_map/all_to_all | solution.py:87
  195.3 3.8 fusion.45
  199.1 36.9 %all-gather.20 = f32[32,1,256]{2,1,0:T(1,128)S(1)} all-gather(f32[1,1,256]{2,1,0:T(1,128)S(1)} %bitcast.79), channel_id=6, replica_groups=mesh['grp'=4,'blk'=8] {'grp','blk'}, dimensions={0}, use_global_device_ids=true | all-gather | bytes 33792 | tf_op jit(solution)/shard_map/all_gather | solution.py:15
  237.0 38.0 %all-gather.21 = f32[32,1,256]{2,1,0:T(1,128)S(1)} all-gather(f32[1,1,256]{2,1,0:T(1,128)S(1)} %bitcast.83), channel_id=7, replica_groups=mesh['grp'=4,'blk'=8] {'grp','blk'}, dimensions={0}, use_global_device_ids=true | all-gather | bytes 33792 | tf_op jit(solution)/shard_map/all_gather | solution.py:15
  275.9 36.9 %all-gather.22 = f32[32,1,256]{2,1,0:T(1,128)S(1)} all-gather(f32[1,1,256]{2,1,0:T(1,128)S(1)} %bitcast.84), channel_id=8, replica_groups=mesh['grp'=4,'blk'=8] {'grp','blk'}, dimensions={0}, use_global_device_ids=true | all-gather | bytes 33792 | tf_op jit(solution)/shard_map/all_gather | solution.py:15
  313.8 37.8 %all-gather.23 = f32[32,1,256]{2,1,0:T(1,128)S(1)} all-gather(f32[1,1,256]{2,1,0:T(1,128)S(1)} %bitcast.85), channel_id=9, replica_groups=mesh['grp'=4,'blk'=8] {'grp','blk'}, dimensions={0}, use_global_device_ids=true | all-gather | bytes 33792 | tf_op jit(solution)/shard_map/all_gather | solution.py:15
  355.2 12.2 %all_to_all.31 = bf16[8,128,256]{2,1,0:T(8,128)(2,1)S(1)} all-to-all(bf16[8,128,256]{2,1,0:T(8,128)(2,1)S(1)} %copy.57), channel_id=1, replica_groups=mesh['grp'=4,'blk'=8] {'blk'}, dimensions={0} | all-to-all | bytes 1048576 | tf_op jit(solution)/shard_map/all_to_all | solution.py:70
  367.8 36.9 %all-gather.24 = f32[32,1,256]{2,1,0:T(1,128)S(1)} all-gather(f32[1,1,256]{2,1,0:T(1,128)S(1)} %bitcast.93), channel_id=10, replica_groups=mesh['grp'=4,'blk'=8] {'grp','blk'}, dimensions={0}, use_global_device_ids=true | all-gather | bytes 33792 | tf_op jit(solution)/shard_map/all_gather | solution.py:15
  405.2 37.8 %all-gather.25 = f32[32,1,256]{2,1,0:T(1,128)S(1)} all-gather(f32[1,1,256]{2,1,0:T(1,128)S(1)} %bitcast.86), channel_id=11, replica_groups=mesh['grp'=4,'blk'=8] {'grp','blk'}, dimensions={0}, use_global_device_ids=true | all-gather | bytes 33792 | tf_op jit(solution)/shard_map/all_gather | solution.py:15
  443.5 36.9 %all-gather.26 = f32[32,1,256]{2,1,0:T(1,128)S(1)} all-gather(f32[1,1,256]{2,1,0:T(1,128)S(1)} %bitcast.87), channel_id=12, replica_groups=mesh['grp'=4,'blk'=8] {'grp','blk'}, dimensions={0}, use_global_device_ids=true | all-gather | bytes 33792 | tf_op jit(solution)/shard_map/all_gather | solution.py:15
  481.0 37.8 %all-gather.27 = f32[32,1,256]{2,1,0:T(1,128)S(1)} all-gather(f32[1,1,256]{2,1,0:T(1,128)S(1)} %bitcast.88), channel_id=13, replica_groups=mesh['grp'=4,'blk'=8] {'grp','blk'}, dimensions={0}, use_global_device_ids=true | all-gather | bytes 33792 | tf_op jit(solution)/shard_map/all_gather | solution.py:15
  525.1 8.5 %all-to-all-done.4 = bf16[8,128,256]{2,1,0:T(8,128)(2,1)S(1)} async-done(((bf16[8,128,256]{2,1,0:T(8,128)(2,1)}), bf16[8,128,256]{2,1,0:T(8,128)(2,1)S(1)}, u32[]{:S(2)}, u32[]{:S(2)}) %all-to-all-start.4) | async-done | bytes 524320 | tf_op jit(solution)/shard_map/all_to_all | solution.py:87
  534.1 3.8 fusion.43
  537.9 36.9 %all-gather.28 = f32[32,1,256]{2,1,0:T(1,128)S(1)} all-gather(f32[1,1,256]{2,1,0:T(1,128)S(1)} %bitcast.78), channel_id=14, replica_groups=mesh['grp'=4,'blk'=8] {'grp','blk'}, dimensions={0}, use_global_device_ids=true | all-gather | bytes 33792 | tf_op jit(solution)/shard_map/all_gather | solution.py:15
  575.8 37.8 %all-gather.29 = f32[32,1,256]{2,1,0:T(1,128)S(1)} all-gather(f32[1,1,256]{2,1,0:T(1,128)S(1)} %bitcast.89), channel_id=15, replica_groups=mesh['grp'=4,'blk'=8] {'grp','blk'}, dimensions={0}, use_global_device_ids=true | all-gather | bytes 33792 | tf_op jit(solution)/shard_map/all_gather | solution.py:15
  614.6 36.9 %all-gather.30 = f32[32,1,256]{2,1,0:T(1,128)S(1)} all-gather(f32[1,1,256]{2,1,0:T(1,128)S(1)} %bitcast.90), channel_id=16, replica_groups=mesh['grp'=4,'blk'=8] {'grp','blk'}, dimensions={0}, use_global_device_ids=true | all-gather | bytes 33792 | tf_op jit(solution)/shard_map/all_gather | solution.py:15
  652.4 37.8 %all-gather.31 = f32[32,1,256]{2,1,0:T(1,128)S(1)} all-gather(f32[1,1,256]{2,1,0:T(1,128)S(1)} %bitcast.91), channel_id=17, replica_groups=mesh['grp'=4,'blk'=8] {'grp','blk'}, dimensions={0}, use_global_device_ids=true | all-gather | bytes 33792 | tf_op jit(solution)/shard_map/all_gather | solution.py:15
  (123 shorter events, 30.7 us)
Async XLA Ops:
  0.6 11.5 %copy-start = (bf16[8,320,128]{2,1,0:T(8,128)(2,1)S(1)}, bf16[8,320,128]{2,1,0:T(8,128)(2,1)}, u32[]{:S(2)}) copy-start(bf16[8,320,128]{2,1,0:T(8,128)(2,1)} %param.8) | copy-start | bytes 1966084
  2.0 11.9 %all-to-all-start = ((bf16[8,1,2]{2,1,0:T(2,128)(2,1)}), bf16[8,1,2]{2,1,0:T(2,128)(2,1)S(1)}, u32[]{:S(2)}, u32[]{:S(2)}) async-start(bf16[8,1,2]{2,1,0:T(2,128)(2,1)} %compare_convert_fusion), calls=%async_computation | async-start | bytes 8192 | tf_op jit(solution)/shard_map/all_to_all | solution.py:71
  12.9 15.1 %copy-start.1 = (f32[256]{0:T(256)S(1)}, f32[256]{0:T(256)}, u32[]{:S(2)}) copy-start(f32[256]{0:T(256)} %param.14) | copy-start | bytes 3076
  13.9 54.5 %copy-start.2 = (f32[256]{0:T(256)S(1)}, f32[256]{0:T(256)}, u32[]{:S(2)}) copy-start(f32[256]{0:T(256)} %param.15) | copy-start | bytes 3076
  13.9 14.1 %all-to-all-start.1 = ((bf16[8,128,256]{2,1,0:T(8,128)(2,1)}), bf16[8,128,256]{2,1,0:T(8,128)(2,1)S(1)}, u32[]{:S(2)}, u32[]{:S(2)}) async-start(bf16[8,128,256]{2,1,0:T(8,128)(2,1)} %copy.52), calls=%async_computation.1 | async-start | bytes 1048576 | tf_op jit(solution)/shard_map/all_to_all | solution.py:70
  194.7 0.7 copy-start.4
  520.4 13.2 %all-to-all-start.4 = ((bf16[8,128,256]{2,1,0:T(8,128)(2,1)}), bf16[8,128,256]{2,1,0:T(8,128)(2,1)S(1)}, u32[]{:S(2)}, u32[]{:S(2)}) async-start(bf16[8,128,256]{2,1,0:T(8,128)(2,1)} %copy.59), calls=%async_computation.4 | async-start | bytes 1048576 | tf_op jit(solution)/shard_map/all_to_all | solution.py:87
  651.9 39.0 %copy-start.3 = (s32[640]{0:T(1024)S(1)}, s32[640]{0:T(1024)}, u32[]{:S(2)}) copy-start(s32[640]{0:T(1024)} %param.12) | copy-start | bytes 7684

commit v5 on v0

v5 whole, which is shorter than its diff:
```python
import functools

import jax
import jax.numpy as jnp
from jax import lax
from jax.experimental import pallas as pl
from jax.experimental.pallas import tpu as pltpu
from jax.sharding import PartitionSpec as P

AT_DEV = 2
ITERS = 4
ROUNDS = 2
LANES = 128
META = 16

keep_share = 0.8

AXES = ("grp", "blk")
VMEM = pl.BlockSpec(memory_space=pltpu.VMEM)
SMEM = pl.BlockSpec(memory_space=pltpu.SMEM)
ANY = pl.BlockSpec(memory_space=pl.ANY)


def call(kernel, out_shape, in_specs, scratch_shapes=()):
    out_specs = jax.tree.map(lambda _: VMEM, out_shape)
    return pl.pallas_call(
        kernel,
        out_shape=out_shape,
        in_specs=in_specs,
        out_specs=out_specs,
        scratch_shapes=list(scratch_shapes),
        compiler_params=pltpu.CompilerParams(vmem_limit_bytes=48 * 1024 * 1024),
    )


def col_scale(parts_ref, target_ref):
    return target_ref[...] / jnp.sum(parts_ref[...], axis=0)


def row_scale(kernel, scale_cols):
    return 1.0 / jnp.sum(kernel * scale_cols, axis=1, keepdims=True)


def spread(value, parts_ref):
    parts_ref[...] = jnp.broadcast_to(value[None], parts_ref.shape)


def pack_kernel(slots, rows, tile_paper, tile_author, tile_count, tiles, codes, out):
    line = lax.broadcasted_iota(jnp.int32, (META, LANES), 0)
    code_rows = -(-rows // LANES)
    for slot in range(slots):
        out[slot, :rows, :] = tiles[slot]
        paper = tile_paper[slot]
        live = slot < tile_count[0]
        block = codes[paper]
        for author in range(AT_DEV):
            chosen = jnp.where(live & (tile_author[slot] == author), 1.0, 0.0)
            block = jnp.where(line == code_rows + author, chosen, block)
        block = jnp.where(line == code_rows + AT_DEV, paper.astype(jnp.float32), block)
        out[slot, rows:, :] = block.astype(jnp.bfloat16)


def finish_mass(mass, class_prior, full, half, parts):
    kernel = mass + class_prior[...]
    full[...] = kernel
    half[...] = kernel.astype(jnp.bfloat16)
    spread(jnp.sum(kernel, axis=0, keepdims=True), parts)


def first_author_kernel(slots, rows, packed, class_prior, full, half, parts):
    classes = full.shape[1]
    code_rows = -(-rows // LANES)
    totals = [jnp.zeros((classes, LANES), jnp.float32) for _ in range(AT_DEV)]
    class_line = lax.broadcasted_iota(jnp.int32, (classes, rows), 0).astype(jnp.float32)
    for slot in range(slots):
        meta = packed[slot, rows:, :].astype(jnp.float32)
        codes = jnp.concatenate([meta[i : i + 1] for i in range(code_rows)], axis=1)[:, :rows]
        seeds = jnp.where(class_line == codes, 1.0, 0.0).astype(jnp.bfloat16)
        parcel = jnp.dot(seeds, packed[slot, :rows, :], preferred_element_type=jnp.float32)
        parcel = parcel.astype(jnp.bfloat16).astype(jnp.float32)
        for author in range(AT_DEV):
            chosen = meta[code_rows + author : code_rows + author + 1]
            totals[author] = totals[author] + parcel * chosen
    mass = jnp.concatenate([total.T for total in totals], axis=0)
    finish_mass(mass, class_prior, full, half, parts)


def author_kernel(
    slots, rows, paper, packed, gathered, seeds, summed, class_prior, class_target,
    full, half, parts, shares_in, seeds_in, arrived,
):
    classes = full.shape[1]
    code_rows = -(-rows // LANES)
    copies = []
    for slot in range(slots):
        start = pl.multiple_of((slot * (gathered.shape[0] // slots // rows) + paper[slot]) * rows, rows)
        pair = (
            pltpu.make_async_copy(
                gathered.at[pl.ds(start, rows)], shares_in.at[slot], arrived.at[0, slot]
            ),
            pltpu.make_async_copy(
                seeds.at[pl.ds(start, rows)], seeds_in.at[slot], arrived.at[1, slot]
            ),
        )
        for copy in pair:
            copy.start()
        copies.append(pair)
    scale_cols = col_scale(summed, class_target)
    totals = [jnp.zeros((LANES, classes), jnp.float32) for _ in range(AT_DEV)]
    lane = lax.broadcasted_iota(jnp.int32, (rows, classes), 1).astype(jnp.float32)
    for slot in range(slots):
        for copy in copies[slot]:
            copy.wait()
        kernel = shares_in[slot].astype(jnp.float32) * scale_cols
        share = kernel * (keep_share / jnp.sum(kernel, axis=1, keepdims=True))
        code = seeds_in[slot].astype(jnp.float32)
        code = jnp.concatenate([code] * (classes // LANES), axis=1)
        labels = share + jnp.where(code == lane, 1.0 - keep_share, 0.0)
        parcel = lax.dot_general(
            packed[slot, :rows, :],
            labels.astype(jnp.bfloat16),
            (((0,), (0,)), ((), ())),
            preferred_element_type=jnp.float32,
        )
        parcel = parcel.astype(jnp.bfloat16).astype(jnp.float32)
        meta = packed[slot, rows:, :].astype(jnp.float32)
        for author in range(AT_DEV):
            chosen = meta[code_rows + author : code_rows + author + 1, :1]
            totals[author] = totals[author] + parcel * chosen
    finish_mass(jnp.concatenate(totals, axis=0), class_prior, full, half, parts)


def paper_kernel(
    slots, tile_paper, tile_author, tile_count, tiles, gathered, own, summed, class_prior,
    class_target, full, half, parts, scores, mass, shares_in, arrived,
):
    columns = tiles.shape[2]
    copies = []
    for slot in range(slots):
        start = pl.multiple_of((slot * AT_DEV + tile_author[slot]) * columns, columns)
        copy = pltpu.make_async_copy(
            gathered.at[pl.ds(start, columns)], shares_in.at[slot], arrived.at[slot]
        )
        copy.start()
        copies.append(copy)
    scale_cols = col_scale(summed, class_target)
    mass[...] = jnp.zeros_like(mass)
    scaled = own[...] * scale_cols
    scores[...] = scaled * (full.shape[1] / jnp.sum(scaled, axis=1, keepdims=True))
    for slot in range(slots):
        copies[slot].wait()

        @pl.when(slot < tile_count[0])
        def _():
            kernel = shares_in[slot].astype(jnp.float32) * scale_cols
            labels = kernel * (1.0 / jnp.sum(kernel, axis=1, keepdims=True))
            mass[tile_paper[slot]] += jnp.dot(
                tiles[slot], labels.astype(jnp.bfloat16), preferred_element_type=jnp.float32
            )

    finish_mass(mass[...].reshape(full.shape), class_prior, full, half, parts)


def balance_kernel(kernel_ref, summed, class_target, parts):
    kernel = kernel_ref[...]
    scale_rows = row_scale(kernel, col_scale(summed, class_target))
    spread(jnp.sum(scale_rows * kernel, axis=0, keepdims=True), parts)


def final_kernel(kernel_ref, summed, class_target, seeds, out):
    classes = out.shape[1]
    scaled = kernel_ref[...] * col_scale(summed, class_target)
    share = scaled * (1.0 / jnp.sum(scaled, axis=1, keepdims=True))
    code = seeds[...].astype(jnp.float32)
    code = jnp.concatenate([code] * (classes // LANES), axis=1)
    lane = lax.broadcasted_iota(jnp.int32, out.shape, 1).astype(jnp.float32)
    updated = keep_share * share + jnp.where(code == lane, 1.0 - keep_share, 0.0)
    out[...] = classes * updated


def exchange(parts):
    return lax.all_to_all(parts, AXES, split_axis=0, concat_axis=0, tiled=True)


def on_device(
    tile_values,
    tile_paper,
    tile_author,
    tile_count,
    seed_class,
    train_mask,
    class_prior,
    class_target,
):
    f32 = jnp.float32
    bf16 = jnp.bfloat16
    shape = jax.ShapeDtypeStruct
    slots, rows, columns = tile_values.shape
    classes = class_prior.shape[0]
    papers = seed_class.shape[0]
    authors = AT_DEV * columns
    paper_tiles = papers // rows
    devices = lax.axis_size(AXES)
    code_rows = -(-rows // LANES)
    prior = class_prior.reshape(1, classes)
    target = class_target.reshape(1, classes)
    parts = shape((devices, 1, classes), f32)

    code = jnp.where(train_mask == 1, seed_class, -1).astype(f32)
    code_lines = jnp.pad(code.reshape(paper_tiles, rows), ((0, 0), (0, code_rows * LANES - rows)))
    code_lines = code_lines.reshape(paper_tiles, code_rows, LANES)
    code_lines = jnp.pad(code_lines, ((0, 0), (0, META - code_rows), (0, 0)))
    seed_codes = jnp.broadcast_to(code.astype(bf16)[:, None], (papers, LANES))
    seed_codes = lax.optimization_barrier(seed_codes)

    packed = call(
        functools.partial(pack_kernel, slots, rows),
        shape((slots, rows + META, columns), bf16),
        [SMEM, SMEM, SMEM, VMEM, VMEM],
    )(tile_paper, tile_author, tile_count, tile_values, code_lines)
    packed = lax.all_to_all(packed, "blk", split_axis=0, concat_axis=0, tiled=True)
    paper_of = packed[:, rows + code_rows + AT_DEV, 0].astype(jnp.int32)
    seeds_all = lax.all_gather(seed_codes, "blk", tiled=True)

    author_out = (shape((authors, classes), f32), shape((authors, classes), bf16), parts)
    paper_out = (
        shape((papers, classes), f32),
        shape((papers, classes), bf16),
        parts,
        shape((authors, classes), f32),
    )

    def balance(kernel, summed):
        for _ in range(ITERS - 1):
            summed = exchange(call(balance_kernel, parts, [VMEM] * 3)(kernel, summed, target))
        return summed

    for repeat in range(ROUNDS):
        if repeat == 0:
            own, half, local = call(
                functools.partial(first_author_kernel, slots, rows), author_out, [VMEM] * 2
            )(packed, prior)
        else:
            own, half, local = call(
                functools.partial(author_kernel, slots, rows),
                author_out,
                [SMEM, VMEM, ANY, ANY, VMEM, VMEM, VMEM],
                [
                    pltpu.VMEM((slots, rows, classes), bf16),
                    pltpu.VMEM((slots, rows, LANES), bf16),
                    pltpu.SemaphoreType.DMA((2, slots)),
                ],
            )(paper_of, packed, gathered, seeds_all, summed, prior, target)
        gathered = lax.all_gather(half, "blk", tiled=True)
        summed = balance(own, exchange(local))
        kernel, half, local, author_scores = call(
            functools.partial(paper_kernel, slots),
            paper_out,
            [SMEM, SMEM, SMEM, VMEM, ANY, VMEM, VMEM, VMEM, VMEM],
            [
                pltpu.VMEM((paper_tiles, rows, classes), f32),
                pltpu.VMEM((slots, columns, classes), bf16),
                pltpu.SemaphoreType.DMA((slots,)),
            ],
        )(tile_paper, tile_author, tile_count, tile_values, gathered, own, summed, prior, target)
        if repeat + 1 < ROUNDS:
            gathered = lax.all_gather(half, "blk", tiled=True)
        summed = balance(kernel, exchange(local))
    paper_scores = call(final_kernel, shape((papers, classes), f32), [VMEM] * 4)(
        kernel, summed, target, seed_codes
    )
    return paper_scores, author_scores


def solution(mesh):
    placed = (
        P(("grp", "blk"), None, None),
        P(("grp", "blk")),
        P(("grp", "blk")),
        P(("grp", "blk")),
        P(("grp", "blk")),
        P(("grp", "blk")),
        P(),
        P(),
    )
    return jax.shard_map(
        on_device,
        mesh=mesh,
        in_specs=placed,
        out_specs=(P(("grp", "blk"), None), P(("grp", "blk"), None)),
        check_vma=False,
    )
```

time: 734 us -> 212 us (0.29)
  blocking collectives: 663 us -> 155 us
  Pallas kernels: 0 us -> 21.8 us
  other arithmetic: 16.6 us -> 0.95 us
  between operations: 1.73 us -> 14.6 us
  matrix products: 11.8 us -> 0 us
  waiting for transfers between devices: 18.5 us -> 7.03 us
  starting transfers between devices: 13.8 us -> 2.73 us
    psum x16 -> x0, blocking collectives: 635 us -> none  [class_balancer(): column = lax.psum(local_mass, ('grp', 'blk'))]
    all_to_all x2 -> x16, blocking collectives: 27.9 us -> 155 us  [the longest x15 139 us: exchange(): return lax.all_to_all(parts, AXES, split_axis=0, concat_axis=0, tiled=True)]
    pallas_call x0 -> x18, Pallas kernels: none -> 21.8 us  [the longest x2 8.99 us: on_device(): call(functools.partial(paper_kernel, slots), paper_out, [SMEM, SMEM, SMEM...]
    dot_general x10 -> x0, matrix products: 11.8 us -> none  [the longest x2 7.59 us: on_device(): paper_mass = jnp.einsum('sq,spc->qpc', paper_pick, products, precision=high)]
    all_to_all x3 -> x1, waiting for transfers between devices: 18.5 us -> 6.94 us  [exchange(): return lax.all_to_all(parts, AXES, split_axis=0, concat_axis=0, tiled=True)]
    all_to_all x3 -> x1, starting transfers between devices: 13.8 us -> 2.57 us  [exchange(): return lax.all_to_all(parts, AXES, split_axis=0, concat_axis=0, tiled=True)]
    reduce_sum x28 -> x0, other arithmetic: 8.93 us -> none  [the longest x16 5.11 us: class_balancer(): scale_rows = 1.0 / jnp.sum(kernel * scale_cols[None, :], axis=1)]
    unnamed x10 -> x26, local copies, waits for them, and re-layouts: 0.19 us -> 7.92 us
  transfers between devices with their start and end apart: 3 -> 5, of which waited for: 2 -> 1; matrix products, arithmetic and copies ran while one was open for 1% -> 0% of each run, Pallas kernels for 0% -> 3%
where the time goes in v5:
time: 212 us; the launch traced here: 211 us
  blocking collectives  155 us (73%)
  Pallas kernels  21.8 us (10%)
  between operations  14.6 us (7%)
  local copies, waits for them, and re-layouts  8.85 us (4%)
  waiting for transfers between devices  7.03 us (3%)
  starting transfers between devices  2.73 us (1%)
    all_to_all x15, blocking collectives, exchange(): return lax.all_to_all(parts, AXES, split_axis=0, concat_axis=0, tiled=True)  139 us
    all_to_all x1, blocking collectives, on_device(): lax.all_to_all(packed, 'blk', split_axis=0, concat_axis=0, tiled=True)  16.5 us
    pallas_call x2, Pallas kernels, on_device(): call(functools.partial(paper_kernel, slots), paper_out, [SMEM, SMEM, SMEM...  8.99 us
    unnamed x26, local copies, waits for them, and re-layouts  7.92 us
    all_to_all x1, waiting for transfers between devices, exchange(): return lax.all_to_all(parts, AXES, split_axis=0, concat_axis=0, tiled=True)  6.94 us
    pallas_call x1, Pallas kernels, on_device(): call(functools.partial(author_kernel, slots, rows), author_out, [SMEM, VM...  6.64 us
  transfers between devices with their start and end apart: 5, of which 1 were waited for; matrix products, arithmetic and copies ran while one was open for 0% of the time, Pallas kernels for 3%

profile of v5, /device:TPU:0, one launch (start us, length us, event | category | flops | bytes accessed | tf_op | source)
XLA Modules:
  0.0 211.0 jit_solution(2861531396189540898)
XLA Ops:
  11.7 16.5 %all_to_all.85.packed = bf16[8,336,128]{2,1,0:T(8,128)(2,1)S(1)} all-to-all(bf16[8,336,128]{2,1,0:T(8,128)(2,1)S(1)} %shard_map.95), channel_id=1, replica_groups=mesh['grp'=4,'blk'=8] {'blk'}, dimensions={0} | all-to-all | bytes 1376256 | tf_op jit(solution)/shard_map/all_to_all | solution.py:221
  28.2 1.4 shard_map.96
  30.5 11.0 %all_to_all.86.summed = f32[32,1,256]{2,1,0:T(1,128)S(1)} all-to-all(f32[32,1,256]{2,1,0:T(1,128)S(1)} %get-tuple-element.16), channel_id=1, replica_groups=mesh['grp'=4,'blk'=8] {'grp','blk'}, dimensions={0} | all-to-all | bytes 65536 | tf_op jit(solution)/shard_map/all_to_all | solution.py:182
  41.7 8.9 %all_to_all.87.summed = f32[32,1,256]{2,1,0:T(1,128)S(1)} all-to-all(f32[32,1,256]{2,1,0:T(1,128)S(1)} %shard_map.97), channel_id=1, replica_groups=mesh['grp'=4,'blk'=8] {'grp','blk'}, dimensions={0} | all-to-all | bytes 65536 | tf_op jit(solution)/shard_map/all_to_all | solution.py:182
  50.9 8.9 %all_to_all.88.summed = f32[32,1,256]{2,1,0:T(1,128)S(1)} all-to-all(f32[32,1,256]{2,1,0:T(1,128)S(1)} %shard_map.98), channel_id=1, replica_groups=mesh['grp'=4,'blk'=8] {'grp','blk'}, dimensions={0} | all-to-all | bytes 65536 | tf_op jit(solution)/shard_map/all_to_all | solution.py:182
  60.0 8.9 %all_to_all.89.summed = f32[32,1,256]{2,1,0:T(1,128)S(1)} all-to-all(f32[32,1,256]{2,1,0:T(1,128)S(1)} %shard_map.99), channel_id=1, replica_groups=mesh['grp'=4,'blk'=8] {'grp','blk'}, dimensions={0} | all-to-all | bytes 65536 | tf_op jit(solution)/shard_map/all_to_all | solution.py:182
  70.2 4.5 %shard_map.100 = (f32[640,256]{1,0:T(8,128)S(1)}, bf16[640,256]{1,0:T(8,128)(2,1)}, f32[32,1,256]{2,1,0:T(1,128)S(1)}, f32[256,256]{1,0:T(8,128)}) custom-call(s32[8]{0:T(128)S(1)} %copy-done.10, s32[8]{0:T(128)S(1)} %copy-done.12, s32[1]{0:T(128)S(6)} %copy.10.tile_count, bf16[8,320,128]{2,1,0:T(8,128)(2,1)S(1)} %copy-done.1, ...), custom_call_target="tpu_custom_call" | custom-call | tf_op jit(solution)/shard_map/pallas_call | solution.py:256
  74.7 8.9 %all_to_all.90.summed = f32[32,1,256]{2,1,0:T(1,128)S(1)} all-to-all(f32[32,1,256]{2,1,0:T(1,128)S(1)} %get-tuple-element.19), channel_id=1, replica_groups=mesh['grp'=4,'blk'=8] {'grp','blk'}, dimensions={0} | all-to-all | bytes 65536 | tf_op jit(solution)/shard_map/all_to_all | solution.py:182
  83.9 8.9 %all_to_all.91.summed = f32[32,1,256]{2,1,0:T(1,128)S(1)} all-to-all(f32[32,1,256]{2,1,0:T(1,128)S(1)} %shard_map.101), channel_id=1, replica_groups=mesh['grp'=4,'blk'=8] {'grp','blk'}, dimensions={0} | all-to-all | bytes 65536 | tf_op jit(solution)/shard_map/all_to_all | solution.py:182
  93.1 8.9 %all_to_all.92.summed = f32[32,1,256]{2,1,0:T(1,128)S(1)} all-to-all(f32[32,1,256]{2,1,0:T(1,128)S(1)} %shard_map.102), channel_id=1, replica_groups=mesh['grp'=4,'blk'=8] {'grp','blk'}, dimensions={0} | all-to-all | bytes 65536 | tf_op jit(solution)/shard_map/all_to_all | solution.py:182
  102.9 2.6 %all-to-all-start.8 = ((f32[32,1,256]{2,1,0:T(1,128)}), f32[32,1,256]{2,1,0:T(1,128)S(1)}, u32[]{:S(2)}, u32[]{:S(2)}) async-start(f32[32,1,256]{2,1,0:T(1,128)} %shard_map.103), calls=%async_computation.8 | async-start | bytes 65536 | tf_op jit(solution)/shard_map/all_to_all | solution.py:182
  105.8 6.9 %all-to-all-done.8.summed = f32[32,1,256]{2,1,0:T(1,128)S(1)} async-done(((f32[32,1,256]{2,1,0:T(1,128)}), f32[32,1,256]{2,1,0:T(1,128)S(1)}, u32[]{:S(2)}, u32[]{:S(2)}) %all-to-all-start.8) | async-done | bytes 32800 | tf_op jit(solution)/shard_map/all_to_all | solution.py:182
  112.7 1.7 copy-done.2
  114.5 1.3 copy-done.4
  115.8 6.6 %shard_map.104 = (f32[256,256]{1,0:T(8,128)S(1)}, bf16[256,256]{1,0:T(8,128)(2,1)}, f32[32,1,256]{2,1,0:T(1,128)S(1)}) custom-call(s32[8]{0:T(128)S(1)} %fusion.paper, bf16[8,336,128]{2,1,0:T(8,128)(2,1)S(1)} %all_to_all.85.packed, bf16[5120,256]{1,0:T(8,128)(2,1)S(1)} %copy-done.2, bf16[5120,128]{1,0:T(8,128)(2,1)S(1)} %copy-done.4, ...), custom_call_target="tpu_custom_call" | custom-call | tf_op jit(solution)/shard_map/pallas_call | solution.py:244
  122.4 11.3 %all_to_all.93.summed = f32[32,1,256]{2,1,0:T(1,128)S(1)} all-to-all(f32[32,1,256]{2,1,0:T(1,128)S(1)} %get-tuple-element.22), channel_id=1, replica_groups=mesh['grp'=4,'blk'=8] {'grp','blk'}, dimensions={0} | all-to-all | bytes 65536 | tf_op jit(solution)/shard_map/all_to_all | solution.py:182
  133.9 9.0 %all_to_all.94.summed = f32[32,1,256]{2,1,0:T(1,128)S(1)} all-to-all(f32[32,1,256]{2,1,0:T(1,128)S(1)} %shard_map.105), channel_id=1, replica_groups=mesh['grp'=4,'blk'=8] {'grp','blk'}, dimensions={0} | all-to-all | bytes 65536 | tf_op jit(solution)/shard_map/all_to_all | solution.py:182
  143.1 8.9 %all_to_all.95.summed = f32[32,1,256]{2,1,0:T(1,128)S(1)} all-to-all(f32[32,1,256]{2,1,0:T(1,128)S(1)} %shard_map.106), channel_id=1, replica_groups=mesh['grp'=4,'blk'=8] {'grp','blk'}, dimensions={0} | all-to-all | bytes 65536 | tf_op jit(solution)/shard_map/all_to_all | solution.py:182
  152.2 8.9 %all_to_all.96.summed = f32[32,1,256]{2,1,0:T(1,128)S(1)} all-to-all(f32[32,1,256]{2,1,0:T(1,128)S(1)} %shard_map.107), channel_id=1, replica_groups=mesh['grp'=4,'blk'=8] {'grp','blk'}, dimensions={0} | all-to-all | bytes 65536 | tf_op jit(solution)/shard_map/all_to_all | solution.py:182
  162.4 4.5 %shard_map.108 = (f32[640,256]{1,0:T(8,128)S(1)}, bf16[640,256]{1,0:T(8,128)(2,1)}, f32[32,1,256]{2,1,0:T(1,128)S(1)}, f32[256,256]{1,0:T(8,128)}) custom-call(s32[8]{0:T(128)S(1)} %copy-done.10, s32[8]{0:T(128)S(1)} %copy-done.12, s32[1]{0:T(128)S(6)} %copy.10.tile_count, bf16[8,320,128]{2,1,0:T(8,128)(2,1)S(1)} %copy-done.1, ...), custom_call_target="tpu_custom_call" | custom-call | tf_op jit(solution)/shard_map/pallas_call | solution.py:256
  166.9 8.9 %all_to_all.97.summed = f32[32,1,256]{2,1,0:T(1,128)S(1)} all-to-all(f32[32,1,256]{2,1,0:T(1,128)S(1)} %get-tuple-element.24), channel_id=1, replica_groups=mesh['grp'=4,'blk'=8] {'grp','blk'}, dimensions={0} | all-to-all | bytes 65536 | tf_op jit(solution)/shard_map/all_to_all | solution.py:182
  176.1 8.9 %all_to_all.98.summed = f32[32,1,256]{2,1,0:T(1,128)S(1)} all-to-all(f32[32,1,256]{2,1,0:T(1,128)S(1)} %shard_map.109), channel_id=1, replica_groups=mesh['grp'=4,'blk'=8] {'grp','blk'}, dimensions={0} | all-to-all | bytes 65536 | tf_op jit(solution)/shard_map/all_to_all | solution.py:182
  185.2 8.9 %all_to_all.99.summed = f32[32,1,256]{2,1,0:T(1,128)S(1)} all-to-all(f32[32,1,256]{2,1,0:T(1,128)S(1)} %shard_map.110), channel_id=1, replica_groups=mesh['grp'=4,'blk'=8] {'grp','blk'}, dimensions={0} | all-to-all | bytes 65536 | tf_op jit(solution)/shard_map/all_to_all | solution.py:182
  194.4 8.9 %all_to_all.100.summed = f32[32,1,256]{2,1,0:T(1,128)S(1)} all-to-all(f32[32,1,256]{2,1,0:T(1,128)S(1)} %shard_map.111), channel_id=1, replica_groups=mesh['grp'=4,'blk'=8] {'grp','blk'}, dimensions={0} | all-to-all | bytes 65536 | tf_op jit(solution)/shard_map/all_to_all | solution.py:182
  (57 shorter events, 11.8 us)
Async XLA Ops:
  7.2 61.8 %copy-start.12 = (s32[8]{0:T(128)S(1)}, s32[8]{0:T(128)}, u32[]{:S(2)}) copy-start(s32[8]{0:T(128)} %tile_author.5) | copy-start | bytes 100
  7.2 61.8 %copy-start.10 = (s32[8]{0:T(128)S(1)}, s32[8]{0:T(128)}, u32[]{:S(2)}) copy-start(s32[8]{0:T(128)} %tile_paper.5) | copy-start | bytes 100
  7.2 21.0 %copy-start.8 = (f32[256]{0:T(256)S(1)}, f32[256]{0:T(256)}, u32[]{:S(2)}) copy-start(f32[256]{0:T(256)} %param.14) | copy-start | bytes 3076
  7.2 34.4 %copy-start.7 = (f32[256]{0:T(256)S(1)}, f32[256]{0:T(256)}, u32[]{:S(2)}) copy-start(f32[256]{0:T(256)} %param.15) | copy-start | bytes 3076
  7.2 61.7 %all-gather.5.cloned.1.call-start = ((), (), s32[]{:S(2)}) async-start(), calls=%async_computation.17 | async-start | bytes 1179648 | tf_op jit(solution)/shard_map/all_gather | solution.py:254
  8.7 1.1 copy-start
  9.8 0.7 copy-start.9
  10.5 0.7 copy-start.11
  11.1 57.8 %copy-start.1 = (bf16[8,320,128]{2,1,0:T(8,128)(2,1)S(1)}, bf16[8,320,128]{2,1,0:T(8,128)(2,1)}, u32[]{:S(2)}) copy-start(bf16[8,320,128]{2,1,0:T(8,128)(2,1)} %tiles.5) | copy-start | bytes 1966084
  29.6 76.2 %all-gather.9.cloned.1.call-start = ((), (), s32[]{:S(2)}) async-start(), calls=%async_computation.19 | async-start | bytes 1474560 | tf_op jit(solution)/shard_map/all_gather | solution.py:223
  30.5 82.2 %all-gather.7.cloned.1.call-start = ((), (), s32[]{:S(2)}) async-start(), calls=%async_computation.18 | async-start | bytes 2949120 | tf_op jit(solution)/shard_map/all_gather | solution.py:267
  69.0 1.2 copy-start.5
  102.9 9.8 %all-to-all-start.8 = ((f32[32,1,256]{2,1,0:T(1,128)}), f32[32,1,256]{2,1,0:T(1,128)S(1)}, u32[]{:S(2)}, u32[]{:S(2)}) async-start(f32[32,1,256]{2,1,0:T(1,128)} %shard_map.103), calls=%async_computation.8 | async-start | bytes 65536 | tf_op jit(solution)/shard_map/all_to_all | solution.py:182
  105.5 55.7 %all-gather.11.cloned.1.call-start = ((), (), s32[]{:S(2)}) async-start(), calls=%async_computation.20 | async-start | bytes 1179648 | tf_op jit(solution)/shard_map/all_gather | solution.py:254
  112.7 1.7 copy-start.2
  114.5 1.3 copy-start.4
  142.9 60.5 %copy-start.3 = (bf16[640,128]{1,0:T(8,128)(2,1)S(1)}, bf16[640,128]{1,0:T(8,128)(2,1)}, u32[]{:S(2)}) copy-start(bf16[640,128]{1,0:T(8,128)(2,1)} %broadcast_in_dim.11.seeds) | copy-start | bytes 491524
  161.1 1.2 copy-start.6
Sparse Core Ops, SparseCore 0:
  29.7 23.0 all-gather.4
  54.7 24.6 all-gather.8
  81.9 30.2 all-gather.6
  122.6 23.1 all-gather.10

commit v6 on v5

v6 whole, which is shorter than its diff:
```python
import functools

import jax
import jax.numpy as jnp
from jax import lax
from jax.experimental import pallas as pl
from jax.experimental.pallas import tpu as pltpu
from jax.sharding import PartitionSpec as P

AT_DEV = 2
ITERS = 4
ROUNDS = 2
LANES = 128
META = 16

keep_share = 0.8

AXES = ("grp", "blk")
VMEM = pl.BlockSpec(memory_space=pltpu.VMEM)
SMEM = pl.BlockSpec(memory_space=pltpu.SMEM)
HBM = pl.BlockSpec(memory_space=pltpu.HBM)


def call(kernel, out_shape, in_specs, scratch_shapes=()):
    out_specs = jax.tree.map(lambda _: VMEM, out_shape)
    return pl.pallas_call(
        kernel,
        out_shape=out_shape,
        in_specs=in_specs,
        out_specs=out_specs,
        scratch_shapes=list(scratch_shapes),
        compiler_params=pltpu.CompilerParams(vmem_limit_bytes=48 * 1024 * 1024),
    )


def col_scale(parts_ref, target_ref):
    return target_ref[...] / jnp.sum(parts_ref[...], axis=0)


def row_scale(kernel, scale_cols):
    return 1.0 / jnp.sum(kernel * scale_cols, axis=1, keepdims=True)


def spread(value, parts_ref):
    parts_ref[...] = jnp.broadcast_to(value[None], parts_ref.shape)


def split(value):
    high = value.astype(jnp.bfloat16)
    return high, (value - high.astype(jnp.float32)).astype(jnp.bfloat16)


def scale_block(scale_cols):
    wide = jnp.broadcast_to(scale_cols, (LANES, scale_cols.shape[1])).T
    return jnp.concatenate(split(wide), axis=1)


def row_sums(half, block):
    sums = jnp.dot(half, block, preferred_element_type=jnp.float32)
    return sums[:, :LANES] + sums[:, LANES:]


def across(column, classes):
    return jnp.concatenate([column] * (classes // LANES), axis=1)


def dot_rows(left, right):
    return lax.dot_general(
        left, right, (((1,), (1,)), ((), ())), preferred_element_type=jnp.float32
    )


def code_line(lines, rows):
    count = -(-rows // LANES)
    return jnp.concatenate([lines[i : i + 1] for i in range(count)], axis=1)[:, :rows]


def code_column(line, eye):
    wide = jnp.broadcast_to(line, (LANES, line.shape[1])).astype(jnp.bfloat16)
    return dot_rows(eye, wide)


def identity(rows):
    line = lax.broadcasted_iota(jnp.int32, (rows, rows), 0)
    lane = lax.broadcasted_iota(jnp.int32, (rows, rows), 1)
    return jnp.where(line == lane, 1.0, 0.0).astype(jnp.bfloat16)


def seeds_of(line, classes):
    class_line = lax.broadcasted_iota(jnp.int32, (classes, line.shape[1]), 0)
    return jnp.where(class_line.astype(jnp.float32) == line, 1.0, 0.0).astype(jnp.bfloat16)


def pack_kernel(rows, papers_in, authors_in, count_in, tiles, codes, *rest):
    *outs, tile_paper, tile_author, tile_count, arrived, ready = rest
    slots = len(outs)
    me = lax.axis_index("blk")
    scalars = [
        pltpu.make_async_copy(source, target, ready.at[i])
        for i, (source, target) in enumerate(
            zip((papers_in, authors_in, count_in), (tile_paper, tile_author, tile_count))
        )
    ]
    for copy in scalars:
        copy.start()
    copies = []
    for shift, out in enumerate(outs):
        slot = lax.rem(me + shift, slots)
        copy = pltpu.make_async_copy(tiles.at[slot], out.at[pl.ds(0, rows)], arrived.at[shift])
        copy.start()
        copies.append(copy)
    for copy in scalars:
        copy.wait()
    line = lax.broadcasted_iota(jnp.int32, (META, LANES), 0)
    code_rows = -(-rows // LANES)
    for shift, out in enumerate(outs):
        slot = lax.rem(me + shift, slots)
        paper = tile_paper[slot]
        live = slot < tile_count[0]
        block = codes[paper]
        for author in range(AT_DEV):
            chosen = jnp.where(live & (tile_author[slot] == author), 1.0, 0.0)
            block = jnp.where(line == code_rows + author, chosen, block)
        block = jnp.where(line == code_rows + AT_DEV, paper.astype(jnp.float32), block)
        out[rows:, :] = block.astype(jnp.bfloat16)
    for copy in copies:
        copy.wait()


def first_sum_kernel(authors, tile_paper, tile_count, tiles, codes, class_prior, parts):
    slots, rows, columns = tiles.shape
    classes = parts.shape[2]
    ones = jnp.ones((8, columns), jnp.bfloat16)
    total = authors * class_prior[...]
    for paper in range(codes.shape[0]):
        weight = jnp.zeros((rows, columns), jnp.float32)
        for slot in range(slots):
            chosen = (slot < tile_count[0]) & (tile_paper[slot] == paper)
            weight = weight + jnp.where(chosen, tiles[slot].astype(jnp.float32), 0.0)
        high, low = split(weight)
        high, low = split(dot_rows(ones, high) + dot_rows(ones, low))
        seeds = seeds_of(code_line(codes[paper], rows), classes)
        total = total + (dot_rows(high, seeds) + dot_rows(low, seeds))[:1]
    spread(total, parts)


def next_sum(kernel, summed, class_target, parts):
    scale_rows = row_scale(kernel, col_scale(summed, class_target))
    spread(jnp.sum(scale_rows * kernel, axis=0, keepdims=True), parts)


def first_author_kernel(rows, summed, class_prior, class_target, *rest):
    *packed, full, parts = rest
    classes = full.shape[1]
    code_rows = -(-rows // LANES)
    totals = [jnp.zeros((classes, LANES), jnp.float32) for _ in range(AT_DEV)]
    for one in packed:
        meta = one[rows:, :].astype(jnp.float32)
        seeds = seeds_of(code_line(meta, rows), classes)
        parcel = jnp.dot(seeds, one[:rows, :], preferred_element_type=jnp.float32)
        parcel = parcel.astype(jnp.bfloat16).astype(jnp.float32)
        for author in range(AT_DEV):
            chosen = meta[code_rows + author : code_rows + author + 1]
            totals[author] = totals[author] + parcel * chosen
    kernel = jnp.concatenate([total.T for total in totals], axis=0) + class_prior[...]
    full[...] = kernel
    next_sum(kernel, summed, class_target, parts)


def author_kernel(
    rows, paper, gathered, summed, class_prior, class_target, *rest
):
    *packed, full, parts, shares_in, arrived = rest
    slots = len(packed)
    classes = full.shape[1]
    code_rows = -(-rows // LANES)
    paper_tiles = gathered.shape[0] // slots // rows
    me = lax.axis_index("blk")
    copies = []
    for shift in range(slots):
        source = lax.rem(me + slots - shift, slots)
        start = pl.multiple_of((source * paper_tiles + paper[shift]) * rows, rows)
        copy = pltpu.make_async_copy(
            gathered.at[pl.ds(start, rows)], shares_in.at[shift], arrived.at[shift]
        )
        copy.start()
        copies.append(copy)
    scale_cols = col_scale(summed, class_target)
    block = scale_block(scale_cols)
    eye = identity(rows)
    totals = [jnp.zeros((LANES, classes), jnp.float32) for _ in range(AT_DEV)]
    lane = lax.broadcasted_iota(jnp.int32, (rows, classes), 1).astype(jnp.float32)
    for shift, one in enumerate(packed):
        meta = one[rows:, :].astype(jnp.float32)
        code = across(code_column(code_line(meta, rows), eye), classes)
        copies[shift].wait()
        half = shares_in[shift]
        scale_rows = across(keep_share / row_sums(half, block), classes)
        share = half.astype(jnp.float32) * scale_cols * scale_rows
        labels = share + jnp.where(code == lane, 1.0 - keep_share, 0.0)
        parcel = lax.dot_general(
            one[:rows, :],
            labels.astype(jnp.bfloat16),
            (((0,), (0,)), ((), ())),
            preferred_element_type=jnp.float32,
        )
        parcel = parcel.astype(jnp.bfloat16).astype(jnp.float32)
        for author in range(AT_DEV):
            chosen = meta[code_rows + author : code_rows + author + 1, :1]
            totals[author] = totals[author] + parcel * chosen
    kernel = jnp.concatenate(totals, axis=0) + class_prior[...]
    full[...] = kernel
    spread(jnp.sum(kernel, axis=0, keepdims=True), parts)


def paper_kernel(
    tile_paper, tile_author, tile_count, tiles, gathered, own, summed, class_prior,
    class_target, full, half, parts, scores, shares_in, arrived,
):
    slots, rows, columns = tiles.shape
    classes = full.shape[1]
    copies = []
    for slot in range(slots):
        start = pl.multiple_of((slot * AT_DEV + tile_author[slot]) * columns, columns)
        copy = pltpu.make_async_copy(
            gathered.at[pl.ds(start, columns)], shares_in.at[slot], arrived.at[slot]
        )
        copy.start()
        copies.append(copy)
    scale_cols = col_scale(summed, class_target)
    block = scale_block(scale_cols)
    scaled = own[...] * scale_cols
    scores[...] = scaled * (classes / jnp.sum(scaled, axis=1, keepdims=True))
    wide = jnp.concatenate([tiles[slot] for slot in range(slots)], axis=1)
    labels = []
    for slot in range(slots):
        copies[slot].wait()
        kernel = shares_in[slot]
        high, low = split(kernel)
        sums = row_sums(high, block) + jnp.dot(
            low, block[:, :LANES], preferred_element_type=jnp.float32
        )
        share = kernel * scale_cols * across(1.0 / sums, classes)
        labels.append(share.astype(jnp.bfloat16))
    column = jnp.zeros((1, classes), jnp.float32)
    for paper in range(full.shape[0] // rows):
        chosen = []
        for slot in range(slots):
            keep = (slot < tile_count[0]) & (tile_paper[slot] == paper)
            chosen.append(jnp.where(keep, labels[slot], jnp.zeros_like(labels[slot])))
        mass = jnp.dot(wide, jnp.concatenate(chosen, axis=0), preferred_element_type=jnp.float32)
        kernel = mass + class_prior[...]
        full[paper * rows : (paper + 1) * rows, :] = kernel
        half[paper * rows : (paper + 1) * rows, :] = kernel.astype(jnp.bfloat16)
        column = column + jnp.sum(kernel, axis=0, keepdims=True)
    spread(column, parts)


def balance_kernel(kernel_ref, summed, class_target, parts):
    next_sum(kernel_ref[...], summed, class_target, parts)


def final_kernel(rows, kernel_ref, summed, class_target, codes, out):
    classes = out.shape[1]
    scale_cols = col_scale(summed, class_target)
    eye = identity(rows)
    lane = lax.broadcasted_iota(jnp.int32, (rows, classes), 1).astype(jnp.float32)
    for paper in range(codes.shape[0]):
        part = slice(paper * rows, (paper + 1) * rows)
        scaled = kernel_ref[part, :] * scale_cols
        share = scaled * (1.0 / jnp.sum(scaled, axis=1, keepdims=True))
        code = across(code_column(code_line(codes[paper], rows), eye), classes)
        updated = keep_share * share + jnp.where(code == lane, 1.0 - keep_share, 0.0)
        out[part, :] = classes * updated


def exchange(parts):
    return lax.all_to_all(parts, AXES, split_axis=0, concat_axis=0, tiled=True)


def on_device(
    tile_values,
    tile_paper,
    tile_author,
    tile_count,
    seed_class,
    train_mask,
    class_prior,
    class_target,
):
    f32 = jnp.float32
    bf16 = jnp.bfloat16
    i32 = jnp.int32
    shape = jax.ShapeDtypeStruct
    slots, rows, columns = tile_values.shape
    classes = class_prior.shape[0]
    papers = seed_class.shape[0]
    authors = AT_DEV * columns
    paper_tiles = papers // rows
    devices = lax.axis_size(AXES)
    code_rows = -(-rows // LANES)
    prior = class_prior.reshape(1, classes)
    target = class_target.reshape(1, classes)
    parts = shape((devices, 1, classes), f32)

    code = jnp.where(train_mask == 1, seed_class, -1).astype(f32)
    codes = jnp.pad(code.reshape(paper_tiles, rows), ((0, 0), (0, code_rows * LANES - rows)))
    codes = codes.reshape(paper_tiles, code_rows, LANES)
    codes = jnp.pad(codes, ((0, 0), (0, META - code_rows), (0, 0)))

    packed = call(
        functools.partial(pack_kernel, rows),
        (shape((rows + META, columns), bf16),) * slots,
        [HBM, HBM, HBM, HBM, VMEM],
        [
            pltpu.SMEM((slots,), i32),
            pltpu.SMEM((slots,), i32),
            pltpu.SMEM((1,), i32),
            pltpu.SemaphoreType.DMA((slots,)),
            pltpu.SemaphoreType.DMA((3,)),
        ],
    )(tile_paper, tile_author, tile_count, tile_values, codes)
    packed = [
        lax.ppermute(one, "blk", [(i, (i + shift) % slots) for i in range(slots)]) if shift else one
        for shift, one in enumerate(packed)
    ]
    local = call(
        functools.partial(first_sum_kernel, authors), parts, [SMEM, SMEM, VMEM, VMEM, VMEM]
    )(tile_paper, tile_count, tile_values, codes, prior)
    summed = exchange(local)
    paper_of = jnp.stack([one[rows + code_rows + AT_DEV, 0] for one in packed]).astype(i32)
    paper_of, *packed = lax.optimization_barrier((paper_of, *packed))

    author_out = (shape((authors, classes), f32), parts)
    paper_out = (
        shape((papers, classes), f32),
        shape((papers, classes), bf16),
        parts,
        shape((authors, classes), f32),
    )

    def balance(kernel, summed, count):
        for _ in range(count):
            summed = exchange(call(balance_kernel, parts, [VMEM] * 3)(kernel, summed, target))
        return summed

    for repeat in range(ROUNDS):
        if repeat == 0:
            own, local = call(
                functools.partial(first_author_kernel, rows), author_out, [VMEM] * (3 + slots)
            )(summed, prior, target, *packed)
            left = ITERS - 2
        else:
            own, local = call(
                functools.partial(author_kernel, rows),
                author_out,
                [SMEM, HBM] + [VMEM] * (3 + slots),
                [
                    pltpu.VMEM((slots, rows, classes), bf16),
                    pltpu.SemaphoreType.DMA((slots,)),
                ],
            )(paper_of, gathered, summed, prior, target, *packed)
            left = ITERS - 1
        gathered = lax.all_gather(own, "blk", tiled=True)
        summed = balance(own, exchange(local), left)
        kernel, half, local, author_scores = call(
            paper_kernel,
            paper_out,
            [SMEM, SMEM, SMEM, VMEM, HBM, VMEM, VMEM, VMEM, VMEM],
            [
                pltpu.VMEM((slots, columns, classes), f32),
                pltpu.SemaphoreType.DMA((slots,)),
            ],
        )(tile_paper, tile_author, tile_count, tile_values, gathered, own, summed, prior, target)
        if repeat + 1 < ROUNDS:
            gathered = lax.all_gather(half, "blk", tiled=True)
        summed = balance(kernel, exchange(local), ITERS - 1)
    paper_scores = call(
        functools.partial(final_kernel, rows), shape((papers, classes), f32), [VMEM] * 4
    )(kernel, summed, target, codes)
    return paper_scores, author_scores


def solution(mesh):
    placed = (
        P(("grp", "blk"), None, None),
        P(("grp", "blk")),
        P(("grp", "blk")),
        P(("grp", "blk")),
        P(("grp", "blk")),
        P(("grp", "blk")),
        P(),
        P(),
    )
    return jax.shard_map(
        on_device,
        mesh=mesh,
        in_specs=placed,
        out_specs=(P(("grp", "blk"), None), P(("grp", "blk"), None)),
        check_vma=False,
    )
```

time: 212 us -> 218 us (1.028)
  blocking collectives: 155 us -> 138 us
  starting transfers between devices: 2.73 us -> 14.5 us
  local copies, waits for them, and re-layouts: 8.85 us -> 18.9 us
  Pallas kernels: 21.8 us -> 30.1 us
  waiting for transfers between devices: 7.03 us -> 0.08 us
    all_to_all x1 -> x0, blocking collectives: 16.5 us -> none  [on_device(): lax.all_to_all(packed, 'blk', split_axis=0, concat_axis=0, tiled=True)]
    ppermute x0 -> x7, starting transfers between devices: none -> 9.78 us  [on_device(): lax.ppermute(one, 'blk', [(i, (i + shift) % slots) for i in range(slots)])]
    all_to_all x1, waiting for transfers between devices: 6.94 us -> 0.01 us  [exchange(): return lax.all_to_all(parts, AXES, split_axis=0, concat_axis=0, tiled=True)]
    another operation x0 -> x1, local copies, waits for them, and re-layouts: none -> 5.11 us  [on_device(): jnp.stack([one[rows + code_rows + AT_DEV, 0] for one in packed]).astype(i32)]
    slice x0 -> x8, local copies, waits for them, and re-layouts: none -> 4.34 us  [on_device(): one[rows + code_rows + AT_DEV, 0]]
    pallas_call x6 -> x7, Pallas kernels: 18.7 us -> 23 us  [the longest x2 10.6 us: on_device(): call(paper_kernel, paper_out, [SMEM, SMEM, SMEM, VMEM, HBM, VMEM, VMEM, V...]
    pallas_call x12 -> x11, Pallas kernels: 3.1 us -> 7.04 us  [balance(): call(balance_kernel, parts, [VMEM] * 3)(kernel, summed, target)]
    unnamed x26 -> x28, local copies, waits for them, and re-layouts: 7.92 us -> 9.37 us
  transfers between devices with their start and end apart: 5 -> 11, of which waited for: 1 -> 0; matrix products, arithmetic and copies ran while one was open for 0% -> 4% of each run, Pallas kernels for 3% -> 4%
where the time goes in v6:
time: 218 us; the launch traced here: 217 us
  blocking collectives  138 us (63%)
  Pallas kernels  30.1 us (14%)
  local copies, waits for them, and re-layouts  18.9 us (9%)
  between operations  14.6 us (7%)
  starting transfers between devices  14.5 us (7%)
    all_to_all x15, blocking collectives, exchange(): return lax.all_to_all(parts, AXES, split_axis=0, concat_axis=0, tiled=True)  138 us
    pallas_call x2, Pallas kernels, on_device(): call(paper_kernel, paper_out, [SMEM, SMEM, SMEM, VMEM, HBM, VMEM, VMEM, V...  10.6 us
    ppermute x7, starting transfers between devices, on_device(): lax.ppermute(one, 'blk', [(i, (i + shift) % slots) for i in range(slots)])  9.78 us
    unnamed x28, local copies, waits for them, and re-layouts  9.37 us
    pallas_call x11, Pallas kernels, balance(): call(balance_kernel, parts, [VMEM] * 3)(kernel, summed, target)  7.04 us
    pallas_call x1, Pallas kernels, on_device(): call(functools.partial(author_kernel, rows), author_out, [SMEM, HBM] + [V...  6.94 us
    another operation x1, local copies, waits for them, and re-layouts, on_device(): jnp.stack([one[rows + code_rows + AT_DEV, 0] for one in packed]).astype(i32)  5.11 us
    all_to_all x1, starting transfers between devices, exchange(): return lax.all_to_all(parts, AXES, split_axis=0, concat_axis=0, tiled=True)  4.61 us
  transfers between devices with their start and end apart: 11, of which 0 were waited for; matrix products, arithmetic and copies ran while one was open for 4% of the time, Pallas kernels for 4%

profile of v6, /device:TPU:0, one launch (start us, length us, event | category | flops | bytes accessed | tf_op | source)
XLA Modules:
  0.0 217.2 jit_solution(11384689308140649020)
XLA Ops:
  12.6 2.6 %collective-permute-start.1 = (bf16[336,128]{1,0:T(8,128)(2,1)S(1)}, bf16[336,128]{1,0:T(8,128)(2,1)S(1)}, u32[]{:S(2)}, u32[]{:S(2)}) collective-permute-start(bf16[336,128]{1,0:T(8,128)(2,1)S(1)} %get-tuple-element.31), channel_id=1, source_target_pairs={{0,2},{1,3},{2,4},{3,5},{4,6},{5,7},{6,0},{7,1},{8,10},{9,11},{10,... | collective-permute-start | bytes 258056 | tf_op jit(solution)/shard_map/ppermute | solution.py:324
  15.2 2.4 %collective-permute-start.2 = (bf16[336,128]{1,0:T(8,128)(2,1)S(1)}, bf16[336,128]{1,0:T(8,128)(2,1)S(1)}, u32[]{:S(2)}, u32[]{:S(2)}) collective-permute-start(bf16[336,128]{1,0:T(8,128)(2,1)S(1)} %get-tuple-element.32), channel_id=1, source_target_pairs={{0,3},{1,4},{2,5},{3,6},{4,7},{5,0},{6,1},{7,2},{8,11},{9,12},{10,... | collective-permute-start | bytes 258056 | tf_op jit(solution)/shard_map/ppermute | solution.py:324
  18.2 2.1 collective-permute-start.5
  22.6 1.8 shard_map.96
  24.5 4.6 %all-to-all-start = ((f32[32,1,256]{2,1,0:T(1,128)}), f32[32,1,256]{2,1,0:T(1,128)S(1)}, u32[]{:S(2)}, u32[]{:S(2)}) async-start(f32[32,1,256]{2,1,0:T(1,128)} %shard_map.96), calls=%async_computation | async-start | bytes 65536 | tf_op jit(solution)/shard_map/all_to_all | solution.py:278
  33.5 5.1 %stack.3 = bf16[8]{0:T(256)(128)(2,1)S(1)} concatenate(bf16[1]{0:T(256)(128)(2,1)} %bitcast, bf16[1]{0:T(256)(128)(2,1)} %bitcast.1, bf16[1]{0:T(256)(128)(2,1)} %bitcast.2, bf16[1]{0:T(256)(128)(2,1)} %bitcast.3, bf16[1]{0:T(256)(128)(2,1)} %bitcast.4, bf16[1]{0:T(256)(128)(2,1)} %bitcast.5, bf16[1]{0:T(256)(128)(2,1)} %bitcast.6, bf16[1]{0:T(256)(128)(2,1)} %bitcast.7), dimensions={0} | concatenate | bytes 32 | tf_op jit(solution)/shard_map/stack | solution.py:331
  41.5 12.9 %all_to_all.80.summed = f32[32,1,256]{2,1,0:T(1,128)S(1)} all-to-all(f32[32,1,256]{2,1,0:T(1,128)S(1)} %get-tuple-element.47), channel_id=1, replica_groups=mesh['grp'=4,'blk'=8] {'grp','blk'}, dimensions={0} | all-to-all | bytes 65536 | tf_op jit(solution)/shard_map/all_to_all | solution.py:278
  55.5 9.0 %all_to_all.81.summed = f32[32,1,256]{2,1,0:T(1,128)S(1)} all-to-all(f32[32,1,256]{2,1,0:T(1,128)S(1)} %shard_map.98), channel_id=1, replica_groups=mesh['grp'=4,'blk'=8] {'grp','blk'}, dimensions={0} | all-to-all | bytes 65536 | tf_op jit(solution)/shard_map/all_to_all | solution.py:278
  65.7 8.9 %all_to_all.82.summed = f32[32,1,256]{2,1,0:T(1,128)S(1)} all-to-all(f32[32,1,256]{2,1,0:T(1,128)S(1)} %shard_map.99), channel_id=1, replica_groups=mesh['grp'=4,'blk'=8] {'grp','blk'}, dimensions={0} | all-to-all | bytes 65536 | tf_op jit(solution)/shard_map/all_to_all | solution.py:278
  76.2 5.3 %shard_map.100 = (f32[640,256]{1,0:T(8,128)S(1)}, bf16[640,256]{1,0:T(8,128)(2,1)}, f32[32,1,256]{2,1,0:T(1,128)S(1)}, f32[256,256]{1,0:T(8,128)}) custom-call(s32[8]{0:T(128)S(1)} %copy-done.11, s32[8]{0:T(128)S(1)} %copy-done.13, s32[1]{0:T(128)S(6)} %copy.10.count_in.tile_count, bf16[8,320,128]{2,1,0:T(8,128)(2,1)S(1)} %copy-done.1, ...), custom_call_target="tpu_custom_call" | custom-call | tf_op jit(solution)/shard_map/pallas_call | solution.py:366
  81.6 9.0 %all_to_all.83.summed = f32[32,1,256]{2,1,0:T(1,128)S(1)} all-to-all(f32[32,1,256]{2,1,0:T(1,128)S(1)} %get-tuple-element.50), channel_id=1, replica_groups=mesh['grp'=4,'blk'=8] {'grp','blk'}, dimensions={0} | all-to-all | bytes 65536 | tf_op jit(solution)/shard_map/all_to_all | solution.py:278
  90.8 9.0 %all_to_all.84.summed = f32[32,1,256]{2,1,0:T(1,128)S(1)} all-to-all(f32[32,1,256]{2,1,0:T(1,128)S(1)} %shard_map.101), channel_id=1, replica_groups=mesh['grp'=4,'blk'=8] {'grp','blk'}, dimensions={0} | all-to-all | bytes 65536 | tf_op jit(solution)/shard_map/all_to_all | solution.py:278
  100.0 8.9 %all_to_all.85.summed = f32[32,1,256]{2,1,0:T(1,128)S(1)} all-to-all(f32[32,1,256]{2,1,0:T(1,128)S(1)} %shard_map.102), channel_id=1, replica_groups=mesh['grp'=4,'blk'=8] {'grp','blk'}, dimensions={0} | all-to-all | bytes 65536 | tf_op jit(solution)/shard_map/all_to_all | solution.py:278
  109.2 8.9 %all_to_all.86.summed = f32[32,1,256]{2,1,0:T(1,128)S(1)} all-to-all(f32[32,1,256]{2,1,0:T(1,128)S(1)} %shard_map.103), channel_id=1, replica_groups=mesh['grp'=4,'blk'=8] {'grp','blk'}, dimensions={0} | all-to-all | bytes 65536 | tf_op jit(solution)/shard_map/all_to_all | solution.py:278
  119.9 6.9 %shard_map.104 = (f32[256,256]{1,0:T(8,128)}, f32[32,1,256]{2,1,0:T(1,128)S(1)}) custom-call(s32[8]{0:T(128)S(1)} %convert_element_type.11.paper, bf16[5120,256]{1,0:T(8,128)(2,1)S(1)} %copy-done.2, f32[32,1,256]{2,1,0:T(1,128)S(1)} %all_to_all.86.summed, f32[1,256]{1,0:T(1,128)S(1)} %bitcast.29, f32[1,256]{1,0:T(1,128)S(1)} %bitcast.17, ...), custom_call_target="tpu_custom_call" | custom-call | tf_op jit(solution)/shard_map/pallas_call | solution.py:354
  126.8 8.9 %all_to_all.87.summed = f32[32,1,256]{2,1,0:T(1,128)S(1)} all-to-all(f32[32,1,256]{2,1,0:T(1,128)S(1)} %get-tuple-element.52), channel_id=1, replica_groups=mesh['grp'=4,'blk'=8] {'grp','blk'}, dimensions={0} | all-to-all | bytes 65536 | tf_op jit(solution)/shard_map/all_to_all | solution.py:278
  136.9 9.0 %all_to_all.88.summed = f32[32,1,256]{2,1,0:T(1,128)S(1)} all-to-all(f32[32,1,256]{2,1,0:T(1,128)S(1)} %shard_map.105), channel_id=1, replica_groups=mesh['grp'=4,'blk'=8] {'grp','blk'}, dimensions={0} | all-to-all | bytes 65536 | tf_op jit(solution)/shard_map/all_to_all | solution.py:278
  147.0 8.9 %all_to_all.89.summed = f32[32,1,256]{2,1,0:T(1,128)S(1)} all-to-all(f32[32,1,256]{2,1,0:T(1,128)S(1)} %shard_map.106), channel_id=1, replica_groups=mesh['grp'=4,'blk'=8] {'grp','blk'}, dimensions={0} | all-to-all | bytes 65536 | tf_op jit(solution)/shard_map/all_to_all | solution.py:278
  157.1 8.9 %all_to_all.90.summed = f32[32,1,256]{2,1,0:T(1,128)S(1)} all-to-all(f32[32,1,256]{2,1,0:T(1,128)S(1)} %shard_map.107), channel_id=1, replica_groups=mesh['grp'=4,'blk'=8] {'grp','blk'}, dimensions={0} | all-to-all | bytes 65536 | tf_op jit(solution)/shard_map/all_to_all | solution.py:278
  167.6 5.3 %shard_map.108 = (f32[640,256]{1,0:T(8,128)S(1)}, bf16[640,256]{1,0:T(8,128)(2,1)}, f32[32,1,256]{2,1,0:T(1,128)S(1)}, f32[256,256]{1,0:T(8,128)}) custom-call(s32[8]{0:T(128)S(1)} %copy-done.11, s32[8]{0:T(128)S(1)} %copy-done.13, s32[1]{0:T(128)S(6)} %copy.10.count_in.tile_count, bf16[8,320,128]{2,1,0:T(8,128)(2,1)S(1)} %copy-done.1, ...), custom_call_target="tpu_custom_call" | custom-call | tf_op jit(solution)/shard_map/pallas_call | solution.py:366
  172.9 8.9 %all_to_all.91.summed = f32[32,1,256]{2,1,0:T(1,128)S(1)} all-to-all(f32[32,1,256]{2,1,0:T(1,128)S(1)} %get-tuple-element.54), channel_id=1, replica_groups=mesh['grp'=4,'blk'=8] {'grp','blk'}, dimensions={0} | all-to-all | bytes 65536 | tf_op jit(solution)/shard_map/all_to_all | solution.py:278
  182.1 8.9 %all_to_all.92.summed = f32[32,1,256]{2,1,0:T(1,128)S(1)} all-to-all(f32[32,1,256]{2,1,0:T(1,128)S(1)} %shard_map.109), channel_id=1, replica_groups=mesh['grp'=4,'blk'=8] {'grp','blk'}, dimensions={0} | all-to-all | bytes 65536 | tf_op jit(solution)/shard_map/all_to_all | solution.py:278
  191.3 8.9 %all_to_all.93.summed = f32[32,1,256]{2,1,0:T(1,128)S(1)} all-to-all(f32[32,1,256]{2,1,0:T(1,128)S(1)} %shard_map.110), channel_id=1, replica_groups=mesh['grp'=4,'blk'=8] {'grp','blk'}, dimensions={0} | all-to-all | bytes 65536 | tf_op jit(solution)/shard_map/all_to_all | solution.py:278
  200.5 8.9 %all_to_all.94.summed = f32[32,1,256]{2,1,0:T(1,128)S(1)} all-to-all(f32[32,1,256]{2,1,0:T(1,128)S(1)} %shard_map.111), channel_id=1, replica_groups=mesh['grp'=4,'blk'=8] {'grp','blk'}, dimensions={0} | all-to-all | bytes 65536 | tf_op jit(solution)/shard_map/all_to_all | solution.py:278
  (77 shorter events, 28.1 us)
Async XLA Ops:
  7.2 67.4 %copy-start.11 = (s32[8]{0:T(128)S(1)}, s32[8]{0:T(128)}, u32[]{:S(2)}) copy-start(s32[8]{0:T(128)} %tile_paper.5) | copy-start | bytes 100
  7.2 67.4 %copy-start.13 = (s32[8]{0:T(128)S(1)}, s32[8]{0:T(128)}, u32[]{:S(2)}) copy-start(s32[8]{0:T(128)} %tile_author.3) | copy-start | bytes 100
  7.2 67.4 %copy-start.9 = (f32[256]{0:T(256)S(1)}, f32[256]{0:T(256)}, u32[]{:S(2)}) copy-start(f32[256]{0:T(256)} %param.14) | copy-start | bytes 3076
  7.2 47.2 %copy-start.6 = (f32[256]{0:T(256)S(1)}, f32[256]{0:T(256)}, u32[]{:S(2)}) copy-start(f32[256]{0:T(256)} %param.15) | copy-start | bytes 3076
  8.7 1.1 copy-start
  9.8 0.7 copy-start.10
  11.1 63.5 %copy-start.1 = (bf16[8,320,128]{2,1,0:T(8,128)(2,1)S(1)}, bf16[8,320,128]{2,1,0:T(8,128)(2,1)}, u32[]{:S(2)}) copy-start(bf16[8,320,128]{2,1,0:T(8,128)(2,1)} %tiles.7) | copy-start | bytes 1966084
  12.1 6.0 %collective-permute-start = (bf16[336,128]{1,0:T(8,128)(2,1)S(1)}, bf16[336,128]{1,0:T(8,128)(2,1)S(1)}, u32[]{:S(2)}, u32[]{:S(2)}) collective-permute-start(bf16[336,128]{1,0:T(8,128)(2,1)S(1)} %get-tuple-element.30), channel_id=1, source_target_pairs={{0,1},{1,2},{2,3},{3,4},{4,5},{5,6},{6,7},{7,0},{8,9},{9,10},{10,1... | collective-permute-start | bytes 258056 | tf_op jit(solution)/shard_map/ppermute | solution.py:324
  12.6 7.7 %collective-permute-start.1 = (bf16[336,128]{1,0:T(8,128)(2,1)S(1)}, bf16[336,128]{1,0:T(8,128)(2,1)S(1)}, u32[]{:S(2)}, u32[]{:S(2)}) collective-permute-start(bf16[336,128]{1,0:T(8,128)(2,1)S(1)} %get-tuple-element.31), channel_id=1, source_target_pairs={{0,2},{1,3},{2,4},{3,5},{4,6},{5,7},{6,0},{7,1},{8,10},{9,11},{10,... | collective-permute-start | bytes 258056 | tf_op jit(solution)/shard_map/ppermute | solution.py:324
  15.2 15.6 %collective-permute-start.2 = (bf16[336,128]{1,0:T(8,128)(2,1)S(1)}, bf16[336,128]{1,0:T(8,128)(2,1)S(1)}, u32[]{:S(2)}, u32[]{:S(2)}) collective-permute-start(bf16[336,128]{1,0:T(8,128)(2,1)S(1)} %get-tuple-element.32), channel_id=1, source_target_pairs={{0,3},{1,4},{2,5},{3,6},{4,7},{5,0},{6,1},{7,2},{8,11},{9,12},{10,... | collective-permute-start | bytes 258056 | tf_op jit(solution)/shard_map/ppermute | solution.py:324
  17.6 13.8 %collective-permute-start.3 = (bf16[336,128]{1,0:T(8,128)(2,1)S(1)}, bf16[336,128]{1,0:T(8,128)(2,1)S(1)}, u32[]{:S(2)}, u32[]{:S(2)}) collective-permute-start(bf16[336,128]{1,0:T(8,128)(2,1)S(1)} %get-tuple-element.33), channel_id=1, source_target_pairs={{0,4},{1,5},{2,6},{3,7},{4,0},{5,1},{6,2},{7,3},{8,12},{9,13},{10,... | collective-permute-start | bytes 258056 | tf_op jit(solution)/shard_map/ppermute | solution.py:324
  18.1 13.8 %collective-permute-start.4 = (bf16[336,128]{1,0:T(8,128)(2,1)S(1)}, bf16[336,128]{1,0:T(8,128)(2,1)S(1)}, u32[]{:S(2)}, u32[]{:S(2)}) collective-permute-start(bf16[336,128]{1,0:T(8,128)(2,1)S(1)} %get-tuple-element.34), channel_id=1, source_target_pairs={{0,5},{1,6},{2,7},{3,0},{4,1},{5,2},{6,3},{7,4},{8,13},{9,14},{10,... | collective-permute-start | bytes 258056 | tf_op jit(solution)/shard_map/ppermute | solution.py:324
  18.2 14.2 %collective-permute-start.5 = (bf16[336,128]{1,0:T(8,128)(2,1)S(1)}, bf16[336,128]{1,0:T(8,128)(2,1)S(1)}, u32[]{:S(2)}, u32[]{:S(2)}) collective-permute-start(bf16[336,128]{1,0:T(8,128)(2,1)S(1)} %get-tuple-element.35), channel_id=1, source_target_pairs={{0,6},{1,7},{2,0},{3,1},{4,2},{5,3},{6,4},{7,5},{8,14},{9,15},{10,... | collective-permute-start | bytes 258056 | tf_op jit(solution)/shard_map/ppermute | solution.py:324
  20.3 12.6 %collective-permute-start.6 = (bf16[336,128]{1,0:T(8,128)(2,1)S(1)}, bf16[336,128]{1,0:T(8,128)(2,1)S(1)}, u32[]{:S(2)}, u32[]{:S(2)}) collective-permute-start(bf16[336,128]{1,0:T(8,128)(2,1)S(1)} %get-tuple-element.36), channel_id=1, source_target_pairs={{0,7},{1,0},{2,1},{3,2},{4,3},{5,4},{6,5},{7,6},{8,15},{9,8},{10,9... | collective-permute-start | bytes 258056 | tf_op jit(solution)/shard_map/ppermute | solution.py:324
  21.9 0.7 copy-start.7
  24.5 14.2 %all-to-all-start = ((f32[32,1,256]{2,1,0:T(1,128)}), f32[32,1,256]{2,1,0:T(1,128)S(1)}, u32[]{:S(2)}, u32[]{:S(2)}) async-start(f32[32,1,256]{2,1,0:T(1,128)} %shard_map.96), calls=%async_computation | async-start | bytes 65536 | tf_op jit(solution)/shard_map/all_to_all | solution.py:278
  29.1 45.5 %all-gather.4.cloned.1.call-start = ((), (), s32[]{:S(2)}) async-start(), calls=%async_computation.16 | async-start | bytes 2359296 | tf_op jit(solution)/shard_map/all_gather | solution.py:364
  38.6 0.7 copy-start.5
  39.3 0.7 copy-start.8
  41.4 76.7 %all-gather.6.cloned.1.call-start = ((), (), s32[]{:S(2)}) async-start(), calls=%async_computation.17 | async-start | bytes 2949120 | tf_op jit(solution)/shard_map/all_gather | solution.py:376
  74.6 1.6 copy-start.4
  81.6 84.5 %all-gather.8.cloned.1.call-start = ((), (), s32[]{:S(2)}) async-start(), calls=%async_computation.18 | async-start | bytes 2359296 | tf_op jit(solution)/shard_map/all_gather | solution.py:364
  118.1 1.7 copy-start.2
  166.0 1.6 copy-start.3
  (1 other events, 0.7 us)
Sparse Core Ops, SparseCore 0:
  41.5 29.1 all-gather.3
  81.7 26.7 all-gather.5
  127.0 24.4 all-gather.7

commit v7 on v6

v7 whole, which is shorter than its diff:
```python
import functools

import jax
import jax.numpy as jnp
from jax import lax
from jax.experimental import pallas as pl
from jax.experimental.pallas import tpu as pltpu
from jax.sharding import PartitionSpec as P

AT_DEV = 2
ITERS = 4
ROUNDS = 2
LANES = 128
META = 16

keep_share = 0.8

AXES = ("grp", "blk")
VMEM = pl.BlockSpec(memory_space=pltpu.VMEM)
SMEM = pl.BlockSpec(memory_space=pltpu.SMEM)
HBM = pl.BlockSpec(memory_space=pltpu.HBM)


def call(kernel, out_shape, in_specs, scratch_shapes=(), out_specs=None):
    if out_specs is None:
        out_specs = jax.tree.map(lambda _: VMEM, out_shape)
    return pl.pallas_call(
        kernel,
        out_shape=out_shape,
        in_specs=in_specs,
        out_specs=out_specs,
        scratch_shapes=list(scratch_shapes),
        compiler_params=pltpu.CompilerParams(vmem_limit_bytes=48 * 1024 * 1024),
    )


def col_scale(parts_ref, target_ref):
    return target_ref[...] / jnp.sum(parts_ref[...], axis=0)


def row_scale(kernel, scale_cols):
    return 1.0 / jnp.sum(kernel * scale_cols, axis=1, keepdims=True)


def spread(value, parts_ref):
    parts_ref[...] = jnp.broadcast_to(value[None], parts_ref.shape)


def split(value):
    high = value.astype(jnp.bfloat16)
    return high, (value - high.astype(jnp.float32)).astype(jnp.bfloat16)


def scale_block(scale_cols):
    wide = jnp.broadcast_to(scale_cols, (LANES, scale_cols.shape[1])).T
    return jnp.concatenate(split(wide), axis=1)


def row_sums(half, block):
    sums = jnp.dot(half, block, preferred_element_type=jnp.float32)
    return sums[:, :LANES] + sums[:, LANES:]


def across(column, classes):
    return jnp.concatenate([column] * (classes // LANES), axis=1)


def dot_rows(left, right):
    return lax.dot_general(
        left, right, (((1,), (1,)), ((), ())), preferred_element_type=jnp.float32
    )


def code_lines(seed_class, train_mask, rows):
    code = jnp.where(train_mask[...] == 1, seed_class[...], -1).astype(jnp.float32)
    line = jnp.concatenate([code[i : i + 1] for i in range(code.shape[0])], axis=1)
    papers = line.shape[1]
    wide = jnp.broadcast_to(line, (8, papers))
    lines = []
    for start in range(0, papers, rows):
        lines.append((pltpu.roll(wide, papers - start, 1) if start else wide)[:1, :rows])
    return lines


def meta_line(meta, rows):
    count = -(-rows // LANES)
    return jnp.concatenate([meta[i : i + 1] for i in range(count)], axis=1)[:, :rows]


def code_column(line, eye):
    wide = jnp.broadcast_to(line, (LANES, line.shape[1])).astype(jnp.bfloat16)
    return dot_rows(eye, wide)


def identity(rows):
    line = lax.broadcasted_iota(jnp.int32, (rows, rows), 0)
    lane = lax.broadcasted_iota(jnp.int32, (rows, rows), 1)
    return jnp.where(line == lane, 1.0, 0.0).astype(jnp.bfloat16)


def seeds_of(line, classes):
    class_line = lax.broadcasted_iota(jnp.int32, (classes, line.shape[1]), 0)
    return jnp.where(class_line.astype(jnp.float32) == line, 1.0, 0.0).astype(jnp.bfloat16)


def pack_kernel(rows, tile_count, *refs):
    count = 7
    ins, places, outs = refs[:count], refs[count : 2 * count], refs[2 * count : -2]
    ready, arrived = refs[-2:]
    tile_paper, tile_author, seed_class, train_mask = places[:4]
    tiles = ins[-1]
    slots = len(outs)
    me = lax.axis_index("blk")
    moves = [
        pltpu.make_async_copy(source, place, ready.at[i])
        for i, (source, place) in enumerate(zip(ins, places))
    ]
    for copy in moves:
        copy.start()
    copies = []
    for shift, out in enumerate(outs):
        slot = lax.rem(me + shift, slots)
        copy = pltpu.make_async_copy(tiles.at[slot], out.at[pl.ds(0, rows)], arrived.at[shift])
        copy.start()
        copies.append(copy)
    for copy in moves[:4]:
        copy.wait()
    line = lax.broadcasted_iota(jnp.int32, (META, LANES), 0)
    code_rows = -(-rows // LANES)
    blocks = []
    for codes in code_lines(seed_class, train_mask, rows):
        pad = jnp.full((1, code_rows * LANES - rows), -1.0, jnp.float32)
        codes = jnp.concatenate([codes, pad], axis=1)
        block = jnp.zeros((META, LANES), jnp.float32)
        for i in range(code_rows):
            block = jnp.where(line == i, codes[:, i * LANES : (i + 1) * LANES], block)
        blocks.append(block)
    for shift, out in enumerate(outs):
        slot = lax.rem(me + shift, slots)
        paper = tile_paper[slot]
        live = slot < tile_count[0]
        block = blocks[0]
        for i in range(1, len(blocks)):
            block = jnp.where(paper == i, blocks[i], block)
        for author in range(AT_DEV):
            chosen = jnp.where(live & (tile_author[slot] == author), 1.0, 0.0)
            block = jnp.where(line == code_rows + author, chosen, block)
        block = jnp.where(line == code_rows + AT_DEV, paper.astype(jnp.float32), block)
        out[rows:, :] = block.astype(jnp.bfloat16)
    for copy in moves[4:] + copies:
        copy.wait()


def first_sum_kernel(
    authors, tile_paper, tile_count, tiles, seed_class, train_mask, class_prior, parts
):
    slots, rows, columns = tiles.shape
    classes = parts.shape[2]
    ones = jnp.ones((8, columns), jnp.bfloat16)
    total = authors * class_prior[...]
    for paper, codes in enumerate(code_lines(seed_class, train_mask, rows)):
        weight = jnp.zeros((rows, columns), jnp.float32)
        for slot in range(slots):
            chosen = (slot < tile_count[0]) & (tile_paper[slot] == paper)
            weight = weight + jnp.where(chosen, tiles[slot].astype(jnp.float32), 0.0)
        high, low = split(weight)
        high, low = split(dot_rows(ones, high) + dot_rows(ones, low))
        seeds = seeds_of(codes, classes)
        total = total + (dot_rows(high, seeds) + dot_rows(low, seeds))[:1]
    spread(total, parts)


def next_sum(kernel, summed, class_target, parts):
    scale_rows = row_scale(kernel, col_scale(summed, class_target))
    spread(jnp.sum(scale_rows * kernel, axis=0, keepdims=True), parts)


def first_author_kernel(rows, summed, class_prior, class_target, *rest):
    *packed, full, sent, parts = rest
    classes = full.shape[1]
    code_rows = -(-rows // LANES)
    totals = [jnp.zeros((classes, LANES), jnp.float32) for _ in range(AT_DEV)]
    for one in packed:
        meta = one[rows:, :].astype(jnp.float32)
        seeds = seeds_of(meta_line(meta, rows), classes)
        parcel = jnp.dot(seeds, one[:rows, :], preferred_element_type=jnp.float32)
        parcel = parcel.astype(jnp.bfloat16).astype(jnp.float32)
        for author in range(AT_DEV):
            chosen = meta[code_rows + author : code_rows + author + 1]
            totals[author] = totals[author] + parcel * chosen
    kernel = jnp.concatenate([total.T for total in totals], axis=0) + class_prior[...]
    full[...] = kernel
    sent[...] = kernel
    next_sum(kernel, summed, class_target, parts)


def author_kernel(rows, gathered, summed, class_prior, class_target, *rest):
    *packed, full, sent, parts, shares_in, arrived = rest
    slots = len(packed)
    classes = full.shape[1]
    code_rows = -(-rows // LANES)
    paper_tiles = gathered.shape[0] // slots // rows
    me = lax.axis_index("blk")
    metas = [one[rows:, :].astype(jnp.float32) for one in packed]
    copies = []
    for shift in range(slots):
        source = lax.rem(me + slots - shift, slots)
        at = code_rows + AT_DEV
        paper = jnp.max(metas[shift][at : at + 1]).astype(jnp.int32)
        start = pl.multiple_of((source * paper_tiles + paper) * rows, rows)
        copy = pltpu.make_async_copy(
            gathered.at[pl.ds(start, rows)], shares_in.at[shift], arrived.at[shift]
        )
        copy.start()
        copies.append(copy)
    scale_cols = col_scale(summed, class_target)
    block = scale_block(scale_cols)
    eye = identity(rows)
    codes = [code_column(meta_line(meta, rows), eye) for meta in metas]
    totals = [jnp.zeros((LANES, classes), jnp.float32) for _ in range(AT_DEV)]
    lane = lax.broadcasted_iota(jnp.int32, (rows, classes), 1).astype(jnp.float32)
    for copy in copies:
        copy.wait()
    for shift, one in enumerate(packed):
        half = shares_in[shift]
        scale_rows = across(keep_share / row_sums(half, block), classes)
        share = half.astype(jnp.float32) * scale_cols * scale_rows
        labels = share + jnp.where(across(codes[shift], classes) == lane, 1.0 - keep_share, 0.0)
        parcel = lax.dot_general(
            one[:rows, :],
            labels.astype(jnp.bfloat16),
            (((0,), (0,)), ((), ())),
            preferred_element_type=jnp.float32,
        )
        parcel = parcel.astype(jnp.bfloat16).astype(jnp.float32)
        for author in range(AT_DEV):
            at = code_rows + author
            totals[author] = totals[author] + parcel * metas[shift][at : at + 1, :1]
    kernel = jnp.concatenate(totals, axis=0) + class_prior[...]
    full[...] = kernel
    sent[...] = kernel
    spread(jnp.sum(kernel, axis=0, keepdims=True), parts)


def paper_kernel(
    tile_paper, tile_author, tile_count, tiles, gathered, summed, class_prior, class_target,
    full, half, parts, shares_in, arrived,
):
    slots, rows, columns = tiles.shape
    classes = full.shape[1]
    copies = []
    for slot in range(slots):
        start = pl.multiple_of((slot * AT_DEV + tile_author[slot]) * columns, columns)
        copy = pltpu.make_async_copy(
            gathered.at[pl.ds(start, columns)], shares_in.at[slot], arrived.at[slot]
        )
        copy.start()
        copies.append(copy)
    scale_cols = col_scale(summed, class_target)
    block = scale_block(scale_cols)
    wide = jnp.concatenate([tiles[slot] for slot in range(slots)], axis=1)
    labels = []
    for copy in copies:
        copy.wait()
    for slot in range(slots):
        kernel = shares_in[slot]
        high, low = split(kernel)
        sums = row_sums(high, block) + jnp.dot(
            low, block[:, :LANES], preferred_element_type=jnp.float32
        )
        share = kernel * scale_cols * across(1.0 / sums, classes)
        labels.append(share.astype(jnp.bfloat16))
    column = jnp.zeros((1, classes), jnp.float32)
    for paper in range(full.shape[0] // rows):
        chosen = []
        for slot in range(slots):
            keep = (slot < tile_count[0]) & (tile_paper[slot] == paper)
            chosen.append(jnp.where(keep, labels[slot], jnp.zeros_like(labels[slot])))
        mass = jnp.dot(wide, jnp.concatenate(chosen, axis=0), preferred_element_type=jnp.float32)
        kernel = mass + class_prior[...]
        full[paper * rows : (paper + 1) * rows, :] = kernel
        half[paper * rows : (paper + 1) * rows, :] = kernel.astype(jnp.bfloat16)
        column = column + jnp.sum(kernel, axis=0, keepdims=True)
    spread(column, parts)


def balance_kernel(kernel_ref, summed, class_target, parts):
    next_sum(kernel_ref[...], summed, class_target, parts)


def final_kernel(
    rows, kernel_ref, summed, own, author_summed, class_target, seed_class, train_mask, out, scores
):
    classes = out.shape[1]
    scaled = own[...] * col_scale(author_summed, class_target)
    scores[...] = scaled * (classes / jnp.sum(scaled, axis=1, keepdims=True))
    scale_cols = col_scale(summed, class_target)
    eye = identity(rows)
    lane = lax.broadcasted_iota(jnp.int32, (rows, classes), 1).astype(jnp.float32)
    for paper, line in enumerate(code_lines(seed_class, train_mask, rows)):
        part = slice(paper * rows, (paper + 1) * rows)
        scaled = kernel_ref[part, :] * scale_cols
        share = scaled * (1.0 / jnp.sum(scaled, axis=1, keepdims=True))
        code = across(code_column(line, eye), classes)
        updated = keep_share * share + jnp.where(code == lane, 1.0 - keep_share, 0.0)
        out[part, :] = classes * updated


def in_hbm(value):
    return pltpu.with_memory_space_constraint(value, pltpu.HBM)


def exchange(parts):
    return lax.all_to_all(parts, AXES, split_axis=0, concat_axis=0, tiled=True)


def on_device(
    tile_values,
    tile_paper,
    tile_author,
    tile_count,
    seed_class,
    train_mask,
    class_prior,
    class_target,
):
    f32 = jnp.float32
    bf16 = jnp.bfloat16
    shape = jax.ShapeDtypeStruct
    slots, rows, columns = tile_values.shape
    classes = class_prior.shape[0]
    papers = seed_class.shape[0]
    authors = AT_DEV * columns
    paper_tiles = papers // rows
    devices = lax.axis_size(AXES)
    prior = class_prior.reshape(1, classes)
    target = class_target.reshape(1, classes)
    seed_class = seed_class.reshape(papers // LANES, LANES)
    train_mask = train_mask.reshape(papers // LANES, LANES)
    parts = shape((devices, 1, classes), f32)

    inputs = (
        tile_paper, tile_author, seed_class, train_mask, prior, target, tile_values,
    )
    places = (SMEM, SMEM, VMEM, VMEM, VMEM, VMEM, VMEM)
    moved = call(
        functools.partial(pack_kernel, rows),
        tuple(shape(one.shape, one.dtype) for one in inputs)
        + (shape((rows + META, columns), bf16),) * slots,
        [SMEM] + [HBM] * len(inputs),
        [pltpu.SemaphoreType.DMA((len(inputs),)), pltpu.SemaphoreType.DMA((slots,))],
        places + (VMEM,) * slots,
    )(tile_count, *(in_hbm(one) for one in inputs))
    packed = moved[len(inputs) :]
    tile_paper, tile_author, seed_class, train_mask, prior, target, tile_values = (
        moved[: len(inputs)]
    )
    packed = [
        lax.ppermute(one, "blk", [(i, (i + shift) % slots) for i in range(slots)]) if shift else one
        for shift, one in enumerate(packed)
    ]
    local = call(
        functools.partial(first_sum_kernel, authors), parts, [SMEM, SMEM] + [VMEM] * 4
    )(tile_paper, tile_count, tile_values, seed_class, train_mask, prior)
    summed = exchange(local)

    author_out = (shape((authors, classes), f32), shape((authors, classes), f32), parts)
    paper_out = (shape((papers, classes), f32), shape((papers, classes), bf16), parts)

    def balance(kernel, summed, count):
        for _ in range(count):
            summed = exchange(call(balance_kernel, parts, [VMEM] * 3)(kernel, summed, target))
        return summed

    for repeat in range(ROUNDS):
        if repeat == 0:
            own, sent, local = call(
                functools.partial(first_author_kernel, rows), author_out, [VMEM] * (3 + slots)
            )(summed, prior, target, *packed)
            left = ITERS - 2
        else:
            own, sent, local = call(
                functools.partial(author_kernel, rows),
                author_out,
                [HBM] + [VMEM] * (3 + slots),
                [
                    pltpu.VMEM((slots, rows, classes), bf16),
                    pltpu.SemaphoreType.DMA((slots,)),
                ],
            )(in_hbm(gathered), summed, prior, target, *packed)
            left = ITERS - 1
        gathered = lax.all_gather(sent, "blk", tiled=True)
        author_summed = balance(own, exchange(local), left)
        kernel, half, local = call(
            paper_kernel,
            paper_out,
            [SMEM, SMEM, SMEM, VMEM, HBM, VMEM, VMEM, VMEM],
            [
                pltpu.VMEM((slots, columns, classes), f32),
                pltpu.SemaphoreType.DMA((slots,)),
            ],
        )(
            tile_paper, tile_author, tile_count, tile_values, in_hbm(gathered), author_summed,
            prior, target,
        )
        if repeat + 1 < ROUNDS:
            gathered = lax.all_gather(half, "blk", tiled=True)
        summed = balance(kernel, exchange(local), ITERS - 1)
    return call(
        functools.partial(final_kernel, rows),
        (shape((papers, classes), f32), shape((authors, classes), f32)),
        [VMEM] * 7,
    )(kernel, summed, own, author_summed, target, seed_class, train_mask)


def solution(mesh):
    placed = (
        P(("grp", "blk"), None, None),
        P(("grp", "blk")),
        P(("grp", "blk")),
        P(("grp", "blk")),
        P(("grp", "blk")),
        P(("grp", "blk")),
        P(),
        P(),
    )
    return jax.shard_map(
        on_device,
        mesh=mesh,
        in_specs=placed,
        out_specs=(P(("grp", "blk"), None), P(("grp", "blk"), None)),
        check_vma=False,
    )
```

time: 218 us -> 191 us (0.88)
  local copies, waits for them, and re-layouts: 18.9 us -> 0 us
  Pallas kernels: 30.1 us -> 20.2 us
  blocking collectives: 138 us -> 146 us
  starting transfers between devices: 14.5 us -> 9.88 us
    unnamed x28 -> x0, local copies, waits for them, and re-layouts: 9.37 us -> none
    all_to_all x15 -> x16, blocking collectives: 138 us -> 146 us  [exchange(): return lax.all_to_all(parts, AXES, split_axis=0, concat_axis=0, tiled=True)]
    another operation x1 -> x0, local copies, waits for them, and re-layouts: 5.11 us -> none  [on_device(): jnp.stack([one[rows + code_rows + AT_DEV, 0] for one in packed]).astype(i32)]
    pallas_call x11, Pallas kernels: 7.04 us -> 2.3 us  [balance(): call(balance_kernel, parts, [VMEM] * 3)(kernel, summed, target)]
    all_to_all x1 -> x0, starting transfers between devices: 4.61 us -> none  [exchange(): return lax.all_to_all(parts, AXES, split_axis=0, concat_axis=0, tiled=True)]
    slice x8 -> x0, local copies, waits for them, and re-layouts: 4.34 us -> none  [on_device(): one[rows + code_rows + AT_DEV, 0]]
    pallas_call x2, Pallas kernels: 10.6 us -> 6.85 us  [on_device(): call(paper_kernel, paper_out, [SMEM, SMEM, SMEM, VMEM, HBM, VMEM, VMEM, V...]
  transfers between devices with their start and end apart: 11 -> 10, of which waited for: 0 -> 0; matrix products, arithmetic and copies ran while one was open for 4% -> 0% of each run, Pallas kernels for 4% -> 1%
where the time goes in v7:
time: 191 us
  blocking collectives  146 us (76%)
  Pallas kernels  20.2 us (11%)
  between operations  14.5 us (8%)
  starting transfers between devices  9.88 us (5%)
    all_to_all x16, blocking collectives, exchange(): return lax.all_to_all(parts, AXES, split_axis=0, concat_axis=0, tiled=True)  146 us
    ppermute x7, starting transfers between devices, on_device(): lax.ppermute(one, 'blk', [(i, (i + shift) % slots) for i in range(slots)])  9.76 us
    pallas_call x2, Pallas kernels, on_device(): call(paper_kernel, paper_out, [SMEM, SMEM, SMEM, VMEM, HBM, VMEM, VMEM, V...  6.85 us
    pallas_call x1, Pallas kernels, on_device(): call(functools.partial(author_kernel, rows), author_out, [HBM] + [VMEM] *...  5.04 us
  transfers between devices with their start and end apart: 10, of which 0 were waited for; matrix products, arithmetic and copies ran while one was open for 0% of the time, Pallas kernels for 1%

profile of v7, /device:TPU:0, one launch (start us, length us, event | category | flops | bytes accessed | tf_op | source)
XLA Modules:
  0.0 190.7 jit_solution(6026792418439887135)
XLA Ops:
  7.9 2.2 %shard_map.95 = (s32[8]{0:T(128)S(1)}, s32[8]{0:T(128)S(1)}, s32[5,128]{1,0:T(8,128)S(1)}, s32[5,128]{1,0:T(8,128)S(1)}, f32[1,256]{1,0:T(1,128)S(1)}, /*index=5...) custom-call(s32[1]{0:T(128)S(6)} %copy.10.tile_count, ...), custom_call_target="tpu_custom_call" | custom-call | tf_op jit(solution)/shard_map/pallas_call | solution.py:346
  10.5 2.6 %collective-permute-start.1 = (bf16[336,128]{1,0:T(8,128)(2,1)S(1)}, bf16[336,128]{1,0:T(8,128)(2,1)S(1)}, u32[]{:S(2)}, u32[]{:S(2)}) collective-permute-start(bf16[336,128]{1,0:T(8,128)(2,1)S(1)} %get-tuple-element.37), channel_id=1, source_target_pairs={{0,2},{1,3},{2,4},{3,5},{4,6},{5,7},{6,0},{7,1},{8,10},{9,11},{10,... | collective-permute-start | bytes 258056 | tf_op jit(solution)/shard_map/ppermute | solution.py:359
  13.1 2.4 %collective-permute-start.2 = (bf16[336,128]{1,0:T(8,128)(2,1)S(1)}, bf16[336,128]{1,0:T(8,128)(2,1)S(1)}, u32[]{:S(2)}, u32[]{:S(2)}) collective-permute-start(bf16[336,128]{1,0:T(8,128)(2,1)S(1)} %get-tuple-element.38), channel_id=1, source_target_pairs={{0,3},{1,4},{2,5},{3,6},{4,7},{5,0},{6,1},{7,2},{8,11},{9,12},{10,... | collective-permute-start | bytes 258056 | tf_op jit(solution)/shard_map/ppermute | solution.py:359
  16.1 2.1 %collective-permute-start.5 = (bf16[336,128]{1,0:T(8,128)(2,1)S(1)}, bf16[336,128]{1,0:T(8,128)(2,1)S(1)}, u32[]{:S(2)}, u32[]{:S(2)}) collective-permute-start(bf16[336,128]{1,0:T(8,128)(2,1)S(1)} %get-tuple-element.41), channel_id=1, source_target_pairs={{0,6},{1,7},{2,0},{3,1},{4,2},{5,3},{6,4},{7,5},{8,14},{9,15},{10,... | collective-permute-start | bytes 258056 | tf_op jit(solution)/shard_map/ppermute | solution.py:359
  18.2 1.6 collective-permute-start.6
  21.1 11.7 %all_to_all.80.summed = f32[32,1,256]{2,1,0:T(1,128)S(1)} all-to-all(f32[32,1,256]{2,1,0:T(1,128)S(1)} %shard_map.96), channel_id=1, replica_groups=mesh['grp'=4,'blk'=8] {'grp','blk'}, dimensions={0} | all-to-all | bytes 65536 | tf_op jit(solution)/shard_map/all_to_all | solution.py:314
  34.2 8.9 %all_to_all.81.summed = f32[32,1,256]{2,1,0:T(1,128)S(1)} all-to-all(f32[32,1,256]{2,1,0:T(1,128)S(1)} %get-tuple-element.45), channel_id=1, replica_groups=mesh['grp'=4,'blk'=8] {'grp','blk'}, dimensions={0} | all-to-all | bytes 65536 | tf_op jit(solution)/shard_map/all_to_all | solution.py:314
  43.4 8.9 %all_to_all.82.summed = f32[32,1,256]{2,1,0:T(1,128)S(1)} all-to-all(f32[32,1,256]{2,1,0:T(1,128)S(1)} %shard_map.98), channel_id=1, replica_groups=mesh['grp'=4,'blk'=8] {'grp','blk'}, dimensions={0} | all-to-all | bytes 65536 | tf_op jit(solution)/shard_map/all_to_all | solution.py:314
  52.5 8.9 %all_to_all.83.summed = f32[32,1,256]{2,1,0:T(1,128)S(1)} all-to-all(f32[32,1,256]{2,1,0:T(1,128)S(1)} %shard_map.99), channel_id=1, replica_groups=mesh['grp'=4,'blk'=8] {'grp','blk'}, dimensions={0} | all-to-all | bytes 65536 | tf_op jit(solution)/shard_map/all_to_all | solution.py:314
  61.5 3.4 %shard_map.100 = (f32[640,256]{1,0:T(8,128)S(1)}, bf16[640,256]{1,0:T(8,128)(2,1)}, f32[32,1,256]{2,1,0:T(1,128)S(1)}) custom-call(s32[8]{0:T(128)S(1)} %get-tuple-element.28.tile_paper, s32[8]{0:T(128)S(1)} %get-tuple-element.29.tile_author, s32[1]{0:T(128)S(6)} %copy.10.tile_count, bf16[8,320,128]{2,1,0:T(8,128)(2,1)S(1)} %get-tuple-element.30.tiles, ...), custom_call_target="tpu_custom_call" | custom-call | tf_op jit(solution)/shard_map/pallas_call | solution.py:394
  65.0 9.1 %all_to_all.84.summed = f32[32,1,256]{2,1,0:T(1,128)S(1)} all-to-all(f32[32,1,256]{2,1,0:T(1,128)S(1)} %get-tuple-element.48), channel_id=1, replica_groups=mesh['grp'=4,'blk'=8] {'grp','blk'}, dimensions={0} | all-to-all | bytes 65536 | tf_op jit(solution)/shard_map/all_to_all | solution.py:314
  74.3 8.9 %all_to_all.85.summed = f32[32,1,256]{2,1,0:T(1,128)S(1)} all-to-all(f32[32,1,256]{2,1,0:T(1,128)S(1)} %shard_map.101), channel_id=1, replica_groups=mesh['grp'=4,'blk'=8] {'grp','blk'}, dimensions={0} | all-to-all | bytes 65536 | tf_op jit(solution)/shard_map/all_to_all | solution.py:314
  83.5 8.9 %all_to_all.86.summed = f32[32,1,256]{2,1,0:T(1,128)S(1)} all-to-all(f32[32,1,256]{2,1,0:T(1,128)S(1)} %shard_map.102), channel_id=1, replica_groups=mesh['grp'=4,'blk'=8] {'grp','blk'}, dimensions={0} | all-to-all | bytes 65536 | tf_op jit(solution)/shard_map/all_to_all | solution.py:314
  92.7 8.9 %all_to_all.87.summed = f32[32,1,256]{2,1,0:T(1,128)S(1)} all-to-all(f32[32,1,256]{2,1,0:T(1,128)S(1)} %shard_map.103), channel_id=1, replica_groups=mesh['grp'=4,'blk'=8] {'grp','blk'}, dimensions={0} | all-to-all | bytes 65536 | tf_op jit(solution)/shard_map/all_to_all | solution.py:314
  101.6 5.0 %shard_map.104 = (f32[256,256]{1,0:T(8,128)S(1)}, f32[256,256]{1,0:T(8,128)}, f32[32,1,256]{2,1,0:T(1,128)S(1)}) custom-call(bf16[5120,256]{1,0:T(8,128)(2,1)} %all-gather.6.cloned.1.call-done.gathered, f32[32,1,256]{2,1,0:T(1,128)S(1)} %all_to_all.87.summed, f32[1,256]{1,0:T(1,128)S(1)} %get-tuple-element.33.class_prior, ...), custom_call_target="tpu_custom_call" | custom-call | tf_op jit(solution)/shard_map/pallas_call | solution.py:382
  106.7 9.0 %all_to_all.88.summed = f32[32,1,256]{2,1,0:T(1,128)S(1)} all-to-all(f32[32,1,256]{2,1,0:T(1,128)S(1)} %get-tuple-element.51), channel_id=1, replica_groups=mesh['grp'=4,'blk'=8] {'grp','blk'}, dimensions={0} | all-to-all | bytes 65536 | tf_op jit(solution)/shard_map/all_to_all | solution.py:314
  115.8 8.9 %all_to_all.89.summed = f32[32,1,256]{2,1,0:T(1,128)S(1)} all-to-all(f32[32,1,256]{2,1,0:T(1,128)S(1)} %shard_map.105), channel_id=1, replica_groups=mesh['grp'=4,'blk'=8] {'grp','blk'}, dimensions={0} | all-to-all | bytes 65536 | tf_op jit(solution)/shard_map/all_to_all | solution.py:314
  125.0 8.9 %all_to_all.90.summed = f32[32,1,256]{2,1,0:T(1,128)S(1)} all-to-all(f32[32,1,256]{2,1,0:T(1,128)S(1)} %shard_map.106), channel_id=1, replica_groups=mesh['grp'=4,'blk'=8] {'grp','blk'}, dimensions={0} | all-to-all | bytes 65536 | tf_op jit(solution)/shard_map/all_to_all | solution.py:314
  134.1 8.9 %all_to_all.91.summed.author_summed = f32[32,1,256]{2,1,0:T(1,128)S(1)} all-to-all(f32[32,1,256]{2,1,0:T(1,128)S(1)} %shard_map.107), channel_id=1, replica_groups=mesh['grp'=4,'blk'=8] {'grp','blk'}, dimensions={0} | all-to-all | bytes 65536 | tf_op jit(solution)/shard_map/all_to_all | solution.py:314
  143.0 3.4 %shard_map.108 = (f32[640,256]{1,0:T(8,128)S(1)}, bf16[640,256]{1,0:T(8,128)(2,1)}, f32[32,1,256]{2,1,0:T(1,128)S(1)}) custom-call(s32[8]{0:T(128)S(1)} %get-tuple-element.28.tile_paper, s32[8]{0:T(128)S(1)} %get-tuple-element.29.tile_author, s32[1]{0:T(128)S(6)} %copy.10.tile_count, bf16[8,320,128]{2,1,0:T(8,128)(2,1)S(1)} %get-tuple-element.30.tiles, ...), custom_call_target="tpu_custom_call" | custom-call | tf_op jit(solution)/shard_map/pallas_call | solution.py:394
  146.5 8.9 %all_to_all.92.summed = f32[32,1,256]{2,1,0:T(1,128)S(1)} all-to-all(f32[32,1,256]{2,1,0:T(1,128)S(1)} %get-tuple-element.53), channel_id=1, replica_groups=mesh['grp'=4,'blk'=8] {'grp','blk'}, dimensions={0} | all-to-all | bytes 65536 | tf_op jit(solution)/shard_map/all_to_all | solution.py:314
  155.7 8.9 %all_to_all.93.summed = f32[32,1,256]{2,1,0:T(1,128)S(1)} all-to-all(f32[32,1,256]{2,1,0:T(1,128)S(1)} %shard_map.109), channel_id=1, replica_groups=mesh['grp'=4,'blk'=8] {'grp','blk'}, dimensions={0} | all-to-all | bytes 65536 | tf_op jit(solution)/shard_map/all_to_all | solution.py:314
  164.8 8.9 %all_to_all.94.summed = f32[32,1,256]{2,1,0:T(1,128)S(1)} all-to-all(f32[32,1,256]{2,1,0:T(1,128)S(1)} %shard_map.110), channel_id=1, replica_groups=mesh['grp'=4,'blk'=8] {'grp','blk'}, dimensions={0} | all-to-all | bytes 65536 | tf_op jit(solution)/shard_map/all_to_all | solution.py:314
  174.0 8.9 %all_to_all.95.summed = f32[32,1,256]{2,1,0:T(1,128)S(1)} all-to-all(f32[32,1,256]{2,1,0:T(1,128)S(1)} %shard_map.111), channel_id=1, replica_groups=mesh['grp'=4,'blk'=8] {'grp','blk'}, dimensions={0} | all-to-all | bytes 65536 | tf_op jit(solution)/shard_map/all_to_all | solution.py:314
  (33 shorter events, 7.4 us)
Async XLA Ops:
  7.2 54.3 %all-gather.4.cloned.1.call-start = ((), (), s32[]{:S(2)}) async-start(), calls=%async_computation.16 | async-start | bytes 2359296 | tf_op jit(solution)/shard_map/all_gather | solution.py:392
  10.1 6.0 %collective-permute-start = (bf16[336,128]{1,0:T(8,128)(2,1)S(1)}, bf16[336,128]{1,0:T(8,128)(2,1)S(1)}, u32[]{:S(2)}, u32[]{:S(2)}) collective-permute-start(bf16[336,128]{1,0:T(8,128)(2,1)S(1)} %get-tuple-element.36), channel_id=1, source_target_pairs={{0,1},{1,2},{2,3},{3,4},{4,5},{5,6},{6,7},{7,0},{8,9},{9,10},{10,1... | collective-permute-start | bytes 258056 | tf_op jit(solution)/shard_map/ppermute | solution.py:359
  10.5 7.7 %collective-permute-start.1 = (bf16[336,128]{1,0:T(8,128)(2,1)S(1)}, bf16[336,128]{1,0:T(8,128)(2,1)S(1)}, u32[]{:S(2)}, u32[]{:S(2)}) collective-permute-start(bf16[336,128]{1,0:T(8,128)(2,1)S(1)} %get-tuple-element.37), channel_id=1, source_target_pairs={{0,2},{1,3},{2,4},{3,5},{4,6},{5,7},{6,0},{7,1},{8,10},{9,11},{10,... | collective-permute-start | bytes 258056 | tf_op jit(solution)/shard_map/ppermute | solution.py:359
  13.1 19.6 %collective-permute-start.2 = (bf16[336,128]{1,0:T(8,128)(2,1)S(1)}, bf16[336,128]{1,0:T(8,128)(2,1)S(1)}, u32[]{:S(2)}, u32[]{:S(2)}) collective-permute-start(bf16[336,128]{1,0:T(8,128)(2,1)S(1)} %get-tuple-element.38), channel_id=1, source_target_pairs={{0,3},{1,4},{2,5},{3,6},{4,7},{5,0},{6,1},{7,2},{8,11},{9,12},{10,... | collective-permute-start | bytes 258056 | tf_op jit(solution)/shard_map/ppermute | solution.py:359
  15.4 17.3 %collective-permute-start.3 = (bf16[336,128]{1,0:T(8,128)(2,1)S(1)}, bf16[336,128]{1,0:T(8,128)(2,1)S(1)}, u32[]{:S(2)}, u32[]{:S(2)}) collective-permute-start(bf16[336,128]{1,0:T(8,128)(2,1)S(1)} %get-tuple-element.39), channel_id=1, source_target_pairs={{0,4},{1,5},{2,6},{3,7},{4,0},{5,1},{6,2},{7,3},{8,12},{9,13},{10,... | collective-permute-start | bytes 258056 | tf_op jit(solution)/shard_map/ppermute | solution.py:359
  16.0 16.8 %collective-permute-start.4 = (bf16[336,128]{1,0:T(8,128)(2,1)S(1)}, bf16[336,128]{1,0:T(8,128)(2,1)S(1)}, u32[]{:S(2)}, u32[]{:S(2)}) collective-permute-start(bf16[336,128]{1,0:T(8,128)(2,1)S(1)} %get-tuple-element.40), channel_id=1, source_target_pairs={{0,5},{1,6},{2,7},{3,0},{4,1},{5,2},{6,3},{7,4},{8,13},{9,14},{10,... | collective-permute-start | bytes 258056 | tf_op jit(solution)/shard_map/ppermute | solution.py:359
  16.1 16.7 %collective-permute-start.5 = (bf16[336,128]{1,0:T(8,128)(2,1)S(1)}, bf16[336,128]{1,0:T(8,128)(2,1)S(1)}, u32[]{:S(2)}, u32[]{:S(2)}) collective-permute-start(bf16[336,128]{1,0:T(8,128)(2,1)S(1)} %get-tuple-element.41), channel_id=1, source_target_pairs={{0,6},{1,7},{2,0},{3,1},{4,2},{5,3},{6,4},{7,5},{8,14},{9,15},{10,... | collective-permute-start | bytes 258056 | tf_op jit(solution)/shard_map/ppermute | solution.py:359
  18.2 14.5 %collective-permute-start.6 = (bf16[336,128]{1,0:T(8,128)(2,1)S(1)}, bf16[336,128]{1,0:T(8,128)(2,1)S(1)}, u32[]{:S(2)}, u32[]{:S(2)}) collective-permute-start(bf16[336,128]{1,0:T(8,128)(2,1)S(1)} %get-tuple-element.42), channel_id=1, source_target_pairs={{0,7},{1,0},{2,1},{3,2},{4,3},{5,4},{6,5},{7,6},{8,15},{9,8},{10,9... | collective-permute-start | bytes 258056 | tf_op jit(solution)/shard_map/ppermute | solution.py:359
  34.2 67.4 %all-gather.6.cloned.1.call-start = ((), (), s32[]{:S(2)}) async-start(), calls=%async_computation.17 | async-start | bytes 2949120 | tf_op jit(solution)/shard_map/all_gather | solution.py:407
  64.9 78.1 %all-gather.8.cloned.1.call-start = ((), (), s32[]{:S(2)}) async-start(), calls=%async_computation.18 | async-start | bytes 2359296 | tf_op jit(solution)/shard_map/all_gather | solution.py:392
Sparse Core Ops, SparseCore 0:
  34.3 24.3 all-gather.3
  65.0 27.7 all-gather.5
  106.8 24.3 all-gather.7

commit v8 on v7

--- a/solution.py
+++ b/solution.py
@@ -105,24 +105,30 @@
 
 def pack_kernel(rows, tile_count, *refs):
     count = 7
-    ins, places, outs = refs[:count], refs[count : 2 * count], refs[2 * count : -2]
-    ready, arrived = refs[-2:]
+    ins, places = refs[:count], refs[count : 2 * count]
+    keep, swap, ready, arrived = refs[2 * count :]
     tile_paper, tile_author, seed_class, train_mask = places[:4]
     tiles = ins[-1]
-    slots = len(outs)
+    pairs = keep.shape[0]
     me = lax.axis_index("blk")
+    pair, side = lax.div(me, 2), lax.rem(me, 2)
     moves = [
         pltpu.make_async_copy(source, place, ready.at[i])
         for i, (source, place) in enumerate(zip(ins, places))
     ]
     for copy in moves:
         copy.start()
+    outs = []
     copies = []
-    for shift, out in enumerate(outs):
-        slot = lax.rem(me + shift, slots)
-        copy = pltpu.make_async_copy(tiles.at[slot], out.at[pl.ds(0, rows)], arrived.at[shift])
-        copy.start()
-        copies.append(copy)
+    for k in range(pairs):
+        for way, (out, to) in enumerate(((keep, side), (swap, 1 - side))):
+            slot = 2 * lax.bitwise_xor(pair, k) + to
+            copy = pltpu.make_async_copy(
+                tiles.at[slot], out.at[k, pl.ds(0, rows)], arrived.at[way, k]
+            )
+            copy.start()
+            copies.append(copy)
+            outs.append((out, k, slot))
     for copy in moves[:4]:
         copy.wait()
     line = lax.broadcasted_iota(jnp.int32, (META, LANES), 0)
@@ -135,8 +141,7 @@
         for i in range(code_rows):
             block = jnp.where(line == i, codes[:, i * LANES : (i + 1) * LANES], block)
         blocks.append(block)
-    for shift, out in enumerate(outs):
-        slot = lax.rem(me + shift, slots)
+    for out, k, slot in outs:
         paper = tile_paper[slot]
         live = slot < tile_count[0]
         block = blocks[0]
@@ -146,9 +151,25 @@
             chosen = jnp.where(live & (tile_author[slot] == author), 1.0, 0.0)
             block = jnp.where(line == code_rows + author, chosen, block)
         block = jnp.where(line == code_rows + AT_DEV, paper.astype(jnp.float32), block)
-        out[rows:, :] = block.astype(jnp.bfloat16)
+        out[k, rows:, :] = block.astype(jnp.bfloat16)
     for copy in moves[4:] + copies:
         copy.wait()
+
+
+def pair_kernel(keep, swapped, *outs):
+    for k, out in enumerate(outs, 1):
+        out[0] = keep[k]
+        out[1] = swapped[k]
+
+
+def slots_of(keep, swapped, *pairs):
+    me = lax.axis_index("blk")
+    pair, side = lax.div(me, 2), lax.rem(me, 2)
+    held = [(keep, 0, me), (swapped, 0, 2 * pair + 1 - side)]
+    for k, ref in enumerate(pairs, 1):
+        other = 2 * lax.bitwise_xor(pair, k)
+        held += [(ref, 0, other + side), (ref, 1, other + 1 - side)]
+    return held
 
 
 def first_sum_kernel(
@@ -176,14 +197,14 @@
 
 
 def first_author_kernel(rows, summed, class_prior, class_target, *rest):
-    *packed, full, sent, parts = rest
+    *held, full, sent, parts = rest
     classes = full.shape[1]
     code_rows = -(-rows // LANES)
     totals = [jnp.zeros((classes, LANES), jnp.float32) for _ in range(AT_DEV)]
-    for one in packed:
-        meta = one[rows:, :].astype(jnp.float32)
+    for ref, place, _ in slots_of(*held):
+        meta = ref[place, rows:, :].astype(jnp.float32)
         seeds = seeds_of(meta_line(meta, rows), classes)
-        parcel = jnp.dot(seeds, one[:rows, :], preferred_element_type=jnp.float32)
+        parcel = jnp.dot(seeds, ref[place, :rows, :], preferred_element_type=jnp.float32)
         parcel = parcel.astype(jnp.bfloat16).astype(jnp.float32)
         for author in range(AT_DEV):
             chosen = meta[code_rows + author : code_rows + author + 1]
@@ -195,16 +216,15 @@
 
 
 def author_kernel(rows, gathered, summed, class_prior, class_target, *rest):
-    *packed, full, sent, parts, shares_in, arrived = rest
-    slots = len(packed)
+    *held, full, sent, parts, shares_in, arrived = rest
+    held = slots_of(*held)
+    slots = len(held)
     classes = full.shape[1]
     code_rows = -(-rows // LANES)
     paper_tiles = gathered.shape[0] // slots // rows
-    me = lax.axis_index("blk")
-    metas = [one[rows:, :].astype(jnp.float32) for one in packed]
+    metas = [ref[place, rows:, :].astype(jnp.float32) for ref, place, _ in held]
     copies = []
-    for shift in range(slots):
-        source = lax.rem(me + slots - shift, slots)
+    for shift, (_, _, source) in enumerate(held):
         at = code_rows + AT_DEV
         paper = jnp.max(metas[shift][at : at + 1]).astype(jnp.int32)
         start = pl.multiple_of((source * paper_tiles + paper) * rows, rows)
@@ -221,13 +241,13 @@
     lane = lax.broadcasted_iota(jnp.int32, (rows, classes), 1).astype(jnp.float32)
     for copy in copies:
         copy.wait()
-    for shift, one in enumerate(packed):
+    for shift, (ref, place, _) in enumerate(held):
         half = shares_in[shift]
         scale_rows = across(keep_share / row_sums(half, block), classes)
         share = half.astype(jnp.float32) * scale_cols * scale_rows
         labels = share + jnp.where(across(codes[shift], classes) == lane, 1.0 - keep_share, 0.0)
         parcel = lax.dot_general(
-            one[:rows, :],
+            ref[place, :rows, :],
             labels.astype(jnp.bfloat16),
             (((0,), (0,)), ((), ())),
             preferred_element_type=jnp.float32,
@@ -244,8 +264,9 @@
 
 def paper_kernel(
     tile_paper, tile_author, tile_count, tiles, gathered, summed, class_prior, class_target,
-    full, half, parts, shares_in, arrived,
+    full, parts, *rest,
 ):
+    *half, shares_in, arrived = rest
     slots, rows, columns = tiles.shape
     classes = full.shape[1]
     copies = []
@@ -279,7 +300,8 @@
         mass = jnp.dot(wide, jnp.concatenate(chosen, axis=0), preferred_element_type=jnp.float32)
         kernel = mass + class_prior[...]
         full[paper * rows : (paper + 1) * rows, :] = kernel
-        half[paper * rows : (paper + 1) * rows, :] = kernel.astype(jnp.bfloat16)
+        for out in half:
+            out[paper * rows : (paper + 1) * rows, :] = kernel.astype(jnp.bfloat16)
         column = column + jnp.sum(kernel, axis=0, keepdims=True)
     spread(column, parts)
 
@@ -343,29 +365,31 @@
         tile_paper, tile_author, seed_class, train_mask, prior, target, tile_values,
     )
     places = (SMEM, SMEM, VMEM, VMEM, VMEM, VMEM, VMEM)
+    blocks = lax.axis_size("blk")
+    load = shape((blocks // 2, rows + META, columns), bf16)
     moved = call(
         functools.partial(pack_kernel, rows),
-        tuple(shape(one.shape, one.dtype) for one in inputs)
-        + (shape((rows + META, columns), bf16),) * slots,
+        tuple(shape(one.shape, one.dtype) for one in inputs) + (load, load),
         [SMEM] + [HBM] * len(inputs),
-        [pltpu.SemaphoreType.DMA((len(inputs),)), pltpu.SemaphoreType.DMA((slots,))],
-        places + (VMEM,) * slots,
+        [pltpu.SemaphoreType.DMA((len(inputs),)), pltpu.SemaphoreType.DMA((2, blocks // 2))],
+        places + (VMEM, VMEM),
     )(tile_count, *(in_hbm(one) for one in inputs))
-    packed = moved[len(inputs) :]
-    tile_paper, tile_author, seed_class, train_mask, prior, target, tile_values = (
-        moved[: len(inputs)]
-    )
-    packed = [
-        lax.ppermute(one, "blk", [(i, (i + shift) % slots) for i in range(slots)]) if shift else one
-        for shift, one in enumerate(packed)
-    ]
+    tile_paper, tile_author, seed_class, train_mask, prior, target, tile_values, keep, swap = moved
+    swapped = lax.ppermute(swap, "blk", [(i, i ^ 1) for i in range(blocks)])
     local = call(
         functools.partial(first_sum_kernel, authors), parts, [SMEM, SMEM] + [VMEM] * 4
     )(tile_paper, tile_count, tile_values, seed_class, train_mask, prior)
+    both = shape((2, rows + META, columns), bf16)
+    pairs = call(pair_kernel, (both,) * (blocks // 2 - 1), [VMEM] * 2)(keep, swapped)
+    local, *pairs = lax.optimization_barrier((local, *pairs))
+    held = [keep, swapped] + [
+        lax.ppermute(one, "blk", [(i, i ^ (2 * k)) for i in range(blocks)])
+        for k, one in enumerate(pairs, 1)
+    ]
     summed = exchange(local)
 
     author_out = (shape((authors, classes), f32), shape((authors, classes), f32), parts)
-    paper_out = (shape((papers, classes), f32), shape((papers, classes), bf16), parts)
+    paper_out = (shape((papers, classes), f32), parts, shape((papers, classes), bf16))
 
     def balance(kernel, summed, count):
         for _ in range(count):
@@ -375,25 +399,26 @@
     for repeat in range(ROUNDS):
         if repeat == 0:
             own, sent, local = call(
-                functools.partial(first_author_kernel, rows), author_out, [VMEM] * (3 + slots)
-            )(summed, prior, target, *packed)
+                functools.partial(first_author_kernel, rows), author_out, [VMEM] * (3 + len(held))
+            )(summed, prior, target, *held)
             left = ITERS - 2
         else:
             own, sent, local = call(
                 functools.partial(author_kernel, rows),
                 author_out,
-                [HBM] + [VMEM] * (3 + slots),
+                [HBM] + [VMEM] * (3 + len(held)),
                 [
                     pltpu.VMEM((slots, rows, classes), bf16),
                     pltpu.SemaphoreType.DMA((slots,)),
                 ],
-            )(in_hbm(gathered), summed, prior, target, *packed)
+            )(in_hbm(gathered), summed, prior, target, *held)
             left = ITERS - 1
         gathered = lax.all_gather(sent, "blk", tiled=True)
         author_summed = balance(own, exchange(local), left)
-        kernel, half, local = call(
+        last = repeat + 1 == ROUNDS
+        kernel, local, *half = call(
             paper_kernel,
-            paper_out,
+            paper_out[:2] if last else paper_out,
             [SMEM, SMEM, SMEM, VMEM, HBM, VMEM, VMEM, VMEM],
             [
                 pltpu.VMEM((slots, columns, classes), f32),
@@ -403,8 +428,8 @@
             tile_paper, tile_author, tile_count, tile_values, in_hbm(gathered), author_summed,
             prior, target,
         )
-        if repeat + 1 < ROUNDS:
-            gathered = lax.all_gather(half, "blk", tiled=True)
+        if not last:
+            gathered = lax.all_gather(half[0], "blk", tiled=True)
         summed = balance(kernel, exchange(local), ITERS - 1)
     return call(
         functools.partial(final_kernel, rows),

time: 191 us -> 187 us (0.979)
  starting transfers between devices: 9.88 us -> 5.1 us
  blocking collectives: 146 us -> 148 us
    ppermute x7 -> x4, starting transfers between devices: 9.76 us -> 4.98 us  [the longest x3 4.47 us: on_device(): lax.ppermute(one, 'blk', [(i, i ^ 2 * k) for i in range(blocks)])]
    pallas_call x2 -> x3, Pallas kernels: 6.85 us -> 6.19 us  [the longest x2 6.16 us: on_device(): call(paper_kernel, paper_out[:2] if last else paper_out, [SMEM, SMEM, SME...]
  transfers between devices with their start and end apart: 10 -> 7, of which waited for: 0 -> 0; matrix products, arithmetic and copies ran while one was open for 0% -> 0% of each run, Pallas kernels for 1% -> 2%
where the time goes in v8:
time: 187 us
  blocking collectives  148 us (79%)
  Pallas kernels  19.6 us (10%)
  between operations  14.5 us (8%)
  starting transfers between devices  5.1 us (3%)
    all_to_all x16, blocking collectives, exchange(): return lax.all_to_all(parts, AXES, split_axis=0, concat_axis=0, tiled=True)  148 us
    pallas_call x2, Pallas kernels, on_device(): call(paper_kernel, paper_out[:2] if last else paper_out, [SMEM, SMEM, SME...  6.16 us
    pallas_call x1, Pallas kernels, on_device(): call(functools.partial(author_kernel, rows), author_out, [HBM] + [VMEM] *...  5.04 us
    ppermute x3, starting transfers between devices, on_device(): lax.ppermute(one, 'blk', [(i, i ^ 2 * k) for i in range(blocks)])  4.47 us
  transfers between devices with their start and end apart: 7, of which 0 were waited for; matrix products, arithmetic and copies ran while one was open for 0% of the time, Pallas kernels for 2%

profile of v8, /device:TPU:0, one launch (start us, length us, event | category | flops | bytes accessed | tf_op | source)
XLA Modules:
  0.0 186.9 jit_solution(2575097299628637536)
XLA Ops:
  7.9 2.2 %shard_map.95 = (s32[8]{0:T(128)S(1)}, s32[8]{0:T(128)S(1)}, s32[5,128]{1,0:T(8,128)S(1)}, s32[5,128]{1,0:T(8,128)S(1)}, f32[1,256]{1,0:T(1,128)S(1)}, /*index=5...) custom-call(s32[1]{0:T(128)S(6)} %copy.10.tile_count, ...), custom_call_target="tpu_custom_call" | custom-call | tf_op jit(solution)/shard_map/pallas_call | solution.py:370
  10.6 1.2 shard_map.96
  11.9 2.9 %collective-permute-start.1 = (bf16[2,336,128]{2,1,0:T(8,128)(2,1)S(1)}, bf16[2,336,128]{2,1,0:T(8,128)(2,1)S(1)}, u32[]{:S(2)}, u32[]{:S(2)}) collective-permute-start(bf16[2,336,128]{2,1,0:T(8,128)(2,1)S(1)} %get-tuple-element.42), channel_id=1, source_target_pairs={{0,2},{1,3},{2,0},{3,1},{4,6},{5,7},{6,4},{7,5},{8,10},{9,11},{10,... | collective-permute-start | bytes 516104 | tf_op jit(solution)/shard_map/ppermute | solution.py:386
  14.8 1.5 collective-permute-start.2
  16.4 13.4 %all_to_all.80.summed = f32[32,1,256]{2,1,0:T(1,128)S(1)} all-to-all(f32[32,1,256]{2,1,0:T(1,128)S(1)} %shard_map.96), channel_id=1, replica_groups=mesh['grp'=4,'blk'=8] {'grp','blk'}, dimensions={0} | all-to-all | bytes 65536 | tf_op jit(solution)/shard_map/all_to_all | solution.py:336
  29.7 1.4 shard_map.98
  31.2 8.9 %all_to_all.81.summed = f32[32,1,256]{2,1,0:T(1,128)S(1)} all-to-all(f32[32,1,256]{2,1,0:T(1,128)S(1)} %get-tuple-element.47), channel_id=1, replica_groups=mesh['grp'=4,'blk'=8] {'grp','blk'}, dimensions={0} | all-to-all | bytes 65536 | tf_op jit(solution)/shard_map/all_to_all | solution.py:336
  40.3 8.9 %all_to_all.82.summed = f32[32,1,256]{2,1,0:T(1,128)S(1)} all-to-all(f32[32,1,256]{2,1,0:T(1,128)S(1)} %shard_map.99), channel_id=1, replica_groups=mesh['grp'=4,'blk'=8] {'grp','blk'}, dimensions={0} | all-to-all | bytes 65536 | tf_op jit(solution)/shard_map/all_to_all | solution.py:336
  49.5 8.9 %all_to_all.83.summed = f32[32,1,256]{2,1,0:T(1,128)S(1)} all-to-all(f32[32,1,256]{2,1,0:T(1,128)S(1)} %shard_map.100), channel_id=1, replica_groups=mesh['grp'=4,'blk'=8] {'grp','blk'}, dimensions={0} | all-to-all | bytes 65536 | tf_op jit(solution)/shard_map/all_to_all | solution.py:336
  58.4 3.4 %shard_map.101 = (f32[640,256]{1,0:T(8,128)S(1)}, f32[32,1,256]{2,1,0:T(1,128)S(1)}, bf16[640,256]{1,0:T(8,128)(2,1)}) custom-call(s32[8]{0:T(128)S(1)} %get-tuple-element.29.tile_paper, s32[8]{0:T(128)S(1)} %get-tuple-element.30.tile_author, s32[1]{0:T(128)S(6)} %copy.10.tile_count, bf16[8,320,128]{2,1,0:T(8,128)(2,1)S(1)} %get-tuple-element.31.tiles, ...), custom_call_target="tpu_custom_call" | custom-call | tf_op jit(solution)/shard_map/pallas_call | solution.py:419
  61.9 9.1 %all_to_all.84.summed = f32[32,1,256]{2,1,0:T(1,128)S(1)} all-to-all(f32[32,1,256]{2,1,0:T(1,128)S(1)} %get-tuple-element.50), channel_id=1, replica_groups=mesh['grp'=4,'blk'=8] {'grp','blk'}, dimensions={0} | all-to-all | bytes 65536 | tf_op jit(solution)/shard_map/all_to_all | solution.py:336
  71.2 8.9 %all_to_all.85.summed = f32[32,1,256]{2,1,0:T(1,128)S(1)} all-to-all(f32[32,1,256]{2,1,0:T(1,128)S(1)} %shard_map.102), channel_id=1, replica_groups=mesh['grp'=4,'blk'=8] {'grp','blk'}, dimensions={0} | all-to-all | bytes 65536 | tf_op jit(solution)/shard_map/all_to_all | solution.py:336
  80.4 8.9 %all_to_all.86.summed = f32[32,1,256]{2,1,0:T(1,128)S(1)} all-to-all(f32[32,1,256]{2,1,0:T(1,128)S(1)} %shard_map.103), channel_id=1, replica_groups=mesh['grp'=4,'blk'=8] {'grp','blk'}, dimensions={0} | all-to-all | bytes 65536 | tf_op jit(solution)/shard_map/all_to_all | solution.py:336
  89.6 8.9 %all_to_all.87.summed = f32[32,1,256]{2,1,0:T(1,128)S(1)} all-to-all(f32[32,1,256]{2,1,0:T(1,128)S(1)} %shard_map.104), channel_id=1, replica_groups=mesh['grp'=4,'blk'=8] {'grp','blk'}, dimensions={0} | all-to-all | bytes 65536 | tf_op jit(solution)/shard_map/all_to_all | solution.py:336
  98.5 5.0 %shard_map.105 = (f32[256,256]{1,0:T(8,128)S(1)}, f32[256,256]{1,0:T(8,128)}, f32[32,1,256]{2,1,0:T(1,128)S(1)}) custom-call(bf16[5120,256]{1,0:T(8,128)(2,1)} %all-gather.6.cloned.1.call-done.gathered, f32[32,1,256]{2,1,0:T(1,128)S(1)} %all_to_all.87.summed, f32[1,256]{1,0:T(1,128)S(1)} %get-tuple-element.34.class_prior, ...), custom_call_target="tpu_custom_call" | custom-call | tf_op jit(solution)/shard_map/pallas_call | solution.py:406
  103.6 9.0 %all_to_all.88.summed = f32[32,1,256]{2,1,0:T(1,128)S(1)} all-to-all(f32[32,1,256]{2,1,0:T(1,128)S(1)} %get-tuple-element.53), channel_id=1, replica_groups=mesh['grp'=4,'blk'=8] {'grp','blk'}, dimensions={0} | all-to-all | bytes 65536 | tf_op jit(solution)/shard_map/all_to_all | solution.py:336
  112.8 8.9 %all_to_all.89.summed = f32[32,1,256]{2,1,0:T(1,128)S(1)} all-to-all(f32[32,1,256]{2,1,0:T(1,128)S(1)} %shard_map.106), channel_id=1, replica_groups=mesh['grp'=4,'blk'=8] {'grp','blk'}, dimensions={0} | all-to-all | bytes 65536 | tf_op jit(solution)/shard_map/all_to_all | solution.py:336
  121.9 8.9 %all_to_all.90.summed = f32[32,1,256]{2,1,0:T(1,128)S(1)} all-to-all(f32[32,1,256]{2,1,0:T(1,128)S(1)} %shard_map.107), channel_id=1, replica_groups=mesh['grp'=4,'blk'=8] {'grp','blk'}, dimensions={0} | all-to-all | bytes 65536 | tf_op jit(solution)/shard_map/all_to_all | solution.py:336
  131.0 8.9 %all_to_all.91.summed.author_summed = f32[32,1,256]{2,1,0:T(1,128)S(1)} all-to-all(f32[32,1,256]{2,1,0:T(1,128)S(1)} %shard_map.108), channel_id=1, replica_groups=mesh['grp'=4,'blk'=8] {'grp','blk'}, dimensions={0} | all-to-all | bytes 65536 | tf_op jit(solution)/shard_map/all_to_all | solution.py:336
  140.0 2.7 %shard_map.109 = (f32[640,256]{1,0:T(8,128)S(1)}, f32[32,1,256]{2,1,0:T(1,128)S(1)}) custom-call(s32[8]{0:T(128)S(1)} %get-tuple-element.29.tile_paper, s32[8]{0:T(128)S(1)} %get-tuple-element.30.tile_author, s32[1]{0:T(128)S(6)} %copy.10.tile_count, bf16[8,320,128]{2,1,0:T(8,128)(2,1)S(1)} %get-tuple-element.31.tiles, ...), custom_call_target="tpu_custom_call" | custom-call | tf_op jit(solution)/shard_map/pallas_call | solution.py:419
  142.7 8.9 %all_to_all.92.summed = f32[32,1,256]{2,1,0:T(1,128)S(1)} all-to-all(f32[32,1,256]{2,1,0:T(1,128)S(1)} %get-tuple-element.55), channel_id=1, replica_groups=mesh['grp'=4,'blk'=8] {'grp','blk'}, dimensions={0} | all-to-all | bytes 65536 | tf_op jit(solution)/shard_map/all_to_all | solution.py:336
  151.9 8.9 %all_to_all.93.summed = f32[32,1,256]{2,1,0:T(1,128)S(1)} all-to-all(f32[32,1,256]{2,1,0:T(1,128)S(1)} %shard_map.110), channel_id=1, replica_groups=mesh['grp'=4,'blk'=8] {'grp','blk'}, dimensions={0} | all-to-all | bytes 65536 | tf_op jit(solution)/shard_map/all_to_all | solution.py:336
  161.1 8.9 %all_to_all.94.summed = f32[32,1,256]{2,1,0:T(1,128)S(1)} all-to-all(f32[32,1,256]{2,1,0:T(1,128)S(1)} %shard_map.111), channel_id=1, replica_groups=mesh['grp'=4,'blk'=8] {'grp','blk'}, dimensions={0} | all-to-all | bytes 65536 | tf_op jit(solution)/shard_map/all_to_all | solution.py:336
  170.3 8.9 %all_to_all.95.summed = f32[32,1,256]{2,1,0:T(1,128)S(1)} all-to-all(f32[32,1,256]{2,1,0:T(1,128)S(1)} %shard_map.112), channel_id=1, replica_groups=mesh['grp'=4,'blk'=8] {'grp','blk'}, dimensions={0} | all-to-all | bytes 65536 | tf_op jit(solution)/shard_map/all_to_all | solution.py:336
  (28 shorter events, 4.3 us)
Async XLA Ops:
  7.2 51.3 %all-gather.4.cloned.1.call-start = ((), (), s32[]{:S(2)}) async-start(), calls=%async_computation.16 | async-start | bytes 2359296 | tf_op jit(solution)/shard_map/all_gather | solution.py:416
  10.1 1.8 collective-permute-start
  11.9 17.8 %collective-permute-start.1 = (bf16[2,336,128]{2,1,0:T(8,128)(2,1)S(1)}, bf16[2,336,128]{2,1,0:T(8,128)(2,1)S(1)}, u32[]{:S(2)}, u32[]{:S(2)}) collective-permute-start(bf16[2,336,128]{2,1,0:T(8,128)(2,1)S(1)} %get-tuple-element.42), channel_id=1, source_target_pairs={{0,2},{1,3},{2,0},{3,1},{4,6},{5,7},{6,4},{7,5},{8,10},{9,11},{10,... | collective-permute-start | bytes 516104 | tf_op jit(solution)/shard_map/ppermute | solution.py:386
  14.8 14.9 %collective-permute-start.2 = (bf16[2,336,128]{2,1,0:T(8,128)(2,1)S(1)}, bf16[2,336,128]{2,1,0:T(8,128)(2,1)S(1)}, u32[]{:S(2)}, u32[]{:S(2)}) collective-permute-start(bf16[2,336,128]{2,1,0:T(8,128)(2,1)S(1)} %get-tuple-element.43), channel_id=1, source_target_pairs={{0,4},{1,5},{2,6},{3,7},{4,0},{5,1},{6,2},{7,3},{8,12},{9,13},{10,... | collective-permute-start | bytes 516104 | tf_op jit(solution)/shard_map/ppermute | solution.py:386
  16.3 13.4 %collective-permute-start.3 = (bf16[2,336,128]{2,1,0:T(8,128)(2,1)S(1)}, bf16[2,336,128]{2,1,0:T(8,128)(2,1)S(1)}, u32[]{:S(2)}, u32[]{:S(2)}) collective-permute-start(bf16[2,336,128]{2,1,0:T(8,128)(2,1)S(1)} %get-tuple-element.44), channel_id=1, source_target_pairs={{0,6},{1,7},{2,4},{3,5},{4,2},{5,3},{6,0},{7,1},{8,14},{9,15},{10,... | collective-permute-start | bytes 516104 | tf_op jit(solution)/shard_map/ppermute | solution.py:386
  31.2 67.4 %all-gather.6.cloned.1.call-start = ((), (), s32[]{:S(2)}) async-start(), calls=%async_computation.17 | async-start | bytes 2949120 | tf_op jit(solution)/shard_map/all_gather | solution.py:432
  61.9 78.1 %all-gather.8.cloned.1.call-start = ((), (), s32[]{:S(2)}) async-start(), calls=%async_computation.18 | async-start | bytes 2359296 | tf_op jit(solution)/shard_map/all_gather | solution.py:416
Sparse Core Ops, SparseCore 0:
  31.3 24.3 all-gather.3
  62.0 27.7 all-gather.5
  103.7 24.3 all-gather.7

commit v9 on v8

--- a/solution.py
+++ b/solution.py
@@ -162,14 +162,15 @@
         out[1] = swapped[k]
 
 
-def slots_of(keep, swapped, *pairs):
+def sources(count):
     me = lax.axis_index("blk")
     pair, side = lax.div(me, 2), lax.rem(me, 2)
-    held = [(keep, 0, me), (swapped, 0, 2 * pair + 1 - side)]
-    for k, ref in enumerate(pairs, 1):
-        other = 2 * lax.bitwise_xor(pair, k)
-        held += [(ref, 0, other + side), (ref, 1, other + 1 - side)]
-    return held
+    pairs = [2 * lax.bitwise_xor(pair, k) for k in range(count // 2)]
+    return [other + side for other in pairs] + [other + 1 - side for other in pairs]
+
+
+def slots_of(keep, swapped, *pairs):
+    return [(keep, 0), *((ref, 0) for ref in pairs), (swapped, 0), *((ref, 1) for ref in pairs)]
 
 
 def first_sum_kernel(
@@ -197,11 +198,11 @@
 
 
 def first_author_kernel(rows, summed, class_prior, class_target, *rest):
-    *held, full, sent, parts = rest
+    *held, full, parts = rest
     classes = full.shape[1]
     code_rows = -(-rows // LANES)
     totals = [jnp.zeros((classes, LANES), jnp.float32) for _ in range(AT_DEV)]
-    for ref, place, _ in slots_of(*held):
+    for ref, place in slots_of(*held):
         meta = ref[place, rows:, :].astype(jnp.float32)
         seeds = seeds_of(meta_line(meta, rows), classes)
         parcel = jnp.dot(seeds, ref[place, :rows, :], preferred_element_type=jnp.float32)
@@ -211,38 +212,25 @@
             totals[author] = totals[author] + parcel * chosen
     kernel = jnp.concatenate([total.T for total in totals], axis=0) + class_prior[...]
     full[...] = kernel
-    sent[...] = kernel
     next_sum(kernel, summed, class_target, parts)
 
 
-def author_kernel(rows, gathered, summed, class_prior, class_target, *rest):
-    *held, full, sent, parts, shares_in, arrived = rest
-    held = slots_of(*held)
-    slots = len(held)
+def author_kernel(rows, blocks, summed, class_prior, class_target, *rest):
+    *rest, full, parts = rest
+    kernels, held = rest[:blocks], slots_of(*rest[blocks:])
     classes = full.shape[1]
     code_rows = -(-rows // LANES)
-    paper_tiles = gathered.shape[0] // slots // rows
-    metas = [ref[place, rows:, :].astype(jnp.float32) for ref, place, _ in held]
-    copies = []
-    for shift, (_, _, source) in enumerate(held):
-        at = code_rows + AT_DEV
-        paper = jnp.max(metas[shift][at : at + 1]).astype(jnp.int32)
-        start = pl.multiple_of((source * paper_tiles + paper) * rows, rows)
-        copy = pltpu.make_async_copy(
-            gathered.at[pl.ds(start, rows)], shares_in.at[shift], arrived.at[shift]
-        )
-        copy.start()
-        copies.append(copy)
+    metas = [ref[place, rows:, :].astype(jnp.float32) for ref, place in held]
+    at = code_rows + AT_DEV
+    papers = [jnp.max(meta[at : at + 1]).astype(jnp.int32) for meta in metas]
     scale_cols = col_scale(summed, class_target)
     block = scale_block(scale_cols)
     eye = identity(rows)
     codes = [code_column(meta_line(meta, rows), eye) for meta in metas]
     totals = [jnp.zeros((LANES, classes), jnp.float32) for _ in range(AT_DEV)]
     lane = lax.broadcasted_iota(jnp.int32, (rows, classes), 1).astype(jnp.float32)
-    for copy in copies:
-        copy.wait()
-    for shift, (ref, place, _) in enumerate(held):
-        half = shares_in[shift]
+    for shift, (ref, place) in enumerate(held):
+        half = kernels[shift][pl.ds(pl.multiple_of(papers[shift] * rows, rows), rows), :]
         scale_rows = across(keep_share / row_sums(half, block), classes)
         share = half.astype(jnp.float32) * scale_cols * scale_rows
         labels = share + jnp.where(across(codes[shift], classes) == lane, 1.0 - keep_share, 0.0)
@@ -258,33 +246,23 @@
             totals[author] = totals[author] + parcel * metas[shift][at : at + 1, :1]
     kernel = jnp.concatenate(totals, axis=0) + class_prior[...]
     full[...] = kernel
-    sent[...] = kernel
     spread(jnp.sum(kernel, axis=0, keepdims=True), parts)
 
 
 def paper_kernel(
-    tile_paper, tile_author, tile_count, tiles, gathered, summed, class_prior, class_target,
-    full, parts, *rest,
+    blocks, tile_paper, tile_author, tile_count, tiles, summed, class_prior, class_target, *rest
 ):
-    *half, shares_in, arrived = rest
-    slots, rows, columns = tiles.shape
+    kernels, (full, parts, *half) = rest[:blocks], rest[blocks:]
+    _, rows, columns = tiles.shape
     classes = full.shape[1]
-    copies = []
-    for slot in range(slots):
-        start = pl.multiple_of((slot * AT_DEV + tile_author[slot]) * columns, columns)
-        copy = pltpu.make_async_copy(
-            gathered.at[pl.ds(start, columns)], shares_in.at[slot], arrived.at[slot]
-        )
-        copy.start()
-        copies.append(copy)
     scale_cols = col_scale(summed, class_target)
     block = scale_block(scale_cols)
-    wide = jnp.concatenate([tiles[slot] for slot in range(slots)], axis=1)
+    slots = sources(blocks)
+    wide = jnp.concatenate([tiles[slot] for slot in slots], axis=1)
     labels = []
-    for copy in copies:
-        copy.wait()
-    for slot in range(slots):
-        kernel = shares_in[slot]
+    for ref, slot in zip(kernels, slots):
+        start = pl.multiple_of(tile_author[slot] * columns, columns)
+        kernel = ref[pl.ds(start, columns), :]
         high, low = split(kernel)
         sums = row_sums(high, block) + jnp.dot(
             low, block[:, :LANES], preferred_element_type=jnp.float32
@@ -294,9 +272,9 @@
     column = jnp.zeros((1, classes), jnp.float32)
     for paper in range(full.shape[0] // rows):
         chosen = []
-        for slot in range(slots):
+        for one, slot in zip(labels, slots):
             keep = (slot < tile_count[0]) & (tile_paper[slot] == paper)
-            chosen.append(jnp.where(keep, labels[slot], jnp.zeros_like(labels[slot])))
+            chosen.append(jnp.where(keep, one, jnp.zeros_like(one)))
         mass = jnp.dot(wide, jnp.concatenate(chosen, axis=0), preferred_element_type=jnp.float32)
         kernel = mass + class_prior[...]
         full[paper * rows : (paper + 1) * rows, :] = kernel
@@ -388,49 +366,60 @@
     ]
     summed = exchange(local)
 
-    author_out = (shape((authors, classes), f32), shape((authors, classes), f32), parts)
+    author_out = (shape((authors, classes), f32), parts)
     paper_out = (shape((papers, classes), f32), parts, shape((papers, classes), bf16))
 
-    def balance(kernel, summed, count):
-        for _ in range(count):
-            summed = exchange(call(balance_kernel, parts, [VMEM] * 3)(kernel, summed, target))
+    def across_pairs(value, k):
+        return lax.ppermute(value, "blk", [(i, i ^ (2 * k)) for i in range(blocks)])
+
+    def to_other(value):
+        return lax.ppermute(value, "blk", [(i, i ^ 1) for i in range(blocks)])
+
+    def balance(kernel, sent, local, count):
+        here = [sent] + [across_pairs(sent, k) for k in range(1, blocks // 2)]
+        there = [to_other(sent)]
+        for step in range(count):
+            if step + 1 == count:
+                local, *here = lax.optimization_barrier((local, *here))
+                there += [to_other(one) for one in here[1:]]
+            summed = exchange(local)
+            if step + 1 < count:
+                local = call(balance_kernel, parts, [VMEM] * 3)(kernel, summed, target)
+        return summed, here + there
+
+    def last_balance(kernel, local):
+        for step in range(ITERS):
+            summed = exchange(local)
+            if step + 1 < ITERS:
+                local = call(balance_kernel, parts, [VMEM] * 3)(kernel, summed, target)
         return summed
 
     for repeat in range(ROUNDS):
         if repeat == 0:
-            own, sent, local = call(
+            own, local = call(
                 functools.partial(first_author_kernel, rows), author_out, [VMEM] * (3 + len(held))
             )(summed, prior, target, *held)
-            left = ITERS - 2
+            left = ITERS - 1
         else:
-            own, sent, local = call(
-                functools.partial(author_kernel, rows),
+            own, local = call(
+                functools.partial(author_kernel, rows, blocks),
                 author_out,
-                [HBM] + [VMEM] * (3 + len(held)),
-                [
-                    pltpu.VMEM((slots, rows, classes), bf16),
-                    pltpu.SemaphoreType.DMA((slots,)),
-                ],
-            )(in_hbm(gathered), summed, prior, target, *held)
-            left = ITERS - 1
-        gathered = lax.all_gather(sent, "blk", tiled=True)
-        author_summed = balance(own, exchange(local), left)
+                [VMEM] * (3 + blocks + len(held)),
+            )(summed, prior, target, *kernels, *held)
+            left = ITERS
+        author_summed, kernels = balance(own, own, local, left)
         last = repeat + 1 == ROUNDS
         kernel, local, *half = call(
-            paper_kernel,
+            functools.partial(paper_kernel, blocks),
             paper_out[:2] if last else paper_out,
-            [SMEM, SMEM, SMEM, VMEM, HBM, VMEM, VMEM, VMEM],
-            [
-                pltpu.VMEM((slots, columns, classes), f32),
-                pltpu.SemaphoreType.DMA((slots,)),
-            ],
+            [SMEM, SMEM, SMEM] + [VMEM] * (4 + blocks),
         )(
-            tile_paper, tile_author, tile_count, tile_values, in_hbm(gathered), author_summed,
-            prior, target,
+            tile_paper, tile_author, tile_count, tile_values, author_summed, prior, target, *kernels
         )
-        if not last:
-            gathered = lax.all_gather(half[0], "blk", tiled=True)
-        summed = balance(kernel, exchange(local), ITERS - 1)
+        if last:
+            summed = last_balance(kernel, local)
+        else:
+            summed, kernels = balance(kernel, half[0], local, ITERS)
     return call(
         functools.partial(final_kernel, rows),
         (shape((papers, classes), f32), shape((authors, classes), f32)),

time: 187 us -> 207 us (1.11)
  blocking collectives: 148 us -> 105 us
  waiting for transfers between devices: 0.11 us -> 42.3 us
  starting transfers between devices: 5.1 us -> 33.6 us
  between operations: 14.5 us -> 1.51 us
  local copies, waits for them, and re-layouts: 0 us -> 4.94 us
    all_to_all x16 -> x10, blocking collectives: 148 us -> 105 us  [exchange(): return lax.all_to_all(parts, AXES, split_axis=0, concat_axis=0, tiled=True)]
    all_to_all x0 -> x6, waiting for transfers between devices: none -> 42.2 us  [exchange(): return lax.all_to_all(parts, AXES, split_axis=0, concat_axis=0, tiled=True)]
    all_to_all x0 -> x6, starting transfers between devices: none -> 15.4 us  [exchange(): return lax.all_to_all(parts, AXES, split_axis=0, concat_axis=0, tiled=True)]
    ppermute x0 -> x21, starting transfers between devices: none -> 13.3 us  [the longest x9 10.7 us: across_pairs(): return lax.ppermute(value, 'blk', [(i, i ^ 2 * k) for i in range(blocks)])]
    unnamed x0 -> x12, local copies, waits for them, and re-layouts: none -> 4.94 us
  transfers between devices with their start and end apart: 7 -> 31, of which waited for: 0 -> 6; matrix products, arithmetic and copies ran while one was open for 0% -> 0% of each run, Pallas kernels for 2% -> 3%
where the time goes in v9:
time: 207 us
  blocking collectives  105 us (51%)
  waiting for transfers between devices  42.3 us (20%)
  starting transfers between devices  33.6 us (16%)
  Pallas kernels  19.2 us (9%)
  local copies, waits for them, and re-layouts  4.94 us (2%)
    all_to_all x10, blocking collectives, exchange(): return lax.all_to_all(parts, AXES, split_axis=0, concat_axis=0, tiled=True)  105 us
    all_to_all x6, waiting for transfers between devices, exchange(): return lax.all_to_all(parts, AXES, split_axis=0, concat_axis=0, tiled=True)  42.2 us
    all_to_all x6, starting transfers between devices, exchange(): return lax.all_to_all(parts, AXES, split_axis=0, concat_axis=0, tiled=True)  15.4 us
    ppermute x9, starting transfers between devices, across_pairs(): return lax.ppermute(value, 'blk', [(i, i ^ 2 * k) for i in range(blocks)])  10.7 us
    pallas_call x8, Pallas kernels, balance(): local = call(balance_kernel, parts, [VMEM] * 3)(kernel, summed, target)  5.32 us
    unnamed x12, local copies, waits for them, and re-layouts  4.94 us
    ppermute x3, starting transfers between devices, on_device(): lax.ppermute(one, 'blk', [(i, i ^ 2 * k) for i in range(blocks)])  4.47 us
    pallas_call x1, Pallas kernels, on_device(): call(functools.partial(author_kernel, rows, blocks), author_out, [VMEM] *...  4.25 us
  transfers between devices with their start and end apart: 31, of which 6 were waited for; matrix products, arithmetic and copies ran while one was open for 0% of the time, Pallas kernels for 3%

profile of v9, /device:TPU:0, one launch (start us, length us, event | category | flops | bytes accessed | tf_op | source)
XLA Modules:
  0.0 206.7 jit_solution(2392767959452217949)
XLA Ops:
  5.3 2.9 %collective-permute-start.1 = (bf16[2,336,128]{2,1,0:T(8,128)(2,1)S(1)}, bf16[2,336,128]{2,1,0:T(8,128)(2,1)S(1)}, u32[]{:S(2)}, u32[]{:S(2)}) collective-permute-start(bf16[2,336,128]{2,1,0:T(8,128)(2,1)S(1)} %get-tuple-element.55), channel_id=1, source_target_pairs={{0,2},{1,3},{2,0},{3,1},{4,6},{5,7},{6,4},{7,5},{8,10},{9,11},{10,... | collective-permute-start | bytes 516104 | tf_op jit(solution)/shard_map/ppermute | solution.py:364
  9.8 13.4 %all_to_all.80.summed = f32[32,1,256]{2,1,0:T(1,128)S(1)} all-to-all(f32[32,1,256]{2,1,0:T(1,128)S(1)} %shard_map.96), channel_id=1, replica_groups=mesh['grp'=4,'blk'=8] {'grp','blk'}, dimensions={0} | all-to-all | bytes 65536 | tf_op jit(solution)/shard_map/all_to_all | solution.py:314
  27.5 11.7 %all_to_all.81.summed = f32[32,1,256]{2,1,0:T(1,128)S(1)} all-to-all(f32[32,1,256]{2,1,0:T(1,128)S(1)} %get-tuple-element.59), channel_id=1, replica_groups=mesh['grp'=4,'blk'=8] {'grp','blk'}, dimensions={0} | all-to-all | bytes 65536 | tf_op jit(solution)/shard_map/all_to_all | solution.py:314
  40.1 2.6 %all-to-all-start.2 = ((f32[32,1,256]{2,1,0:T(1,128)}), f32[32,1,256]{2,1,0:T(1,128)S(1)}, u32[]{:S(2)}, u32[]{:S(2)}) async-start(f32[32,1,256]{2,1,0:T(1,128)} %shard_map.99), calls=%async_computation.2 | async-start | bytes 65536 | tf_op jit(solution)/shard_map/all_to_all | solution.py:314
  42.8 7.1 %all-to-all-done.2.summed = f32[32,1,256]{2,1,0:T(1,128)S(1)} async-done(((f32[32,1,256]{2,1,0:T(1,128)}), f32[32,1,256]{2,1,0:T(1,128)S(1)}, u32[]{:S(2)}, u32[]{:S(2)}) %all-to-all-start.2) | async-done | bytes 32800 | tf_op jit(solution)/shard_map/all_to_all | solution.py:314
  52.8 2.6 %all-to-all-start.3 = ((f32[32,1,256]{2,1,0:T(1,128)}), f32[32,1,256]{2,1,0:T(1,128)S(1)}, u32[]{:S(2)}, u32[]{:S(2)}) async-start(f32[32,1,256]{2,1,0:T(1,128)} %shard_map.100), calls=%async_computation.3 | async-start | bytes 65536 | tf_op jit(solution)/shard_map/all_to_all | solution.py:314
  56.1 6.5 %all-to-all-done.3.summed = f32[32,1,256]{2,1,0:T(1,128)S(1)} async-done(((f32[32,1,256]{2,1,0:T(1,128)}), f32[32,1,256]{2,1,0:T(1,128)S(1)}, u32[]{:S(2)}, u32[]{:S(2)}) %all-to-all-start.3) | async-done | bytes 32800 | tf_op jit(solution)/shard_map/all_to_all | solution.py:314
  71.1 14.6 %all_to_all.82.summed = f32[32,1,256]{2,1,0:T(1,128)S(1)} all-to-all(f32[32,1,256]{2,1,0:T(1,128)S(1)} %get-tuple-element.66), channel_id=1, replica_groups=mesh['grp'=4,'blk'=8] {'grp','blk'}, dimensions={0} | all-to-all | bytes 65536 | tf_op jit(solution)/shard_map/all_to_all | solution.py:314
  85.9 8.9 %all_to_all.83.summed = f32[32,1,256]{2,1,0:T(1,128)S(1)} all-to-all(f32[32,1,256]{2,1,0:T(1,128)S(1)} %shard_map.102), channel_id=1, replica_groups=mesh['grp'=4,'blk'=8] {'grp','blk'}, dimensions={0} | all-to-all | bytes 65536 | tf_op jit(solution)/shard_map/all_to_all | solution.py:314
  95.7 2.6 %all-to-all-start.6 = ((f32[32,1,256]{2,1,0:T(1,128)}), f32[32,1,256]{2,1,0:T(1,128)S(1)}, u32[]{:S(2)}, u32[]{:S(2)}) async-start(f32[32,1,256]{2,1,0:T(1,128)} %shard_map.103), calls=%async_computation.6 | async-start | bytes 65536 | tf_op jit(solution)/shard_map/all_to_all | solution.py:314
  98.4 7.1 %all-to-all-done.6.summed = f32[32,1,256]{2,1,0:T(1,128)S(1)} async-done(((f32[32,1,256]{2,1,0:T(1,128)}), f32[32,1,256]{2,1,0:T(1,128)S(1)}, u32[]{:S(2)}, u32[]{:S(2)}) %all-to-all-start.6) | async-done | bytes 32800 | tf_op jit(solution)/shard_map/all_to_all | solution.py:314
  107.1 2.6 %all-to-all-start.7 = ((f32[32,1,256]{2,1,0:T(1,128)}), f32[32,1,256]{2,1,0:T(1,128)S(1)}, u32[]{:S(2)}, u32[]{:S(2)}) async-start(f32[32,1,256]{2,1,0:T(1,128)} %shard_map.104), calls=%async_computation.7 | async-start | bytes 65536 | tf_op jit(solution)/shard_map/all_to_all | solution.py:314
  109.6 7.2 %all-to-all-done.7.summed = f32[32,1,256]{2,1,0:T(1,128)S(1)} async-done(((f32[32,1,256]{2,1,0:T(1,128)}), f32[32,1,256]{2,1,0:T(1,128)S(1)}, u32[]{:S(2)}, u32[]{:S(2)}) %all-to-all-start.7) | async-done | bytes 32800 | tf_op jit(solution)/shard_map/all_to_all | solution.py:314
  116.9 4.2 %shard_map.105 = (f32[256,256]{1,0:T(8,128)S(1)}, f32[32,1,256]{2,1,0:T(1,128)S(1)}) custom-call(f32[32,1,256]{2,1,0:T(1,128)S(1)} %all-to-all-done.7.summed, f32[1,256]{1,0:T(1,128)S(1)} %get-tuple-element.47.class_prior, f32[1,256]{1,0:T(1,128)S(1)} %get-tuple-element.54.class_target, bf16[640,256]{1,0:T(8,128)(2,1)S(1)} %get-tuple-element.69.rest_0_, ...), custom_call_target="tpu_custom_call" | custom-call | tf_op jit(solution)/shard_map/pallas_call | solution.py:404
  124.7 11.7 %all_to_all.84.summed = f32[32,1,256]{2,1,0:T(1,128)S(1)} all-to-all(f32[32,1,256]{2,1,0:T(1,128)S(1)} %get-tuple-element.74), channel_id=1, replica_groups=mesh['grp'=4,'blk'=8] {'grp','blk'}, dimensions={0} | all-to-all | bytes 65536 | tf_op jit(solution)/shard_map/all_to_all | solution.py:314
  136.6 8.9 %all_to_all.85.summed = f32[32,1,256]{2,1,0:T(1,128)S(1)} all-to-all(f32[32,1,256]{2,1,0:T(1,128)S(1)} %shard_map.106), channel_id=1, replica_groups=mesh['grp'=4,'blk'=8] {'grp','blk'}, dimensions={0} | all-to-all | bytes 65536 | tf_op jit(solution)/shard_map/all_to_all | solution.py:314
  146.4 2.6 %all-to-all-start.10 = ((f32[32,1,256]{2,1,0:T(1,128)}), f32[32,1,256]{2,1,0:T(1,128)S(1)}, u32[]{:S(2)}, u32[]{:S(2)}) async-start(f32[32,1,256]{2,1,0:T(1,128)} %shard_map.107), calls=%async_computation.10 | async-start | bytes 65536 | tf_op jit(solution)/shard_map/all_to_all | solution.py:314
  149.1 7.1 %all-to-all-done.10.summed = f32[32,1,256]{2,1,0:T(1,128)S(1)} async-done(((f32[32,1,256]{2,1,0:T(1,128)}), f32[32,1,256]{2,1,0:T(1,128)S(1)}, u32[]{:S(2)}, u32[]{:S(2)}) %all-to-all-start.10) | async-done | bytes 32800 | tf_op jit(solution)/shard_map/all_to_all | solution.py:314
  157.7 2.6 %all-to-all-start.11 = ((f32[32,1,256]{2,1,0:T(1,128)}), f32[32,1,256]{2,1,0:T(1,128)S(1)}, u32[]{:S(2)}, u32[]{:S(2)}) async-start(f32[32,1,256]{2,1,0:T(1,128)} %shard_map.108), calls=%async_computation.11 | async-start | bytes 65536 | tf_op jit(solution)/shard_map/all_to_all | solution.py:314
  160.3 7.2 %all-to-all-done.11.summed.author_summed = f32[32,1,256]{2,1,0:T(1,128)S(1)} async-done(((f32[32,1,256]{2,1,0:T(1,128)}), f32[32,1,256]{2,1,0:T(1,128)S(1)}, u32[]{:S(2)}, u32[]{:S(2)}) %all-to-all-start.11) | async-done | bytes 32800 | tf_op jit(solution)/shard_map/all_to_all | solution.py:314
  169.0 8.9 %all_to_all.86.summed = f32[32,1,256]{2,1,0:T(1,128)S(1)} all-to-all(f32[32,1,256]{2,1,0:T(1,128)S(1)} %get-tuple-element.81), channel_id=1, replica_groups=mesh['grp'=4,'blk'=8] {'grp','blk'}, dimensions={0} | all-to-all | bytes 65536 | tf_op jit(solution)/shard_map/all_to_all | solution.py:314
  178.2 8.9 %all_to_all.87.summed = f32[32,1,256]{2,1,0:T(1,128)S(1)} all-to-all(f32[32,1,256]{2,1,0:T(1,128)S(1)} %shard_map.110), channel_id=1, replica_groups=mesh['grp'=4,'blk'=8] {'grp','blk'}, dimensions={0} | all-to-all | bytes 65536 | tf_op jit(solution)/shard_map/all_to_all | solution.py:314
  187.4 8.9 %all_to_all.88.summed = f32[32,1,256]{2,1,0:T(1,128)S(1)} all-to-all(f32[32,1,256]{2,1,0:T(1,128)S(1)} %shard_map.111), channel_id=1, replica_groups=mesh['grp'=4,'blk'=8] {'grp','blk'}, dimensions={0} | all-to-all | bytes 65536 | tf_op jit(solution)/shard_map/all_to_all | solution.py:314
  196.6 8.9 %all_to_all.89.summed = f32[32,1,256]{2,1,0:T(1,128)S(1)} all-to-all(f32[32,1,256]{2,1,0:T(1,128)S(1)} %shard_map.112), channel_id=1, replica_groups=mesh['grp'=4,'blk'=8] {'grp','blk'}, dimensions={0} | all-to-all | bytes 65536 | tf_op jit(solution)/shard_map/all_to_all | solution.py:314
  (79 shorter events, 35.4 us)
Async XLA Ops:
  5.3 17.8 %collective-permute-start.1 = (bf16[2,336,128]{2,1,0:T(8,128)(2,1)S(1)}, bf16[2,336,128]{2,1,0:T(8,128)(2,1)S(1)}, u32[]{:S(2)}, u32[]{:S(2)}) collective-permute-start(bf16[2,336,128]{2,1,0:T(8,128)(2,1)S(1)} %get-tuple-element.55), channel_id=1, source_target_pairs={{0,2},{1,3},{2,0},{3,1},{4,6},{5,7},{6,4},{7,5},{8,10},{9,11},{10,... | collective-permute-start | bytes 516104 | tf_op jit(solution)/shard_map/ppermute | solution.py:364
  8.2 14.9 %collective-permute-start.2 = (bf16[2,336,128]{2,1,0:T(8,128)(2,1)S(1)}, bf16[2,336,128]{2,1,0:T(8,128)(2,1)S(1)}, u32[]{:S(2)}, u32[]{:S(2)}) collective-permute-start(bf16[2,336,128]{2,1,0:T(8,128)(2,1)S(1)} %get-tuple-element.56), channel_id=1, source_target_pairs={{0,4},{1,5},{2,6},{3,7},{4,0},{5,1},{6,2},{7,3},{8,12},{9,13},{10,... | collective-permute-start | bytes 516104 | tf_op jit(solution)/shard_map/ppermute | solution.py:364
  9.8 13.4 %collective-permute-start.3 = (bf16[2,336,128]{2,1,0:T(8,128)(2,1)S(1)}, bf16[2,336,128]{2,1,0:T(8,128)(2,1)S(1)}, u32[]{:S(2)}, u32[]{:S(2)}) collective-permute-start(bf16[2,336,128]{2,1,0:T(8,128)(2,1)S(1)} %get-tuple-element.57), channel_id=1, source_target_pairs={{0,6},{1,7},{2,4},{3,5},{4,2},{5,3},{6,0},{7,1},{8,14},{9,15},{10,... | collective-permute-start | bytes 516104 | tf_op jit(solution)/shard_map/ppermute | solution.py:364
  24.0 26.7 %collective-permute-start.6 = (f32[256,256]{1,0:T(8,128)S(1)}, f32[256,256]{1,0:T(8,128)S(1)}, u32[]{:S(2)}, u32[]{:S(2)}) collective-permute-start(f32[256,256]{1,0:T(8,128)S(1)} %get-tuple-element.61.kernel_ref.rest_0_), channel_id=1, source_target_pairs={{0,6},{1,7},{2,4},{3,5},{4,2},{5,3},{6,0},{7,1},{8,14},{9,15},{10,... | collective-permute-start | bytes 786440 | tf_op jit(solution)/shard_map/ppermute | solution.py:373
  24.7 26.0 %collective-permute-start.5 = (f32[256,256]{1,0:T(8,128)S(1)}, f32[256,256]{1,0:T(8,128)S(1)}, u32[]{:S(2)}, u32[]{:S(2)}) collective-permute-start(f32[256,256]{1,0:T(8,128)S(1)} %get-tuple-element.61.kernel_ref.rest_0_), channel_id=1, source_target_pairs={{0,4},{1,5},{2,6},{3,7},{4,0},{5,1},{6,2},{7,3},{8,12},{9,13},{10,... | collective-permute-start | bytes 786440 | tf_op jit(solution)/shard_map/ppermute | solution.py:373
  26.0 24.7 %collective-permute-start.4 = (f32[256,256]{1,0:T(8,128)S(1)}, f32[256,256]{1,0:T(8,128)S(1)}, u32[]{:S(2)}, u32[]{:S(2)}) collective-permute-start(f32[256,256]{1,0:T(8,128)S(1)} %get-tuple-element.61.kernel_ref.rest_0_), channel_id=1, source_target_pairs={{0,2},{1,3},{2,0},{3,1},{4,6},{5,7},{6,4},{7,5},{8,10},{9,11},{10,... | collective-permute-start | bytes 786440 | tf_op jit(solution)/shard_map/ppermute | solution.py:373
  42.6 12.7 %collective-permute-start.7 = (f32[256,256]{1,0:T(8,128)S(1)}, f32[256,256]{1,0:T(8,128)S(1)}, u32[]{:S(2)}, u32[]{:S(2)}) collective-permute-start(f32[256,256]{1,0:T(8,128)S(1)} %get-tuple-element.61.kernel_ref.rest_0_), channel_id=1, source_target_pairs={{0,1},{1,0},{2,3},{3,2},{4,5},{5,4},{6,7},{7,6},{8,9},{9,8},{10,11... | collective-permute-start | bytes 786440 | tf_op jit(solution)/shard_map/ppermute | solution.py:376
  50.7 11.9 %collective-permute-start.8 = (f32[256,256]{1,0:T(8,128)S(1)}, f32[256,256]{1,0:T(8,128)}, u32[]{:S(2)}, u32[]{:S(2)}) collective-permute-start(f32[256,256]{1,0:T(8,128)S(1)} %collective-permute-done.4.rest_1_), channel_id=1, source_target_pairs={{0,1},{1,0},{2,3},{3,2},{4,5},{5,4},{6,7},{7,6},{8,9},{9,8},{10,11... | collective-permute-start | bytes 786440 | tf_op jit(solution)/shard_map/ppermute | solution.py:376
  51.6 11.0 %collective-permute-start.9 = (f32[256,256]{1,0:T(8,128)S(1)}, f32[256,256]{1,0:T(8,128)}, u32[]{:S(2)}, u32[]{:S(2)}) collective-permute-start(f32[256,256]{1,0:T(8,128)S(1)} %collective-permute-done.5.rest_2_), channel_id=1, source_target_pairs={{0,1},{1,0},{2,3},{3,2},{4,5},{5,4},{6,7},{7,6},{8,9},{9,8},{10,11... | collective-permute-start | bytes 786440 | tf_op jit(solution)/shard_map/ppermute | solution.py:376
  52.7 9.9 %collective-permute-start.10 = (f32[256,256]{1,0:T(8,128)S(1)}, f32[256,256]{1,0:T(8,128)}, u32[]{:S(2)}, u32[]{:S(2)}) collective-permute-start(f32[256,256]{1,0:T(8,128)S(1)} %collective-permute-done.6.rest_3_), channel_id=1, source_target_pairs={{0,1},{1,0},{2,3},{3,2},{4,5},{5,4},{6,7},{7,6},{8,9},{9,8},{10,11... | collective-permute-start | bytes 786440 | tf_op jit(solution)/shard_map/ppermute | solution.py:376
  67.5 38.8 %collective-permute-start.13 = (bf16[640,256]{1,0:T(8,128)(2,1)S(1)}, bf16[640,256]{1,0:T(8,128)(2,1)S(1)}, u32[]{:S(2)}, u32[]{:S(2)}) collective-permute-start(bf16[640,256]{1,0:T(8,128)(2,1)S(1)} %get-tuple-element.69.rest_0_), channel_id=1, source_target_pairs={{0,6},{1,7},{2,4},{3,5},{4,2},{5,3},{6,0},{7,1},{8,14},{9,15},{10,... | collective-permute-start | bytes 983048 | tf_op jit(solution)/shard_map/ppermute | solution.py:373
  68.2 38.1 %collective-permute-start.12 = (bf16[640,256]{1,0:T(8,128)(2,1)S(1)}, bf16[640,256]{1,0:T(8,128)(2,1)}, u32[]{:S(2)}, u32[]{:S(2)}) collective-permute-start(bf16[640,256]{1,0:T(8,128)(2,1)S(1)} %get-tuple-element.69.rest_0_), channel_id=1, source_target_pairs={{0,4},{1,5},{2,6},{3,7},{4,0},{5,1},{6,2},{7,3},{8,12},{9,13},{10,... | collective-permute-start | bytes 983048 | tf_op jit(solution)/shard_map/ppermute | solution.py:373
  69.5 36.8 %collective-permute-start.11 = (bf16[640,256]{1,0:T(8,128)(2,1)S(1)}, bf16[640,256]{1,0:T(8,128)(2,1)}, u32[]{:S(2)}, u32[]{:S(2)}) collective-permute-start(bf16[640,256]{1,0:T(8,128)(2,1)S(1)} %get-tuple-element.69.rest_0_), channel_id=1, source_target_pairs={{0,2},{1,3},{2,0},{3,1},{4,6},{5,7},{6,4},{7,5},{8,10},{9,11},{10,... | collective-permute-start | bytes 983048 | tf_op jit(solution)/shard_map/ppermute | solution.py:373
  98.2 11.4 %collective-permute-start.14 = (bf16[640,256]{1,0:T(8,128)(2,1)S(1)}, bf16[640,256]{1,0:T(8,128)(2,1)}, u32[]{:S(2)}, u32[]{:S(2)}) collective-permute-start(bf16[640,256]{1,0:T(8,128)(2,1)S(1)} %get-tuple-element.69.rest_0_), channel_id=1, source_target_pairs={{0,1},{1,0},{2,3},{3,2},{4,5},{5,4},{6,7},{7,6},{8,9},{9,8},{10,11... | collective-permute-start | bytes 983048 | tf_op jit(solution)/shard_map/ppermute | solution.py:376
  106.4 10.5 %collective-permute-start.15 = (bf16[640,256]{1,0:T(8,128)(2,1)}, bf16[640,256]{1,0:T(8,128)(2,1)S(1)}, u32[]{:S(2)}, u32[]{:S(2)}) collective-permute-start(bf16[640,256]{1,0:T(8,128)(2,1)} %collective-permute-done.11.rest_1_), channel_id=1, source_target_pairs={{0,1},{1,0},{2,3},{3,2},{4,5},{5,4},{6,7},{7,6},{8,9},{9,8},{10,11... | collective-permute-start | bytes 983048 | tf_op jit(solution)/shard_map/ppermute | solution.py:376
  106.5 10.3 %collective-permute-start.16 = (bf16[640,256]{1,0:T(8,128)(2,1)}, bf16[640,256]{1,0:T(8,128)(2,1)}, u32[]{:S(2)}, u32[]{:S(2)}) collective-permute-start(bf16[640,256]{1,0:T(8,128)(2,1)} %collective-permute-done.12.rest_2_), channel_id=1, source_target_pairs={{0,1},{1,0},{2,3},{3,2},{4,5},{5,4},{6,7},{7,6},{8,9},{9,8},{10,11... | collective-permute-start | bytes 983048 | tf_op jit(solution)/shard_map/ppermute | solution.py:376
  106.9 10.0 %collective-permute-start.17 = (bf16[640,256]{1,0:T(8,128)(2,1)S(1)}, bf16[640,256]{1,0:T(8,128)(2,1)}, u32[]{:S(2)}, u32[]{:S(2)}) collective-permute-start(bf16[640,256]{1,0:T(8,128)(2,1)S(1)} %collective-permute-done.13.rest_3_), channel_id=1, source_target_pairs={{0,1},{1,0},{2,3},{3,2},{4,5},{5,4},{6,7},{7,6},{8,9},{9,8},{10,11... | collective-permute-start | bytes 983048 | tf_op jit(solution)/shard_map/ppermute | solution.py:376
  121.1 35.9 %collective-permute-start.20 = (f32[256,256]{1,0:T(8,128)S(1)}, f32[256,256]{1,0:T(8,128)S(1)}, u32[]{:S(2)}, u32[]{:S(2)}) collective-permute-start(f32[256,256]{1,0:T(8,128)S(1)} %get-tuple-element.76.kernel_ref.rest_0_.own), channel_id=1, source_target_pairs={{0,6},{1,7},{2,4},{3,5},{4,2},{5,3},{6,0},{7,1},{8,14},{9,15},{10,... | collective-permute-start | bytes 786440 | tf_op jit(solution)/shard_map/ppermute | solution.py:373
  121.8 35.2 %collective-permute-start.19 = (f32[256,256]{1,0:T(8,128)S(1)}, f32[256,256]{1,0:T(8,128)S(1)}, u32[]{:S(2)}, u32[]{:S(2)}) collective-permute-start(f32[256,256]{1,0:T(8,128)S(1)} %get-tuple-element.76.kernel_ref.rest_0_.own), channel_id=1, source_target_pairs={{0,4},{1,5},{2,6},{3,7},{4,0},{5,1},{6,2},{7,3},{8,12},{9,13},{10,... | collective-permute-start | bytes 786440 | tf_op jit(solution)/shard_map/ppermute | solution.py:373
  123.2 33.8 %collective-permute-start.18 = (f32[256,256]{1,0:T(8,128)S(1)}, f32[256,256]{1,0:T(8,128)S(1)}, u32[]{:S(2)}, u32[]{:S(2)}) collective-permute-start(f32[256,256]{1,0:T(8,128)S(1)} %get-tuple-element.76.kernel_ref.rest_0_.own), channel_id=1, source_target_pairs={{0,2},{1,3},{2,0},{3,1},{4,6},{5,7},{6,4},{7,5},{8,10},{9,11},{10,... | collective-permute-start | bytes 786440 | tf_op jit(solution)/shard_map/ppermute | solution.py:373
  148.9 11.3 %collective-permute-start.21 = (f32[256,256]{1,0:T(8,128)S(1)}, f32[256,256]{1,0:T(8,128)S(1)}, u32[]{:S(2)}, u32[]{:S(2)}) collective-permute-start(f32[256,256]{1,0:T(8,128)S(1)} %get-tuple-element.76.kernel_ref.rest_0_.own), channel_id=1, source_target_pairs={{0,1},{1,0},{2,3},{3,2},{4,5},{5,4},{6,7},{7,6},{8,9},{9,8},{10,11... | collective-permute-start | bytes 786440 | tf_op jit(solution)/shard_map/ppermute | solution.py:376
  157.0 10.5 %collective-permute-start.22 = (f32[256,256]{1,0:T(8,128)S(1)}, f32[256,256]{1,0:T(8,128)S(1)}, u32[]{:S(2)}, u32[]{:S(2)}) collective-permute-start(f32[256,256]{1,0:T(8,128)S(1)} %collective-permute-done.18.rest_1_), channel_id=1, source_target_pairs={{0,1},{1,0},{2,3},{3,2},{4,5},{5,4},{6,7},{7,6},{8,9},{9,8},{10,11... | collective-permute-start | bytes 786440 | tf_op jit(solution)/shard_map/ppermute | solution.py:376
  157.2 10.3 %collective-permute-start.23 = (f32[256,256]{1,0:T(8,128)S(1)}, f32[256,256]{1,0:T(8,128)S(1)}, u32[]{:S(2)}, u32[]{:S(2)}) collective-permute-start(f32[256,256]{1,0:T(8,128)S(1)} %collective-permute-done.19.rest_2_), channel_id=1, source_target_pairs={{0,1},{1,0},{2,3},{3,2},{4,5},{5,4},{6,7},{7,6},{8,9},{9,8},{10,11... | collective-permute-start | bytes 786440 | tf_op jit(solution)/shard_map/ppermute | solution.py:376
  157.6 10.0 %collective-permute-start.24 = (f32[256,256]{1,0:T(8,128)S(1)}, f32[256,256]{1,0:T(8,128)S(1)}, u32[]{:S(2)}, u32[]{:S(2)}) collective-permute-start(f32[256,256]{1,0:T(8,128)S(1)} %collective-permute-done.20.rest_3_), channel_id=1, source_target_pairs={{0,1},{1,0},{2,3},{3,2},{4,5},{5,4},{6,7},{7,6},{8,9},{9,8},{10,11... | collective-permute-start | bytes 786440 | tf_op jit(solution)/shard_map/ppermute | solution.py:376
  (13 other events, 65.7 us)

commit v10 on v9

--- a/solution.py
+++ b/solution.py
@@ -376,16 +376,28 @@
         return lax.ppermute(value, "blk", [(i, i ^ 1) for i in range(blocks)])
 
     def balance(kernel, sent, local, count):
-        here = [sent] + [across_pairs(sent, k) for k in range(1, blocks // 2)]
-        there = [to_other(sent)]
+        here, there = {0: sent}, {}
         for step in range(count):
-            if step + 1 == count:
-                local, *here = lax.optimization_barrier((local, *here))
-                there += [to_other(one) for one in here[1:]]
+            if step == 0:
+                moves = [(here, k, across_pairs(sent, k)) for k in range(1, blocks // 2)][:2]
+            elif step == 1:
+                moves = [(there, 0, to_other(sent))]
+                moves += [(here, k, across_pairs(sent, k)) for k in range(3, blocks // 2)]
+            else:
+                ready = [k for k in here if k not in there]
+                if step + 1 < count:
+                    ready = ready[:2]
+                moves = [(there, k, to_other(here[k])) for k in ready]
             summed = exchange(local)
+            summed, *moved = lax.optimization_barrier((summed, *(one for _, _, one in moves)))
+            for (place, k, _), one in zip(moves, moved):
+                place[k] = one
             if step + 1 < count:
                 local = call(balance_kernel, parts, [VMEM] * 3)(kernel, summed, target)
-        return summed, here + there
+                local, sent, *moved = lax.optimization_barrier((local, sent, *here.values()))
+                here = dict(zip(here, moved))
+        order = range(blocks // 2)
+        return summed, [here[k] for k in order] + [there[k] for k in order]
 
     def last_balance(kernel, local):
         for step in range(ITERS):

time: 207 us -> 182 us (0.88)
  blocking collectives: 105 us -> 153 us
  waiting for transfers between devices: 42.3 us -> 0.11 us
  starting transfers between devices: 33.6 us -> 13 us
  Pallas kernels: 19.2 us -> 13.6 us
  local copies, waits for them, and re-layouts: 4.94 us -> 0 us
    all_to_all x10 -> x16, blocking collectives: 105 us -> 153 us  [exchange(): return lax.all_to_all(parts, AXES, split_axis=0, concat_axis=0, tiled=True)]
    all_to_all x6 -> x0, waiting for transfers between devices: 42.2 us -> none  [exchange(): return lax.all_to_all(parts, AXES, split_axis=0, concat_axis=0, tiled=True)]
    all_to_all x6 -> x0, starting transfers between devices: 15.4 us -> none  [exchange(): return lax.all_to_all(parts, AXES, split_axis=0, concat_axis=0, tiled=True)]
    unnamed x12 -> x0, local copies, waits for them, and re-layouts: 4.94 us -> none
    ppermute x9, starting transfers between devices: 10.7 us -> 5.82 us  [across_pairs(): return lax.ppermute(value, 'blk', [(i, i ^ 2 * k) for i in range(blocks)])]
    pallas_call x8, Pallas kernels: 5.32 us -> 1.62 us  [balance(): local = call(balance_kernel, parts, [VMEM] * 3)(kernel, summed, target)]
  transfers between devices with their start and end apart: 31 -> 25, of which waited for: 6 -> 0; matrix products, arithmetic and copies ran while one was open for 0% -> 0% of each run, Pallas kernels for 3% -> 1%
where the time goes in v10:
time: 182 us; the launch traced here: 181 us
  blocking collectives  153 us (84%)
  Pallas kernels  13.6 us (7%)
  starting transfers between devices  13 us (7%)
    all_to_all x16, blocking collectives, exchange(): return lax.all_to_all(parts, AXES, split_axis=0, concat_axis=0, tiled=True)  153 us
    ppermute x9, starting transfers between devices, across_pairs(): return lax.ppermute(value, 'blk', [(i, i ^ 2 * k) for i in range(blocks)])  5.82 us
    ppermute x3, starting transfers between devices, on_device(): lax.ppermute(one, 'blk', [(i, i ^ 2 * k) for i in range(blocks)])  4.47 us
  transfers between devices with their start and end apart: 25, of which 0 were waited for; matrix products, arithmetic and copies ran while one was open for 0% of the time, Pallas kernels for 1%

profile of v10, /device:TPU:0, one launch (start us, length us, event | category | flops | bytes accessed | tf_op | source)
XLA Modules:
  0.0 181.4 jit_solution(12904238110348933502)
XLA Ops:
  1.3 2.2 %shard_map.95 = (s32[8]{0:T(128)S(1)}, s32[8]{0:T(128)S(1)}, s32[5,128]{1,0:T(8,128)S(1)}, s32[5,128]{1,0:T(8,128)S(1)}, f32[1,256]{1,0:T(1,128)S(1)}, /*index=5...) custom-call(s32[1]{0:T(128)S(6)} %copy.10.tile_count, ...), custom_call_target="tpu_custom_call" | custom-call | tf_op jit(solution)/shard_map/pallas_call | solution.py:348
  4.0 1.2 shard_map.96
  5.3 2.9 %collective-permute-start.1 = (bf16[2,336,128]{2,1,0:T(8,128)(2,1)S(1)}, bf16[2,336,128]{2,1,0:T(8,128)(2,1)S(1)}, u32[]{:S(2)}, u32[]{:S(2)}) collective-permute-start(bf16[2,336,128]{2,1,0:T(8,128)(2,1)S(1)} %get-tuple-element.112), channel_id=1, source_target_pairs={{0,2},{1,3},{2,0},{3,1},{4,6},{5,7},{6,4},{7,5},{8,10},{9,11},{10,... | collective-permute-start | bytes 516104 | tf_op jit(solution)/shard_map/ppermute | solution.py:364
  8.2 1.5 collective-permute-start.2
  9.8 13.4 %all_to_all.80.summed = f32[32,1,256]{2,1,0:T(1,128)S(1)} all-to-all(f32[32,1,256]{2,1,0:T(1,128)S(1)} %shard_map.96), channel_id=1, replica_groups=mesh['grp'=4,'blk'=8] {'grp','blk'}, dimensions={0} | all-to-all | bytes 65536 | tf_op jit(solution)/shard_map/all_to_all | solution.py:314
  25.2 9.8 %all_to_all.81.summed = f32[32,1,256]{2,1,0:T(1,128)S(1)} all-to-all(f32[32,1,256]{2,1,0:T(1,128)S(1)} %get-tuple-element.116), channel_id=1, replica_groups=mesh['grp'=4,'blk'=8] {'grp','blk'}, dimensions={0} | all-to-all | bytes 65536 | tf_op jit(solution)/shard_map/all_to_all | solution.py:314
  35.9 9.9 %all_to_all.82.summed = f32[32,1,256]{2,1,0:T(1,128)S(1)} all-to-all(f32[32,1,256]{2,1,0:T(1,128)S(1)} %shard_map.99), channel_id=1, replica_groups=mesh['grp'=4,'blk'=8] {'grp','blk'}, dimensions={0} | all-to-all | bytes 65536 | tf_op jit(solution)/shard_map/all_to_all | solution.py:314
  46.6 8.9 %all_to_all.83.summed = f32[32,1,256]{2,1,0:T(1,128)S(1)} all-to-all(f32[32,1,256]{2,1,0:T(1,128)S(1)} %shard_map.100), channel_id=1, replica_groups=mesh['grp'=4,'blk'=8] {'grp','blk'}, dimensions={0} | all-to-all | bytes 65536 | tf_op jit(solution)/shard_map/all_to_all | solution.py:314
  55.6 1.5 shard_map.101
  58.3 10.1 %all_to_all.84.summed = f32[32,1,256]{2,1,0:T(1,128)S(1)} all-to-all(f32[32,1,256]{2,1,0:T(1,128)S(1)} %get-tuple-element.138), channel_id=1, replica_groups=mesh['grp'=4,'blk'=8] {'grp','blk'}, dimensions={0} | all-to-all | bytes 65536 | tf_op jit(solution)/shard_map/all_to_all | solution.py:314
  69.2 10.2 %all_to_all.85.summed = f32[32,1,256]{2,1,0:T(1,128)S(1)} all-to-all(f32[32,1,256]{2,1,0:T(1,128)S(1)} %shard_map.102), channel_id=1, replica_groups=mesh['grp'=4,'blk'=8] {'grp','blk'}, dimensions={0} | all-to-all | bytes 65536 | tf_op jit(solution)/shard_map/all_to_all | solution.py:314
  80.2 8.9 %all_to_all.86.summed = f32[32,1,256]{2,1,0:T(1,128)S(1)} all-to-all(f32[32,1,256]{2,1,0:T(1,128)S(1)} %shard_map.103), channel_id=1, replica_groups=mesh['grp'=4,'blk'=8] {'grp','blk'}, dimensions={0} | all-to-all | bytes 65536 | tf_op jit(solution)/shard_map/all_to_all | solution.py:314
  89.6 8.9 %all_to_all.87.summed = f32[32,1,256]{2,1,0:T(1,128)S(1)} all-to-all(f32[32,1,256]{2,1,0:T(1,128)S(1)} %shard_map.104), channel_id=1, replica_groups=mesh['grp'=4,'blk'=8] {'grp','blk'}, dimensions={0} | all-to-all | bytes 65536 | tf_op jit(solution)/shard_map/all_to_all | solution.py:314
  98.5 2.9 %shard_map.105 = (f32[256,256]{1,0:T(8,128)S(1)}, f32[32,1,256]{2,1,0:T(1,128)S(1)}) custom-call(f32[32,1,256]{2,1,0:T(1,128)S(1)} %all_to_all.87.summed, f32[1,256]{1,0:T(1,128)S(1)} %get-tuple-element.104.class_prior, f32[1,256]{1,0:T(1,128)S(1)} %get-tuple-element.111.class_target, bf16[640,256]{1,0:T(8,128)(2,1)S(1)} %get-tuple-element.159.rest_0_, ...), custom_call_target="tpu_custom_call" | custom-call | tf_op jit(solution)/shard_map/pallas_call | solution.py:416
  102.7 9.7 %all_to_all.88.summed = f32[32,1,256]{2,1,0:T(1,128)S(1)} all-to-all(f32[32,1,256]{2,1,0:T(1,128)S(1)} %get-tuple-element.167), channel_id=1, replica_groups=mesh['grp'=4,'blk'=8] {'grp','blk'}, dimensions={0} | all-to-all | bytes 65536 | tf_op jit(solution)/shard_map/all_to_all | solution.py:314
  113.3 9.9 %all_to_all.89.summed = f32[32,1,256]{2,1,0:T(1,128)S(1)} all-to-all(f32[32,1,256]{2,1,0:T(1,128)S(1)} %shard_map.106), channel_id=1, replica_groups=mesh['grp'=4,'blk'=8] {'grp','blk'}, dimensions={0} | all-to-all | bytes 65536 | tf_op jit(solution)/shard_map/all_to_all | solution.py:314
  124.0 8.9 %all_to_all.90.summed = f32[32,1,256]{2,1,0:T(1,128)S(1)} all-to-all(f32[32,1,256]{2,1,0:T(1,128)S(1)} %shard_map.107), channel_id=1, replica_groups=mesh['grp'=4,'blk'=8] {'grp','blk'}, dimensions={0} | all-to-all | bytes 65536 | tf_op jit(solution)/shard_map/all_to_all | solution.py:314
  133.3 8.9 %all_to_all.91.summed.author_summed = f32[32,1,256]{2,1,0:T(1,128)S(1)} all-to-all(f32[32,1,256]{2,1,0:T(1,128)S(1)} %shard_map.108), channel_id=1, replica_groups=mesh['grp'=4,'blk'=8] {'grp','blk'}, dimensions={0} | all-to-all | bytes 65536 | tf_op jit(solution)/shard_map/all_to_all | solution.py:314
  142.2 1.5 shard_map.109
  143.7 8.9 %all_to_all.92.summed = f32[32,1,256]{2,1,0:T(1,128)S(1)} all-to-all(f32[32,1,256]{2,1,0:T(1,128)S(1)} %get-tuple-element.195), channel_id=1, replica_groups=mesh['grp'=4,'blk'=8] {'grp','blk'}, dimensions={0} | all-to-all | bytes 65536 | tf_op jit(solution)/shard_map/all_to_all | solution.py:314
  152.9 8.9 %all_to_all.93.summed = f32[32,1,256]{2,1,0:T(1,128)S(1)} all-to-all(f32[32,1,256]{2,1,0:T(1,128)S(1)} %shard_map.110), channel_id=1, replica_groups=mesh['grp'=4,'blk'=8] {'grp','blk'}, dimensions={0} | all-to-all | bytes 65536 | tf_op jit(solution)/shard_map/all_to_all | solution.py:314
  162.0 8.9 %all_to_all.94.summed = f32[32,1,256]{2,1,0:T(1,128)S(1)} all-to-all(f32[32,1,256]{2,1,0:T(1,128)S(1)} %shard_map.111), channel_id=1, replica_groups=mesh['grp'=4,'blk'=8] {'grp','blk'}, dimensions={0} | all-to-all | bytes 65536 | tf_op jit(solution)/shard_map/all_to_all | solution.py:314
  171.2 8.9 %all_to_all.95.summed = f32[32,1,256]{2,1,0:T(1,128)S(1)} all-to-all(f32[32,1,256]{2,1,0:T(1,128)S(1)} %shard_map.112), channel_id=1, replica_groups=mesh['grp'=4,'blk'=8] {'grp','blk'}, dimensions={0} | all-to-all | bytes 65536 | tf_op jit(solution)/shard_map/all_to_all | solution.py:314
  180.2 1.2 shard_map.113
  (61 shorter events, 11.8 us)
Async XLA Ops:
  5.3 17.8 %collective-permute-start.1 = (bf16[2,336,128]{2,1,0:T(8,128)(2,1)S(1)}, bf16[2,336,128]{2,1,0:T(8,128)(2,1)S(1)}, u32[]{:S(2)}, u32[]{:S(2)}) collective-permute-start(bf16[2,336,128]{2,1,0:T(8,128)(2,1)S(1)} %get-tuple-element.112), channel_id=1, source_target_pairs={{0,2},{1,3},{2,0},{3,1},{4,6},{5,7},{6,4},{7,5},{8,10},{9,11},{10,... | collective-permute-start | bytes 516104 | tf_op jit(solution)/shard_map/ppermute | solution.py:364
  8.2 14.9 %collective-permute-start.2 = (bf16[2,336,128]{2,1,0:T(8,128)(2,1)S(1)}, bf16[2,336,128]{2,1,0:T(8,128)(2,1)S(1)}, u32[]{:S(2)}, u32[]{:S(2)}) collective-permute-start(bf16[2,336,128]{2,1,0:T(8,128)(2,1)S(1)} %get-tuple-element.113), channel_id=1, source_target_pairs={{0,4},{1,5},{2,6},{3,7},{4,0},{5,1},{6,2},{7,3},{8,12},{9,13},{10,... | collective-permute-start | bytes 516104 | tf_op jit(solution)/shard_map/ppermute | solution.py:364
  9.8 13.4 %collective-permute-start.3 = (bf16[2,336,128]{2,1,0:T(8,128)(2,1)S(1)}, bf16[2,336,128]{2,1,0:T(8,128)(2,1)S(1)}, u32[]{:S(2)}, u32[]{:S(2)}) collective-permute-start(bf16[2,336,128]{2,1,0:T(8,128)(2,1)S(1)} %get-tuple-element.114), channel_id=1, source_target_pairs={{0,6},{1,7},{2,4},{3,5},{4,2},{5,3},{6,0},{7,1},{8,14},{9,15},{10,... | collective-permute-start | bytes 516104 | tf_op jit(solution)/shard_map/ppermute | solution.py:364
  24.0 11.0 %collective-permute-start.5 = (f32[256,256]{1,0:T(8,128)S(1)}, f32[256,256]{1,0:T(8,128)S(1)}, u32[]{:S(2)}, u32[]{:S(2)}) collective-permute-start(f32[256,256]{1,0:T(8,128)S(1)} %get-tuple-element.132.kernel_ref.rest_0_), channel_id=1, source_target_pairs={{0,4},{1,5},{2,6},{3,7},{4,0},{5,1},{6,2},{7,3},{8,12},{9,13},{10,... | collective-permute-start | bytes 786440 | tf_op jit(solution)/shard_map/ppermute | solution.py:373
  24.6 10.4 %collective-permute-start.4 = (f32[256,256]{1,0:T(8,128)S(1)}, f32[256,256]{1,0:T(8,128)S(1)}, u32[]{:S(2)}, u32[]{:S(2)}) collective-permute-start(f32[256,256]{1,0:T(8,128)S(1)} %get-tuple-element.132.kernel_ref.rest_0_), channel_id=1, source_target_pairs={{0,2},{1,3},{2,0},{3,1},{4,6},{5,7},{6,4},{7,5},{8,10},{9,11},{10,... | collective-permute-start | bytes 786440 | tf_op jit(solution)/shard_map/ppermute | solution.py:373
  35.2 10.6 %collective-permute-start.7 = (f32[256,256]{1,0:T(8,128)S(1)}, f32[256,256]{1,0:T(8,128)S(1)}, u32[]{:S(2)}, u32[]{:S(2)}) collective-permute-start(f32[256,256]{1,0:T(8,128)S(1)} %get-tuple-element.132.kernel_ref.rest_0_), channel_id=1, source_target_pairs={{0,6},{1,7},{2,4},{3,5},{4,2},{5,3},{6,0},{7,1},{8,14},{9,15},{10,... | collective-permute-start | bytes 786440 | tf_op jit(solution)/shard_map/ppermute | solution.py:373
  35.9 9.9 %collective-permute-start.6 = (f32[256,256]{1,0:T(8,128)S(1)}, f32[256,256]{1,0:T(8,128)S(1)}, u32[]{:S(2)}, u32[]{:S(2)}) collective-permute-start(f32[256,256]{1,0:T(8,128)S(1)} %get-tuple-element.132.kernel_ref.rest_0_), channel_id=1, source_target_pairs={{0,1},{1,0},{2,3},{3,2},{4,5},{5,4},{6,7},{7,6},{8,9},{9,8},{10,11... | collective-permute-start | bytes 786440 | tf_op jit(solution)/shard_map/ppermute | solution.py:376
  45.9 9.6 %collective-permute-start.8 = (f32[256,256]{1,0:T(8,128)S(1)}, f32[256,256]{1,0:T(8,128)S(1)}, u32[]{:S(2)}, u32[]{:S(2)}) collective-permute-start(f32[256,256]{1,0:T(8,128)S(1)} %collective-permute-done.4.rest_1_), channel_id=1, source_target_pairs={{0,1},{1,0},{2,3},{3,2},{4,5},{5,4},{6,7},{7,6},{8,9},{9,8},{10,11... | collective-permute-start | bytes 786440 | tf_op jit(solution)/shard_map/ppermute | solution.py:376
  46.1 9.4 %collective-permute-start.9 = (f32[256,256]{1,0:T(8,128)S(1)}, f32[256,256]{1,0:T(8,128)S(1)}, u32[]{:S(2)}, u32[]{:S(2)}) collective-permute-start(f32[256,256]{1,0:T(8,128)S(1)} %collective-permute-done.5.rest_2_), channel_id=1, source_target_pairs={{0,1},{1,0},{2,3},{3,2},{4,5},{5,4},{6,7},{7,6},{8,9},{9,8},{10,11... | collective-permute-start | bytes 786440 | tf_op jit(solution)/shard_map/ppermute | solution.py:376
  46.5 9.1 %collective-permute-start.10 = (f32[256,256]{1,0:T(8,128)S(1)}, f32[256,256]{1,0:T(8,128)S(1)}, u32[]{:S(2)}, u32[]{:S(2)}) collective-permute-start(f32[256,256]{1,0:T(8,128)S(1)} %collective-permute-done.7.rest_3_), channel_id=1, source_target_pairs={{0,1},{1,0},{2,3},{3,2},{4,5},{5,4},{6,7},{7,6},{8,9},{9,8},{10,11... | collective-permute-start | bytes 786440 | tf_op jit(solution)/shard_map/ppermute | solution.py:376
  57.1 11.3 %collective-permute-start.12 = (bf16[640,256]{1,0:T(8,128)(2,1)S(1)}, bf16[640,256]{1,0:T(8,128)(2,1)S(1)}, u32[]{:S(2)}, u32[]{:S(2)}) collective-permute-start(bf16[640,256]{1,0:T(8,128)(2,1)S(1)} %get-tuple-element.159.rest_0_), channel_id=1, source_target_pairs={{0,4},{1,5},{2,6},{3,7},{4,0},{5,1},{6,2},{7,3},{8,12},{9,13},{10,... | collective-permute-start | bytes 983048 | tf_op jit(solution)/shard_map/ppermute | solution.py:373
  57.7 10.7 %collective-permute-start.11 = (bf16[640,256]{1,0:T(8,128)(2,1)S(1)}, bf16[640,256]{1,0:T(8,128)(2,1)S(1)}, u32[]{:S(2)}, u32[]{:S(2)}) collective-permute-start(bf16[640,256]{1,0:T(8,128)(2,1)S(1)} %get-tuple-element.159.rest_0_), channel_id=1, source_target_pairs={{0,2},{1,3},{2,0},{3,1},{4,6},{5,7},{6,4},{7,5},{8,10},{9,11},{10,... | collective-permute-start | bytes 983048 | tf_op jit(solution)/shard_map/ppermute | solution.py:373
  68.6 10.8 %collective-permute-start.14 = (bf16[640,256]{1,0:T(8,128)(2,1)S(1)}, bf16[640,256]{1,0:T(8,128)(2,1)S(1)}, u32[]{:S(2)}, u32[]{:S(2)}) collective-permute-start(bf16[640,256]{1,0:T(8,128)(2,1)S(1)} %get-tuple-element.159.rest_0_), channel_id=1, source_target_pairs={{0,6},{1,7},{2,4},{3,5},{4,2},{5,3},{6,0},{7,1},{8,14},{9,15},{10,... | collective-permute-start | bytes 983048 | tf_op jit(solution)/shard_map/ppermute | solution.py:373
  69.2 10.2 %collective-permute-start.13 = (bf16[640,256]{1,0:T(8,128)(2,1)S(1)}, bf16[640,256]{1,0:T(8,128)(2,1)S(1)}, u32[]{:S(2)}, u32[]{:S(2)}) collective-permute-start(bf16[640,256]{1,0:T(8,128)(2,1)S(1)} %get-tuple-element.159.rest_0_), channel_id=1, source_target_pairs={{0,1},{1,0},{2,3},{3,2},{4,5},{5,4},{6,7},{7,6},{8,9},{9,8},{10,11... | collective-permute-start | bytes 983048 | tf_op jit(solution)/shard_map/ppermute | solution.py:376
  79.7 9.5 %collective-permute-start.15 = (bf16[640,256]{1,0:T(8,128)(2,1)S(1)}, bf16[640,256]{1,0:T(8,128)(2,1)S(1)}, u32[]{:S(2)}, u32[]{:S(2)}) collective-permute-start(bf16[640,256]{1,0:T(8,128)(2,1)S(1)} %collective-permute-done.11.rest_1_), channel_id=1, source_target_pairs={{0,1},{1,0},{2,3},{3,2},{4,5},{5,4},{6,7},{7,6},{8,9},{9,8},{10,11... | collective-permute-start | bytes 983048 | tf_op jit(solution)/shard_map/ppermute | solution.py:376
  79.8 9.4 %collective-permute-start.16 = (bf16[640,256]{1,0:T(8,128)(2,1)S(1)}, bf16[640,256]{1,0:T(8,128)(2,1)S(1)}, u32[]{:S(2)}, u32[]{:S(2)}) collective-permute-start(bf16[640,256]{1,0:T(8,128)(2,1)S(1)} %collective-permute-done.12.rest_2_), channel_id=1, source_target_pairs={{0,1},{1,0},{2,3},{3,2},{4,5},{5,4},{6,7},{7,6},{8,9},{9,8},{10,11... | collective-permute-start | bytes 983048 | tf_op jit(solution)/shard_map/ppermute | solution.py:376
  89.4 9.1 %collective-permute-start.17 = (bf16[640,256]{1,0:T(8,128)(2,1)S(1)}, bf16[640,256]{1,0:T(8,128)(2,1)S(1)}, u32[]{:S(2)}, u32[]{:S(2)}) collective-permute-start(bf16[640,256]{1,0:T(8,128)(2,1)S(1)} %collective-permute-done.14.rest_3_), channel_id=1, source_target_pairs={{0,1},{1,0},{2,3},{3,2},{4,5},{5,4},{6,7},{7,6},{8,9},{9,8},{10,11... | collective-permute-start | bytes 983048 | tf_op jit(solution)/shard_map/ppermute | solution.py:376
  101.4 11.0 %collective-permute-start.19 = (f32[256,256]{1,0:T(8,128)S(1)}, f32[256,256]{1,0:T(8,128)S(1)}, u32[]{:S(2)}, u32[]{:S(2)}) collective-permute-start(f32[256,256]{1,0:T(8,128)S(1)} %get-tuple-element.187.kernel_ref.rest_0_.own), channel_id=1, source_target_pairs={{0,4},{1,5},{2,6},{3,7},{4,0},{5,1},{6,2},{7,3},{8,12},{9,13},{10,... | collective-permute-start | bytes 786440 | tf_op jit(solution)/shard_map/ppermute | solution.py:373
  102.0 10.4 %collective-permute-start.18 = (f32[256,256]{1,0:T(8,128)S(1)}, f32[256,256]{1,0:T(8,128)S(1)}, u32[]{:S(2)}, u32[]{:S(2)}) collective-permute-start(f32[256,256]{1,0:T(8,128)S(1)} %get-tuple-element.187.kernel_ref.rest_0_.own), channel_id=1, source_target_pairs={{0,2},{1,3},{2,0},{3,1},{4,6},{5,7},{6,4},{7,5},{8,10},{9,11},{10,... | collective-permute-start | bytes 786440 | tf_op jit(solution)/shard_map/ppermute | solution.py:373
  112.6 10.6 %collective-permute-start.21 = (f32[256,256]{1,0:T(8,128)S(1)}, f32[256,256]{1,0:T(8,128)S(1)}, u32[]{:S(2)}, u32[]{:S(2)}) collective-permute-start(f32[256,256]{1,0:T(8,128)S(1)} %get-tuple-element.187.kernel_ref.rest_0_.own), channel_id=1, source_target_pairs={{0,6},{1,7},{2,4},{3,5},{4,2},{5,3},{6,0},{7,1},{8,14},{9,15},{10,... | collective-permute-start | bytes 786440 | tf_op jit(solution)/shard_map/ppermute | solution.py:373
  113.3 9.9 %collective-permute-start.20 = (f32[256,256]{1,0:T(8,128)S(1)}, f32[256,256]{1,0:T(8,128)S(1)}, u32[]{:S(2)}, u32[]{:S(2)}) collective-permute-start(f32[256,256]{1,0:T(8,128)S(1)} %get-tuple-element.187.kernel_ref.rest_0_.own), channel_id=1, source_target_pairs={{0,1},{1,0},{2,3},{3,2},{4,5},{5,4},{6,7},{7,6},{8,9},{9,8},{10,11... | collective-permute-start | bytes 786440 | tf_op jit(solution)/shard_map/ppermute | solution.py:376
  123.4 9.5 %collective-permute-start.22 = (f32[256,256]{1,0:T(8,128)S(1)}, f32[256,256]{1,0:T(8,128)S(1)}, u32[]{:S(2)}, u32[]{:S(2)}) collective-permute-start(f32[256,256]{1,0:T(8,128)S(1)} %collective-permute-done.18.rest_1_), channel_id=1, source_target_pairs={{0,1},{1,0},{2,3},{3,2},{4,5},{5,4},{6,7},{7,6},{8,9},{9,8},{10,11... | collective-permute-start | bytes 786440 | tf_op jit(solution)/shard_map/ppermute | solution.py:376
  123.6 9.3 %collective-permute-start.23 = (f32[256,256]{1,0:T(8,128)S(1)}, f32[256,256]{1,0:T(8,128)S(1)}, u32[]{:S(2)}, u32[]{:S(2)}) collective-permute-start(f32[256,256]{1,0:T(8,128)S(1)} %collective-permute-done.19.rest_2_), channel_id=1, source_target_pairs={{0,1},{1,0},{2,3},{3,2},{4,5},{5,4},{6,7},{7,6},{8,9},{9,8},{10,11... | collective-permute-start | bytes 786440 | tf_op jit(solution)/shard_map/ppermute | solution.py:376
  133.1 9.1 %collective-permute-start.24 = (f32[256,256]{1,0:T(8,128)S(1)}, f32[256,256]{1,0:T(8,128)S(1)}, u32[]{:S(2)}, u32[]{:S(2)}) collective-permute-start(f32[256,256]{1,0:T(8,128)S(1)} %collective-permute-done.21.rest_3_), channel_id=1, source_target_pairs={{0,1},{1,0},{2,3},{3,2},{4,5},{5,4},{6,7},{7,6},{8,9},{9,8},{10,11... | collective-permute-start | bytes 786440 | tf_op jit(solution)/shard_map/ppermute | solution.py:376
  (1 other events, 1.8 us)

commit v11 on v10

--- a/solution.py
+++ b/solution.py
@@ -289,21 +289,28 @@
 
 
 def final_kernel(
-    rows, kernel_ref, summed, own, author_summed, class_target, seed_class, train_mask, out, scores
+    rows, kernel_ref, summed, own, author_summed, class_target, seed_class, train_mask,
+    out, scores, out_made, scores_made, left,
 ):
     classes = out.shape[1]
     scaled = own[...] * col_scale(author_summed, class_target)
-    scores[...] = scaled * (classes / jnp.sum(scaled, axis=1, keepdims=True))
+    scores_made[...] = scaled * (classes / jnp.sum(scaled, axis=1, keepdims=True))
+    copies = [pltpu.make_async_copy(scores_made, scores, left.at[0])]
+    copies[0].start()
     scale_cols = col_scale(summed, class_target)
     eye = identity(rows)
     lane = lax.broadcasted_iota(jnp.int32, (rows, classes), 1).astype(jnp.float32)
     for paper, line in enumerate(code_lines(seed_class, train_mask, rows)):
-        part = slice(paper * rows, (paper + 1) * rows)
+        part = pl.ds(paper * rows, rows)
         scaled = kernel_ref[part, :] * scale_cols
         share = scaled * (1.0 / jnp.sum(scaled, axis=1, keepdims=True))
         code = across(code_column(line, eye), classes)
         updated = keep_share * share + jnp.where(code == lane, 1.0 - keep_share, 0.0)
-        out[part, :] = classes * updated
+        out_made[part, :] = classes * updated
+        copies.append(pltpu.make_async_copy(out_made.at[part], out.at[part], left.at[paper + 1]))
+        copies[-1].start()
+    for copy in copies:
+        copy.wait()
 
 
 def in_hbm(value):
@@ -311,7 +318,12 @@
 
 
 def exchange(parts):
-    return lax.all_to_all(parts, AXES, split_axis=0, concat_axis=0, tiled=True)
+    groups, blocks = lax.axis_size("grp"), lax.axis_size("blk")
+    planes = [i // 2 if i % 2 == 0 else groups - 1 - i // 2 for i in range(groups)]
+    order = [plane * blocks + i for plane in planes for i in range(blocks)]
+    return lax.all_to_all(
+        parts, AXES, split_axis=0, concat_axis=0, axis_index_groups=[order], tiled=True
+    )
 
 
 def on_device(
@@ -436,6 +448,12 @@
         functools.partial(final_kernel, rows),
         (shape((papers, classes), f32), shape((authors, classes), f32)),
         [VMEM] * 7,
+        [
+            pltpu.VMEM((papers, classes), f32),
+            pltpu.VMEM((authors, classes), f32),
+            pltpu.SemaphoreType.DMA((1 + papers // rows,)),
+        ],
+        (HBM, HBM),
     )(kernel, summed, own, author_summed, target, seed_class, train_mask)
 
 

time: 182 us -> 182 us (level)
  no operation moved by 1% of the time
where the time goes in v11:
time: 182 us; the launch traced here: 181 us
  blocking collectives  154 us (85%)
  Pallas kernels  13.5 us (7%)
  starting transfers between devices  12.7 us (7%)
    all_to_all x16, blocking collectives, exchange(): lax.all_to_all(parts, AXES, split_axis=0, concat_axis=0, axis_index_group...  154 us
    ppermute x9, starting transfers between devices, across_pairs(): return lax.ppermute(value, 'blk', [(i, i ^ 2 * k) for i in range(blocks)])  5.74 us
    ppermute x3, starting transfers between devices, on_device(): lax.ppermute(one, 'blk', [(i, i ^ 2 * k) for i in range(blocks)])  4.47 us
  transfers between devices with their start and end apart: 25, of which 0 were waited for; matrix products, arithmetic and copies ran while one was open for 0% of the time, Pallas kernels for 1%

profile of v11, /device:TPU:0, one launch (start us, length us, event | category | flops | bytes accessed | tf_op | source)
XLA Modules:
  0.0 181.5 jit_solution(17460075434319289871)
XLA Ops:
  1.3 2.2 %shard_map.95 = (s32[8]{0:T(128)S(1)}, s32[8]{0:T(128)S(1)}, s32[5,128]{1,0:T(8,128)S(1)}, s32[5,128]{1,0:T(8,128)S(1)}, f32[1,256]{1,0:T(1,128)S(1)}, /*index=5...) custom-call(s32[1]{0:T(128)S(6)} %copy.10.tile_count, ...), custom_call_target="tpu_custom_call" | custom-call | tf_op jit(solution)/shard_map/pallas_call | solution.py:360
  4.0 1.2 shard_map.96
  5.3 2.9 %collective-permute-start.1 = (bf16[2,336,128]{2,1,0:T(8,128)(2,1)S(1)}, bf16[2,336,128]{2,1,0:T(8,128)(2,1)S(1)}, u32[]{:S(2)}, u32[]{:S(2)}) collective-permute-start(bf16[2,336,128]{2,1,0:T(8,128)(2,1)S(1)} %get-tuple-element.112), channel_id=1, source_target_pairs={{0,2},{1,3},{2,0},{3,1},{4,6},{5,7},{6,4},{7,5},{8,10},{9,11},{10,... | collective-permute-start | bytes 516104 | tf_op jit(solution)/shard_map/ppermute | solution.py:376
  8.2 1.5 collective-permute-start.2
  9.8 13.4 %all_to_all.80.summed = f32[32,1,256]{2,1,0:T(1,128)S(1)} all-to-all(f32[32,1,256]{2,1,0:T(1,128)S(1)} %shard_map.96), channel_id=1, replica_groups={{0,1,2,3,4,5,6,7,24,25,26,27,28,29,30,31,8,9,10,11,12,13,14,15,16,17,18..., dimensions={0} | all-to-all | bytes 65536 | tf_op jit(solution)/shard_map/all_to_all | solution.py:324
  25.2 9.8 %all_to_all.81.summed = f32[32,1,256]{2,1,0:T(1,128)S(1)} all-to-all(f32[32,1,256]{2,1,0:T(1,128)S(1)} %get-tuple-element.116), channel_id=1, replica_groups={{0,1,2,3,4,5,6,7,24,25,26,27,28,29,30,31,8,9,10,11,12,13,14,15,16,17,18..., dimensions={0} | all-to-all | bytes 65536 | tf_op jit(solution)/shard_map/all_to_all | solution.py:324
  35.9 9.9 %all_to_all.82.summed = f32[32,1,256]{2,1,0:T(1,128)S(1)} all-to-all(f32[32,1,256]{2,1,0:T(1,128)S(1)} %shard_map.99), channel_id=1, replica_groups={{0,1,2,3,4,5,6,7,24,25,26,27,28,29,30,31,8,9,10,11,12,13,14,15,16,17,18..., dimensions={0} | all-to-all | bytes 65536 | tf_op jit(solution)/shard_map/all_to_all | solution.py:324
  46.7 9.0 %all_to_all.83.summed = f32[32,1,256]{2,1,0:T(1,128)S(1)} all-to-all(f32[32,1,256]{2,1,0:T(1,128)S(1)} %shard_map.100), channel_id=1, replica_groups={{0,1,2,3,4,5,6,7,24,25,26,27,28,29,30,31,8,9,10,11,12,13,14,15,16,17,18..., dimensions={0} | all-to-all | bytes 65536 | tf_op jit(solution)/shard_map/all_to_all | solution.py:324
  55.7 1.5 shard_map.101
  58.3 9.8 %all_to_all.84.summed = f32[32,1,256]{2,1,0:T(1,128)S(1)} all-to-all(f32[32,1,256]{2,1,0:T(1,128)S(1)} %get-tuple-element.138), channel_id=1, replica_groups={{0,1,2,3,4,5,6,7,24,25,26,27,28,29,30,31,8,9,10,11,12,13,14,15,16,17,18..., dimensions={0} | all-to-all | bytes 65536 | tf_op jit(solution)/shard_map/all_to_all | solution.py:324
  69.3 9.9 %all_to_all.85.summed = f32[32,1,256]{2,1,0:T(1,128)S(1)} all-to-all(f32[32,1,256]{2,1,0:T(1,128)S(1)} %shard_map.102), channel_id=1, replica_groups={{0,1,2,3,4,5,6,7,24,25,26,27,28,29,30,31,8,9,10,11,12,13,14,15,16,17,18..., dimensions={0} | all-to-all | bytes 65536 | tf_op jit(solution)/shard_map/all_to_all | solution.py:324
  80.1 9.0 %all_to_all.86.summed = f32[32,1,256]{2,1,0:T(1,128)S(1)} all-to-all(f32[32,1,256]{2,1,0:T(1,128)S(1)} %shard_map.103), channel_id=1, replica_groups={{0,1,2,3,4,5,6,7,24,25,26,27,28,29,30,31,8,9,10,11,12,13,14,15,16,17,18..., dimensions={0} | all-to-all | bytes 65536 | tf_op jit(solution)/shard_map/all_to_all | solution.py:324
  89.4 9.0 %all_to_all.87.summed = f32[32,1,256]{2,1,0:T(1,128)S(1)} all-to-all(f32[32,1,256]{2,1,0:T(1,128)S(1)} %shard_map.104), channel_id=1, replica_groups={{0,1,2,3,4,5,6,7,24,25,26,27,28,29,30,31,8,9,10,11,12,13,14,15,16,17,18..., dimensions={0} | all-to-all | bytes 65536 | tf_op jit(solution)/shard_map/all_to_all | solution.py:324
  98.4 2.9 %shard_map.105 = (f32[256,256]{1,0:T(8,128)S(1)}, f32[32,1,256]{2,1,0:T(1,128)S(1)}) custom-call(f32[32,1,256]{2,1,0:T(1,128)S(1)} %all_to_all.87.summed, f32[1,256]{1,0:T(1,128)S(1)} %get-tuple-element.104.class_prior, f32[1,256]{1,0:T(1,128)S(1)} %get-tuple-element.111.class_target, bf16[640,256]{1,0:T(8,128)(2,1)S(1)} %get-tuple-element.159.rest_0_, ...), custom_call_target="tpu_custom_call" | custom-call | tf_op jit(solution)/shard_map/pallas_call | solution.py:428
  102.5 9.8 %all_to_all.88.summed = f32[32,1,256]{2,1,0:T(1,128)S(1)} all-to-all(f32[32,1,256]{2,1,0:T(1,128)S(1)} %get-tuple-element.167), channel_id=1, replica_groups={{0,1,2,3,4,5,6,7,24,25,26,27,28,29,30,31,8,9,10,11,12,13,14,15,16,17,18..., dimensions={0} | all-to-all | bytes 65536 | tf_op jit(solution)/shard_map/all_to_all | solution.py:324
  113.1 9.9 %all_to_all.89.summed = f32[32,1,256]{2,1,0:T(1,128)S(1)} all-to-all(f32[32,1,256]{2,1,0:T(1,128)S(1)} %shard_map.106), channel_id=1, replica_groups={{0,1,2,3,4,5,6,7,24,25,26,27,28,29,30,31,8,9,10,11,12,13,14,15,16,17,18..., dimensions={0} | all-to-all | bytes 65536 | tf_op jit(solution)/shard_map/all_to_all | solution.py:324
  123.8 9.0 %all_to_all.90.summed = f32[32,1,256]{2,1,0:T(1,128)S(1)} all-to-all(f32[32,1,256]{2,1,0:T(1,128)S(1)} %shard_map.107), channel_id=1, replica_groups={{0,1,2,3,4,5,6,7,24,25,26,27,28,29,30,31,8,9,10,11,12,13,14,15,16,17,18..., dimensions={0} | all-to-all | bytes 65536 | tf_op jit(solution)/shard_map/all_to_all | solution.py:324
  133.1 9.0 %all_to_all.91.summed.author_summed = f32[32,1,256]{2,1,0:T(1,128)S(1)} all-to-all(f32[32,1,256]{2,1,0:T(1,128)S(1)} %shard_map.108), channel_id=1, replica_groups={{0,1,2,3,4,5,6,7,24,25,26,27,28,29,30,31,8,9,10,11,12,13,14,15,16,17,18..., dimensions={0} | all-to-all | bytes 65536 | tf_op jit(solution)/shard_map/all_to_all | solution.py:324
  142.1 1.5 shard_map.109
  143.6 9.0 %all_to_all.92.summed = f32[32,1,256]{2,1,0:T(1,128)S(1)} all-to-all(f32[32,1,256]{2,1,0:T(1,128)S(1)} %get-tuple-element.195), channel_id=1, replica_groups={{0,1,2,3,4,5,6,7,24,25,26,27,28,29,30,31,8,9,10,11,12,13,14,15,16,17,18..., dimensions={0} | all-to-all | bytes 65536 | tf_op jit(solution)/shard_map/all_to_all | solution.py:324
  152.8 9.0 %all_to_all.93.summed = f32[32,1,256]{2,1,0:T(1,128)S(1)} all-to-all(f32[32,1,256]{2,1,0:T(1,128)S(1)} %shard_map.110), channel_id=1, replica_groups={{0,1,2,3,4,5,6,7,24,25,26,27,28,29,30,31,8,9,10,11,12,13,14,15,16,17,18..., dimensions={0} | all-to-all | bytes 65536 | tf_op jit(solution)/shard_map/all_to_all | solution.py:324
  162.1 9.0 %all_to_all.94.summed = f32[32,1,256]{2,1,0:T(1,128)S(1)} all-to-all(f32[32,1,256]{2,1,0:T(1,128)S(1)} %shard_map.111), channel_id=1, replica_groups={{0,1,2,3,4,5,6,7,24,25,26,27,28,29,30,31,8,9,10,11,12,13,14,15,16,17,18..., dimensions={0} | all-to-all | bytes 65536 | tf_op jit(solution)/shard_map/all_to_all | solution.py:324
  171.3 9.0 %all_to_all.95.summed = f32[32,1,256]{2,1,0:T(1,128)S(1)} all-to-all(f32[32,1,256]{2,1,0:T(1,128)S(1)} %shard_map.112), channel_id=1, replica_groups={{0,1,2,3,4,5,6,7,24,25,26,27,28,29,30,31,8,9,10,11,12,13,14,15,16,17,18..., dimensions={0} | all-to-all | bytes 65536 | tf_op jit(solution)/shard_map/all_to_all | solution.py:324
  180.3 1.2 shard_map.113
  (61 shorter events, 11.5 us)
Async XLA Ops:
  5.3 17.9 %collective-permute-start.1 = (bf16[2,336,128]{2,1,0:T(8,128)(2,1)S(1)}, bf16[2,336,128]{2,1,0:T(8,128)(2,1)S(1)}, u32[]{:S(2)}, u32[]{:S(2)}) collective-permute-start(bf16[2,336,128]{2,1,0:T(8,128)(2,1)S(1)} %get-tuple-element.112), channel_id=1, source_target_pairs={{0,2},{1,3},{2,0},{3,1},{4,6},{5,7},{6,4},{7,5},{8,10},{9,11},{10,... | collective-permute-start | bytes 516104 | tf_op jit(solution)/shard_map/ppermute | solution.py:376
  8.2 15.0 %collective-permute-start.2 = (bf16[2,336,128]{2,1,0:T(8,128)(2,1)S(1)}, bf16[2,336,128]{2,1,0:T(8,128)(2,1)S(1)}, u32[]{:S(2)}, u32[]{:S(2)}) collective-permute-start(bf16[2,336,128]{2,1,0:T(8,128)(2,1)S(1)} %get-tuple-element.113), channel_id=1, source_target_pairs={{0,4},{1,5},{2,6},{3,7},{4,0},{5,1},{6,2},{7,3},{8,12},{9,13},{10,... | collective-permute-start | bytes 516104 | tf_op jit(solution)/shard_map/ppermute | solution.py:376
  9.8 13.4 %collective-permute-start.3 = (bf16[2,336,128]{2,1,0:T(8,128)(2,1)S(1)}, bf16[2,336,128]{2,1,0:T(8,128)(2,1)S(1)}, u32[]{:S(2)}, u32[]{:S(2)}) collective-permute-start(bf16[2,336,128]{2,1,0:T(8,128)(2,1)S(1)} %get-tuple-element.114), channel_id=1, source_target_pairs={{0,6},{1,7},{2,4},{3,5},{4,2},{5,3},{6,0},{7,1},{8,14},{9,15},{10,... | collective-permute-start | bytes 516104 | tf_op jit(solution)/shard_map/ppermute | solution.py:376
  24.0 11.0 %collective-permute-start.5 = (f32[256,256]{1,0:T(8,128)S(1)}, f32[256,256]{1,0:T(8,128)S(1)}, u32[]{:S(2)}, u32[]{:S(2)}) collective-permute-start(f32[256,256]{1,0:T(8,128)S(1)} %get-tuple-element.132.kernel_ref.rest_0_), channel_id=1, source_target_pairs={{0,4},{1,5},{2,6},{3,7},{4,0},{5,1},{6,2},{7,3},{8,12},{9,13},{10,... | collective-permute-start | bytes 786440 | tf_op jit(solution)/shard_map/ppermute | solution.py:385
  24.6 10.4 %collective-permute-start.4 = (f32[256,256]{1,0:T(8,128)S(1)}, f32[256,256]{1,0:T(8,128)S(1)}, u32[]{:S(2)}, u32[]{:S(2)}) collective-permute-start(f32[256,256]{1,0:T(8,128)S(1)} %get-tuple-element.132.kernel_ref.rest_0_), channel_id=1, source_target_pairs={{0,2},{1,3},{2,0},{3,1},{4,6},{5,7},{6,4},{7,5},{8,10},{9,11},{10,... | collective-permute-start | bytes 786440 | tf_op jit(solution)/shard_map/ppermute | solution.py:385
  35.2 10.6 %collective-permute-start.7 = (f32[256,256]{1,0:T(8,128)S(1)}, f32[256,256]{1,0:T(8,128)S(1)}, u32[]{:S(2)}, u32[]{:S(2)}) collective-permute-start(f32[256,256]{1,0:T(8,128)S(1)} %get-tuple-element.132.kernel_ref.rest_0_), channel_id=1, source_target_pairs={{0,6},{1,7},{2,4},{3,5},{4,2},{5,3},{6,0},{7,1},{8,14},{9,15},{10,... | collective-permute-start | bytes 786440 | tf_op jit(solution)/shard_map/ppermute | solution.py:385
  35.9 10.0 %collective-permute-start.6 = (f32[256,256]{1,0:T(8,128)S(1)}, f32[256,256]{1,0:T(8,128)S(1)}, u32[]{:S(2)}, u32[]{:S(2)}) collective-permute-start(f32[256,256]{1,0:T(8,128)S(1)} %get-tuple-element.132.kernel_ref.rest_0_), channel_id=1, source_target_pairs={{0,1},{1,0},{2,3},{3,2},{4,5},{5,4},{6,7},{7,6},{8,9},{9,8},{10,11... | collective-permute-start | bytes 786440 | tf_op jit(solution)/shard_map/ppermute | solution.py:388
  46.0 9.6 %collective-permute-start.8 = (f32[256,256]{1,0:T(8,128)S(1)}, f32[256,256]{1,0:T(8,128)S(1)}, u32[]{:S(2)}, u32[]{:S(2)}) collective-permute-start(f32[256,256]{1,0:T(8,128)S(1)} %collective-permute-done.4.rest_1_), channel_id=1, source_target_pairs={{0,1},{1,0},{2,3},{3,2},{4,5},{5,4},{6,7},{7,6},{8,9},{9,8},{10,11... | collective-permute-start | bytes 786440 | tf_op jit(solution)/shard_map/ppermute | solution.py:388
  46.1 9.6 %collective-permute-start.9 = (f32[256,256]{1,0:T(8,128)S(1)}, f32[256,256]{1,0:T(8,128)S(1)}, u32[]{:S(2)}, u32[]{:S(2)}) collective-permute-start(f32[256,256]{1,0:T(8,128)S(1)} %collective-permute-done.5.rest_2_), channel_id=1, source_target_pairs={{0,1},{1,0},{2,3},{3,2},{4,5},{5,4},{6,7},{7,6},{8,9},{9,8},{10,11... | collective-permute-start | bytes 786440 | tf_op jit(solution)/shard_map/ppermute | solution.py:388
  46.6 9.1 %collective-permute-start.10 = (f32[256,256]{1,0:T(8,128)S(1)}, f32[256,256]{1,0:T(8,128)S(1)}, u32[]{:S(2)}, u32[]{:S(2)}) collective-permute-start(f32[256,256]{1,0:T(8,128)S(1)} %collective-permute-done.7.rest_3_), channel_id=1, source_target_pairs={{0,1},{1,0},{2,3},{3,2},{4,5},{5,4},{6,7},{7,6},{8,9},{9,8},{10,11... | collective-permute-start | bytes 786440 | tf_op jit(solution)/shard_map/ppermute | solution.py:388
  57.2 11.0 %collective-permute-start.12 = (bf16[640,256]{1,0:T(8,128)(2,1)S(1)}, bf16[640,256]{1,0:T(8,128)(2,1)S(1)}, u32[]{:S(2)}, u32[]{:S(2)}) collective-permute-start(bf16[640,256]{1,0:T(8,128)(2,1)S(1)} %get-tuple-element.159.rest_0_), channel_id=1, source_target_pairs={{0,4},{1,5},{2,6},{3,7},{4,0},{5,1},{6,2},{7,3},{8,12},{9,13},{10,... | collective-permute-start | bytes 983048 | tf_op jit(solution)/shard_map/ppermute | solution.py:385
  57.8 10.4 %collective-permute-start.11 = (bf16[640,256]{1,0:T(8,128)(2,1)S(1)}, bf16[640,256]{1,0:T(8,128)(2,1)S(1)}, u32[]{:S(2)}, u32[]{:S(2)}) collective-permute-start(bf16[640,256]{1,0:T(8,128)(2,1)S(1)} %get-tuple-element.159.rest_0_), channel_id=1, source_target_pairs={{0,2},{1,3},{2,0},{3,1},{4,6},{5,7},{6,4},{7,5},{8,10},{9,11},{10,... | collective-permute-start | bytes 983048 | tf_op jit(solution)/shard_map/ppermute | solution.py:385
  68.4 10.8 %collective-permute-start.14 = (bf16[640,256]{1,0:T(8,128)(2,1)S(1)}, bf16[640,256]{1,0:T(8,128)(2,1)S(1)}, u32[]{:S(2)}, u32[]{:S(2)}) collective-permute-start(bf16[640,256]{1,0:T(8,128)(2,1)S(1)} %get-tuple-element.159.rest_0_), channel_id=1, source_target_pairs={{0,6},{1,7},{2,4},{3,5},{4,2},{5,3},{6,0},{7,1},{8,14},{9,15},{10,... | collective-permute-start | bytes 983048 | tf_op jit(solution)/shard_map/ppermute | solution.py:385
  69.3 10.0 %collective-permute-start.13 = (bf16[640,256]{1,0:T(8,128)(2,1)S(1)}, bf16[640,256]{1,0:T(8,128)(2,1)S(1)}, u32[]{:S(2)}, u32[]{:S(2)}) collective-permute-start(bf16[640,256]{1,0:T(8,128)(2,1)S(1)} %get-tuple-element.159.rest_0_), channel_id=1, source_target_pairs={{0,1},{1,0},{2,3},{3,2},{4,5},{5,4},{6,7},{7,6},{8,9},{9,8},{10,11... | collective-permute-start | bytes 983048 | tf_op jit(solution)/shard_map/ppermute | solution.py:388
  79.5 9.6 %collective-permute-start.15 = (bf16[640,256]{1,0:T(8,128)(2,1)S(1)}, bf16[640,256]{1,0:T(8,128)(2,1)S(1)}, u32[]{:S(2)}, u32[]{:S(2)}) collective-permute-start(bf16[640,256]{1,0:T(8,128)(2,1)S(1)} %collective-permute-done.11.rest_1_), channel_id=1, source_target_pairs={{0,1},{1,0},{2,3},{3,2},{4,5},{5,4},{6,7},{7,6},{8,9},{9,8},{10,11... | collective-permute-start | bytes 983048 | tf_op jit(solution)/shard_map/ppermute | solution.py:388
  79.6 9.5 %collective-permute-start.16 = (bf16[640,256]{1,0:T(8,128)(2,1)S(1)}, bf16[640,256]{1,0:T(8,128)(2,1)S(1)}, u32[]{:S(2)}, u32[]{:S(2)}) collective-permute-start(bf16[640,256]{1,0:T(8,128)(2,1)S(1)} %collective-permute-done.12.rest_2_), channel_id=1, source_target_pairs={{0,1},{1,0},{2,3},{3,2},{4,5},{5,4},{6,7},{7,6},{8,9},{9,8},{10,11... | collective-permute-start | bytes 983048 | tf_op jit(solution)/shard_map/ppermute | solution.py:388
  89.3 9.1 %collective-permute-start.17 = (bf16[640,256]{1,0:T(8,128)(2,1)S(1)}, bf16[640,256]{1,0:T(8,128)(2,1)S(1)}, u32[]{:S(2)}, u32[]{:S(2)}) collective-permute-start(bf16[640,256]{1,0:T(8,128)(2,1)S(1)} %collective-permute-done.14.rest_3_), channel_id=1, source_target_pairs={{0,1},{1,0},{2,3},{3,2},{4,5},{5,4},{6,7},{7,6},{8,9},{9,8},{10,11... | collective-permute-start | bytes 983048 | tf_op jit(solution)/shard_map/ppermute | solution.py:388
  101.3 11.0 %collective-permute-start.19 = (f32[256,256]{1,0:T(8,128)S(1)}, f32[256,256]{1,0:T(8,128)S(1)}, u32[]{:S(2)}, u32[]{:S(2)}) collective-permute-start(f32[256,256]{1,0:T(8,128)S(1)} %get-tuple-element.187.kernel_ref.rest_0_.own), channel_id=1, source_target_pairs={{0,4},{1,5},{2,6},{3,7},{4,0},{5,1},{6,2},{7,3},{8,12},{9,13},{10,... | collective-permute-start | bytes 786440 | tf_op jit(solution)/shard_map/ppermute | solution.py:385
  101.9 10.4 %collective-permute-start.18 = (f32[256,256]{1,0:T(8,128)S(1)}, f32[256,256]{1,0:T(8,128)S(1)}, u32[]{:S(2)}, u32[]{:S(2)}) collective-permute-start(f32[256,256]{1,0:T(8,128)S(1)} %get-tuple-element.187.kernel_ref.rest_0_.own), channel_id=1, source_target_pairs={{0,2},{1,3},{2,0},{3,1},{4,6},{5,7},{6,4},{7,5},{8,10},{9,11},{10,... | collective-permute-start | bytes 786440 | tf_op jit(solution)/shard_map/ppermute | solution.py:385
  112.5 10.6 %collective-permute-start.21 = (f32[256,256]{1,0:T(8,128)S(1)}, f32[256,256]{1,0:T(8,128)S(1)}, u32[]{:S(2)}, u32[]{:S(2)}) collective-permute-start(f32[256,256]{1,0:T(8,128)S(1)} %get-tuple-element.187.kernel_ref.rest_0_.own), channel_id=1, source_target_pairs={{0,6},{1,7},{2,4},{3,5},{4,2},{5,3},{6,0},{7,1},{8,14},{9,15},{10,... | collective-permute-start | bytes 786440 | tf_op jit(solution)/shard_map/ppermute | solution.py:385
  113.1 10.0 %collective-permute-start.20 = (f32[256,256]{1,0:T(8,128)S(1)}, f32[256,256]{1,0:T(8,128)S(1)}, u32[]{:S(2)}, u32[]{:S(2)}) collective-permute-start(f32[256,256]{1,0:T(8,128)S(1)} %get-tuple-element.187.kernel_ref.rest_0_.own), channel_id=1, source_target_pairs={{0,1},{1,0},{2,3},{3,2},{4,5},{5,4},{6,7},{7,6},{8,9},{9,8},{10,11... | collective-permute-start | bytes 786440 | tf_op jit(solution)/shard_map/ppermute | solution.py:388
  123.3 9.6 %collective-permute-start.22 = (f32[256,256]{1,0:T(8,128)S(1)}, f32[256,256]{1,0:T(8,128)S(1)}, u32[]{:S(2)}, u32[]{:S(2)}) collective-permute-start(f32[256,256]{1,0:T(8,128)S(1)} %collective-permute-done.18.rest_1_), channel_id=1, source_target_pairs={{0,1},{1,0},{2,3},{3,2},{4,5},{5,4},{6,7},{7,6},{8,9},{9,8},{10,11... | collective-permute-start | bytes 786440 | tf_op jit(solution)/shard_map/ppermute | solution.py:388
  123.4 9.5 %collective-permute-start.23 = (f32[256,256]{1,0:T(8,128)S(1)}, f32[256,256]{1,0:T(8,128)S(1)}, u32[]{:S(2)}, u32[]{:S(2)}) collective-permute-start(f32[256,256]{1,0:T(8,128)S(1)} %collective-permute-done.19.rest_2_), channel_id=1, source_target_pairs={{0,1},{1,0},{2,3},{3,2},{4,5},{5,4},{6,7},{7,6},{8,9},{9,8},{10,11... | collective-permute-start | bytes 786440 | tf_op jit(solution)/shard_map/ppermute | solution.py:388
  133.0 9.1 %collective-permute-start.24 = (f32[256,256]{1,0:T(8,128)S(1)}, f32[256,256]{1,0:T(8,128)S(1)}, u32[]{:S(2)}, u32[]{:S(2)}) collective-permute-start(f32[256,256]{1,0:T(8,128)S(1)} %collective-permute-done.21.rest_3_), channel_id=1, source_target_pairs={{0,1},{1,0},{2,3},{3,2},{4,5},{5,4},{6,7},{7,6},{8,9},{9,8},{10,11... | collective-permute-start | bytes 786440 | tf_op jit(solution)/shard_map/ppermute | solution.py:388
  (1 other events, 1.8 us)

commit v12 on v11

--- a/solution.py
+++ b/solution.py
@@ -87,15 +87,12 @@
     return jnp.concatenate([meta[i : i + 1] for i in range(count)], axis=1)[:, :rows]
 
 
-def code_column(line, eye):
-    wide = jnp.broadcast_to(line, (LANES, line.shape[1])).astype(jnp.bfloat16)
-    return dot_rows(eye, wide)
-
-
-def identity(rows):
-    line = lax.broadcasted_iota(jnp.int32, (rows, rows), 0)
-    lane = lax.broadcasted_iota(jnp.int32, (rows, rows), 1)
-    return jnp.where(line == lane, 1.0, 0.0).astype(jnp.bfloat16)
+def code_columns(lines):
+    rows = lines[0].shape[1]
+    wide = jnp.concatenate(lines, axis=0)
+    wide = jnp.pad(wide, ((0, -len(lines) % 8), (0, -rows % LANES)))
+    columns = wide.T
+    return [columns[:rows, i : i + 1] for i in range(len(lines))]
 
 
 def seeds_of(line, classes):
@@ -116,7 +113,7 @@
         pltpu.make_async_copy(source, place, ready.at[i])
         for i, (source, place) in enumerate(zip(ins, places))
     ]
-    for copy in moves:
+    for copy in moves[:-1]:
         copy.start()
     outs = []
     copies = []
@@ -129,6 +126,7 @@
             copy.start()
             copies.append(copy)
             outs.append((out, k, slot))
+    moves[-1].start()
     for copy in moves[:4]:
         copy.wait()
     line = lax.broadcasted_iota(jnp.int32, (META, LANES), 0)
@@ -225,15 +223,14 @@
     papers = [jnp.max(meta[at : at + 1]).astype(jnp.int32) for meta in metas]
     scale_cols = col_scale(summed, class_target)
     block = scale_block(scale_cols)
-    eye = identity(rows)
-    codes = [code_column(meta_line(meta, rows), eye) for meta in metas]
+    codes = code_columns([meta_line(meta, rows) for meta in metas])
     totals = [jnp.zeros((LANES, classes), jnp.float32) for _ in range(AT_DEV)]
     lane = lax.broadcasted_iota(jnp.int32, (rows, classes), 1).astype(jnp.float32)
     for shift, (ref, place) in enumerate(held):
         half = kernels[shift][pl.ds(pl.multiple_of(papers[shift] * rows, rows), rows), :]
         scale_rows = across(keep_share / row_sums(half, block), classes)
         share = half.astype(jnp.float32) * scale_cols * scale_rows
-        labels = share + jnp.where(across(codes[shift], classes) == lane, 1.0 - keep_share, 0.0)
+        labels = share + jnp.where(codes[shift] == lane, 1.0 - keep_share, 0.0)
         parcel = lax.dot_general(
             ref[place, :rows, :],
             labels.astype(jnp.bfloat16),
@@ -259,16 +256,17 @@
     block = scale_block(scale_cols)
     slots = sources(blocks)
     wide = jnp.concatenate([tiles[slot] for slot in slots], axis=1)
-    labels = []
+    chosen = []
     for ref, slot in zip(kernels, slots):
         start = pl.multiple_of(tile_author[slot] * columns, columns)
-        kernel = ref[pl.ds(start, columns), :]
-        high, low = split(kernel)
-        sums = row_sums(high, block) + jnp.dot(
-            low, block[:, :LANES], preferred_element_type=jnp.float32
-        )
-        share = kernel * scale_cols * across(1.0 / sums, classes)
-        labels.append(share.astype(jnp.bfloat16))
+        chosen.append(ref[pl.ds(start, columns), :])
+    kernel = jnp.concatenate(chosen, axis=0)
+    high, low = split(kernel)
+    sums = row_sums(high, block) + jnp.dot(
+        low, block[:, :LANES], preferred_element_type=jnp.float32
+    )
+    share = (kernel * scale_cols * across(1.0 / sums, classes)).astype(jnp.bfloat16)
+    labels = [share[i * columns : (i + 1) * columns] for i in range(blocks)]
     column = jnp.zeros((1, classes), jnp.float32)
     for paper in range(full.shape[0] // rows):
         chosen = []
@@ -298,13 +296,12 @@
     copies = [pltpu.make_async_copy(scores_made, scores, left.at[0])]
     copies[0].start()
     scale_cols = col_scale(summed, class_target)
-    eye = identity(rows)
+    codes = code_columns(code_lines(seed_class, train_mask, rows))
     lane = lax.broadcasted_iota(jnp.int32, (rows, classes), 1).astype(jnp.float32)
-    for paper, line in enumerate(code_lines(seed_class, train_mask, rows)):
+    for paper, code in enumerate(codes):
         part = pl.ds(paper * rows, rows)
         scaled = kernel_ref[part, :] * scale_cols
         share = scaled * (1.0 / jnp.sum(scaled, axis=1, keepdims=True))
-        code = across(code_column(line, eye), classes)
         updated = keep_share * share + jnp.where(code == lane, 1.0 - keep_share, 0.0)
         out_made[part, :] = classes * updated
         copies.append(pltpu.make_async_copy(out_made.at[part], out.at[part], left.at[paper + 1]))
@@ -318,12 +315,7 @@
 
 
 def exchange(parts):
-    groups, blocks = lax.axis_size("grp"), lax.axis_size("blk")
-    planes = [i // 2 if i % 2 == 0 else groups - 1 - i // 2 for i in range(groups)]
-    order = [plane * blocks + i for plane in planes for i in range(blocks)]
-    return lax.all_to_all(
-        parts, AXES, split_axis=0, concat_axis=0, axis_index_groups=[order], tiled=True
-    )
+    return lax.all_to_all(parts, AXES, split_axis=0, concat_axis=0, tiled=True)
 
 
 def on_device(
@@ -391,15 +383,14 @@
         here, there = {0: sent}, {}
         for step in range(count):
             if step == 0:
-                moves = [(here, k, across_pairs(sent, k)) for k in range(1, blocks // 2)][:2]
+                moves = [(here, k, across_pairs(sent, k)) for k in (1, 2) if k < blocks // 2]
             elif step == 1:
                 moves = [(there, 0, to_other(sent))]
-                moves += [(here, k, across_pairs(sent, k)) for k in range(3, blocks // 2)]
+                for k in range(3, blocks // 2):
+                    got = across_pairs(here[1], 2) if k == 3 else across_pairs(sent, k)
+                    moves.append((here, k, got))
             else:
-                ready = [k for k in here if k not in there]
-                if step + 1 < count:
-                    ready = ready[:2]
-                moves = [(there, k, to_other(here[k])) for k in ready]
+                moves = [(there, k, to_other(here[k])) for k in here if k not in there]
             summed = exchange(local)
             summed, *moved = lax.optimization_barrier((summed, *(one for _, _, one in moves)))
             for (place, k, _), one in zip(moves, moved):

time: 182 us -> 179 us (0.984)
  blocking collectives: 154 us -> 151 us
    all_to_all x16, blocking collectives: 154 us -> 151 us  [exchange(): return lax.all_to_all(parts, AXES, split_axis=0, concat_axis=0, tiled=True)]
where the time goes in v12:
time: 179 us
  blocking collectives  151 us (84%)
  Pallas kernels  13.4 us (7%)
  starting transfers between devices  13 us (7%)
    all_to_all x16, blocking collectives, exchange(): return lax.all_to_all(parts, AXES, split_axis=0, concat_axis=0, tiled=True)  151 us
    ppermute x9, starting transfers between devices, across_pairs(): return lax.ppermute(value, 'blk', [(i, i ^ 2 * k) for i in range(blocks)])  5.54 us
    ppermute x3, starting transfers between devices, on_device(): lax.ppermute(one, 'blk', [(i, i ^ 2 * k) for i in range(blocks)])  4.47 us
  transfers between devices with their start and end apart: 25, of which 0 were waited for; matrix products, arithmetic and copies ran while one was open for 0% of the time, Pallas kernels for 1%

profile of v12, /device:TPU:0, one launch (start us, length us, event | category | flops | bytes accessed | tf_op | source)
XLA Modules:
  0.0 179.0 jit_solution(9759553154471477558)
XLA Ops:
  1.3 2.2 %shard_map.95 = (s32[8]{0:T(128)S(1)}, s32[8]{0:T(128)S(1)}, s32[5,128]{1,0:T(8,128)S(1)}, s32[5,128]{1,0:T(8,128)S(1)}, f32[1,256]{1,0:T(1,128)S(1)}, /*index=5...) custom-call(s32[1]{0:T(128)S(6)} %copy.10.tile_count, ...), custom_call_target="tpu_custom_call" | custom-call | tf_op jit(solution)/shard_map/pallas_call | solution.py:352
  4.0 1.2 shard_map.96
  5.3 2.9 %collective-permute-start.1 = (bf16[2,336,128]{2,1,0:T(8,128)(2,1)S(1)}, bf16[2,336,128]{2,1,0:T(8,128)(2,1)S(1)}, u32[]{:S(2)}, u32[]{:S(2)}) collective-permute-start(bf16[2,336,128]{2,1,0:T(8,128)(2,1)S(1)} %get-tuple-element.110), channel_id=1, source_target_pairs={{0,2},{1,3},{2,0},{3,1},{4,6},{5,7},{6,4},{7,5},{8,10},{9,11},{10,... | collective-permute-start | bytes 516104 | tf_op jit(solution)/shard_map/ppermute | solution.py:368
  8.3 1.5 collective-permute-start.2
  9.8 13.4 %all_to_all.80.summed = f32[32,1,256]{2,1,0:T(1,128)S(1)} all-to-all(f32[32,1,256]{2,1,0:T(1,128)S(1)} %shard_map.96), channel_id=1, replica_groups=mesh['grp'=4,'blk'=8] {'grp','blk'}, dimensions={0} | all-to-all | bytes 65536 | tf_op jit(solution)/shard_map/all_to_all | solution.py:318
  25.2 9.8 %all_to_all.81.summed = f32[32,1,256]{2,1,0:T(1,128)S(1)} all-to-all(f32[32,1,256]{2,1,0:T(1,128)S(1)} %get-tuple-element.114), channel_id=1, replica_groups=mesh['grp'=4,'blk'=8] {'grp','blk'}, dimensions={0} | all-to-all | bytes 65536 | tf_op jit(solution)/shard_map/all_to_all | solution.py:318
  35.9 8.9 %all_to_all.82.summed = f32[32,1,256]{2,1,0:T(1,128)S(1)} all-to-all(f32[32,1,256]{2,1,0:T(1,128)S(1)} %shard_map.99), channel_id=1, replica_groups=mesh['grp'=4,'blk'=8] {'grp','blk'}, dimensions={0} | all-to-all | bytes 65536 | tf_op jit(solution)/shard_map/all_to_all | solution.py:318
  45.7 8.9 %all_to_all.83.summed = f32[32,1,256]{2,1,0:T(1,128)S(1)} all-to-all(f32[32,1,256]{2,1,0:T(1,128)S(1)} %shard_map.100), channel_id=1, replica_groups=mesh['grp'=4,'blk'=8] {'grp','blk'}, dimensions={0} | all-to-all | bytes 65536 | tf_op jit(solution)/shard_map/all_to_all | solution.py:318
  54.7 1.5 shard_map.101
  57.5 10.1 %all_to_all.84.summed = f32[32,1,256]{2,1,0:T(1,128)S(1)} all-to-all(f32[32,1,256]{2,1,0:T(1,128)S(1)} %get-tuple-element.136), channel_id=1, replica_groups=mesh['grp'=4,'blk'=8] {'grp','blk'}, dimensions={0} | all-to-all | bytes 65536 | tf_op jit(solution)/shard_map/all_to_all | solution.py:318
  68.5 9.9 %all_to_all.85.summed = f32[32,1,256]{2,1,0:T(1,128)S(1)} all-to-all(f32[32,1,256]{2,1,0:T(1,128)S(1)} %shard_map.102), channel_id=1, replica_groups=mesh['grp'=4,'blk'=8] {'grp','blk'}, dimensions={0} | all-to-all | bytes 65536 | tf_op jit(solution)/shard_map/all_to_all | solution.py:318
  79.3 8.9 %all_to_all.86.summed = f32[32,1,256]{2,1,0:T(1,128)S(1)} all-to-all(f32[32,1,256]{2,1,0:T(1,128)S(1)} %shard_map.103), channel_id=1, replica_groups=mesh['grp'=4,'blk'=8] {'grp','blk'}, dimensions={0} | all-to-all | bytes 65536 | tf_op jit(solution)/shard_map/all_to_all | solution.py:318
  88.4 8.9 %all_to_all.87.summed = f32[32,1,256]{2,1,0:T(1,128)S(1)} all-to-all(f32[32,1,256]{2,1,0:T(1,128)S(1)} %shard_map.104), channel_id=1, replica_groups=mesh['grp'=4,'blk'=8] {'grp','blk'}, dimensions={0} | all-to-all | bytes 65536 | tf_op jit(solution)/shard_map/all_to_all | solution.py:318
  97.4 2.6 %shard_map.105 = (f32[256,256]{1,0:T(8,128)S(1)}, f32[32,1,256]{2,1,0:T(1,128)S(1)}) custom-call(f32[32,1,256]{2,1,0:T(1,128)S(1)} %all_to_all.87.summed, f32[1,256]{1,0:T(1,128)S(1)} %get-tuple-element.102.class_prior, f32[1,256]{1,0:T(1,128)S(1)} %get-tuple-element.109.class_target, bf16[640,256]{1,0:T(8,128)(2,1)S(1)} %get-tuple-element.155.rest_0_, ...), custom_call_target="tpu_custom_call" | custom-call | tf_op jit(solution)/shard_map/pallas_call | solution.py:419
  101.2 9.8 %all_to_all.88.summed = f32[32,1,256]{2,1,0:T(1,128)S(1)} all-to-all(f32[32,1,256]{2,1,0:T(1,128)S(1)} %get-tuple-element.164), channel_id=1, replica_groups=mesh['grp'=4,'blk'=8] {'grp','blk'}, dimensions={0} | all-to-all | bytes 65536 | tf_op jit(solution)/shard_map/all_to_all | solution.py:318
  111.9 8.9 %all_to_all.89.summed = f32[32,1,256]{2,1,0:T(1,128)S(1)} all-to-all(f32[32,1,256]{2,1,0:T(1,128)S(1)} %shard_map.106), channel_id=1, replica_groups=mesh['grp'=4,'blk'=8] {'grp','blk'}, dimensions={0} | all-to-all | bytes 65536 | tf_op jit(solution)/shard_map/all_to_all | solution.py:318
  121.7 8.9 %all_to_all.90.summed = f32[32,1,256]{2,1,0:T(1,128)S(1)} all-to-all(f32[32,1,256]{2,1,0:T(1,128)S(1)} %shard_map.107), channel_id=1, replica_groups=mesh['grp'=4,'blk'=8] {'grp','blk'}, dimensions={0} | all-to-all | bytes 65536 | tf_op jit(solution)/shard_map/all_to_all | solution.py:318
  130.8 8.9 %all_to_all.91.summed.author_summed = f32[32,1,256]{2,1,0:T(1,128)S(1)} all-to-all(f32[32,1,256]{2,1,0:T(1,128)S(1)} %shard_map.108), channel_id=1, replica_groups=mesh['grp'=4,'blk'=8] {'grp','blk'}, dimensions={0} | all-to-all | bytes 65536 | tf_op jit(solution)/shard_map/all_to_all | solution.py:318
  139.8 1.5 shard_map.109
  141.3 8.9 %all_to_all.92.summed = f32[32,1,256]{2,1,0:T(1,128)S(1)} all-to-all(f32[32,1,256]{2,1,0:T(1,128)S(1)} %get-tuple-element.191), channel_id=1, replica_groups=mesh['grp'=4,'blk'=8] {'grp','blk'}, dimensions={0} | all-to-all | bytes 65536 | tf_op jit(solution)/shard_map/all_to_all | solution.py:318
  150.5 8.9 %all_to_all.93.summed = f32[32,1,256]{2,1,0:T(1,128)S(1)} all-to-all(f32[32,1,256]{2,1,0:T(1,128)S(1)} %shard_map.110), channel_id=1, replica_groups=mesh['grp'=4,'blk'=8] {'grp','blk'}, dimensions={0} | all-to-all | bytes 65536 | tf_op jit(solution)/shard_map/all_to_all | solution.py:318
  159.6 8.9 %all_to_all.94.summed = f32[32,1,256]{2,1,0:T(1,128)S(1)} all-to-all(f32[32,1,256]{2,1,0:T(1,128)S(1)} %shard_map.111), channel_id=1, replica_groups=mesh['grp'=4,'blk'=8] {'grp','blk'}, dimensions={0} | all-to-all | bytes 65536 | tf_op jit(solution)/shard_map/all_to_all | solution.py:318
  168.8 8.9 %all_to_all.95.summed = f32[32,1,256]{2,1,0:T(1,128)S(1)} all-to-all(f32[32,1,256]{2,1,0:T(1,128)S(1)} %shard_map.112), channel_id=1, replica_groups=mesh['grp'=4,'blk'=8] {'grp','blk'}, dimensions={0} | all-to-all | bytes 65536 | tf_op jit(solution)/shard_map/all_to_all | solution.py:318
  177.8 1.3 shard_map.113
  (61 shorter events, 11.8 us)
Async XLA Ops:
  5.3 17.8 %collective-permute-start.1 = (bf16[2,336,128]{2,1,0:T(8,128)(2,1)S(1)}, bf16[2,336,128]{2,1,0:T(8,128)(2,1)S(1)}, u32[]{:S(2)}, u32[]{:S(2)}) collective-permute-start(bf16[2,336,128]{2,1,0:T(8,128)(2,1)S(1)} %get-tuple-element.110), channel_id=1, source_target_pairs={{0,2},{1,3},{2,0},{3,1},{4,6},{5,7},{6,4},{7,5},{8,10},{9,11},{10,... | collective-permute-start | bytes 516104 | tf_op jit(solution)/shard_map/ppermute | solution.py:368
  8.3 14.9 %collective-permute-start.2 = (bf16[2,336,128]{2,1,0:T(8,128)(2,1)S(1)}, bf16[2,336,128]{2,1,0:T(8,128)(2,1)S(1)}, u32[]{:S(2)}, u32[]{:S(2)}) collective-permute-start(bf16[2,336,128]{2,1,0:T(8,128)(2,1)S(1)} %get-tuple-element.111), channel_id=1, source_target_pairs={{0,4},{1,5},{2,6},{3,7},{4,0},{5,1},{6,2},{7,3},{8,12},{9,13},{10,... | collective-permute-start | bytes 516104 | tf_op jit(solution)/shard_map/ppermute | solution.py:368
  9.8 13.4 %collective-permute-start.3 = (bf16[2,336,128]{2,1,0:T(8,128)(2,1)S(1)}, bf16[2,336,128]{2,1,0:T(8,128)(2,1)S(1)}, u32[]{:S(2)}, u32[]{:S(2)}) collective-permute-start(bf16[2,336,128]{2,1,0:T(8,128)(2,1)S(1)} %get-tuple-element.112), channel_id=1, source_target_pairs={{0,6},{1,7},{2,4},{3,5},{4,2},{5,3},{6,0},{7,1},{8,14},{9,15},{10,... | collective-permute-start | bytes 516104 | tf_op jit(solution)/shard_map/ppermute | solution.py:368
  24.0 11.0 %collective-permute-start.5 = (f32[256,256]{1,0:T(8,128)S(1)}, f32[256,256]{1,0:T(8,128)S(1)}, u32[]{:S(2)}, u32[]{:S(2)}) collective-permute-start(f32[256,256]{1,0:T(8,128)S(1)} %get-tuple-element.130.kernel_ref.rest_0_), channel_id=1, source_target_pairs={{0,4},{1,5},{2,6},{3,7},{4,0},{5,1},{6,2},{7,3},{8,12},{9,13},{10,... | collective-permute-start | bytes 786440 | tf_op jit(solution)/shard_map/ppermute | solution.py:377
  24.6 10.4 %collective-permute-start.4 = (f32[256,256]{1,0:T(8,128)S(1)}, f32[256,256]{1,0:T(8,128)S(1)}, u32[]{:S(2)}, u32[]{:S(2)}) collective-permute-start(f32[256,256]{1,0:T(8,128)S(1)} %get-tuple-element.130.kernel_ref.rest_0_), channel_id=1, source_target_pairs={{0,2},{1,3},{2,0},{3,1},{4,6},{5,7},{6,4},{7,5},{8,10},{9,11},{10,... | collective-permute-start | bytes 786440 | tf_op jit(solution)/shard_map/ppermute | solution.py:377
  35.2 9.7 %collective-permute-start.6 = (f32[256,256]{1,0:T(8,128)S(1)}, f32[256,256]{1,0:T(8,128)S(1)}, u32[]{:S(2)}, u32[]{:S(2)}) collective-permute-start(f32[256,256]{1,0:T(8,128)S(1)} %get-tuple-element.130.kernel_ref.rest_0_), channel_id=1, source_target_pairs={{0,1},{1,0},{2,3},{3,2},{4,5},{5,4},{6,7},{7,6},{8,9},{9,8},{10,11... | collective-permute-start | bytes 786440 | tf_op jit(solution)/shard_map/ppermute | solution.py:380
  35.4 9.5 %collective-permute-start.7 = (f32[256,256]{1,0:T(8,128)S(1)}, f32[256,256]{1,0:T(8,128)S(1)}, u32[]{:S(2)}, u32[]{:S(2)}) collective-permute-start(f32[256,256]{1,0:T(8,128)S(1)} %collective-permute-done.4.rest_1_), channel_id=1, source_target_pairs={{0,4},{1,5},{2,6},{3,7},{4,0},{5,1},{6,2},{7,3},{8,12},{9,13},{10,... | collective-permute-start | bytes 786440 | tf_op jit(solution)/shard_map/ppermute | solution.py:377
  45.1 9.6 %collective-permute-start.8 = (f32[256,256]{1,0:T(8,128)S(1)}, f32[256,256]{1,0:T(8,128)S(1)}, u32[]{:S(2)}, u32[]{:S(2)}) collective-permute-start(f32[256,256]{1,0:T(8,128)S(1)} %collective-permute-done.4.rest_1_), channel_id=1, source_target_pairs={{0,1},{1,0},{2,3},{3,2},{4,5},{5,4},{6,7},{7,6},{8,9},{9,8},{10,11... | collective-permute-start | bytes 786440 | tf_op jit(solution)/shard_map/ppermute | solution.py:380
  45.2 9.4 %collective-permute-start.9 = (f32[256,256]{1,0:T(8,128)S(1)}, f32[256,256]{1,0:T(8,128)S(1)}, u32[]{:S(2)}, u32[]{:S(2)}) collective-permute-start(f32[256,256]{1,0:T(8,128)S(1)} %collective-permute-done.5.rest_2_), channel_id=1, source_target_pairs={{0,1},{1,0},{2,3},{3,2},{4,5},{5,4},{6,7},{7,6},{8,9},{9,8},{10,11... | collective-permute-start | bytes 786440 | tf_op jit(solution)/shard_map/ppermute | solution.py:380
  45.6 9.1 %collective-permute-start.10 = (f32[256,256]{1,0:T(8,128)S(1)}, f32[256,256]{1,0:T(8,128)S(1)}, u32[]{:S(2)}, u32[]{:S(2)}) collective-permute-start(f32[256,256]{1,0:T(8,128)S(1)} %collective-permute-done.7.rest_3_), channel_id=1, source_target_pairs={{0,1},{1,0},{2,3},{3,2},{4,5},{5,4},{6,7},{7,6},{8,9},{9,8},{10,11... | collective-permute-start | bytes 786440 | tf_op jit(solution)/shard_map/ppermute | solution.py:380
  56.2 11.3 %collective-permute-start.12 = (bf16[640,256]{1,0:T(8,128)(2,1)S(1)}, bf16[640,256]{1,0:T(8,128)(2,1)S(1)}, u32[]{:S(2)}, u32[]{:S(2)}) collective-permute-start(bf16[640,256]{1,0:T(8,128)(2,1)S(1)} %get-tuple-element.155.rest_0_), channel_id=1, source_target_pairs={{0,4},{1,5},{2,6},{3,7},{4,0},{5,1},{6,2},{7,3},{8,12},{9,13},{10,... | collective-permute-start | bytes 983048 | tf_op jit(solution)/shard_map/ppermute | solution.py:377
  56.8 10.7 %collective-permute-start.11 = (bf16[640,256]{1,0:T(8,128)(2,1)S(1)}, bf16[640,256]{1,0:T(8,128)(2,1)S(1)}, u32[]{:S(2)}, u32[]{:S(2)}) collective-permute-start(bf16[640,256]{1,0:T(8,128)(2,1)S(1)} %get-tuple-element.155.rest_0_), channel_id=1, source_target_pairs={{0,2},{1,3},{2,0},{3,1},{4,6},{5,7},{6,4},{7,5},{8,10},{9,11},{10,... | collective-permute-start | bytes 983048 | tf_op jit(solution)/shard_map/ppermute | solution.py:377
  67.8 10.6 %collective-permute-start.13 = (bf16[640,256]{1,0:T(8,128)(2,1)S(1)}, bf16[640,256]{1,0:T(8,128)(2,1)S(1)}, u32[]{:S(2)}, u32[]{:S(2)}) collective-permute-start(bf16[640,256]{1,0:T(8,128)(2,1)S(1)} %get-tuple-element.155.rest_0_), channel_id=1, source_target_pairs={{0,1},{1,0},{2,3},{3,2},{4,5},{5,4},{6,7},{7,6},{8,9},{9,8},{10,11... | collective-permute-start | bytes 983048 | tf_op jit(solution)/shard_map/ppermute | solution.py:380
  67.8 10.5 %collective-permute-start.14 = (bf16[640,256]{1,0:T(8,128)(2,1)S(1)}, bf16[640,256]{1,0:T(8,128)(2,1)S(1)}, u32[]{:S(2)}, u32[]{:S(2)}) collective-permute-start(bf16[640,256]{1,0:T(8,128)(2,1)S(1)} %collective-permute-done.11.rest_1_), channel_id=1, source_target_pairs={{0,4},{1,5},{2,6},{3,7},{4,0},{5,1},{6,2},{7,3},{8,12},{9,13},{10,... | collective-permute-start | bytes 983048 | tf_op jit(solution)/shard_map/ppermute | solution.py:377
  78.6 9.6 %collective-permute-start.15 = (bf16[640,256]{1,0:T(8,128)(2,1)S(1)}, bf16[640,256]{1,0:T(8,128)(2,1)S(1)}, u32[]{:S(2)}, u32[]{:S(2)}) collective-permute-start(bf16[640,256]{1,0:T(8,128)(2,1)S(1)} %collective-permute-done.11.rest_1_), channel_id=1, source_target_pairs={{0,1},{1,0},{2,3},{3,2},{4,5},{5,4},{6,7},{7,6},{8,9},{9,8},{10,11... | collective-permute-start | bytes 983048 | tf_op jit(solution)/shard_map/ppermute | solution.py:380
  78.7 9.5 %collective-permute-start.16 = (bf16[640,256]{1,0:T(8,128)(2,1)S(1)}, bf16[640,256]{1,0:T(8,128)(2,1)S(1)}, u32[]{:S(2)}, u32[]{:S(2)}) collective-permute-start(bf16[640,256]{1,0:T(8,128)(2,1)S(1)} %collective-permute-done.12.rest_2_), channel_id=1, source_target_pairs={{0,1},{1,0},{2,3},{3,2},{4,5},{5,4},{6,7},{7,6},{8,9},{9,8},{10,11... | collective-permute-start | bytes 983048 | tf_op jit(solution)/shard_map/ppermute | solution.py:380
  79.2 9.0 %collective-permute-start.17 = (bf16[640,256]{1,0:T(8,128)(2,1)S(1)}, bf16[640,256]{1,0:T(8,128)(2,1)S(1)}, u32[]{:S(2)}, u32[]{:S(2)}) collective-permute-start(bf16[640,256]{1,0:T(8,128)(2,1)S(1)} %collective-permute-done.14.rest_3_), channel_id=1, source_target_pairs={{0,1},{1,0},{2,3},{3,2},{4,5},{5,4},{6,7},{7,6},{8,9},{9,8},{10,11... | collective-permute-start | bytes 983048 | tf_op jit(solution)/shard_map/ppermute | solution.py:380
  100.0 11.0 %collective-permute-start.19 = (f32[256,256]{1,0:T(8,128)S(1)}, f32[256,256]{1,0:T(8,128)S(1)}, u32[]{:S(2)}, u32[]{:S(2)}) collective-permute-start(f32[256,256]{1,0:T(8,128)S(1)} %get-tuple-element.182.kernel_ref.rest_0_.own), channel_id=1, source_target_pairs={{0,4},{1,5},{2,6},{3,7},{4,0},{5,1},{6,2},{7,3},{8,12},{9,13},{10,... | collective-permute-start | bytes 786440 | tf_op jit(solution)/shard_map/ppermute | solution.py:377
  100.6 10.4 %collective-permute-start.18 = (f32[256,256]{1,0:T(8,128)S(1)}, f32[256,256]{1,0:T(8,128)S(1)}, u32[]{:S(2)}, u32[]{:S(2)}) collective-permute-start(f32[256,256]{1,0:T(8,128)S(1)} %get-tuple-element.182.kernel_ref.rest_0_.own), channel_id=1, source_target_pairs={{0,2},{1,3},{2,0},{3,1},{4,6},{5,7},{6,4},{7,5},{8,10},{9,11},{10,... | collective-permute-start | bytes 786440 | tf_op jit(solution)/shard_map/ppermute | solution.py:377
  111.2 9.7 %collective-permute-start.20 = (f32[256,256]{1,0:T(8,128)S(1)}, f32[256,256]{1,0:T(8,128)S(1)}, u32[]{:S(2)}, u32[]{:S(2)}) collective-permute-start(f32[256,256]{1,0:T(8,128)S(1)} %get-tuple-element.182.kernel_ref.rest_0_.own), channel_id=1, source_target_pairs={{0,1},{1,0},{2,3},{3,2},{4,5},{5,4},{6,7},{7,6},{8,9},{9,8},{10,11... | collective-permute-start | bytes 786440 | tf_op jit(solution)/shard_map/ppermute | solution.py:380
  111.3 9.5 %collective-permute-start.21 = (f32[256,256]{1,0:T(8,128)S(1)}, f32[256,256]{1,0:T(8,128)S(1)}, u32[]{:S(2)}, u32[]{:S(2)}) collective-permute-start(f32[256,256]{1,0:T(8,128)S(1)} %collective-permute-done.18.rest_1_), channel_id=1, source_target_pairs={{0,4},{1,5},{2,6},{3,7},{4,0},{5,1},{6,2},{7,3},{8,12},{9,13},{10,... | collective-permute-start | bytes 786440 | tf_op jit(solution)/shard_map/ppermute | solution.py:377
  121.0 9.6 %collective-permute-start.22 = (f32[256,256]{1,0:T(8,128)S(1)}, f32[256,256]{1,0:T(8,128)S(1)}, u32[]{:S(2)}, u32[]{:S(2)}) collective-permute-start(f32[256,256]{1,0:T(8,128)S(1)} %collective-permute-done.18.rest_1_), channel_id=1, source_target_pairs={{0,1},{1,0},{2,3},{3,2},{4,5},{5,4},{6,7},{7,6},{8,9},{9,8},{10,11... | collective-permute-start | bytes 786440 | tf_op jit(solution)/shard_map/ppermute | solution.py:380
  121.2 9.4 %collective-permute-start.23 = (f32[256,256]{1,0:T(8,128)S(1)}, f32[256,256]{1,0:T(8,128)S(1)}, u32[]{:S(2)}, u32[]{:S(2)}) collective-permute-start(f32[256,256]{1,0:T(8,128)S(1)} %collective-permute-done.19.rest_2_), channel_id=1, source_target_pairs={{0,1},{1,0},{2,3},{3,2},{4,5},{5,4},{6,7},{7,6},{8,9},{9,8},{10,11... | collective-permute-start | bytes 786440 | tf_op jit(solution)/shard_map/ppermute | solution.py:380
  121.6 9.1 %collective-permute-start.24 = (f32[256,256]{1,0:T(8,128)S(1)}, f32[256,256]{1,0:T(8,128)S(1)}, u32[]{:S(2)}, u32[]{:S(2)}) collective-permute-start(f32[256,256]{1,0:T(8,128)S(1)} %collective-permute-done.21.rest_3_), channel_id=1, source_target_pairs={{0,1},{1,0},{2,3},{3,2},{4,5},{5,4},{6,7},{7,6},{8,9},{9,8},{10,11... | collective-permute-start | bytes 786440 | tf_op jit(solution)/shard_map/ppermute | solution.py:380
  (1 other events, 1.8 us)

commit v13 on v12

--- a/solution.py
+++ b/solution.py
@@ -46,31 +46,6 @@
     parts_ref[...] = jnp.broadcast_to(value[None], parts_ref.shape)
 
 
-def split(value):
-    high = value.astype(jnp.bfloat16)
-    return high, (value - high.astype(jnp.float32)).astype(jnp.bfloat16)
-
-
-def scale_block(scale_cols):
-    wide = jnp.broadcast_to(scale_cols, (LANES, scale_cols.shape[1])).T
-    return jnp.concatenate(split(wide), axis=1)
-
-
-def row_sums(half, block):
-    sums = jnp.dot(half, block, preferred_element_type=jnp.float32)
-    return sums[:, :LANES] + sums[:, LANES:]
-
-
-def across(column, classes):
-    return jnp.concatenate([column] * (classes // LANES), axis=1)
-
-
-def dot_rows(left, right):
-    return lax.dot_general(
-        left, right, (((1,), (1,)), ((), ())), preferred_element_type=jnp.float32
-    )
-
-
 def code_lines(seed_class, train_mask, rows):
     code = jnp.where(train_mask[...] == 1, seed_class[...], -1).astype(jnp.float32)
     line = jnp.concatenate([code[i : i + 1] for i in range(code.shape[0])], axis=1)
@@ -101,11 +76,11 @@
 
 
 def pack_kernel(rows, tile_count, *refs):
-    count = 7
+    tiles, *refs = refs
+    count = 6
     ins, places = refs[:count], refs[count : 2 * count]
     keep, swap, ready, arrived = refs[2 * count :]
     tile_paper, tile_author, seed_class, train_mask = places[:4]
-    tiles = ins[-1]
     pairs = keep.shape[0]
     me = lax.axis_index("blk")
     pair, side = lax.div(me, 2), lax.rem(me, 2)
@@ -113,7 +88,7 @@
         pltpu.make_async_copy(source, place, ready.at[i])
         for i, (source, place) in enumerate(zip(ins, places))
     ]
-    for copy in moves[:-1]:
+    for copy in moves:
         copy.start()
     outs = []
     copies = []
@@ -126,7 +101,6 @@
             copy.start()
             copies.append(copy)
             outs.append((out, k, slot))
-    moves[-1].start()
     for copy in moves[:4]:
         copy.wait()
     line = lax.broadcasted_iota(jnp.int32, (META, LANES), 0)
@@ -172,21 +146,22 @@
 
 
 def first_sum_kernel(
-    authors, tile_paper, tile_count, tiles, seed_class, train_mask, class_prior, parts
+    authors, rows, tile_paper, tile_count, keep, swap, seed_class, train_mask, class_prior, parts
 ):
-    slots, rows, columns = tiles.shape
+    pairs, _, columns = keep.shape
     classes = parts.shape[2]
-    ones = jnp.ones((8, columns), jnp.bfloat16)
+    slots = sources(2 * pairs)
+    tiles = [ref[k, :rows, :].astype(jnp.float32) for ref in (keep, swap) for k in range(pairs)]
+    lane = lax.broadcasted_iota(jnp.int32, (rows, classes), 1).astype(jnp.float32)
     total = authors * class_prior[...]
-    for paper, codes in enumerate(code_lines(seed_class, train_mask, rows)):
+    for paper, code in enumerate(code_columns(code_lines(seed_class, train_mask, rows))):
         weight = jnp.zeros((rows, columns), jnp.float32)
-        for slot in range(slots):
+        for slot, tile in zip(slots, tiles):
             chosen = (slot < tile_count[0]) & (tile_paper[slot] == paper)
-            weight = weight + jnp.where(chosen, tiles[slot].astype(jnp.float32), 0.0)
-        high, low = split(weight)
-        high, low = split(dot_rows(ones, high) + dot_rows(ones, low))
-        seeds = seeds_of(codes, classes)
-        total = total + (dot_rows(high, seeds) + dot_rows(low, seeds))[:1]
+            weight = weight + jnp.where(chosen, tile, 0.0)
+        weight = jnp.sum(weight, axis=1, keepdims=True)
+        seeds = jnp.where(code == lane, weight, 0.0)
+        total = total + jnp.sum(seeds, axis=0, keepdims=True)
     spread(total, parts)
 
 
@@ -222,14 +197,13 @@
     at = code_rows + AT_DEV
     papers = [jnp.max(meta[at : at + 1]).astype(jnp.int32) for meta in metas]
     scale_cols = col_scale(summed, class_target)
-    block = scale_block(scale_cols)
     codes = code_columns([meta_line(meta, rows) for meta in metas])
     totals = [jnp.zeros((LANES, classes), jnp.float32) for _ in range(AT_DEV)]
     lane = lax.broadcasted_iota(jnp.int32, (rows, classes), 1).astype(jnp.float32)
     for shift, (ref, place) in enumerate(held):
         half = kernels[shift][pl.ds(pl.multiple_of(papers[shift] * rows, rows), rows), :]
-        scale_rows = across(keep_share / row_sums(half, block), classes)
-        share = half.astype(jnp.float32) * scale_cols * scale_rows
+        scaled = half.astype(jnp.float32) * scale_cols
+        share = scaled * (keep_share / jnp.sum(scaled, axis=1, keepdims=True))
         labels = share + jnp.where(codes[shift] == lane, 1.0 - keep_share, 0.0)
         parcel = lax.dot_general(
             ref[place, :rows, :],
@@ -247,32 +221,28 @@
 
 
 def paper_kernel(
-    blocks, tile_paper, tile_author, tile_count, tiles, summed, class_prior, class_target, *rest
+    blocks, rows, tile_paper, tile_author, tile_count, keep, swap, summed, class_prior,
+    class_target, *rest,
 ):
     kernels, (full, parts, *half) = rest[:blocks], rest[blocks:]
-    _, rows, columns = tiles.shape
+    pairs, _, columns = keep.shape
     classes = full.shape[1]
     scale_cols = col_scale(summed, class_target)
-    block = scale_block(scale_cols)
     slots = sources(blocks)
-    wide = jnp.concatenate([tiles[slot] for slot in slots], axis=1)
-    chosen = []
+    wide = [ref[k, :rows, :] for ref in (keep, swap) for k in range(pairs)]
+    wide = jnp.concatenate(wide, axis=1)
+    labels = []
     for ref, slot in zip(kernels, slots):
         start = pl.multiple_of(tile_author[slot] * columns, columns)
-        chosen.append(ref[pl.ds(start, columns), :])
-    kernel = jnp.concatenate(chosen, axis=0)
-    high, low = split(kernel)
-    sums = row_sums(high, block) + jnp.dot(
-        low, block[:, :LANES], preferred_element_type=jnp.float32
-    )
-    share = (kernel * scale_cols * across(1.0 / sums, classes)).astype(jnp.bfloat16)
-    labels = [share[i * columns : (i + 1) * columns] for i in range(blocks)]
+        scaled = ref[pl.ds(start, columns), :] * scale_cols
+        share = scaled * (1.0 / jnp.sum(scaled, axis=1, keepdims=True))
+        labels.append(share.astype(jnp.bfloat16))
     column = jnp.zeros((1, classes), jnp.float32)
     for paper in range(full.shape[0] // rows):
         chosen = []
         for one, slot in zip(labels, slots):
-            keep = (slot < tile_count[0]) & (tile_paper[slot] == paper)
-            chosen.append(jnp.where(keep, one, jnp.zeros_like(one)))
+            mine = (slot < tile_count[0]) & (tile_paper[slot] == paper)
+            chosen.append(jnp.where(mine, one, jnp.zeros_like(one)))
         mass = jnp.dot(wide, jnp.concatenate(chosen, axis=0), preferred_element_type=jnp.float32)
         kernel = mass + class_prior[...]
         full[paper * rows : (paper + 1) * rows, :] = kernel
@@ -344,23 +314,23 @@
     parts = shape((devices, 1, classes), f32)
 
     inputs = (
-        tile_paper, tile_author, seed_class, train_mask, prior, target, tile_values,
+        tile_paper, tile_author, seed_class, train_mask, prior, target,
     )
-    places = (SMEM, SMEM, VMEM, VMEM, VMEM, VMEM, VMEM)
+    places = (SMEM, SMEM, VMEM, VMEM, VMEM, VMEM)
     blocks = lax.axis_size("blk")
     load = shape((blocks // 2, rows + META, columns), bf16)
     moved = call(
         functools.partial(pack_kernel, rows),
         tuple(shape(one.shape, one.dtype) for one in inputs) + (load, load),
-        [SMEM] + [HBM] * len(inputs),
+        [SMEM, HBM] + [HBM] * len(inputs),
         [pltpu.SemaphoreType.DMA((len(inputs),)), pltpu.SemaphoreType.DMA((2, blocks // 2))],
         places + (VMEM, VMEM),
-    )(tile_count, *(in_hbm(one) for one in inputs))
-    tile_paper, tile_author, seed_class, train_mask, prior, target, tile_values, keep, swap = moved
+    )(tile_count, in_hbm(tile_values), *(in_hbm(one) for one in inputs))
+    tile_paper, tile_author, seed_class, train_mask, prior, target, keep, swap = moved
     swapped = lax.ppermute(swap, "blk", [(i, i ^ 1) for i in range(blocks)])
     local = call(
-        functools.partial(first_sum_kernel, authors), parts, [SMEM, SMEM] + [VMEM] * 4
-    )(tile_paper, tile_count, tile_values, seed_class, train_mask, prior)
+        functools.partial(first_sum_kernel, authors, rows), parts, [SMEM, SMEM] + [VMEM] * 5
+    )(tile_paper, tile_count, keep, swap, seed_class, train_mask, prior)
     both = shape((2, rows + META, columns), bf16)
     pairs = call(pair_kernel, (both,) * (blocks // 2 - 1), [VMEM] * 2)(keep, swapped)
     local, *pairs = lax.optimization_barrier((local, *pairs))
@@ -425,11 +395,11 @@
         author_summed, kernels = balance(own, own, local, left)
         last = repeat + 1 == ROUNDS
         kernel, local, *half = call(
-            functools.partial(paper_kernel, blocks),
+            functools.partial(paper_kernel, blocks, rows),
             paper_out[:2] if last else paper_out,
-            [SMEM, SMEM, SMEM] + [VMEM] * (4 + blocks),
+            [SMEM, SMEM, SMEM] + [VMEM] * (5 + blocks),
         )(
-            tile_paper, tile_author, tile_count, tile_values, author_summed, prior, target, *kernels
+            tile_paper, tile_author, tile_count, keep, swap, author_summed, prior, target, *kernels
         )
         if last:
             summed = last_balance(kernel, local)

time: 179 us -> 178 us (level)
  Pallas kernels: 13.4 us -> 11.5 us
  transfers between devices with their start and end apart: 25 -> 25, of which waited for: 0 -> 1; matrix products, arithmetic and copies ran while one was open for 0% -> 0% of each run, Pallas kernels for 1% -> 1%
where the time goes in v13:
time: 178 us; the launch traced here: 177 us
  blocking collectives  151 us (85%)
  starting transfers between devices  13 us (7%)
  Pallas kernels  11.5 us (6%)
    all_to_all x16, blocking collectives, exchange(): return lax.all_to_all(parts, AXES, split_axis=0, concat_axis=0, tiled=True)  151 us
    ppermute x9, starting transfers between devices, across_pairs(): return lax.ppermute(value, 'blk', [(i, i ^ 2 * k) for i in range(blocks)])  5.55 us
    ppermute x3, starting transfers between devices, on_device(): lax.ppermute(one, 'blk', [(i, i ^ 2 * k) for i in range(blocks)])  4.47 us
  transfers between devices with their start and end apart: 25, of which 1 were waited for; matrix products, arithmetic and copies ran while one was open for 0% of the time, Pallas kernels for 1%

profile of v13, /device:TPU:0, one launch (start us, length us, event | category | flops | bytes accessed | tf_op | source)
XLA Modules:
  0.0 177.4 jit_solution(3536195237237164948)
XLA Ops:
  1.3 1.9 %shard_map.95 = (s32[8]{0:T(128)S(1)}, s32[8]{0:T(128)S(1)}, s32[5,128]{1,0:T(8,128)S(1)}, s32[5,128]{1,0:T(8,128)S(1)}, f32[1,256]{1,0:T(1,128)S(1)}, /*index=5...) custom-call(s32[1]{0:T(128)S(6)} %copy.10.tile_count, ...), custom_call_target="tpu_custom_call" | custom-call | tf_op jit(solution)/shard_map/pallas_call | solution.py:322
  3.8 1.1 shard_map.96
  5.1 2.9 %collective-permute-start.1 = (bf16[2,336,128]{2,1,0:T(8,128)(2,1)S(1)}, bf16[2,336,128]{2,1,0:T(8,128)(2,1)S(1)}, u32[]{:S(2)}, u32[]{:S(2)}) collective-permute-start(bf16[2,336,128]{2,1,0:T(8,128)(2,1)S(1)} %get-tuple-element.108), channel_id=1, source_target_pairs={{0,2},{1,3},{2,0},{3,1},{4,6},{5,7},{6,4},{7,5},{8,10},{9,11},{10,... | collective-permute-start | bytes 516104 | tf_op jit(solution)/shard_map/ppermute | solution.py:338
  8.0 1.5 collective-permute-start.2
  9.5 13.4 %all_to_all.80.summed = f32[32,1,256]{2,1,0:T(1,128)S(1)} all-to-all(f32[32,1,256]{2,1,0:T(1,128)S(1)} %shard_map.96), channel_id=1, replica_groups=mesh['grp'=4,'blk'=8] {'grp','blk'}, dimensions={0} | all-to-all | bytes 65536 | tf_op jit(solution)/shard_map/all_to_all | solution.py:288
  25.0 9.8 %all_to_all.81.summed = f32[32,1,256]{2,1,0:T(1,128)S(1)} all-to-all(f32[32,1,256]{2,1,0:T(1,128)S(1)} %get-tuple-element.112), channel_id=1, replica_groups=mesh['grp'=4,'blk'=8] {'grp','blk'}, dimensions={0} | all-to-all | bytes 65536 | tf_op jit(solution)/shard_map/all_to_all | solution.py:288
  35.7 8.9 %all_to_all.82.summed = f32[32,1,256]{2,1,0:T(1,128)S(1)} all-to-all(f32[32,1,256]{2,1,0:T(1,128)S(1)} %shard_map.99), channel_id=1, replica_groups=mesh['grp'=4,'blk'=8] {'grp','blk'}, dimensions={0} | all-to-all | bytes 65536 | tf_op jit(solution)/shard_map/all_to_all | solution.py:288
  45.5 8.9 %all_to_all.83.summed = f32[32,1,256]{2,1,0:T(1,128)S(1)} all-to-all(f32[32,1,256]{2,1,0:T(1,128)S(1)} %shard_map.100), channel_id=1, replica_groups=mesh['grp'=4,'blk'=8] {'grp','blk'}, dimensions={0} | all-to-all | bytes 65536 | tf_op jit(solution)/shard_map/all_to_all | solution.py:288
  54.4 1.2 shard_map.101
  56.9 10.1 %all_to_all.84.summed = f32[32,1,256]{2,1,0:T(1,128)S(1)} all-to-all(f32[32,1,256]{2,1,0:T(1,128)S(1)} %get-tuple-element.134), channel_id=1, replica_groups=mesh['grp'=4,'blk'=8] {'grp','blk'}, dimensions={0} | all-to-all | bytes 65536 | tf_op jit(solution)/shard_map/all_to_all | solution.py:288
  68.0 9.9 %all_to_all.85.summed = f32[32,1,256]{2,1,0:T(1,128)S(1)} all-to-all(f32[32,1,256]{2,1,0:T(1,128)S(1)} %shard_map.102), channel_id=1, replica_groups=mesh['grp'=4,'blk'=8] {'grp','blk'}, dimensions={0} | all-to-all | bytes 65536 | tf_op jit(solution)/shard_map/all_to_all | solution.py:288
  78.7 8.9 %all_to_all.86.summed = f32[32,1,256]{2,1,0:T(1,128)S(1)} all-to-all(f32[32,1,256]{2,1,0:T(1,128)S(1)} %shard_map.103), channel_id=1, replica_groups=mesh['grp'=4,'blk'=8] {'grp','blk'}, dimensions={0} | all-to-all | bytes 65536 | tf_op jit(solution)/shard_map/all_to_all | solution.py:288
  87.9 8.9 %all_to_all.87.summed = f32[32,1,256]{2,1,0:T(1,128)S(1)} all-to-all(f32[32,1,256]{2,1,0:T(1,128)S(1)} %shard_map.104), channel_id=1, replica_groups=mesh['grp'=4,'blk'=8] {'grp','blk'}, dimensions={0} | all-to-all | bytes 65536 | tf_op jit(solution)/shard_map/all_to_all | solution.py:288
  96.9 1.7 shard_map.105
  99.8 9.8 %all_to_all.88.summed = f32[32,1,256]{2,1,0:T(1,128)S(1)} all-to-all(f32[32,1,256]{2,1,0:T(1,128)S(1)} %get-tuple-element.162), channel_id=1, replica_groups=mesh['grp'=4,'blk'=8] {'grp','blk'}, dimensions={0} | all-to-all | bytes 65536 | tf_op jit(solution)/shard_map/all_to_all | solution.py:288
  110.5 8.9 %all_to_all.89.summed = f32[32,1,256]{2,1,0:T(1,128)S(1)} all-to-all(f32[32,1,256]{2,1,0:T(1,128)S(1)} %shard_map.106), channel_id=1, replica_groups=mesh['grp'=4,'blk'=8] {'grp','blk'}, dimensions={0} | all-to-all | bytes 65536 | tf_op jit(solution)/shard_map/all_to_all | solution.py:288
  120.3 8.9 %all_to_all.90.summed = f32[32,1,256]{2,1,0:T(1,128)S(1)} all-to-all(f32[32,1,256]{2,1,0:T(1,128)S(1)} %shard_map.107), channel_id=1, replica_groups=mesh['grp'=4,'blk'=8] {'grp','blk'}, dimensions={0} | all-to-all | bytes 65536 | tf_op jit(solution)/shard_map/all_to_all | solution.py:288
  129.4 8.9 %all_to_all.91.summed.author_summed = f32[32,1,256]{2,1,0:T(1,128)S(1)} all-to-all(f32[32,1,256]{2,1,0:T(1,128)S(1)} %shard_map.108), channel_id=1, replica_groups=mesh['grp'=4,'blk'=8] {'grp','blk'}, dimensions={0} | all-to-all | bytes 65536 | tf_op jit(solution)/shard_map/all_to_all | solution.py:288
  138.4 1.2 shard_map.109
  139.6 8.9 %all_to_all.92.summed = f32[32,1,256]{2,1,0:T(1,128)S(1)} all-to-all(f32[32,1,256]{2,1,0:T(1,128)S(1)} %get-tuple-element.189), channel_id=1, replica_groups=mesh['grp'=4,'blk'=8] {'grp','blk'}, dimensions={0} | all-to-all | bytes 65536 | tf_op jit(solution)/shard_map/all_to_all | solution.py:288
  148.8 8.9 %all_to_all.93.summed = f32[32,1,256]{2,1,0:T(1,128)S(1)} all-to-all(f32[32,1,256]{2,1,0:T(1,128)S(1)} %shard_map.110), channel_id=1, replica_groups=mesh['grp'=4,'blk'=8] {'grp','blk'}, dimensions={0} | all-to-all | bytes 65536 | tf_op jit(solution)/shard_map/all_to_all | solution.py:288
  158.0 8.9 %all_to_all.94.summed = f32[32,1,256]{2,1,0:T(1,128)S(1)} all-to-all(f32[32,1,256]{2,1,0:T(1,128)S(1)} %shard_map.111), channel_id=1, replica_groups=mesh['grp'=4,'blk'=8] {'grp','blk'}, dimensions={0} | all-to-all | bytes 65536 | tf_op jit(solution)/shard_map/all_to_all | solution.py:288
  167.2 8.9 %all_to_all.95.summed = f32[32,1,256]{2,1,0:T(1,128)S(1)} all-to-all(f32[32,1,256]{2,1,0:T(1,128)S(1)} %shard_map.112), channel_id=1, replica_groups=mesh['grp'=4,'blk'=8] {'grp','blk'}, dimensions={0} | all-to-all | bytes 65536 | tf_op jit(solution)/shard_map/all_to_all | solution.py:288
  176.1 1.3 shard_map.113
  (61 shorter events, 12.0 us)
Async XLA Ops:
  5.1 17.8 %collective-permute-start.1 = (bf16[2,336,128]{2,1,0:T(8,128)(2,1)S(1)}, bf16[2,336,128]{2,1,0:T(8,128)(2,1)S(1)}, u32[]{:S(2)}, u32[]{:S(2)}) collective-permute-start(bf16[2,336,128]{2,1,0:T(8,128)(2,1)S(1)} %get-tuple-element.108), channel_id=1, source_target_pairs={{0,2},{1,3},{2,0},{3,1},{4,6},{5,7},{6,4},{7,5},{8,10},{9,11},{10,... | collective-permute-start | bytes 516104 | tf_op jit(solution)/shard_map/ppermute | solution.py:338
  8.0 14.9 %collective-permute-start.2 = (bf16[2,336,128]{2,1,0:T(8,128)(2,1)S(1)}, bf16[2,336,128]{2,1,0:T(8,128)(2,1)S(1)}, u32[]{:S(2)}, u32[]{:S(2)}) collective-permute-start(bf16[2,336,128]{2,1,0:T(8,128)(2,1)S(1)} %get-tuple-element.109), channel_id=1, source_target_pairs={{0,4},{1,5},{2,6},{3,7},{4,0},{5,1},{6,2},{7,3},{8,12},{9,13},{10,... | collective-permute-start | bytes 516104 | tf_op jit(solution)/shard_map/ppermute | solution.py:338
  9.5 13.4 %collective-permute-start.3 = (bf16[2,336,128]{2,1,0:T(8,128)(2,1)S(1)}, bf16[2,336,128]{2,1,0:T(8,128)(2,1)S(1)}, u32[]{:S(2)}, u32[]{:S(2)}) collective-permute-start(bf16[2,336,128]{2,1,0:T(8,128)(2,1)S(1)} %get-tuple-element.110), channel_id=1, source_target_pairs={{0,6},{1,7},{2,4},{3,5},{4,2},{5,3},{6,0},{7,1},{8,14},{9,15},{10,... | collective-permute-start | bytes 516104 | tf_op jit(solution)/shard_map/ppermute | solution.py:338
  23.7 11.0 %collective-permute-start.5 = (f32[256,256]{1,0:T(8,128)S(1)}, f32[256,256]{1,0:T(8,128)S(1)}, u32[]{:S(2)}, u32[]{:S(2)}) collective-permute-start(f32[256,256]{1,0:T(8,128)S(1)} %get-tuple-element.128.kernel_ref.rest_0_), channel_id=1, source_target_pairs={{0,4},{1,5},{2,6},{3,7},{4,0},{5,1},{6,2},{7,3},{8,12},{9,13},{10,... | collective-permute-start | bytes 786440 | tf_op jit(solution)/shard_map/ppermute | solution.py:347
  24.3 10.4 %collective-permute-start.4 = (f32[256,256]{1,0:T(8,128)S(1)}, f32[256,256]{1,0:T(8,128)S(1)}, u32[]{:S(2)}, u32[]{:S(2)}) collective-permute-start(f32[256,256]{1,0:T(8,128)S(1)} %get-tuple-element.128.kernel_ref.rest_0_), channel_id=1, source_target_pairs={{0,2},{1,3},{2,0},{3,1},{4,6},{5,7},{6,4},{7,5},{8,10},{9,11},{10,... | collective-permute-start | bytes 786440 | tf_op jit(solution)/shard_map/ppermute | solution.py:347
  34.9 9.7 %collective-permute-start.6 = (f32[256,256]{1,0:T(8,128)S(1)}, f32[256,256]{1,0:T(8,128)S(1)}, u32[]{:S(2)}, u32[]{:S(2)}) collective-permute-start(f32[256,256]{1,0:T(8,128)S(1)} %get-tuple-element.128.kernel_ref.rest_0_), channel_id=1, source_target_pairs={{0,1},{1,0},{2,3},{3,2},{4,5},{5,4},{6,7},{7,6},{8,9},{9,8},{10,11... | collective-permute-start | bytes 786440 | tf_op jit(solution)/shard_map/ppermute | solution.py:350
  35.1 9.5 %collective-permute-start.7 = (f32[256,256]{1,0:T(8,128)S(1)}, f32[256,256]{1,0:T(8,128)S(1)}, u32[]{:S(2)}, u32[]{:S(2)}) collective-permute-start(f32[256,256]{1,0:T(8,128)S(1)} %collective-permute-done.4.rest_1_), channel_id=1, source_target_pairs={{0,4},{1,5},{2,6},{3,7},{4,0},{5,1},{6,2},{7,3},{8,12},{9,13},{10,... | collective-permute-start | bytes 786440 | tf_op jit(solution)/shard_map/ppermute | solution.py:347
  44.8 9.6 %collective-permute-start.8 = (f32[256,256]{1,0:T(8,128)S(1)}, f32[256,256]{1,0:T(8,128)S(1)}, u32[]{:S(2)}, u32[]{:S(2)}) collective-permute-start(f32[256,256]{1,0:T(8,128)S(1)} %collective-permute-done.4.rest_1_), channel_id=1, source_target_pairs={{0,1},{1,0},{2,3},{3,2},{4,5},{5,4},{6,7},{7,6},{8,9},{9,8},{10,11... | collective-permute-start | bytes 786440 | tf_op jit(solution)/shard_map/ppermute | solution.py:350
  45.0 9.4 %collective-permute-start.9 = (f32[256,256]{1,0:T(8,128)S(1)}, f32[256,256]{1,0:T(8,128)S(1)}, u32[]{:S(2)}, u32[]{:S(2)}) collective-permute-start(f32[256,256]{1,0:T(8,128)S(1)} %collective-permute-done.5.rest_2_), channel_id=1, source_target_pairs={{0,1},{1,0},{2,3},{3,2},{4,5},{5,4},{6,7},{7,6},{8,9},{9,8},{10,11... | collective-permute-start | bytes 786440 | tf_op jit(solution)/shard_map/ppermute | solution.py:350
  45.4 9.1 %collective-permute-start.10 = (f32[256,256]{1,0:T(8,128)S(1)}, f32[256,256]{1,0:T(8,128)S(1)}, u32[]{:S(2)}, u32[]{:S(2)}) collective-permute-start(f32[256,256]{1,0:T(8,128)S(1)} %collective-permute-done.7.rest_3_), channel_id=1, source_target_pairs={{0,1},{1,0},{2,3},{3,2},{4,5},{5,4},{6,7},{7,6},{8,9},{9,8},{10,11... | collective-permute-start | bytes 786440 | tf_op jit(solution)/shard_map/ppermute | solution.py:350
  55.7 11.3 %collective-permute-start.12 = (bf16[640,256]{1,0:T(8,128)(2,1)S(1)}, bf16[640,256]{1,0:T(8,128)(2,1)S(1)}, u32[]{:S(2)}, u32[]{:S(2)}) collective-permute-start(bf16[640,256]{1,0:T(8,128)(2,1)S(1)} %get-tuple-element.153.rest_0_), channel_id=1, source_target_pairs={{0,4},{1,5},{2,6},{3,7},{4,0},{5,1},{6,2},{7,3},{8,12},{9,13},{10,... | collective-permute-start | bytes 983048 | tf_op jit(solution)/shard_map/ppermute | solution.py:347
  56.3 10.7 %collective-permute-start.11 = (bf16[640,256]{1,0:T(8,128)(2,1)S(1)}, bf16[640,256]{1,0:T(8,128)(2,1)S(1)}, u32[]{:S(2)}, u32[]{:S(2)}) collective-permute-start(bf16[640,256]{1,0:T(8,128)(2,1)S(1)} %get-tuple-element.153.rest_0_), channel_id=1, source_target_pairs={{0,2},{1,3},{2,0},{3,1},{4,6},{5,7},{6,4},{7,5},{8,10},{9,11},{10,... | collective-permute-start | bytes 983048 | tf_op jit(solution)/shard_map/ppermute | solution.py:347
  67.2 10.6 %collective-permute-start.13 = (bf16[640,256]{1,0:T(8,128)(2,1)S(1)}, bf16[640,256]{1,0:T(8,128)(2,1)S(1)}, u32[]{:S(2)}, u32[]{:S(2)}) collective-permute-start(bf16[640,256]{1,0:T(8,128)(2,1)S(1)} %get-tuple-element.153.rest_0_), channel_id=1, source_target_pairs={{0,1},{1,0},{2,3},{3,2},{4,5},{5,4},{6,7},{7,6},{8,9},{9,8},{10,11... | collective-permute-start | bytes 983048 | tf_op jit(solution)/shard_map/ppermute | solution.py:350
  67.3 10.5 %collective-permute-start.14 = (bf16[640,256]{1,0:T(8,128)(2,1)S(1)}, bf16[640,256]{1,0:T(8,128)(2,1)S(1)}, u32[]{:S(2)}, u32[]{:S(2)}) collective-permute-start(bf16[640,256]{1,0:T(8,128)(2,1)S(1)} %collective-permute-done.11.rest_1_), channel_id=1, source_target_pairs={{0,4},{1,5},{2,6},{3,7},{4,0},{5,1},{6,2},{7,3},{8,12},{9,13},{10,... | collective-permute-start | bytes 983048 | tf_op jit(solution)/shard_map/ppermute | solution.py:347
  78.1 9.6 %collective-permute-start.15 = (bf16[640,256]{1,0:T(8,128)(2,1)S(1)}, bf16[640,256]{1,0:T(8,128)(2,1)S(1)}, u32[]{:S(2)}, u32[]{:S(2)}) collective-permute-start(bf16[640,256]{1,0:T(8,128)(2,1)S(1)} %collective-permute-done.11.rest_1_), channel_id=1, source_target_pairs={{0,1},{1,0},{2,3},{3,2},{4,5},{5,4},{6,7},{7,6},{8,9},{9,8},{10,11... | collective-permute-start | bytes 983048 | tf_op jit(solution)/shard_map/ppermute | solution.py:350
  78.2 9.5 %collective-permute-start.16 = (bf16[640,256]{1,0:T(8,128)(2,1)S(1)}, bf16[640,256]{1,0:T(8,128)(2,1)S(1)}, u32[]{:S(2)}, u32[]{:S(2)}) collective-permute-start(bf16[640,256]{1,0:T(8,128)(2,1)S(1)} %collective-permute-done.12.rest_2_), channel_id=1, source_target_pairs={{0,1},{1,0},{2,3},{3,2},{4,5},{5,4},{6,7},{7,6},{8,9},{9,8},{10,11... | collective-permute-start | bytes 983048 | tf_op jit(solution)/shard_map/ppermute | solution.py:350
  78.7 9.0 %collective-permute-start.17 = (bf16[640,256]{1,0:T(8,128)(2,1)S(1)}, bf16[640,256]{1,0:T(8,128)(2,1)S(1)}, u32[]{:S(2)}, u32[]{:S(2)}) collective-permute-start(bf16[640,256]{1,0:T(8,128)(2,1)S(1)} %collective-permute-done.14.rest_3_), channel_id=1, source_target_pairs={{0,1},{1,0},{2,3},{3,2},{4,5},{5,4},{6,7},{7,6},{8,9},{9,8},{10,11... | collective-permute-start | bytes 983048 | tf_op jit(solution)/shard_map/ppermute | solution.py:350
  98.5 11.0 %collective-permute-start.19 = (f32[256,256]{1,0:T(8,128)S(1)}, f32[256,256]{1,0:T(8,128)S(1)}, u32[]{:S(2)}, u32[]{:S(2)}) collective-permute-start(f32[256,256]{1,0:T(8,128)S(1)} %get-tuple-element.180.kernel_ref.rest_0_.own), channel_id=1, source_target_pairs={{0,4},{1,5},{2,6},{3,7},{4,0},{5,1},{6,2},{7,3},{8,12},{9,13},{10,... | collective-permute-start | bytes 786440 | tf_op jit(solution)/shard_map/ppermute | solution.py:347
  99.2 10.4 %collective-permute-start.18 = (f32[256,256]{1,0:T(8,128)S(1)}, f32[256,256]{1,0:T(8,128)S(1)}, u32[]{:S(2)}, u32[]{:S(2)}) collective-permute-start(f32[256,256]{1,0:T(8,128)S(1)} %get-tuple-element.180.kernel_ref.rest_0_.own), channel_id=1, source_target_pairs={{0,2},{1,3},{2,0},{3,1},{4,6},{5,7},{6,4},{7,5},{8,10},{9,11},{10,... | collective-permute-start | bytes 786440 | tf_op jit(solution)/shard_map/ppermute | solution.py:347
  109.8 9.7 %collective-permute-start.20 = (f32[256,256]{1,0:T(8,128)S(1)}, f32[256,256]{1,0:T(8,128)S(1)}, u32[]{:S(2)}, u32[]{:S(2)}) collective-permute-start(f32[256,256]{1,0:T(8,128)S(1)} %get-tuple-element.180.kernel_ref.rest_0_.own), channel_id=1, source_target_pairs={{0,1},{1,0},{2,3},{3,2},{4,5},{5,4},{6,7},{7,6},{8,9},{9,8},{10,11... | collective-permute-start | bytes 786440 | tf_op jit(solution)/shard_map/ppermute | solution.py:350
  109.9 9.5 %collective-permute-start.21 = (f32[256,256]{1,0:T(8,128)S(1)}, f32[256,256]{1,0:T(8,128)S(1)}, u32[]{:S(2)}, u32[]{:S(2)}) collective-permute-start(f32[256,256]{1,0:T(8,128)S(1)} %collective-permute-done.18.rest_1_), channel_id=1, source_target_pairs={{0,4},{1,5},{2,6},{3,7},{4,0},{5,1},{6,2},{7,3},{8,12},{9,13},{10,... | collective-permute-start | bytes 786440 | tf_op jit(solution)/shard_map/ppermute | solution.py:347
  119.6 9.6 %collective-permute-start.22 = (f32[256,256]{1,0:T(8,128)S(1)}, f32[256,256]{1,0:T(8,128)S(1)}, u32[]{:S(2)}, u32[]{:S(2)}) collective-permute-start(f32[256,256]{1,0:T(8,128)S(1)} %collective-permute-done.18.rest_1_), channel_id=1, source_target_pairs={{0,1},{1,0},{2,3},{3,2},{4,5},{5,4},{6,7},{7,6},{8,9},{9,8},{10,11... | collective-permute-start | bytes 786440 | tf_op jit(solution)/shard_map/ppermute | solution.py:350
  119.8 9.4 %collective-permute-start.23 = (f32[256,256]{1,0:T(8,128)S(1)}, f32[256,256]{1,0:T(8,128)S(1)}, u32[]{:S(2)}, u32[]{:S(2)}) collective-permute-start(f32[256,256]{1,0:T(8,128)S(1)} %collective-permute-done.19.rest_2_), channel_id=1, source_target_pairs={{0,1},{1,0},{2,3},{3,2},{4,5},{5,4},{6,7},{7,6},{8,9},{9,8},{10,11... | collective-permute-start | bytes 786440 | tf_op jit(solution)/shard_map/ppermute | solution.py:350
  120.2 9.1 %collective-permute-start.24 = (f32[256,256]{1,0:T(8,128)S(1)}, f32[256,256]{1,0:T(8,128)S(1)}, u32[]{:S(2)}, u32[]{:S(2)}) collective-permute-start(f32[256,256]{1,0:T(8,128)S(1)} %collective-permute-done.21.rest_3_), channel_id=1, source_target_pairs={{0,1},{1,0},{2,3},{3,2},{4,5},{5,4},{6,7},{7,6},{8,9},{9,8},{10,11... | collective-permute-start | bytes 786440 | tf_op jit(solution)/shard_map/ppermute | solution.py:350
  (1 other events, 1.8 us)

commit v14 on v13

--- a/solution.py
+++ b/solution.py
@@ -252,8 +252,15 @@
     spread(column, parts)
 
 
-def balance_kernel(kernel_ref, summed, class_target, parts):
-    next_sum(kernel_ref[...], summed, class_target, parts)
+def balance_kernel(*refs):
+    *kernels, summed, class_target, parts = refs
+    scale_cols = col_scale(summed, class_target)
+    total = None
+    for ref in kernels:
+        kernel = ref[...].astype(jnp.float32)
+        local = jnp.sum(row_scale(kernel, scale_cols) * kernel, axis=0, keepdims=True)
+        total = local if total is None else total + local
+    spread(total, parts)
 
 
 def final_kernel(
@@ -286,6 +293,17 @@
 
 def exchange(parts):
     return lax.all_to_all(parts, AXES, split_axis=0, concat_axis=0, tiled=True)
+
+
+def narrow_exchange(parts):
+    groups, blocks = lax.axis_size("grp"), lax.axis_size("blk")
+    sets = [
+        [i * blocks + pair + side for i in range(groups) for side in range(2)]
+        for pair in range(0, blocks, 2)
+    ]
+    return lax.all_to_all(
+        parts, AXES, split_axis=0, concat_axis=0, axis_index_groups=sets, tiled=True
+    )
 
 
 def on_device(
@@ -340,6 +358,7 @@
     ]
     summed = exchange(local)
 
+    narrow = shape((2 * lax.axis_size("grp"), 1, classes), f32)
     author_out = (shape((authors, classes), f32), parts)
     paper_out = (shape((papers, classes), f32), parts, shape((papers, classes), bf16))
 
@@ -361,12 +380,15 @@
                     moves.append((here, k, got))
             else:
                 moves = [(there, k, to_other(here[k])) for k in here if k not in there]
-            summed = exchange(local)
+            summed = narrow_exchange(local) if step > 1 else exchange(local)
             summed, *moved = lax.optimization_barrier((summed, *(one for _, _, one in moves)))
             for (place, k, _), one in zip(moves, moved):
                 place[k] = one
             if step + 1 < count:
-                local = call(balance_kernel, parts, [VMEM] * 3)(kernel, summed, target)
+                rest = [here[k] for k in range(blocks // 2)] if step > 0 else [kernel]
+                local = call(
+                    balance_kernel, narrow if step > 0 else parts, [VMEM] * (len(rest) + 2)
+                )(*rest, summed, target)
                 local, sent, *moved = lax.optimization_barrier((local, sent, *here.values()))
                 here = dict(zip(here, moved))
         order = range(blocks // 2)

time: 178 us -> 174 us (0.978)
  blocking collectives: 151 us -> 146 us
    all_to_all x16 -> x11, blocking collectives: 151 us -> 106 us  [exchange(): return lax.all_to_all(parts, AXES, split_axis=0, concat_axis=0, tiled=True)]
    all_to_all x0 -> x5, blocking collectives: none -> 39.8 us  [narrow_exchange(): lax.all_to_all(parts, AXES, split_axis=0, concat_axis=0, axis_index_group...]
where the time goes in v14:
time: 174 us; the launch traced here: 173 us
  blocking collectives  146 us (84%)
  starting transfers between devices  12.9 us (7%)
  Pallas kernels  12.6 us (7%)
    all_to_all x11, blocking collectives, exchange(): return lax.all_to_all(parts, AXES, split_axis=0, concat_axis=0, tiled=True)  106 us
    all_to_all x5, blocking collectives, narrow_exchange(): lax.all_to_all(parts, AXES, split_axis=0, concat_axis=0, axis_index_group...  39.8 us
    ppermute x9, starting transfers between devices, across_pairs(): return lax.ppermute(value, 'blk', [(i, i ^ 2 * k) for i in range(blocks)])  5.37 us
    ppermute x3, starting transfers between devices, on_device(): lax.ppermute(one, 'blk', [(i, i ^ 2 * k) for i in range(blocks)])  4.47 us
  transfers between devices with their start and end apart: 25, of which 1 were waited for; matrix products, arithmetic and copies ran while one was open for 0% of the time, Pallas kernels for 1%

profile of v14, /device:TPU:0, one launch (start us, length us, event | category | flops | bytes accessed | tf_op | source)
XLA Modules:
  0.0 173.2 jit_solution(17466767416344743336)
XLA Ops:
  1.3 1.9 %shard_map.95 = (s32[8]{0:T(128)S(1)}, s32[8]{0:T(128)S(1)}, s32[5,128]{1,0:T(8,128)S(1)}, s32[5,128]{1,0:T(8,128)S(1)}, f32[1,256]{1,0:T(1,128)S(1)}, /*index=5...) custom-call(s32[1]{0:T(128)S(6)} %copy.10.tile_count, ...), custom_call_target="tpu_custom_call" | custom-call | tf_op jit(solution)/shard_map/pallas_call | solution.py:340
  3.8 1.1 shard_map.96
  5.1 2.9 %collective-permute-start.1 = (bf16[2,336,128]{2,1,0:T(8,128)(2,1)S(1)}, bf16[2,336,128]{2,1,0:T(8,128)(2,1)S(1)}, u32[]{:S(2)}, u32[]{:S(2)}) collective-permute-start(bf16[2,336,128]{2,1,0:T(8,128)(2,1)S(1)} %get-tuple-element.108), channel_id=1, source_target_pairs={{0,2},{1,3},{2,0},{3,1},{4,6},{5,7},{6,4},{7,5},{8,10},{9,11},{10,... | collective-permute-start | bytes 516104 | tf_op jit(solution)/shard_map/ppermute | solution.py:356
  8.0 1.5 collective-permute-start.2
  9.5 13.4 %all_to_all.80.summed = f32[32,1,256]{2,1,0:T(1,128)S(1)} all-to-all(f32[32,1,256]{2,1,0:T(1,128)S(1)} %shard_map.96), channel_id=1, replica_groups=mesh['grp'=4,'blk'=8] {'grp','blk'}, dimensions={0} | all-to-all | bytes 65536 | tf_op jit(solution)/shard_map/all_to_all | solution.py:295
  25.0 9.8 %all_to_all.81.refs_1_ = f32[32,1,256]{2,1,0:T(1,128)S(1)} all-to-all(f32[32,1,256]{2,1,0:T(1,128)S(1)} %get-tuple-element.112), channel_id=1, replica_groups=mesh['grp'=4,'blk'=8] {'grp','blk'}, dimensions={0} | all-to-all | bytes 65536 | tf_op jit(solution)/shard_map/all_to_all | solution.py:295
  35.7 8.9 %all_to_all.82.refs_4_ = f32[32,1,256]{2,1,0:T(1,128)S(1)} all-to-all(f32[32,1,256]{2,1,0:T(1,128)S(1)} %shard_map.99), channel_id=1, replica_groups=mesh['grp'=4,'blk'=8] {'grp','blk'}, dimensions={0} | all-to-all | bytes 65536 | tf_op jit(solution)/shard_map/all_to_all | solution.py:295
  45.6 8.0 %all_to_all.83.summed = f32[8,1,256]{2,1,0:T(1,128)S(1)} all-to-all(f32[8,1,256]{2,1,0:T(1,128)S(1)} %shard_map.100), channel_id=1, replica_groups={{0,1,8,9,16,17,24,25},{2,3,10,11,18,19,26,27},{4,5,12,13,20,21,28,29},{..., dimensions={0} | all-to-all | bytes 16384 | tf_op jit(solution)/shard_map/all_to_all | solution.py:304
  53.6 1.2 shard_map.101
  56.0 9.8 %all_to_all.84.refs_1_ = f32[32,1,256]{2,1,0:T(1,128)S(1)} all-to-all(f32[32,1,256]{2,1,0:T(1,128)S(1)} %get-tuple-element.134), channel_id=1, replica_groups=mesh['grp'=4,'blk'=8] {'grp','blk'}, dimensions={0} | all-to-all | bytes 65536 | tf_op jit(solution)/shard_map/all_to_all | solution.py:295
  66.7 9.9 %all_to_all.85.refs_4_ = f32[32,1,256]{2,1,0:T(1,128)S(1)} all-to-all(f32[32,1,256]{2,1,0:T(1,128)S(1)} %shard_map.102), channel_id=1, replica_groups=mesh['grp'=4,'blk'=8] {'grp','blk'}, dimensions={0} | all-to-all | bytes 65536 | tf_op jit(solution)/shard_map/all_to_all | solution.py:295
  77.9 8.0 %all_to_all.86.refs_4_ = f32[8,1,256]{2,1,0:T(1,128)S(1)} all-to-all(f32[8,1,256]{2,1,0:T(1,128)S(1)} %shard_map.103), channel_id=1, replica_groups={{0,1,8,9,16,17,24,25},{2,3,10,11,18,19,26,27},{4,5,12,13,20,21,28,29},{..., dimensions={0} | all-to-all | bytes 16384 | tf_op jit(solution)/shard_map/all_to_all | solution.py:304
  86.4 8.0 %all_to_all.87.summed = f32[8,1,256]{2,1,0:T(1,128)S(1)} all-to-all(f32[8,1,256]{2,1,0:T(1,128)S(1)} %shard_map.104), channel_id=1, replica_groups={{0,1,8,9,16,17,24,25},{2,3,10,11,18,19,26,27},{4,5,12,13,20,21,28,29},{..., dimensions={0} | all-to-all | bytes 16384 | tf_op jit(solution)/shard_map/all_to_all | solution.py:304
  94.4 1.7 shard_map.105
  97.3 9.7 %all_to_all.88.refs_1_ = f32[32,1,256]{2,1,0:T(1,128)S(1)} all-to-all(f32[32,1,256]{2,1,0:T(1,128)S(1)} %get-tuple-element.162), channel_id=1, replica_groups=mesh['grp'=4,'blk'=8] {'grp','blk'}, dimensions={0} | all-to-all | bytes 65536 | tf_op jit(solution)/shard_map/all_to_all | solution.py:295
  108.0 8.9 %all_to_all.89.refs_4_ = f32[32,1,256]{2,1,0:T(1,128)S(1)} all-to-all(f32[32,1,256]{2,1,0:T(1,128)S(1)} %shard_map.106), channel_id=1, replica_groups=mesh['grp'=4,'blk'=8] {'grp','blk'}, dimensions={0} | all-to-all | bytes 65536 | tf_op jit(solution)/shard_map/all_to_all | solution.py:295
  117.9 8.0 %all_to_all.90.refs_4_ = f32[8,1,256]{2,1,0:T(1,128)S(1)} all-to-all(f32[8,1,256]{2,1,0:T(1,128)S(1)} %shard_map.107), channel_id=1, replica_groups={{0,1,8,9,16,17,24,25},{2,3,10,11,18,19,26,27},{4,5,12,13,20,21,28,29},{..., dimensions={0} | all-to-all | bytes 16384 | tf_op jit(solution)/shard_map/all_to_all | solution.py:304
  126.2 8.0 %all_to_all.91.summed.author_summed = f32[8,1,256]{2,1,0:T(1,128)S(1)} all-to-all(f32[8,1,256]{2,1,0:T(1,128)S(1)} %shard_map.108), channel_id=1, replica_groups={{0,1,8,9,16,17,24,25},{2,3,10,11,18,19,26,27},{4,5,12,13,20,21,28,29},{..., dimensions={0} | all-to-all | bytes 16384 | tf_op jit(solution)/shard_map/all_to_all | solution.py:304
  134.2 1.2 shard_map.109
  135.4 8.9 %all_to_all.92.refs_1_ = f32[32,1,256]{2,1,0:T(1,128)S(1)} all-to-all(f32[32,1,256]{2,1,0:T(1,128)S(1)} %get-tuple-element.189), channel_id=1, replica_groups=mesh['grp'=4,'blk'=8] {'grp','blk'}, dimensions={0} | all-to-all | bytes 65536 | tf_op jit(solution)/shard_map/all_to_all | solution.py:295
  144.5 8.9 %all_to_all.93.refs_1_ = f32[32,1,256]{2,1,0:T(1,128)S(1)} all-to-all(f32[32,1,256]{2,1,0:T(1,128)S(1)} %shard_map.110), channel_id=1, replica_groups=mesh['grp'=4,'blk'=8] {'grp','blk'}, dimensions={0} | all-to-all | bytes 65536 | tf_op jit(solution)/shard_map/all_to_all | solution.py:295
  153.7 8.9 %all_to_all.94.refs_1_ = f32[32,1,256]{2,1,0:T(1,128)S(1)} all-to-all(f32[32,1,256]{2,1,0:T(1,128)S(1)} %shard_map.111), channel_id=1, replica_groups=mesh['grp'=4,'blk'=8] {'grp','blk'}, dimensions={0} | all-to-all | bytes 65536 | tf_op jit(solution)/shard_map/all_to_all | solution.py:295
  162.9 8.9 %all_to_all.95.summed = f32[32,1,256]{2,1,0:T(1,128)S(1)} all-to-all(f32[32,1,256]{2,1,0:T(1,128)S(1)} %shard_map.112), channel_id=1, replica_groups=mesh['grp'=4,'blk'=8] {'grp','blk'}, dimensions={0} | all-to-all | bytes 65536 | tf_op jit(solution)/shard_map/all_to_all | solution.py:295
  171.9 1.3 shard_map.113
  (61 shorter events, 12.9 us)
Async XLA Ops:
  5.1 17.8 %collective-permute-start.1 = (bf16[2,336,128]{2,1,0:T(8,128)(2,1)S(1)}, bf16[2,336,128]{2,1,0:T(8,128)(2,1)S(1)}, u32[]{:S(2)}, u32[]{:S(2)}) collective-permute-start(bf16[2,336,128]{2,1,0:T(8,128)(2,1)S(1)} %get-tuple-element.108), channel_id=1, source_target_pairs={{0,2},{1,3},{2,0},{3,1},{4,6},{5,7},{6,4},{7,5},{8,10},{9,11},{10,... | collective-permute-start | bytes 516104 | tf_op jit(solution)/shard_map/ppermute | solution.py:356
  8.0 14.9 %collective-permute-start.2 = (bf16[2,336,128]{2,1,0:T(8,128)(2,1)S(1)}, bf16[2,336,128]{2,1,0:T(8,128)(2,1)S(1)}, u32[]{:S(2)}, u32[]{:S(2)}) collective-permute-start(bf16[2,336,128]{2,1,0:T(8,128)(2,1)S(1)} %get-tuple-element.109), channel_id=1, source_target_pairs={{0,4},{1,5},{2,6},{3,7},{4,0},{5,1},{6,2},{7,3},{8,12},{9,13},{10,... | collective-permute-start | bytes 516104 | tf_op jit(solution)/shard_map/ppermute | solution.py:356
  9.5 13.4 %collective-permute-start.3 = (bf16[2,336,128]{2,1,0:T(8,128)(2,1)S(1)}, bf16[2,336,128]{2,1,0:T(8,128)(2,1)S(1)}, u32[]{:S(2)}, u32[]{:S(2)}) collective-permute-start(bf16[2,336,128]{2,1,0:T(8,128)(2,1)S(1)} %get-tuple-element.110), channel_id=1, source_target_pairs={{0,6},{1,7},{2,4},{3,5},{4,2},{5,3},{6,0},{7,1},{8,14},{9,15},{10,... | collective-permute-start | bytes 516104 | tf_op jit(solution)/shard_map/ppermute | solution.py:356
  23.7 11.0 %collective-permute-start.5 = (f32[256,256]{1,0:T(8,128)S(1)}, f32[256,256]{1,0:T(8,128)S(1)}, u32[]{:S(2)}, u32[]{:S(2)}) collective-permute-start(f32[256,256]{1,0:T(8,128)S(1)} %get-tuple-element.128.refs_0_.rest_0_), channel_id=1, source_target_pairs={{0,4},{1,5},{2,6},{3,7},{4,0},{5,1},{6,2},{7,3},{8,12},{9,13},{10,... | collective-permute-start | bytes 786440 | tf_op jit(solution)/shard_map/ppermute | solution.py:366
  24.3 10.4 %collective-permute-start.4 = (f32[256,256]{1,0:T(8,128)S(1)}, f32[256,256]{1,0:T(8,128)S(1)}, u32[]{:S(2)}, u32[]{:S(2)}) collective-permute-start(f32[256,256]{1,0:T(8,128)S(1)} %get-tuple-element.128.refs_0_.rest_0_), channel_id=1, source_target_pairs={{0,2},{1,3},{2,0},{3,1},{4,6},{5,7},{6,4},{7,5},{8,10},{9,11},{10,... | collective-permute-start | bytes 786440 | tf_op jit(solution)/shard_map/ppermute | solution.py:366
  34.9 9.7 %collective-permute-start.6 = (f32[256,256]{1,0:T(8,128)S(1)}, f32[256,256]{1,0:T(8,128)S(1)}, u32[]{:S(2)}, u32[]{:S(2)}) collective-permute-start(f32[256,256]{1,0:T(8,128)S(1)} %get-tuple-element.128.refs_0_.rest_0_), channel_id=1, source_target_pairs={{0,1},{1,0},{2,3},{3,2},{4,5},{5,4},{6,7},{7,6},{8,9},{9,8},{10,11... | collective-permute-start | bytes 786440 | tf_op jit(solution)/shard_map/ppermute | solution.py:369
  35.1 9.5 %collective-permute-start.7 = (f32[256,256]{1,0:T(8,128)S(1)}, f32[256,256]{1,0:T(8,128)S(1)}, u32[]{:S(2)}, u32[]{:S(2)}) collective-permute-start(f32[256,256]{1,0:T(8,128)S(1)} %collective-permute-done.4.refs_1_.rest_1_), channel_id=1, source_target_pairs={{0,4},{1,5},{2,6},{3,7},{4,0},{5,1},{6,2},{7,3},{8,12},{9,13},{10,... | collective-permute-start | bytes 786440 | tf_op jit(solution)/shard_map/ppermute | solution.py:366
  44.9 8.7 %collective-permute-start.8 = (f32[256,256]{1,0:T(8,128)S(1)}, f32[256,256]{1,0:T(8,128)S(1)}, u32[]{:S(2)}, u32[]{:S(2)}) collective-permute-start(f32[256,256]{1,0:T(8,128)S(1)} %collective-permute-done.4.refs_1_.rest_1_), channel_id=1, source_target_pairs={{0,1},{1,0},{2,3},{3,2},{4,5},{5,4},{6,7},{7,6},{8,9},{9,8},{10,11... | collective-permute-start | bytes 786440 | tf_op jit(solution)/shard_map/ppermute | solution.py:369
  45.1 8.5 %collective-permute-start.9 = (f32[256,256]{1,0:T(8,128)S(1)}, f32[256,256]{1,0:T(8,128)S(1)}, u32[]{:S(2)}, u32[]{:S(2)}) collective-permute-start(f32[256,256]{1,0:T(8,128)S(1)} %collective-permute-done.5.refs_2_.rest_2_), channel_id=1, source_target_pairs={{0,1},{1,0},{2,3},{3,2},{4,5},{5,4},{6,7},{7,6},{8,9},{9,8},{10,11... | collective-permute-start | bytes 786440 | tf_op jit(solution)/shard_map/ppermute | solution.py:369
  45.5 8.1 %collective-permute-start.10 = (f32[256,256]{1,0:T(8,128)S(1)}, f32[256,256]{1,0:T(8,128)S(1)}, u32[]{:S(2)}, u32[]{:S(2)}) collective-permute-start(f32[256,256]{1,0:T(8,128)S(1)} %collective-permute-done.7.refs_3_.rest_3_), channel_id=1, source_target_pairs={{0,1},{1,0},{2,3},{3,2},{4,5},{5,4},{6,7},{7,6},{8,9},{9,8},{10,11... | collective-permute-start | bytes 786440 | tf_op jit(solution)/shard_map/ppermute | solution.py:369
  54.8 11.0 %collective-permute-start.12 = (bf16[640,256]{1,0:T(8,128)(2,1)S(1)}, bf16[640,256]{1,0:T(8,128)(2,1)S(1)}, u32[]{:S(2)}, u32[]{:S(2)}) collective-permute-start(bf16[640,256]{1,0:T(8,128)(2,1)S(1)} %get-tuple-element.153.refs_0_.rest_0_), channel_id=1, source_target_pairs={{0,4},{1,5},{2,6},{3,7},{4,0},{5,1},{6,2},{7,3},{8,12},{9,13},{10,... | collective-permute-start | bytes 983048 | tf_op jit(solution)/shard_map/ppermute | solution.py:366
  55.4 10.4 %collective-permute-start.11 = (bf16[640,256]{1,0:T(8,128)(2,1)S(1)}, bf16[640,256]{1,0:T(8,128)(2,1)S(1)}, u32[]{:S(2)}, u32[]{:S(2)}) collective-permute-start(bf16[640,256]{1,0:T(8,128)(2,1)S(1)} %get-tuple-element.153.refs_0_.rest_0_), channel_id=1, source_target_pairs={{0,2},{1,3},{2,0},{3,1},{4,6},{5,7},{6,4},{7,5},{8,10},{9,11},{10,... | collective-permute-start | bytes 983048 | tf_op jit(solution)/shard_map/ppermute | solution.py:366
  66.0 10.6 %collective-permute-start.13 = (bf16[640,256]{1,0:T(8,128)(2,1)S(1)}, bf16[640,256]{1,0:T(8,128)(2,1)S(1)}, u32[]{:S(2)}, u32[]{:S(2)}) collective-permute-start(bf16[640,256]{1,0:T(8,128)(2,1)S(1)} %get-tuple-element.153.refs_0_.rest_0_), channel_id=1, source_target_pairs={{0,1},{1,0},{2,3},{3,2},{4,5},{5,4},{6,7},{7,6},{8,9},{9,8},{10,11... | collective-permute-start | bytes 983048 | tf_op jit(solution)/shard_map/ppermute | solution.py:369
  66.2 10.4 %collective-permute-start.14 = (bf16[640,256]{1,0:T(8,128)(2,1)S(1)}, bf16[640,256]{1,0:T(8,128)(2,1)S(1)}, u32[]{:S(2)}, u32[]{:S(2)}) collective-permute-start(bf16[640,256]{1,0:T(8,128)(2,1)S(1)} %collective-permute-done.11.refs_1_.rest_1_), channel_id=1, source_target_pairs={{0,4},{1,5},{2,6},{3,7},{4,0},{5,1},{6,2},{7,3},{8,12},{9,13},{10,... | collective-permute-start | bytes 983048 | tf_op jit(solution)/shard_map/ppermute | solution.py:366
  77.2 8.6 %collective-permute-start.15 = (bf16[640,256]{1,0:T(8,128)(2,1)S(1)}, bf16[640,256]{1,0:T(8,128)(2,1)S(1)}, u32[]{:S(2)}, u32[]{:S(2)}) collective-permute-start(bf16[640,256]{1,0:T(8,128)(2,1)S(1)} %collective-permute-done.11.refs_1_.rest_1_), channel_id=1, source_target_pairs={{0,1},{1,0},{2,3},{3,2},{4,5},{5,4},{6,7},{7,6},{8,9},{9,8},{10,11... | collective-permute-start | bytes 983048 | tf_op jit(solution)/shard_map/ppermute | solution.py:369
  77.3 8.5 %collective-permute-start.16 = (bf16[640,256]{1,0:T(8,128)(2,1)S(1)}, bf16[640,256]{1,0:T(8,128)(2,1)S(1)}, u32[]{:S(2)}, u32[]{:S(2)}) collective-permute-start(bf16[640,256]{1,0:T(8,128)(2,1)S(1)} %collective-permute-done.12.refs_2_.rest_2_), channel_id=1, source_target_pairs={{0,1},{1,0},{2,3},{3,2},{4,5},{5,4},{6,7},{7,6},{8,9},{9,8},{10,11... | collective-permute-start | bytes 983048 | tf_op jit(solution)/shard_map/ppermute | solution.py:369
  77.8 8.0 %collective-permute-start.17 = (bf16[640,256]{1,0:T(8,128)(2,1)S(1)}, bf16[640,256]{1,0:T(8,128)(2,1)S(1)}, u32[]{:S(2)}, u32[]{:S(2)}) collective-permute-start(bf16[640,256]{1,0:T(8,128)(2,1)S(1)} %collective-permute-done.14.refs_3_.rest_3_), channel_id=1, source_target_pairs={{0,1},{1,0},{2,3},{3,2},{4,5},{5,4},{6,7},{7,6},{8,9},{9,8},{10,11... | collective-permute-start | bytes 983048 | tf_op jit(solution)/shard_map/ppermute | solution.py:369
  96.1 11.0 %collective-permute-start.19 = (f32[256,256]{1,0:T(8,128)S(1)}, f32[256,256]{1,0:T(8,128)S(1)}, u32[]{:S(2)}, u32[]{:S(2)}) collective-permute-start(f32[256,256]{1,0:T(8,128)S(1)} %get-tuple-element.180.refs_0_.rest_0_.own), channel_id=1, source_target_pairs={{0,4},{1,5},{2,6},{3,7},{4,0},{5,1},{6,2},{7,3},{8,12},{9,13},{10,... | collective-permute-start | bytes 786440 | tf_op jit(solution)/shard_map/ppermute | solution.py:366
  96.7 10.4 %collective-permute-start.18 = (f32[256,256]{1,0:T(8,128)S(1)}, f32[256,256]{1,0:T(8,128)S(1)}, u32[]{:S(2)}, u32[]{:S(2)}) collective-permute-start(f32[256,256]{1,0:T(8,128)S(1)} %get-tuple-element.180.refs_0_.rest_0_.own), channel_id=1, source_target_pairs={{0,2},{1,3},{2,0},{3,1},{4,6},{5,7},{6,4},{7,5},{8,10},{9,11},{10,... | collective-permute-start | bytes 786440 | tf_op jit(solution)/shard_map/ppermute | solution.py:366
  107.3 9.7 %collective-permute-start.20 = (f32[256,256]{1,0:T(8,128)S(1)}, f32[256,256]{1,0:T(8,128)S(1)}, u32[]{:S(2)}, u32[]{:S(2)}) collective-permute-start(f32[256,256]{1,0:T(8,128)S(1)} %get-tuple-element.180.refs_0_.rest_0_.own), channel_id=1, source_target_pairs={{0,1},{1,0},{2,3},{3,2},{4,5},{5,4},{6,7},{7,6},{8,9},{9,8},{10,11... | collective-permute-start | bytes 786440 | tf_op jit(solution)/shard_map/ppermute | solution.py:369
  107.5 9.5 %collective-permute-start.21 = (f32[256,256]{1,0:T(8,128)S(1)}, f32[256,256]{1,0:T(8,128)S(1)}, u32[]{:S(2)}, u32[]{:S(2)}) collective-permute-start(f32[256,256]{1,0:T(8,128)S(1)} %collective-permute-done.18.refs_1_.rest_1_), channel_id=1, source_target_pairs={{0,4},{1,5},{2,6},{3,7},{4,0},{5,1},{6,2},{7,3},{8,12},{9,13},{10,... | collective-permute-start | bytes 786440 | tf_op jit(solution)/shard_map/ppermute | solution.py:366
  117.3 8.7 %collective-permute-start.22 = (f32[256,256]{1,0:T(8,128)S(1)}, f32[256,256]{1,0:T(8,128)S(1)}, u32[]{:S(2)}, u32[]{:S(2)}) collective-permute-start(f32[256,256]{1,0:T(8,128)S(1)} %collective-permute-done.18.refs_1_.rest_1_), channel_id=1, source_target_pairs={{0,1},{1,0},{2,3},{3,2},{4,5},{5,4},{6,7},{7,6},{8,9},{9,8},{10,11... | collective-permute-start | bytes 786440 | tf_op jit(solution)/shard_map/ppermute | solution.py:369
  117.4 8.5 %collective-permute-start.23 = (f32[256,256]{1,0:T(8,128)S(1)}, f32[256,256]{1,0:T(8,128)S(1)}, u32[]{:S(2)}, u32[]{:S(2)}) collective-permute-start(f32[256,256]{1,0:T(8,128)S(1)} %collective-permute-done.19.refs_2_.rest_2_), channel_id=1, source_target_pairs={{0,1},{1,0},{2,3},{3,2},{4,5},{5,4},{6,7},{7,6},{8,9},{9,8},{10,11... | collective-permute-start | bytes 786440 | tf_op jit(solution)/shard_map/ppermute | solution.py:369
  117.8 8.1 %collective-permute-start.24 = (f32[256,256]{1,0:T(8,128)S(1)}, f32[256,256]{1,0:T(8,128)S(1)}, u32[]{:S(2)}, u32[]{:S(2)}) collective-permute-start(f32[256,256]{1,0:T(8,128)S(1)} %collective-permute-done.21.refs_3_.rest_3_), channel_id=1, source_target_pairs={{0,1},{1,0},{2,3},{3,2},{4,5},{5,4},{6,7},{7,6},{8,9},{9,8},{10,11... | collective-permute-start | bytes 786440 | tf_op jit(solution)/shard_map/ppermute | solution.py:369
  (1 other events, 1.8 us)

commit v15 on v14

--- a/solution.py
+++ b/solution.py
@@ -68,6 +68,20 @@
     wide = jnp.pad(wide, ((0, -len(lines) % 8), (0, -rows % LANES)))
     columns = wide.T
     return [columns[:rows, i : i + 1] for i in range(len(lines))]
+
+
+def code_column(line, classes):
+    rows = line.shape[1]
+    across = lax.broadcasted_iota(jnp.int32, (rows, rows), 1)
+    eye = jnp.where(lax.broadcasted_iota(jnp.int32, (rows, rows), 0) == across, 1.0, 0.0)
+    wide = jnp.broadcast_to(line, (LANES, rows)).astype(jnp.bfloat16)
+    column = lax.dot_general(
+        eye.astype(jnp.bfloat16),
+        wide,
+        (((1,), (1,)), ((), ())),
+        preferred_element_type=jnp.float32,
+    )
+    return jnp.concatenate([column] * (classes // LANES), axis=1)
 
 
 def seeds_of(line, classes):
@@ -273,9 +287,9 @@
     copies = [pltpu.make_async_copy(scores_made, scores, left.at[0])]
     copies[0].start()
     scale_cols = col_scale(summed, class_target)
-    codes = code_columns(code_lines(seed_class, train_mask, rows))
     lane = lax.broadcasted_iota(jnp.int32, (rows, classes), 1).astype(jnp.float32)
-    for paper, code in enumerate(codes):
+    for paper, line in enumerate(code_lines(seed_class, train_mask, rows)):
+        code = code_column(line, classes)
         part = pl.ds(paper * rows, rows)
         scaled = kernel_ref[part, :] * scale_cols
         share = scaled * (1.0 / jnp.sum(scaled, axis=1, keepdims=True))
@@ -295,11 +309,12 @@
     return lax.all_to_all(parts, AXES, split_axis=0, concat_axis=0, tiled=True)
 
 
-def narrow_exchange(parts):
+def narrow_exchange(parts, sides):
     groups, blocks = lax.axis_size("grp"), lax.axis_size("blk")
+    planes = sorted(range(groups), key=lambda i: abs(2 * i + 1 - groups))
     sets = [
-        [i * blocks + pair + side for i in range(groups) for side in range(2)]
-        for pair in range(0, blocks, 2)
+        [i * blocks + first + side for i in planes for side in range(sides)]
+        for first in range(0, blocks, sides)
     ]
     return lax.all_to_all(
         parts, AXES, split_axis=0, concat_axis=0, axis_index_groups=sets, tiled=True
@@ -358,7 +373,6 @@
     ]
     summed = exchange(local)
 
-    narrow = shape((2 * lax.axis_size("grp"), 1, classes), f32)
     author_out = (shape((authors, classes), f32), parts)
     paper_out = (shape((papers, classes), f32), parts, shape((papers, classes), bf16))
 
@@ -370,6 +384,7 @@
 
     def balance(kernel, sent, local, count):
         here, there = {0: sent}, {}
+        sides = 0
         for step in range(count):
             if step == 0:
                 moves = [(here, k, across_pairs(sent, k)) for k in (1, 2) if k < blocks // 2]
@@ -380,15 +395,22 @@
                     moves.append((here, k, got))
             else:
                 moves = [(there, k, to_other(here[k])) for k in here if k not in there]
-            summed = narrow_exchange(local) if step > 1 else exchange(local)
+            summed = narrow_exchange(local, sides) if sides else exchange(local)
             summed, *moved = lax.optimization_barrier((summed, *(one for _, _, one in moves)))
             for (place, k, _), one in zip(moves, moved):
                 place[k] = one
             if step + 1 < count:
-                rest = [here[k] for k in range(blocks // 2)] if step > 0 else [kernel]
+                added, size = [kernel], devices
+                if step > 0:
+                    added = list(here.values())
+                    sides = 2
+                    if step > 1:
+                        added += list(there.values())
+                        sides = 1
+                    size = sides * lax.axis_size("grp")
                 local = call(
-                    balance_kernel, narrow if step > 0 else parts, [VMEM] * (len(rest) + 2)
-                )(*rest, summed, target)
+                    balance_kernel, shape((size, 1, classes), f32), [VMEM] * (len(added) + 2)
+                )(*added, summed, target)
                 local, sent, *moved = lax.optimization_barrier((local, sent, *here.values()))
                 here = dict(zip(here, moved))
         order = range(blocks // 2)

time: 174 us -> 172 us (0.989)
  blocking collectives: 146 us -> 144 us
    all_to_all x5, blocking collectives: 39.8 us -> 36.2 us  [narrow_exchange(): lax.all_to_all(parts, AXES, split_axis=0, concat_axis=0, axis_index_group...]
where the time goes in v15:
time: 172 us
  blocking collectives  144 us (84%)
  Pallas kernels  13.1 us (8%)
  starting transfers between devices  13 us (8%)
    all_to_all x11, blocking collectives, exchange(): return lax.all_to_all(parts, AXES, split_axis=0, concat_axis=0, tiled=True)  108 us
    all_to_all x5, blocking collectives, narrow_exchange(): lax.all_to_all(parts, AXES, split_axis=0, concat_axis=0, axis_index_group...  36.2 us
    ppermute x9, starting transfers between devices, across_pairs(): return lax.ppermute(value, 'blk', [(i, i ^ 2 * k) for i in range(blocks)])  5.42 us
    ppermute x3, starting transfers between devices, on_device(): lax.ppermute(one, 'blk', [(i, i ^ 2 * k) for i in range(blocks)])  4.47 us
  transfers between devices with their start and end apart: 25, of which 1 were waited for; matrix products, arithmetic and copies ran while one was open for 0% of the time, Pallas kernels for 1%

profile of v15, /device:TPU:0, one launch (start us, length us, event | category | flops | bytes accessed | tf_op | source)
XLA Modules:
  0.0 171.8 jit_solution(7138808679375764086)
XLA Ops:
  1.3 1.9 %shard_map.95 = (s32[8]{0:T(128)S(1)}, s32[8]{0:T(128)S(1)}, s32[5,128]{1,0:T(8,128)S(1)}, s32[5,128]{1,0:T(8,128)S(1)}, f32[1,256]{1,0:T(1,128)S(1)}, /*index=5...) custom-call(s32[1]{0:T(128)S(6)} %copy.10.tile_count, ...), custom_call_target="tpu_custom_call" | custom-call | tf_op jit(solution)/shard_map/pallas_call | solution.py:355
  5.1 2.9 %collective-permute-start.1 = (bf16[2,336,128]{2,1,0:T(8,128)(2,1)S(1)}, bf16[2,336,128]{2,1,0:T(8,128)(2,1)S(1)}, u32[]{:S(2)}, u32[]{:S(2)}) collective-permute-start(bf16[2,336,128]{2,1,0:T(8,128)(2,1)S(1)} %get-tuple-element.108), channel_id=1, source_target_pairs={{0,2},{1,3},{2,0},{3,1},{4,6},{5,7},{6,4},{7,5},{8,10},{9,11},{10,... | collective-permute-start | bytes 516104 | tf_op jit(solution)/shard_map/ppermute | solution.py:371
  8.0 1.5 collective-permute-start.2
  9.5 13.4 %all_to_all.80.summed = f32[32,1,256]{2,1,0:T(1,128)S(1)} all-to-all(f32[32,1,256]{2,1,0:T(1,128)S(1)} %shard_map.96), channel_id=1, replica_groups=mesh['grp'=4,'blk'=8] {'grp','blk'}, dimensions={0} | all-to-all | bytes 65536 | tf_op jit(solution)/shard_map/all_to_all | solution.py:309
  25.0 9.8 %all_to_all.81.refs_1_ = f32[32,1,256]{2,1,0:T(1,128)S(1)} all-to-all(f32[32,1,256]{2,1,0:T(1,128)S(1)} %get-tuple-element.112), channel_id=1, replica_groups=mesh['grp'=4,'blk'=8] {'grp','blk'}, dimensions={0} | all-to-all | bytes 65536 | tf_op jit(solution)/shard_map/all_to_all | solution.py:309
  35.7 8.9 %all_to_all.82.refs_4_ = f32[32,1,256]{2,1,0:T(1,128)S(1)} all-to-all(f32[32,1,256]{2,1,0:T(1,128)S(1)} %shard_map.99), channel_id=1, replica_groups=mesh['grp'=4,'blk'=8] {'grp','blk'}, dimensions={0} | all-to-all | bytes 65536 | tf_op jit(solution)/shard_map/all_to_all | solution.py:309
  45.6 7.3 %all_to_all.83.summed = f32[8,1,256]{2,1,0:T(1,128)S(1)} all-to-all(f32[8,1,256]{2,1,0:T(1,128)S(1)} %shard_map.100), channel_id=1, replica_groups={{8,9,16,17,0,1,24,25},{10,11,18,19,2,3,26,27},{12,13,20,21,4,5,28,29},{..., dimensions={0} | all-to-all | bytes 16384 | tf_op jit(solution)/shard_map/all_to_all | solution.py:319
  52.9 1.2 shard_map.101
  55.3 10.6 %all_to_all.84.refs_1_ = f32[32,1,256]{2,1,0:T(1,128)S(1)} all-to-all(f32[32,1,256]{2,1,0:T(1,128)S(1)} %get-tuple-element.134), channel_id=1, replica_groups=mesh['grp'=4,'blk'=8] {'grp','blk'}, dimensions={0} | all-to-all | bytes 65536 | tf_op jit(solution)/shard_map/all_to_all | solution.py:309
  66.9 9.9 %all_to_all.85.refs_4_ = f32[32,1,256]{2,1,0:T(1,128)S(1)} all-to-all(f32[32,1,256]{2,1,0:T(1,128)S(1)} %shard_map.102), channel_id=1, replica_groups=mesh['grp'=4,'blk'=8] {'grp','blk'}, dimensions={0} | all-to-all | bytes 65536 | tf_op jit(solution)/shard_map/all_to_all | solution.py:309
  78.1 7.3 %all_to_all.86.refs_8_ = f32[8,1,256]{2,1,0:T(1,128)S(1)} all-to-all(f32[8,1,256]{2,1,0:T(1,128)S(1)} %shard_map.103), channel_id=1, replica_groups={{8,9,16,17,0,1,24,25},{10,11,18,19,2,3,26,27},{12,13,20,21,4,5,28,29},{..., dimensions={0} | all-to-all | bytes 16384 | tf_op jit(solution)/shard_map/all_to_all | solution.py:319
  85.3 1.1 shard_map.104
  86.4 7.2 %all_to_all.87.summed = f32[4,1,256]{2,1,0:T(1,128)S(1)} all-to-all(f32[4,1,256]{2,1,0:T(1,128)S(1)} %shard_map.104), channel_id=1, replica_groups={{8,16,0,24},{9,17,1,25},{10,18,2,26},{11,19,3,27},{12,20,4,28},{13,21,5..., dimensions={0} | all-to-all | bytes 8192 | tf_op jit(solution)/shard_map/all_to_all | solution.py:319
  93.7 1.7 shard_map.105
  96.6 10.6 %all_to_all.88.refs_1_ = f32[32,1,256]{2,1,0:T(1,128)S(1)} all-to-all(f32[32,1,256]{2,1,0:T(1,128)S(1)} %get-tuple-element.162), channel_id=1, replica_groups=mesh['grp'=4,'blk'=8] {'grp','blk'}, dimensions={0} | all-to-all | bytes 65536 | tf_op jit(solution)/shard_map/all_to_all | solution.py:309
  108.1 8.9 %all_to_all.89.refs_4_ = f32[32,1,256]{2,1,0:T(1,128)S(1)} all-to-all(f32[32,1,256]{2,1,0:T(1,128)S(1)} %shard_map.106), channel_id=1, replica_groups=mesh['grp'=4,'blk'=8] {'grp','blk'}, dimensions={0} | all-to-all | bytes 65536 | tf_op jit(solution)/shard_map/all_to_all | solution.py:309
  118.1 7.3 %all_to_all.90.refs_8_ = f32[8,1,256]{2,1,0:T(1,128)S(1)} all-to-all(f32[8,1,256]{2,1,0:T(1,128)S(1)} %shard_map.107), channel_id=1, replica_groups={{8,9,16,17,0,1,24,25},{10,11,18,19,2,3,26,27},{12,13,20,21,4,5,28,29},{..., dimensions={0} | all-to-all | bytes 16384 | tf_op jit(solution)/shard_map/all_to_all | solution.py:319
  125.7 7.2 %all_to_all.91.summed.author_summed = f32[4,1,256]{2,1,0:T(1,128)S(1)} all-to-all(f32[4,1,256]{2,1,0:T(1,128)S(1)} %shard_map.108), channel_id=1, replica_groups={{8,16,0,24},{9,17,1,25},{10,18,2,26},{11,19,3,27},{12,20,4,28},{13,21,5..., dimensions={0} | all-to-all | bytes 8192 | tf_op jit(solution)/shard_map/all_to_all | solution.py:319
  133.0 1.2 shard_map.109
  134.2 8.9 %all_to_all.92.refs_1_ = f32[32,1,256]{2,1,0:T(1,128)S(1)} all-to-all(f32[32,1,256]{2,1,0:T(1,128)S(1)} %get-tuple-element.189), channel_id=1, replica_groups=mesh['grp'=4,'blk'=8] {'grp','blk'}, dimensions={0} | all-to-all | bytes 65536 | tf_op jit(solution)/shard_map/all_to_all | solution.py:309
  143.4 8.9 %all_to_all.93.refs_1_ = f32[32,1,256]{2,1,0:T(1,128)S(1)} all-to-all(f32[32,1,256]{2,1,0:T(1,128)S(1)} %shard_map.110), channel_id=1, replica_groups=mesh['grp'=4,'blk'=8] {'grp','blk'}, dimensions={0} | all-to-all | bytes 65536 | tf_op jit(solution)/shard_map/all_to_all | solution.py:309
  152.5 8.9 %all_to_all.94.refs_1_ = f32[32,1,256]{2,1,0:T(1,128)S(1)} all-to-all(f32[32,1,256]{2,1,0:T(1,128)S(1)} %shard_map.111), channel_id=1, replica_groups=mesh['grp'=4,'blk'=8] {'grp','blk'}, dimensions={0} | all-to-all | bytes 65536 | tf_op jit(solution)/shard_map/all_to_all | solution.py:309
  161.7 8.9 %all_to_all.95.summed = f32[32,1,256]{2,1,0:T(1,128)S(1)} all-to-all(f32[32,1,256]{2,1,0:T(1,128)S(1)} %shard_map.112), channel_id=1, replica_groups=mesh['grp'=4,'blk'=8] {'grp','blk'}, dimensions={0} | all-to-all | bytes 65536 | tf_op jit(solution)/shard_map/all_to_all | solution.py:309
  170.7 1.1 shard_map.113
  (61 shorter events, 13.6 us)
Async XLA Ops:
  5.1 17.8 %collective-permute-start.1 = (bf16[2,336,128]{2,1,0:T(8,128)(2,1)S(1)}, bf16[2,336,128]{2,1,0:T(8,128)(2,1)S(1)}, u32[]{:S(2)}, u32[]{:S(2)}) collective-permute-start(bf16[2,336,128]{2,1,0:T(8,128)(2,1)S(1)} %get-tuple-element.108), channel_id=1, source_target_pairs={{0,2},{1,3},{2,0},{3,1},{4,6},{5,7},{6,4},{7,5},{8,10},{9,11},{10,... | collective-permute-start | bytes 516104 | tf_op jit(solution)/shard_map/ppermute | solution.py:371
  8.0 14.9 %collective-permute-start.2 = (bf16[2,336,128]{2,1,0:T(8,128)(2,1)S(1)}, bf16[2,336,128]{2,1,0:T(8,128)(2,1)S(1)}, u32[]{:S(2)}, u32[]{:S(2)}) collective-permute-start(bf16[2,336,128]{2,1,0:T(8,128)(2,1)S(1)} %get-tuple-element.109), channel_id=1, source_target_pairs={{0,4},{1,5},{2,6},{3,7},{4,0},{5,1},{6,2},{7,3},{8,12},{9,13},{10,... | collective-permute-start | bytes 516104 | tf_op jit(solution)/shard_map/ppermute | solution.py:371
  9.5 13.4 %collective-permute-start.3 = (bf16[2,336,128]{2,1,0:T(8,128)(2,1)S(1)}, bf16[2,336,128]{2,1,0:T(8,128)(2,1)S(1)}, u32[]{:S(2)}, u32[]{:S(2)}) collective-permute-start(bf16[2,336,128]{2,1,0:T(8,128)(2,1)S(1)} %get-tuple-element.110), channel_id=1, source_target_pairs={{0,6},{1,7},{2,4},{3,5},{4,2},{5,3},{6,0},{7,1},{8,14},{9,15},{10,... | collective-permute-start | bytes 516104 | tf_op jit(solution)/shard_map/ppermute | solution.py:371
  23.7 11.0 %collective-permute-start.5 = (f32[256,256]{1,0:T(8,128)S(1)}, f32[256,256]{1,0:T(8,128)S(1)}, u32[]{:S(2)}, u32[]{:S(2)}) collective-permute-start(f32[256,256]{1,0:T(8,128)S(1)} %get-tuple-element.128.refs_0_.rest_0_), channel_id=1, source_target_pairs={{0,4},{1,5},{2,6},{3,7},{4,0},{5,1},{6,2},{7,3},{8,12},{9,13},{10,... | collective-permute-start | bytes 786440 | tf_op jit(solution)/shard_map/ppermute | solution.py:380
  24.4 10.4 %collective-permute-start.4 = (f32[256,256]{1,0:T(8,128)S(1)}, f32[256,256]{1,0:T(8,128)S(1)}, u32[]{:S(2)}, u32[]{:S(2)}) collective-permute-start(f32[256,256]{1,0:T(8,128)S(1)} %get-tuple-element.128.refs_0_.rest_0_), channel_id=1, source_target_pairs={{0,2},{1,3},{2,0},{3,1},{4,6},{5,7},{6,4},{7,5},{8,10},{9,11},{10,... | collective-permute-start | bytes 786440 | tf_op jit(solution)/shard_map/ppermute | solution.py:380
  34.9 9.7 %collective-permute-start.6 = (f32[256,256]{1,0:T(8,128)S(1)}, f32[256,256]{1,0:T(8,128)S(1)}, u32[]{:S(2)}, u32[]{:S(2)}) collective-permute-start(f32[256,256]{1,0:T(8,128)S(1)} %get-tuple-element.128.refs_0_.rest_0_), channel_id=1, source_target_pairs={{0,1},{1,0},{2,3},{3,2},{4,5},{5,4},{6,7},{7,6},{8,9},{9,8},{10,11... | collective-permute-start | bytes 786440 | tf_op jit(solution)/shard_map/ppermute | solution.py:383
  35.1 9.5 %collective-permute-start.7 = (f32[256,256]{1,0:T(8,128)S(1)}, f32[256,256]{1,0:T(8,128)S(1)}, u32[]{:S(2)}, u32[]{:S(2)}) collective-permute-start(f32[256,256]{1,0:T(8,128)S(1)} %collective-permute-done.4.refs_1_.rest_1_), channel_id=1, source_target_pairs={{0,4},{1,5},{2,6},{3,7},{4,0},{5,1},{6,2},{7,3},{8,12},{9,13},{10,... | collective-permute-start | bytes 786440 | tf_op jit(solution)/shard_map/ppermute | solution.py:380
  44.9 7.9 %collective-permute-start.8 = (f32[256,256]{1,0:T(8,128)S(1)}, f32[256,256]{1,0:T(8,128)S(1)}, u32[]{:S(2)}, u32[]{:S(2)}) collective-permute-start(f32[256,256]{1,0:T(8,128)S(1)} %collective-permute-done.4.refs_1_.rest_1_), channel_id=1, source_target_pairs={{0,1},{1,0},{2,3},{3,2},{4,5},{5,4},{6,7},{7,6},{8,9},{9,8},{10,11... | collective-permute-start | bytes 786440 | tf_op jit(solution)/shard_map/ppermute | solution.py:383
  45.1 7.8 %collective-permute-start.9 = (f32[256,256]{1,0:T(8,128)S(1)}, f32[256,256]{1,0:T(8,128)S(1)}, u32[]{:S(2)}, u32[]{:S(2)}) collective-permute-start(f32[256,256]{1,0:T(8,128)S(1)} %collective-permute-done.5.refs_2_.rest_2_), channel_id=1, source_target_pairs={{0,1},{1,0},{2,3},{3,2},{4,5},{5,4},{6,7},{7,6},{8,9},{9,8},{10,11... | collective-permute-start | bytes 786440 | tf_op jit(solution)/shard_map/ppermute | solution.py:383
  45.5 7.4 %collective-permute-start.10 = (f32[256,256]{1,0:T(8,128)S(1)}, f32[256,256]{1,0:T(8,128)S(1)}, u32[]{:S(2)}, u32[]{:S(2)}) collective-permute-start(f32[256,256]{1,0:T(8,128)S(1)} %collective-permute-done.7.refs_3_.rest_3_), channel_id=1, source_target_pairs={{0,1},{1,0},{2,3},{3,2},{4,5},{5,4},{6,7},{7,6},{8,9},{9,8},{10,11... | collective-permute-start | bytes 786440 | tf_op jit(solution)/shard_map/ppermute | solution.py:383
  54.1 11.9 %collective-permute-start.12 = (bf16[640,256]{1,0:T(8,128)(2,1)S(1)}, bf16[640,256]{1,0:T(8,128)(2,1)S(1)}, u32[]{:S(2)}, u32[]{:S(2)}) collective-permute-start(bf16[640,256]{1,0:T(8,128)(2,1)S(1)} %get-tuple-element.157.refs_0_.rest_0_), channel_id=1, source_target_pairs={{0,4},{1,5},{2,6},{3,7},{4,0},{5,1},{6,2},{7,3},{8,12},{9,13},{10,... | collective-permute-start | bytes 983048 | tf_op jit(solution)/shard_map/ppermute | solution.py:380
  54.7 11.3 %collective-permute-start.11 = (bf16[640,256]{1,0:T(8,128)(2,1)S(1)}, bf16[640,256]{1,0:T(8,128)(2,1)S(1)}, u32[]{:S(2)}, u32[]{:S(2)}) collective-permute-start(bf16[640,256]{1,0:T(8,128)(2,1)S(1)} %get-tuple-element.157.refs_0_.rest_0_), channel_id=1, source_target_pairs={{0,2},{1,3},{2,0},{3,1},{4,6},{5,7},{6,4},{7,5},{8,10},{9,11},{10,... | collective-permute-start | bytes 983048 | tf_op jit(solution)/shard_map/ppermute | solution.py:380
  66.2 10.6 %collective-permute-start.13 = (bf16[640,256]{1,0:T(8,128)(2,1)S(1)}, bf16[640,256]{1,0:T(8,128)(2,1)S(1)}, u32[]{:S(2)}, u32[]{:S(2)}) collective-permute-start(bf16[640,256]{1,0:T(8,128)(2,1)S(1)} %get-tuple-element.157.refs_0_.rest_0_), channel_id=1, source_target_pairs={{0,1},{1,0},{2,3},{3,2},{4,5},{5,4},{6,7},{7,6},{8,9},{9,8},{10,11... | collective-permute-start | bytes 983048 | tf_op jit(solution)/shard_map/ppermute | solution.py:383
  66.4 10.4 %collective-permute-start.14 = (bf16[640,256]{1,0:T(8,128)(2,1)S(1)}, bf16[640,256]{1,0:T(8,128)(2,1)S(1)}, u32[]{:S(2)}, u32[]{:S(2)}) collective-permute-start(bf16[640,256]{1,0:T(8,128)(2,1)S(1)} %collective-permute-done.11.refs_1_.rest_1_), channel_id=1, source_target_pairs={{0,4},{1,5},{2,6},{3,7},{4,0},{5,1},{6,2},{7,3},{8,12},{9,13},{10,... | collective-permute-start | bytes 983048 | tf_op jit(solution)/shard_map/ppermute | solution.py:380
  77.4 7.9 %collective-permute-start.15 = (bf16[640,256]{1,0:T(8,128)(2,1)S(1)}, bf16[640,256]{1,0:T(8,128)(2,1)S(1)}, u32[]{:S(2)}, u32[]{:S(2)}) collective-permute-start(bf16[640,256]{1,0:T(8,128)(2,1)S(1)} %collective-permute-done.11.refs_1_.rest_1_), channel_id=1, source_target_pairs={{0,1},{1,0},{2,3},{3,2},{4,5},{5,4},{6,7},{7,6},{8,9},{9,8},{10,11... | collective-permute-start | bytes 983048 | tf_op jit(solution)/shard_map/ppermute | solution.py:383
  77.5 7.8 %collective-permute-start.16 = (bf16[640,256]{1,0:T(8,128)(2,1)S(1)}, bf16[640,256]{1,0:T(8,128)(2,1)S(1)}, u32[]{:S(2)}, u32[]{:S(2)}) collective-permute-start(bf16[640,256]{1,0:T(8,128)(2,1)S(1)} %collective-permute-done.12.refs_2_.rest_2_), channel_id=1, source_target_pairs={{0,1},{1,0},{2,3},{3,2},{4,5},{5,4},{6,7},{7,6},{8,9},{9,8},{10,11... | collective-permute-start | bytes 983048 | tf_op jit(solution)/shard_map/ppermute | solution.py:383
  78.0 7.4 %collective-permute-start.17 = (bf16[640,256]{1,0:T(8,128)(2,1)S(1)}, bf16[640,256]{1,0:T(8,128)(2,1)S(1)}, u32[]{:S(2)}, u32[]{:S(2)}) collective-permute-start(bf16[640,256]{1,0:T(8,128)(2,1)S(1)} %collective-permute-done.14.refs_3_.rest_3_), channel_id=1, source_target_pairs={{0,1},{1,0},{2,3},{3,2},{4,5},{5,4},{6,7},{7,6},{8,9},{9,8},{10,11... | collective-permute-start | bytes 983048 | tf_op jit(solution)/shard_map/ppermute | solution.py:383
  95.4 11.9 %collective-permute-start.19 = (f32[256,256]{1,0:T(8,128)S(1)}, f32[256,256]{1,0:T(8,128)S(1)}, u32[]{:S(2)}, u32[]{:S(2)}) collective-permute-start(f32[256,256]{1,0:T(8,128)S(1)} %get-tuple-element.184.refs_0_.rest_0_.own), channel_id=1, source_target_pairs={{0,4},{1,5},{2,6},{3,7},{4,0},{5,1},{6,2},{7,3},{8,12},{9,13},{10,... | collective-permute-start | bytes 786440 | tf_op jit(solution)/shard_map/ppermute | solution.py:380
  96.0 11.2 %collective-permute-start.18 = (f32[256,256]{1,0:T(8,128)S(1)}, f32[256,256]{1,0:T(8,128)S(1)}, u32[]{:S(2)}, u32[]{:S(2)}) collective-permute-start(f32[256,256]{1,0:T(8,128)S(1)} %get-tuple-element.184.refs_0_.rest_0_.own), channel_id=1, source_target_pairs={{0,2},{1,3},{2,0},{3,1},{4,6},{5,7},{6,4},{7,5},{8,10},{9,11},{10,... | collective-permute-start | bytes 786440 | tf_op jit(solution)/shard_map/ppermute | solution.py:380
  107.4 9.7 %collective-permute-start.20 = (f32[256,256]{1,0:T(8,128)S(1)}, f32[256,256]{1,0:T(8,128)S(1)}, u32[]{:S(2)}, u32[]{:S(2)}) collective-permute-start(f32[256,256]{1,0:T(8,128)S(1)} %get-tuple-element.184.refs_0_.rest_0_.own), channel_id=1, source_target_pairs={{0,1},{1,0},{2,3},{3,2},{4,5},{5,4},{6,7},{7,6},{8,9},{9,8},{10,11... | collective-permute-start | bytes 786440 | tf_op jit(solution)/shard_map/ppermute | solution.py:383
  107.6 9.5 %collective-permute-start.21 = (f32[256,256]{1,0:T(8,128)S(1)}, f32[256,256]{1,0:T(8,128)S(1)}, u32[]{:S(2)}, u32[]{:S(2)}) collective-permute-start(f32[256,256]{1,0:T(8,128)S(1)} %collective-permute-done.18.refs_1_.rest_1_), channel_id=1, source_target_pairs={{0,4},{1,5},{2,6},{3,7},{4,0},{5,1},{6,2},{7,3},{8,12},{9,13},{10,... | collective-permute-start | bytes 786440 | tf_op jit(solution)/shard_map/ppermute | solution.py:380
  117.4 7.9 %collective-permute-start.22 = (f32[256,256]{1,0:T(8,128)S(1)}, f32[256,256]{1,0:T(8,128)S(1)}, u32[]{:S(2)}, u32[]{:S(2)}) collective-permute-start(f32[256,256]{1,0:T(8,128)S(1)} %collective-permute-done.18.refs_1_.rest_1_), channel_id=1, source_target_pairs={{0,1},{1,0},{2,3},{3,2},{4,5},{5,4},{6,7},{7,6},{8,9},{9,8},{10,11... | collective-permute-start | bytes 786440 | tf_op jit(solution)/shard_map/ppermute | solution.py:383
  117.6 7.8 %collective-permute-start.23 = (f32[256,256]{1,0:T(8,128)S(1)}, f32[256,256]{1,0:T(8,128)S(1)}, u32[]{:S(2)}, u32[]{:S(2)}) collective-permute-start(f32[256,256]{1,0:T(8,128)S(1)} %collective-permute-done.19.refs_2_.rest_2_), channel_id=1, source_target_pairs={{0,1},{1,0},{2,3},{3,2},{4,5},{5,4},{6,7},{7,6},{8,9},{9,8},{10,11... | collective-permute-start | bytes 786440 | tf_op jit(solution)/shard_map/ppermute | solution.py:383
  118.0 7.4 %collective-permute-start.24 = (f32[256,256]{1,0:T(8,128)S(1)}, f32[256,256]{1,0:T(8,128)S(1)}, u32[]{:S(2)}, u32[]{:S(2)}) collective-permute-start(f32[256,256]{1,0:T(8,128)S(1)} %collective-permute-done.21.refs_3_.rest_3_), channel_id=1, source_target_pairs={{0,1},{1,0},{2,3},{3,2},{4,5},{5,4},{6,7},{7,6},{8,9},{9,8},{10,11... | collective-permute-start | bytes 786440 | tf_op jit(solution)/shard_map/ppermute | solution.py:383
  (1 other events, 1.8 us)

commit v16 on v15

--- a/solution.py
+++ b/solution.py
@@ -311,9 +311,9 @@
 
 def narrow_exchange(parts, sides):
     groups, blocks = lax.axis_size("grp"), lax.axis_size("blk")
-    planes = sorted(range(groups), key=lambda i: abs(2 * i + 1 - groups))
+    planes = sorted(reversed(range(groups)), key=lambda i: abs(2 * i + 1 - groups))
     sets = [
-        [i * blocks + first + side for i in planes for side in range(sides)]
+        [i * blocks + first + side for i in planes for side in reversed(range(sides))]
         for first in range(0, blocks, sides)
     ]
     return lax.all_to_all(

time: 172 us -> 174 us (1.012)
  blocking collectives: 144 us -> 146 us
    all_to_all x11, blocking collectives: 108 us -> 111 us  [exchange(): return lax.all_to_all(parts, AXES, split_axis=0, concat_axis=0, tiled=True)]
where the time goes in v16:
time: 174 us
  blocking collectives  146 us (84%)
  Pallas kernels  13.1 us (8%)
  starting transfers between devices  13 us (7%)
    all_to_all x11, blocking collectives, exchange(): return lax.all_to_all(parts, AXES, split_axis=0, concat_axis=0, tiled=True)  111 us
    all_to_all x5, blocking collectives, narrow_exchange(): lax.all_to_all(parts, AXES, split_axis=0, concat_axis=0, axis_index_group...  35.4 us
    ppermute x9, starting transfers between devices, across_pairs(): return lax.ppermute(value, 'blk', [(i, i ^ 2 * k) for i in range(blocks)])  5.43 us
    ppermute x3, starting transfers between devices, on_device(): lax.ppermute(one, 'blk', [(i, i ^ 2 * k) for i in range(blocks)])  4.47 us
  transfers between devices with their start and end apart: 25, of which 1 were waited for; matrix products, arithmetic and copies ran while one was open for 0% of the time, Pallas kernels for 1%

profile of v16, /device:TPU:0, one launch (start us, length us, event | category | flops | bytes accessed | tf_op | source)
XLA Modules:
  0.0 173.7 jit_solution(4251925335682228406)
XLA Ops:
  1.3 1.9 %shard_map.95 = (s32[8]{0:T(128)S(1)}, s32[8]{0:T(128)S(1)}, s32[5,128]{1,0:T(8,128)S(1)}, s32[5,128]{1,0:T(8,128)S(1)}, f32[1,256]{1,0:T(1,128)S(1)}, /*index=5...) custom-call(s32[1]{0:T(128)S(6)} %copy.10.tile_count, ...), custom_call_target="tpu_custom_call" | custom-call | tf_op jit(solution)/shard_map/pallas_call | solution.py:355
  5.1 2.9 %collective-permute-start.1 = (bf16[2,336,128]{2,1,0:T(8,128)(2,1)S(1)}, bf16[2,336,128]{2,1,0:T(8,128)(2,1)S(1)}, u32[]{:S(2)}, u32[]{:S(2)}) collective-permute-start(bf16[2,336,128]{2,1,0:T(8,128)(2,1)S(1)} %get-tuple-element.108), channel_id=1, source_target_pairs={{0,2},{1,3},{2,0},{3,1},{4,6},{5,7},{6,4},{7,5},{8,10},{9,11},{10,... | collective-permute-start | bytes 516104 | tf_op jit(solution)/shard_map/ppermute | solution.py:371
  8.0 1.5 collective-permute-start.2
  9.5 13.4 %all_to_all.80.summed = f32[32,1,256]{2,1,0:T(1,128)S(1)} all-to-all(f32[32,1,256]{2,1,0:T(1,128)S(1)} %shard_map.96), channel_id=1, replica_groups=mesh['grp'=4,'blk'=8] {'grp','blk'}, dimensions={0} | all-to-all | bytes 65536 | tf_op jit(solution)/shard_map/all_to_all | solution.py:309
  25.0 9.8 %all_to_all.81.refs_1_ = f32[32,1,256]{2,1,0:T(1,128)S(1)} all-to-all(f32[32,1,256]{2,1,0:T(1,128)S(1)} %get-tuple-element.112), channel_id=1, replica_groups=mesh['grp'=4,'blk'=8] {'grp','blk'}, dimensions={0} | all-to-all | bytes 65536 | tf_op jit(solution)/shard_map/all_to_all | solution.py:309
  35.7 8.9 %all_to_all.82.refs_4_ = f32[32,1,256]{2,1,0:T(1,128)S(1)} all-to-all(f32[32,1,256]{2,1,0:T(1,128)S(1)} %shard_map.99), channel_id=1, replica_groups=mesh['grp'=4,'blk'=8] {'grp','blk'}, dimensions={0} | all-to-all | bytes 65536 | tf_op jit(solution)/shard_map/all_to_all | solution.py:309
  45.6 7.0 %all_to_all.83.summed = f32[8,1,256]{2,1,0:T(1,128)S(1)} all-to-all(f32[8,1,256]{2,1,0:T(1,128)S(1)} %shard_map.100), channel_id=1, replica_groups={{17,16,9,8,25,24,1,0},{19,18,11,10,27,26,3,2},{21,20,13,12,29,28,5,4},{..., dimensions={0} | all-to-all | bytes 16384 | tf_op jit(solution)/shard_map/all_to_all | solution.py:319
  52.6 1.2 shard_map.101
  55.1 11.5 %all_to_all.84.refs_1_ = f32[32,1,256]{2,1,0:T(1,128)S(1)} all-to-all(f32[32,1,256]{2,1,0:T(1,128)S(1)} %get-tuple-element.134), channel_id=1, replica_groups=mesh['grp'=4,'blk'=8] {'grp','blk'}, dimensions={0} | all-to-all | bytes 65536 | tf_op jit(solution)/shard_map/all_to_all | solution.py:309
  67.6 9.9 %all_to_all.85.refs_4_ = f32[32,1,256]{2,1,0:T(1,128)S(1)} all-to-all(f32[32,1,256]{2,1,0:T(1,128)S(1)} %shard_map.102), channel_id=1, replica_groups=mesh['grp'=4,'blk'=8] {'grp','blk'}, dimensions={0} | all-to-all | bytes 65536 | tf_op jit(solution)/shard_map/all_to_all | solution.py:309
  78.7 7.0 %all_to_all.86.refs_8_ = f32[8,1,256]{2,1,0:T(1,128)S(1)} all-to-all(f32[8,1,256]{2,1,0:T(1,128)S(1)} %shard_map.103), channel_id=1, replica_groups={{17,16,9,8,25,24,1,0},{19,18,11,10,27,26,3,2},{21,20,13,12,29,28,5,4},{..., dimensions={0} | all-to-all | bytes 16384 | tf_op jit(solution)/shard_map/all_to_all | solution.py:319
  85.7 1.1 shard_map.104
  86.8 7.2 %all_to_all.87.summed = f32[4,1,256]{2,1,0:T(1,128)S(1)} all-to-all(f32[4,1,256]{2,1,0:T(1,128)S(1)} %shard_map.104), channel_id=1, replica_groups={{16,8,24,0},{17,9,25,1},{18,10,26,2},{19,11,27,3},{20,12,28,4},{21,13,2..., dimensions={0} | all-to-all | bytes 8192 | tf_op jit(solution)/shard_map/all_to_all | solution.py:319
  94.0 1.7 shard_map.105
  97.0 11.5 %all_to_all.88.refs_1_ = f32[32,1,256]{2,1,0:T(1,128)S(1)} all-to-all(f32[32,1,256]{2,1,0:T(1,128)S(1)} %get-tuple-element.162), channel_id=1, replica_groups=mesh['grp'=4,'blk'=8] {'grp','blk'}, dimensions={0} | all-to-all | bytes 65536 | tf_op jit(solution)/shard_map/all_to_all | solution.py:309
  109.4 8.9 %all_to_all.89.refs_4_ = f32[32,1,256]{2,1,0:T(1,128)S(1)} all-to-all(f32[32,1,256]{2,1,0:T(1,128)S(1)} %shard_map.106), channel_id=1, replica_groups=mesh['grp'=4,'blk'=8] {'grp','blk'}, dimensions={0} | all-to-all | bytes 65536 | tf_op jit(solution)/shard_map/all_to_all | solution.py:309
  119.4 7.0 %all_to_all.90.refs_8_ = f32[8,1,256]{2,1,0:T(1,128)S(1)} all-to-all(f32[8,1,256]{2,1,0:T(1,128)S(1)} %shard_map.107), channel_id=1, replica_groups={{17,16,9,8,25,24,1,0},{19,18,11,10,27,26,3,2},{21,20,13,12,29,28,5,4},{..., dimensions={0} | all-to-all | bytes 16384 | tf_op jit(solution)/shard_map/all_to_all | solution.py:319
  126.8 7.2 %all_to_all.91.summed.author_summed = f32[4,1,256]{2,1,0:T(1,128)S(1)} all-to-all(f32[4,1,256]{2,1,0:T(1,128)S(1)} %shard_map.108), channel_id=1, replica_groups={{16,8,24,0},{17,9,25,1},{18,10,26,2},{19,11,27,3},{20,12,28,4},{21,13,2..., dimensions={0} | all-to-all | bytes 8192 | tf_op jit(solution)/shard_map/all_to_all | solution.py:319
  134.0 1.2 shard_map.109
  135.2 9.9 %all_to_all.92.refs_1_ = f32[32,1,256]{2,1,0:T(1,128)S(1)} all-to-all(f32[32,1,256]{2,1,0:T(1,128)S(1)} %get-tuple-element.189), channel_id=1, replica_groups=mesh['grp'=4,'blk'=8] {'grp','blk'}, dimensions={0} | all-to-all | bytes 65536 | tf_op jit(solution)/shard_map/all_to_all | solution.py:309
  145.3 8.9 %all_to_all.93.refs_1_ = f32[32,1,256]{2,1,0:T(1,128)S(1)} all-to-all(f32[32,1,256]{2,1,0:T(1,128)S(1)} %shard_map.110), channel_id=1, replica_groups=mesh['grp'=4,'blk'=8] {'grp','blk'}, dimensions={0} | all-to-all | bytes 65536 | tf_op jit(solution)/shard_map/all_to_all | solution.py:309
  154.5 8.9 %all_to_all.94.refs_1_ = f32[32,1,256]{2,1,0:T(1,128)S(1)} all-to-all(f32[32,1,256]{2,1,0:T(1,128)S(1)} %shard_map.111), channel_id=1, replica_groups=mesh['grp'=4,'blk'=8] {'grp','blk'}, dimensions={0} | all-to-all | bytes 65536 | tf_op jit(solution)/shard_map/all_to_all | solution.py:309
  163.6 8.9 %all_to_all.95.summed = f32[32,1,256]{2,1,0:T(1,128)S(1)} all-to-all(f32[32,1,256]{2,1,0:T(1,128)S(1)} %shard_map.112), channel_id=1, replica_groups=mesh['grp'=4,'blk'=8] {'grp','blk'}, dimensions={0} | all-to-all | bytes 65536 | tf_op jit(solution)/shard_map/all_to_all | solution.py:309
  172.6 1.1 shard_map.113
  (61 shorter events, 13.6 us)
Async XLA Ops:
  5.1 17.8 %collective-permute-start.1 = (bf16[2,336,128]{2,1,0:T(8,128)(2,1)S(1)}, bf16[2,336,128]{2,1,0:T(8,128)(2,1)S(1)}, u32[]{:S(2)}, u32[]{:S(2)}) collective-permute-start(bf16[2,336,128]{2,1,0:T(8,128)(2,1)S(1)} %get-tuple-element.108), channel_id=1, source_target_pairs={{0,2},{1,3},{2,0},{3,1},{4,6},{5,7},{6,4},{7,5},{8,10},{9,11},{10,... | collective-permute-start | bytes 516104 | tf_op jit(solution)/shard_map/ppermute | solution.py:371
  8.0 14.9 %collective-permute-start.2 = (bf16[2,336,128]{2,1,0:T(8,128)(2,1)S(1)}, bf16[2,336,128]{2,1,0:T(8,128)(2,1)S(1)}, u32[]{:S(2)}, u32[]{:S(2)}) collective-permute-start(bf16[2,336,128]{2,1,0:T(8,128)(2,1)S(1)} %get-tuple-element.109), channel_id=1, source_target_pairs={{0,4},{1,5},{2,6},{3,7},{4,0},{5,1},{6,2},{7,3},{8,12},{9,13},{10,... | collective-permute-start | bytes 516104 | tf_op jit(solution)/shard_map/ppermute | solution.py:371
  9.5 13.4 %collective-permute-start.3 = (bf16[2,336,128]{2,1,0:T(8,128)(2,1)S(1)}, bf16[2,336,128]{2,1,0:T(8,128)(2,1)S(1)}, u32[]{:S(2)}, u32[]{:S(2)}) collective-permute-start(bf16[2,336,128]{2,1,0:T(8,128)(2,1)S(1)} %get-tuple-element.110), channel_id=1, source_target_pairs={{0,6},{1,7},{2,4},{3,5},{4,2},{5,3},{6,0},{7,1},{8,14},{9,15},{10,... | collective-permute-start | bytes 516104 | tf_op jit(solution)/shard_map/ppermute | solution.py:371
  23.7 11.0 %collective-permute-start.5 = (f32[256,256]{1,0:T(8,128)S(1)}, f32[256,256]{1,0:T(8,128)S(1)}, u32[]{:S(2)}, u32[]{:S(2)}) collective-permute-start(f32[256,256]{1,0:T(8,128)S(1)} %get-tuple-element.128.refs_0_.rest_0_), channel_id=1, source_target_pairs={{0,4},{1,5},{2,6},{3,7},{4,0},{5,1},{6,2},{7,3},{8,12},{9,13},{10,... | collective-permute-start | bytes 786440 | tf_op jit(solution)/shard_map/ppermute | solution.py:380
  24.4 10.4 %collective-permute-start.4 = (f32[256,256]{1,0:T(8,128)S(1)}, f32[256,256]{1,0:T(8,128)S(1)}, u32[]{:S(2)}, u32[]{:S(2)}) collective-permute-start(f32[256,256]{1,0:T(8,128)S(1)} %get-tuple-element.128.refs_0_.rest_0_), channel_id=1, source_target_pairs={{0,2},{1,3},{2,0},{3,1},{4,6},{5,7},{6,4},{7,5},{8,10},{9,11},{10,... | collective-permute-start | bytes 786440 | tf_op jit(solution)/shard_map/ppermute | solution.py:380
  34.9 9.7 %collective-permute-start.6 = (f32[256,256]{1,0:T(8,128)S(1)}, f32[256,256]{1,0:T(8,128)S(1)}, u32[]{:S(2)}, u32[]{:S(2)}) collective-permute-start(f32[256,256]{1,0:T(8,128)S(1)} %get-tuple-element.128.refs_0_.rest_0_), channel_id=1, source_target_pairs={{0,1},{1,0},{2,3},{3,2},{4,5},{5,4},{6,7},{7,6},{8,9},{9,8},{10,11... | collective-permute-start | bytes 786440 | tf_op jit(solution)/shard_map/ppermute | solution.py:383
  35.1 9.5 %collective-permute-start.7 = (f32[256,256]{1,0:T(8,128)S(1)}, f32[256,256]{1,0:T(8,128)S(1)}, u32[]{:S(2)}, u32[]{:S(2)}) collective-permute-start(f32[256,256]{1,0:T(8,128)S(1)} %collective-permute-done.4.refs_1_.rest_1_), channel_id=1, source_target_pairs={{0,4},{1,5},{2,6},{3,7},{4,0},{5,1},{6,2},{7,3},{8,12},{9,13},{10,... | collective-permute-start | bytes 786440 | tf_op jit(solution)/shard_map/ppermute | solution.py:380
  44.9 7.7 %collective-permute-start.8 = (f32[256,256]{1,0:T(8,128)S(1)}, f32[256,256]{1,0:T(8,128)S(1)}, u32[]{:S(2)}, u32[]{:S(2)}) collective-permute-start(f32[256,256]{1,0:T(8,128)S(1)} %collective-permute-done.4.refs_1_.rest_1_), channel_id=1, source_target_pairs={{0,1},{1,0},{2,3},{3,2},{4,5},{5,4},{6,7},{7,6},{8,9},{9,8},{10,11... | collective-permute-start | bytes 786440 | tf_op jit(solution)/shard_map/ppermute | solution.py:383
  45.1 7.5 %collective-permute-start.9 = (f32[256,256]{1,0:T(8,128)S(1)}, f32[256,256]{1,0:T(8,128)S(1)}, u32[]{:S(2)}, u32[]{:S(2)}) collective-permute-start(f32[256,256]{1,0:T(8,128)S(1)} %collective-permute-done.5.refs_2_.rest_2_), channel_id=1, source_target_pairs={{0,1},{1,0},{2,3},{3,2},{4,5},{5,4},{6,7},{7,6},{8,9},{9,8},{10,11... | collective-permute-start | bytes 786440 | tf_op jit(solution)/shard_map/ppermute | solution.py:383
  45.5 7.1 %collective-permute-start.10 = (f32[256,256]{1,0:T(8,128)S(1)}, f32[256,256]{1,0:T(8,128)S(1)}, u32[]{:S(2)}, u32[]{:S(2)}) collective-permute-start(f32[256,256]{1,0:T(8,128)S(1)} %collective-permute-done.7.refs_3_.rest_3_), channel_id=1, source_target_pairs={{0,1},{1,0},{2,3},{3,2},{4,5},{5,4},{6,7},{7,6},{8,9},{9,8},{10,11... | collective-permute-start | bytes 786440 | tf_op jit(solution)/shard_map/ppermute | solution.py:383
  53.8 12.8 %collective-permute-start.12 = (bf16[640,256]{1,0:T(8,128)(2,1)S(1)}, bf16[640,256]{1,0:T(8,128)(2,1)S(1)}, u32[]{:S(2)}, u32[]{:S(2)}) collective-permute-start(bf16[640,256]{1,0:T(8,128)(2,1)S(1)} %get-tuple-element.157.refs_0_.rest_0_), channel_id=1, source_target_pairs={{0,4},{1,5},{2,6},{3,7},{4,0},{5,1},{6,2},{7,3},{8,12},{9,13},{10,... | collective-permute-start | bytes 983048 | tf_op jit(solution)/shard_map/ppermute | solution.py:380
  54.5 12.2 %collective-permute-start.11 = (bf16[640,256]{1,0:T(8,128)(2,1)S(1)}, bf16[640,256]{1,0:T(8,128)(2,1)S(1)}, u32[]{:S(2)}, u32[]{:S(2)}) collective-permute-start(bf16[640,256]{1,0:T(8,128)(2,1)S(1)} %get-tuple-element.157.refs_0_.rest_0_), channel_id=1, source_target_pairs={{0,2},{1,3},{2,0},{3,1},{4,6},{5,7},{6,4},{7,5},{8,10},{9,11},{10,... | collective-permute-start | bytes 983048 | tf_op jit(solution)/shard_map/ppermute | solution.py:380
  66.8 10.6 %collective-permute-start.13 = (bf16[640,256]{1,0:T(8,128)(2,1)S(1)}, bf16[640,256]{1,0:T(8,128)(2,1)S(1)}, u32[]{:S(2)}, u32[]{:S(2)}) collective-permute-start(bf16[640,256]{1,0:T(8,128)(2,1)S(1)} %get-tuple-element.157.refs_0_.rest_0_), channel_id=1, source_target_pairs={{0,1},{1,0},{2,3},{3,2},{4,5},{5,4},{6,7},{7,6},{8,9},{9,8},{10,11... | collective-permute-start | bytes 983048 | tf_op jit(solution)/shard_map/ppermute | solution.py:383
  67.0 10.4 %collective-permute-start.14 = (bf16[640,256]{1,0:T(8,128)(2,1)S(1)}, bf16[640,256]{1,0:T(8,128)(2,1)S(1)}, u32[]{:S(2)}, u32[]{:S(2)}) collective-permute-start(bf16[640,256]{1,0:T(8,128)(2,1)S(1)} %collective-permute-done.11.refs_1_.rest_1_), channel_id=1, source_target_pairs={{0,4},{1,5},{2,6},{3,7},{4,0},{5,1},{6,2},{7,3},{8,12},{9,13},{10,... | collective-permute-start | bytes 983048 | tf_op jit(solution)/shard_map/ppermute | solution.py:380
  78.0 7.7 %collective-permute-start.15 = (bf16[640,256]{1,0:T(8,128)(2,1)S(1)}, bf16[640,256]{1,0:T(8,128)(2,1)S(1)}, u32[]{:S(2)}, u32[]{:S(2)}) collective-permute-start(bf16[640,256]{1,0:T(8,128)(2,1)S(1)} %collective-permute-done.11.refs_1_.rest_1_), channel_id=1, source_target_pairs={{0,1},{1,0},{2,3},{3,2},{4,5},{5,4},{6,7},{7,6},{8,9},{9,8},{10,11... | collective-permute-start | bytes 983048 | tf_op jit(solution)/shard_map/ppermute | solution.py:383
  78.2 7.6 %collective-permute-start.16 = (bf16[640,256]{1,0:T(8,128)(2,1)S(1)}, bf16[640,256]{1,0:T(8,128)(2,1)S(1)}, u32[]{:S(2)}, u32[]{:S(2)}) collective-permute-start(bf16[640,256]{1,0:T(8,128)(2,1)S(1)} %collective-permute-done.12.refs_2_.rest_2_), channel_id=1, source_target_pairs={{0,1},{1,0},{2,3},{3,2},{4,5},{5,4},{6,7},{7,6},{8,9},{9,8},{10,11... | collective-permute-start | bytes 983048 | tf_op jit(solution)/shard_map/ppermute | solution.py:383
  78.6 7.1 %collective-permute-start.17 = (bf16[640,256]{1,0:T(8,128)(2,1)S(1)}, bf16[640,256]{1,0:T(8,128)(2,1)S(1)}, u32[]{:S(2)}, u32[]{:S(2)}) collective-permute-start(bf16[640,256]{1,0:T(8,128)(2,1)S(1)} %collective-permute-done.14.refs_3_.rest_3_), channel_id=1, source_target_pairs={{0,1},{1,0},{2,3},{3,2},{4,5},{5,4},{6,7},{7,6},{8,9},{9,8},{10,11... | collective-permute-start | bytes 983048 | tf_op jit(solution)/shard_map/ppermute | solution.py:383
  95.7 12.8 %collective-permute-start.19 = (f32[256,256]{1,0:T(8,128)S(1)}, f32[256,256]{1,0:T(8,128)S(1)}, u32[]{:S(2)}, u32[]{:S(2)}) collective-permute-start(f32[256,256]{1,0:T(8,128)S(1)} %get-tuple-element.184.refs_0_.rest_0_.own), channel_id=1, source_target_pairs={{0,4},{1,5},{2,6},{3,7},{4,0},{5,1},{6,2},{7,3},{8,12},{9,13},{10,... | collective-permute-start | bytes 786440 | tf_op jit(solution)/shard_map/ppermute | solution.py:380
  96.4 12.2 %collective-permute-start.18 = (f32[256,256]{1,0:T(8,128)S(1)}, f32[256,256]{1,0:T(8,128)S(1)}, u32[]{:S(2)}, u32[]{:S(2)}) collective-permute-start(f32[256,256]{1,0:T(8,128)S(1)} %get-tuple-element.184.refs_0_.rest_0_.own), channel_id=1, source_target_pairs={{0,2},{1,3},{2,0},{3,1},{4,6},{5,7},{6,4},{7,5},{8,10},{9,11},{10,... | collective-permute-start | bytes 786440 | tf_op jit(solution)/shard_map/ppermute | solution.py:380
  108.7 9.7 %collective-permute-start.20 = (f32[256,256]{1,0:T(8,128)S(1)}, f32[256,256]{1,0:T(8,128)S(1)}, u32[]{:S(2)}, u32[]{:S(2)}) collective-permute-start(f32[256,256]{1,0:T(8,128)S(1)} %get-tuple-element.184.refs_0_.rest_0_.own), channel_id=1, source_target_pairs={{0,1},{1,0},{2,3},{3,2},{4,5},{5,4},{6,7},{7,6},{8,9},{9,8},{10,11... | collective-permute-start | bytes 786440 | tf_op jit(solution)/shard_map/ppermute | solution.py:383
  108.9 9.5 %collective-permute-start.21 = (f32[256,256]{1,0:T(8,128)S(1)}, f32[256,256]{1,0:T(8,128)S(1)}, u32[]{:S(2)}, u32[]{:S(2)}) collective-permute-start(f32[256,256]{1,0:T(8,128)S(1)} %collective-permute-done.18.refs_1_.rest_1_), channel_id=1, source_target_pairs={{0,4},{1,5},{2,6},{3,7},{4,0},{5,1},{6,2},{7,3},{8,12},{9,13},{10,... | collective-permute-start | bytes 786440 | tf_op jit(solution)/shard_map/ppermute | solution.py:380
  118.7 7.7 %collective-permute-start.22 = (f32[256,256]{1,0:T(8,128)S(1)}, f32[256,256]{1,0:T(8,128)S(1)}, u32[]{:S(2)}, u32[]{:S(2)}) collective-permute-start(f32[256,256]{1,0:T(8,128)S(1)} %collective-permute-done.18.refs_1_.rest_1_), channel_id=1, source_target_pairs={{0,1},{1,0},{2,3},{3,2},{4,5},{5,4},{6,7},{7,6},{8,9},{9,8},{10,11... | collective-permute-start | bytes 786440 | tf_op jit(solution)/shard_map/ppermute | solution.py:383
  118.8 7.5 %collective-permute-start.23 = (f32[256,256]{1,0:T(8,128)S(1)}, f32[256,256]{1,0:T(8,128)S(1)}, u32[]{:S(2)}, u32[]{:S(2)}) collective-permute-start(f32[256,256]{1,0:T(8,128)S(1)} %collective-permute-done.19.refs_2_.rest_2_), channel_id=1, source_target_pairs={{0,1},{1,0},{2,3},{3,2},{4,5},{5,4},{6,7},{7,6},{8,9},{9,8},{10,11... | collective-permute-start | bytes 786440 | tf_op jit(solution)/shard_map/ppermute | solution.py:383
  119.2 7.1 %collective-permute-start.24 = (f32[256,256]{1,0:T(8,128)S(1)}, f32[256,256]{1,0:T(8,128)S(1)}, u32[]{:S(2)}, u32[]{:S(2)}) collective-permute-start(f32[256,256]{1,0:T(8,128)S(1)} %collective-permute-done.21.refs_3_.rest_3_), channel_id=1, source_target_pairs={{0,1},{1,0},{2,3},{3,2},{4,5},{5,4},{6,7},{7,6},{8,9},{9,8},{10,11... | collective-permute-start | bytes 786440 | tf_op jit(solution)/shard_map/ppermute | solution.py:383
  (1 other events, 1.8 us)

commit v17 on v15

--- a/solution.py
+++ b/solution.py
@@ -309,9 +309,11 @@
     return lax.all_to_all(parts, AXES, split_axis=0, concat_axis=0, tiled=True)
 
 
-def narrow_exchange(parts, sides):
+def narrow_exchange(parts, sides, upwards):
     groups, blocks = lax.axis_size("grp"), lax.axis_size("blk")
-    planes = sorted(range(groups), key=lambda i: abs(2 * i + 1 - groups))
+    planes = range(groups)
+    if not upwards:
+        planes = sorted(planes, key=lambda i: abs(2 * i + 1 - groups))
     sets = [
         [i * blocks + first + side for i in planes for side in range(sides)]
         for first in range(0, blocks, sides)
@@ -382,7 +384,7 @@
     def to_other(value):
         return lax.ppermute(value, "blk", [(i, i ^ 1) for i in range(blocks)])
 
-    def balance(kernel, sent, local, count):
+    def balance(kernel, sent, local, count, widest):
         here, there = {0: sent}, {}
         sides = 0
         for step in range(count):
@@ -395,7 +397,10 @@
                     moves.append((here, k, got))
             else:
                 moves = [(there, k, to_other(here[k])) for k in here if k not in there]
-            summed = narrow_exchange(local, sides) if sides else exchange(local)
+            if sides:
+                summed = narrow_exchange(local, sides, step + 1 == count and sides == 2)
+            else:
+                summed = exchange(local)
             summed, *moved = lax.optimization_barrier((summed, *(one for _, _, one in moves)))
             for (place, k, _), one in zip(moves, moved):
                 place[k] = one
@@ -404,7 +409,7 @@
                 if step > 0:
                     added = list(here.values())
                     sides = 2
-                    if step > 1:
+                    if step > 1 and widest:
                         added += list(there.values())
                         sides = 1
                     size = sides * lax.axis_size("grp")
@@ -436,7 +441,7 @@
                 [VMEM] * (3 + blocks + len(held)),
             )(summed, prior, target, *kernels, *held)
             left = ITERS
-        author_summed, kernels = balance(own, own, local, left)
+        author_summed, kernels = balance(own, own, local, left, True)
         last = repeat + 1 == ROUNDS
         kernel, local, *half = call(
             functools.partial(paper_kernel, blocks, rows),
@@ -448,7 +453,7 @@
         if last:
             summed = last_balance(kernel, local)
         else:
-            summed, kernels = balance(kernel, half[0], local, ITERS)
+            summed, kernels = balance(kernel, half[0], local, ITERS, False)
     return call(
         functools.partial(final_kernel, rows),
         (shape((papers, classes), f32), shape((authors, classes), f32)),

time: 172 us -> 172 us (level)
  no operation moved by 1% of the time
where the time goes in v17:
time: 172 us; the launch traced here: 171 us
  blocking collectives  144 us (84%)
  starting transfers between devices  12.9 us (8%)
  Pallas kernels  12.6 us (7%)
    all_to_all x11, blocking collectives, exchange(): return lax.all_to_all(parts, AXES, split_axis=0, concat_axis=0, tiled=True)  106 us
    all_to_all x5, blocking collectives, narrow_exchange(): lax.all_to_all(parts, AXES, split_axis=0, concat_axis=0, axis_index_group...  37.9 us
    ppermute x9, starting transfers between devices, across_pairs(): return lax.ppermute(value, 'blk', [(i, i ^ 2 * k) for i in range(blocks)])  5.38 us
    ppermute x3, starting transfers between devices, on_device(): lax.ppermute(one, 'blk', [(i, i ^ 2 * k) for i in range(blocks)])  4.47 us
  transfers between devices with their start and end apart: 25, of which 1 were waited for; matrix products, arithmetic and copies ran while one was open for 0% of the time, Pallas kernels for 1%

profile of v17, /device:TPU:0, one launch (start us, length us, event | category | flops | bytes accessed | tf_op | source)
XLA Modules:
  0.0 171.2 jit_solution(6408402799210140090)
XLA Ops:
  1.3 1.9 %shard_map.95 = (s32[8]{0:T(128)S(1)}, s32[8]{0:T(128)S(1)}, s32[5,128]{1,0:T(8,128)S(1)}, s32[5,128]{1,0:T(8,128)S(1)}, f32[1,256]{1,0:T(1,128)S(1)}, /*index=5...) custom-call(s32[1]{0:T(128)S(6)} %copy.10.tile_count, ...), custom_call_target="tpu_custom_call" | custom-call | tf_op jit(solution)/shard_map/pallas_call | solution.py:357
  3.8 1.1 shard_map.96
  5.1 2.9 %collective-permute-start.1 = (bf16[2,336,128]{2,1,0:T(8,128)(2,1)S(1)}, bf16[2,336,128]{2,1,0:T(8,128)(2,1)S(1)}, u32[]{:S(2)}, u32[]{:S(2)}) collective-permute-start(bf16[2,336,128]{2,1,0:T(8,128)(2,1)S(1)} %get-tuple-element.108), channel_id=1, source_target_pairs={{0,2},{1,3},{2,0},{3,1},{4,6},{5,7},{6,4},{7,5},{8,10},{9,11},{10,... | collective-permute-start | bytes 516104 | tf_op jit(solution)/shard_map/ppermute | solution.py:373
  8.0 1.5 collective-permute-start.2
  9.5 13.4 %all_to_all.80.summed = f32[32,1,256]{2,1,0:T(1,128)S(1)} all-to-all(f32[32,1,256]{2,1,0:T(1,128)S(1)} %shard_map.96), channel_id=1, replica_groups=mesh['grp'=4,'blk'=8] {'grp','blk'}, dimensions={0} | all-to-all | bytes 65536 | tf_op jit(solution)/shard_map/all_to_all | solution.py:309
  25.0 9.8 %all_to_all.81.refs_1_ = f32[32,1,256]{2,1,0:T(1,128)S(1)} all-to-all(f32[32,1,256]{2,1,0:T(1,128)S(1)} %get-tuple-element.112), channel_id=1, replica_groups=mesh['grp'=4,'blk'=8] {'grp','blk'}, dimensions={0} | all-to-all | bytes 65536 | tf_op jit(solution)/shard_map/all_to_all | solution.py:309
  35.7 8.9 %all_to_all.82.refs_4_ = f32[32,1,256]{2,1,0:T(1,128)S(1)} all-to-all(f32[32,1,256]{2,1,0:T(1,128)S(1)} %shard_map.99), channel_id=1, replica_groups=mesh['grp'=4,'blk'=8] {'grp','blk'}, dimensions={0} | all-to-all | bytes 65536 | tf_op jit(solution)/shard_map/all_to_all | solution.py:309
  45.6 8.0 %all_to_all.83.summed = f32[8,1,256]{2,1,0:T(1,128)S(1)} all-to-all(f32[8,1,256]{2,1,0:T(1,128)S(1)} %shard_map.100), channel_id=1, replica_groups={{0,1,8,9,16,17,24,25},{2,3,10,11,18,19,26,27},{4,5,12,13,20,21,28,29},{..., dimensions={0} | all-to-all | bytes 16384 | tf_op jit(solution)/shard_map/all_to_all | solution.py:321
  53.6 1.2 shard_map.101
  56.0 9.8 %all_to_all.84.refs_1_ = f32[32,1,256]{2,1,0:T(1,128)S(1)} all-to-all(f32[32,1,256]{2,1,0:T(1,128)S(1)} %get-tuple-element.134), channel_id=1, replica_groups=mesh['grp'=4,'blk'=8] {'grp','blk'}, dimensions={0} | all-to-all | bytes 65536 | tf_op jit(solution)/shard_map/all_to_all | solution.py:309
  66.7 9.9 %all_to_all.85.refs_4_ = f32[32,1,256]{2,1,0:T(1,128)S(1)} all-to-all(f32[32,1,256]{2,1,0:T(1,128)S(1)} %shard_map.102), channel_id=1, replica_groups=mesh['grp'=4,'blk'=8] {'grp','blk'}, dimensions={0} | all-to-all | bytes 65536 | tf_op jit(solution)/shard_map/all_to_all | solution.py:309
  77.9 7.3 %all_to_all.86.refs_4_ = f32[8,1,256]{2,1,0:T(1,128)S(1)} all-to-all(f32[8,1,256]{2,1,0:T(1,128)S(1)} %shard_map.103), channel_id=1, replica_groups={{8,9,16,17,0,1,24,25},{10,11,18,19,2,3,26,27},{12,13,20,21,4,5,28,29},{..., dimensions={0} | all-to-all | bytes 16384 | tf_op jit(solution)/shard_map/all_to_all | solution.py:321
  85.7 8.2 %all_to_all.87.summed = f32[8,1,256]{2,1,0:T(1,128)S(1)} all-to-all(f32[8,1,256]{2,1,0:T(1,128)S(1)} %shard_map.104), channel_id=1, replica_groups={{0,1,8,9,16,17,24,25},{2,3,10,11,18,19,26,27},{4,5,12,13,20,21,28,29},{..., dimensions={0} | all-to-all | bytes 16384 | tf_op jit(solution)/shard_map/all_to_all | solution.py:321
  93.9 1.7 %shard_map.105 = (f32[256,256]{1,0:T(8,128)S(1)}, f32[32,1,256]{2,1,0:T(1,128)S(1)}) custom-call(f32[8,1,256]{2,1,0:T(1,128)S(1)} %all_to_all.87.summed, f32[1,256]{1,0:T(1,128)S(1)} %get-tuple-element.102.class_prior, f32[1,256]{1,0:T(1,128)S(1)} %get-tuple-element.107.class_target.refs_2_.refs_5_.refs_9_, ...), custom_call_target="tpu_custom_call" | custom-call | tf_op jit(solution)/shard_map/pallas_call | solution.py:438
  96.8 9.7 %all_to_all.88.refs_1_ = f32[32,1,256]{2,1,0:T(1,128)S(1)} all-to-all(f32[32,1,256]{2,1,0:T(1,128)S(1)} %get-tuple-element.162), channel_id=1, replica_groups=mesh['grp'=4,'blk'=8] {'grp','blk'}, dimensions={0} | all-to-all | bytes 65536 | tf_op jit(solution)/shard_map/all_to_all | solution.py:309
  107.5 8.9 %all_to_all.89.refs_4_ = f32[32,1,256]{2,1,0:T(1,128)S(1)} all-to-all(f32[32,1,256]{2,1,0:T(1,128)S(1)} %shard_map.106), channel_id=1, replica_groups=mesh['grp'=4,'blk'=8] {'grp','blk'}, dimensions={0} | all-to-all | bytes 65536 | tf_op jit(solution)/shard_map/all_to_all | solution.py:309
  117.4 7.3 %all_to_all.90.refs_8_ = f32[8,1,256]{2,1,0:T(1,128)S(1)} all-to-all(f32[8,1,256]{2,1,0:T(1,128)S(1)} %shard_map.107), channel_id=1, replica_groups={{8,9,16,17,0,1,24,25},{10,11,18,19,2,3,26,27},{12,13,20,21,4,5,28,29},{..., dimensions={0} | all-to-all | bytes 16384 | tf_op jit(solution)/shard_map/all_to_all | solution.py:321
  125.1 7.2 %all_to_all.91.summed.author_summed = f32[4,1,256]{2,1,0:T(1,128)S(1)} all-to-all(f32[4,1,256]{2,1,0:T(1,128)S(1)} %shard_map.108), channel_id=1, replica_groups={{8,16,0,24},{9,17,1,25},{10,18,2,26},{11,19,3,27},{12,20,4,28},{13,21,5..., dimensions={0} | all-to-all | bytes 8192 | tf_op jit(solution)/shard_map/all_to_all | solution.py:321
  132.3 1.2 shard_map.109
  133.6 8.9 %all_to_all.92.refs_1_ = f32[32,1,256]{2,1,0:T(1,128)S(1)} all-to-all(f32[32,1,256]{2,1,0:T(1,128)S(1)} %get-tuple-element.189), channel_id=1, replica_groups=mesh['grp'=4,'blk'=8] {'grp','blk'}, dimensions={0} | all-to-all | bytes 65536 | tf_op jit(solution)/shard_map/all_to_all | solution.py:309
  142.7 8.9 %all_to_all.93.refs_1_ = f32[32,1,256]{2,1,0:T(1,128)S(1)} all-to-all(f32[32,1,256]{2,1,0:T(1,128)S(1)} %shard_map.110), channel_id=1, replica_groups=mesh['grp'=4,'blk'=8] {'grp','blk'}, dimensions={0} | all-to-all | bytes 65536 | tf_op jit(solution)/shard_map/all_to_all | solution.py:309
  151.9 8.9 %all_to_all.94.refs_1_ = f32[32,1,256]{2,1,0:T(1,128)S(1)} all-to-all(f32[32,1,256]{2,1,0:T(1,128)S(1)} %shard_map.111), channel_id=1, replica_groups=mesh['grp'=4,'blk'=8] {'grp','blk'}, dimensions={0} | all-to-all | bytes 65536 | tf_op jit(solution)/shard_map/all_to_all | solution.py:309
  161.1 8.9 %all_to_all.95.summed = f32[32,1,256]{2,1,0:T(1,128)S(1)} all-to-all(f32[32,1,256]{2,1,0:T(1,128)S(1)} %shard_map.112), channel_id=1, replica_groups=mesh['grp'=4,'blk'=8] {'grp','blk'}, dimensions={0} | all-to-all | bytes 65536 | tf_op jit(solution)/shard_map/all_to_all | solution.py:309
  170.1 1.1 shard_map.113
  (61 shorter events, 13.0 us)
Async XLA Ops:
  5.1 17.8 %collective-permute-start.1 = (bf16[2,336,128]{2,1,0:T(8,128)(2,1)S(1)}, bf16[2,336,128]{2,1,0:T(8,128)(2,1)S(1)}, u32[]{:S(2)}, u32[]{:S(2)}) collective-permute-start(bf16[2,336,128]{2,1,0:T(8,128)(2,1)S(1)} %get-tuple-element.108), channel_id=1, source_target_pairs={{0,2},{1,3},{2,0},{3,1},{4,6},{5,7},{6,4},{7,5},{8,10},{9,11},{10,... | collective-permute-start | bytes 516104 | tf_op jit(solution)/shard_map/ppermute | solution.py:373
  8.0 14.9 %collective-permute-start.2 = (bf16[2,336,128]{2,1,0:T(8,128)(2,1)S(1)}, bf16[2,336,128]{2,1,0:T(8,128)(2,1)S(1)}, u32[]{:S(2)}, u32[]{:S(2)}) collective-permute-start(bf16[2,336,128]{2,1,0:T(8,128)(2,1)S(1)} %get-tuple-element.109), channel_id=1, source_target_pairs={{0,4},{1,5},{2,6},{3,7},{4,0},{5,1},{6,2},{7,3},{8,12},{9,13},{10,... | collective-permute-start | bytes 516104 | tf_op jit(solution)/shard_map/ppermute | solution.py:373
  9.5 13.4 %collective-permute-start.3 = (bf16[2,336,128]{2,1,0:T(8,128)(2,1)S(1)}, bf16[2,336,128]{2,1,0:T(8,128)(2,1)S(1)}, u32[]{:S(2)}, u32[]{:S(2)}) collective-permute-start(bf16[2,336,128]{2,1,0:T(8,128)(2,1)S(1)} %get-tuple-element.110), channel_id=1, source_target_pairs={{0,6},{1,7},{2,4},{3,5},{4,2},{5,3},{6,0},{7,1},{8,14},{9,15},{10,... | collective-permute-start | bytes 516104 | tf_op jit(solution)/shard_map/ppermute | solution.py:373
  23.7 11.0 %collective-permute-start.5 = (f32[256,256]{1,0:T(8,128)S(1)}, f32[256,256]{1,0:T(8,128)S(1)}, u32[]{:S(2)}, u32[]{:S(2)}) collective-permute-start(f32[256,256]{1,0:T(8,128)S(1)} %get-tuple-element.128.refs_0_.rest_0_), channel_id=1, source_target_pairs={{0,4},{1,5},{2,6},{3,7},{4,0},{5,1},{6,2},{7,3},{8,12},{9,13},{10,... | collective-permute-start | bytes 786440 | tf_op jit(solution)/shard_map/ppermute | solution.py:382
  24.3 10.4 %collective-permute-start.4 = (f32[256,256]{1,0:T(8,128)S(1)}, f32[256,256]{1,0:T(8,128)S(1)}, u32[]{:S(2)}, u32[]{:S(2)}) collective-permute-start(f32[256,256]{1,0:T(8,128)S(1)} %get-tuple-element.128.refs_0_.rest_0_), channel_id=1, source_target_pairs={{0,2},{1,3},{2,0},{3,1},{4,6},{5,7},{6,4},{7,5},{8,10},{9,11},{10,... | collective-permute-start | bytes 786440 | tf_op jit(solution)/shard_map/ppermute | solution.py:382
  34.9 9.7 %collective-permute-start.6 = (f32[256,256]{1,0:T(8,128)S(1)}, f32[256,256]{1,0:T(8,128)S(1)}, u32[]{:S(2)}, u32[]{:S(2)}) collective-permute-start(f32[256,256]{1,0:T(8,128)S(1)} %get-tuple-element.128.refs_0_.rest_0_), channel_id=1, source_target_pairs={{0,1},{1,0},{2,3},{3,2},{4,5},{5,4},{6,7},{7,6},{8,9},{9,8},{10,11... | collective-permute-start | bytes 786440 | tf_op jit(solution)/shard_map/ppermute | solution.py:385
  35.1 9.5 %collective-permute-start.7 = (f32[256,256]{1,0:T(8,128)S(1)}, f32[256,256]{1,0:T(8,128)S(1)}, u32[]{:S(2)}, u32[]{:S(2)}) collective-permute-start(f32[256,256]{1,0:T(8,128)S(1)} %collective-permute-done.4.refs_1_.rest_1_), channel_id=1, source_target_pairs={{0,4},{1,5},{2,6},{3,7},{4,0},{5,1},{6,2},{7,3},{8,12},{9,13},{10,... | collective-permute-start | bytes 786440 | tf_op jit(solution)/shard_map/ppermute | solution.py:382
  44.9 8.7 %collective-permute-start.8 = (f32[256,256]{1,0:T(8,128)S(1)}, f32[256,256]{1,0:T(8,128)S(1)}, u32[]{:S(2)}, u32[]{:S(2)}) collective-permute-start(f32[256,256]{1,0:T(8,128)S(1)} %collective-permute-done.4.refs_1_.rest_1_), channel_id=1, source_target_pairs={{0,1},{1,0},{2,3},{3,2},{4,5},{5,4},{6,7},{7,6},{8,9},{9,8},{10,11... | collective-permute-start | bytes 786440 | tf_op jit(solution)/shard_map/ppermute | solution.py:385
  45.1 8.5 %collective-permute-start.9 = (f32[256,256]{1,0:T(8,128)S(1)}, f32[256,256]{1,0:T(8,128)S(1)}, u32[]{:S(2)}, u32[]{:S(2)}) collective-permute-start(f32[256,256]{1,0:T(8,128)S(1)} %collective-permute-done.5.refs_2_.rest_2_), channel_id=1, source_target_pairs={{0,1},{1,0},{2,3},{3,2},{4,5},{5,4},{6,7},{7,6},{8,9},{9,8},{10,11... | collective-permute-start | bytes 786440 | tf_op jit(solution)/shard_map/ppermute | solution.py:385
  45.5 8.1 %collective-permute-start.10 = (f32[256,256]{1,0:T(8,128)S(1)}, f32[256,256]{1,0:T(8,128)S(1)}, u32[]{:S(2)}, u32[]{:S(2)}) collective-permute-start(f32[256,256]{1,0:T(8,128)S(1)} %collective-permute-done.7.refs_3_.rest_3_), channel_id=1, source_target_pairs={{0,1},{1,0},{2,3},{3,2},{4,5},{5,4},{6,7},{7,6},{8,9},{9,8},{10,11... | collective-permute-start | bytes 786440 | tf_op jit(solution)/shard_map/ppermute | solution.py:385
  54.8 11.0 %collective-permute-start.12 = (bf16[640,256]{1,0:T(8,128)(2,1)S(1)}, bf16[640,256]{1,0:T(8,128)(2,1)S(1)}, u32[]{:S(2)}, u32[]{:S(2)}) collective-permute-start(bf16[640,256]{1,0:T(8,128)(2,1)S(1)} %get-tuple-element.153.refs_0_.rest_0_), channel_id=1, source_target_pairs={{0,4},{1,5},{2,6},{3,7},{4,0},{5,1},{6,2},{7,3},{8,12},{9,13},{10,... | collective-permute-start | bytes 983048 | tf_op jit(solution)/shard_map/ppermute | solution.py:382
  55.4 10.4 %collective-permute-start.11 = (bf16[640,256]{1,0:T(8,128)(2,1)S(1)}, bf16[640,256]{1,0:T(8,128)(2,1)S(1)}, u32[]{:S(2)}, u32[]{:S(2)}) collective-permute-start(bf16[640,256]{1,0:T(8,128)(2,1)S(1)} %get-tuple-element.153.refs_0_.rest_0_), channel_id=1, source_target_pairs={{0,2},{1,3},{2,0},{3,1},{4,6},{5,7},{6,4},{7,5},{8,10},{9,11},{10,... | collective-permute-start | bytes 983048 | tf_op jit(solution)/shard_map/ppermute | solution.py:382
  66.0 10.6 %collective-permute-start.13 = (bf16[640,256]{1,0:T(8,128)(2,1)S(1)}, bf16[640,256]{1,0:T(8,128)(2,1)S(1)}, u32[]{:S(2)}, u32[]{:S(2)}) collective-permute-start(bf16[640,256]{1,0:T(8,128)(2,1)S(1)} %get-tuple-element.153.refs_0_.rest_0_), channel_id=1, source_target_pairs={{0,1},{1,0},{2,3},{3,2},{4,5},{5,4},{6,7},{7,6},{8,9},{9,8},{10,11... | collective-permute-start | bytes 983048 | tf_op jit(solution)/shard_map/ppermute | solution.py:385
  66.2 10.4 %collective-permute-start.14 = (bf16[640,256]{1,0:T(8,128)(2,1)S(1)}, bf16[640,256]{1,0:T(8,128)(2,1)S(1)}, u32[]{:S(2)}, u32[]{:S(2)}) collective-permute-start(bf16[640,256]{1,0:T(8,128)(2,1)S(1)} %collective-permute-done.11.refs_1_.rest_1_), channel_id=1, source_target_pairs={{0,4},{1,5},{2,6},{3,7},{4,0},{5,1},{6,2},{7,3},{8,12},{9,13},{10,... | collective-permute-start | bytes 983048 | tf_op jit(solution)/shard_map/ppermute | solution.py:382
  77.2 7.9 %collective-permute-start.15 = (bf16[640,256]{1,0:T(8,128)(2,1)S(1)}, bf16[640,256]{1,0:T(8,128)(2,1)S(1)}, u32[]{:S(2)}, u32[]{:S(2)}) collective-permute-start(bf16[640,256]{1,0:T(8,128)(2,1)S(1)} %collective-permute-done.11.refs_1_.rest_1_), channel_id=1, source_target_pairs={{0,1},{1,0},{2,3},{3,2},{4,5},{5,4},{6,7},{7,6},{8,9},{9,8},{10,11... | collective-permute-start | bytes 983048 | tf_op jit(solution)/shard_map/ppermute | solution.py:385
  77.3 7.8 %collective-permute-start.16 = (bf16[640,256]{1,0:T(8,128)(2,1)S(1)}, bf16[640,256]{1,0:T(8,128)(2,1)S(1)}, u32[]{:S(2)}, u32[]{:S(2)}) collective-permute-start(bf16[640,256]{1,0:T(8,128)(2,1)S(1)} %collective-permute-done.12.refs_2_.rest_2_), channel_id=1, source_target_pairs={{0,1},{1,0},{2,3},{3,2},{4,5},{5,4},{6,7},{7,6},{8,9},{9,8},{10,11... | collective-permute-start | bytes 983048 | tf_op jit(solution)/shard_map/ppermute | solution.py:385
  77.8 7.4 %collective-permute-start.17 = (bf16[640,256]{1,0:T(8,128)(2,1)S(1)}, bf16[640,256]{1,0:T(8,128)(2,1)S(1)}, u32[]{:S(2)}, u32[]{:S(2)}) collective-permute-start(bf16[640,256]{1,0:T(8,128)(2,1)S(1)} %collective-permute-done.14.refs_3_.rest_3_), channel_id=1, source_target_pairs={{0,1},{1,0},{2,3},{3,2},{4,5},{5,4},{6,7},{7,6},{8,9},{9,8},{10,11... | collective-permute-start | bytes 983048 | tf_op jit(solution)/shard_map/ppermute | solution.py:385
  95.6 11.0 %collective-permute-start.19 = (f32[256,256]{1,0:T(8,128)S(1)}, f32[256,256]{1,0:T(8,128)S(1)}, u32[]{:S(2)}, u32[]{:S(2)}) collective-permute-start(f32[256,256]{1,0:T(8,128)S(1)} %get-tuple-element.184.refs_0_.rest_0_.own), channel_id=1, source_target_pairs={{0,4},{1,5},{2,6},{3,7},{4,0},{5,1},{6,2},{7,3},{8,12},{9,13},{10,... | collective-permute-start | bytes 786440 | tf_op jit(solution)/shard_map/ppermute | solution.py:382
  96.2 10.4 %collective-permute-start.18 = (f32[256,256]{1,0:T(8,128)S(1)}, f32[256,256]{1,0:T(8,128)S(1)}, u32[]{:S(2)}, u32[]{:S(2)}) collective-permute-start(f32[256,256]{1,0:T(8,128)S(1)} %get-tuple-element.184.refs_0_.rest_0_.own), channel_id=1, source_target_pairs={{0,2},{1,3},{2,0},{3,1},{4,6},{5,7},{6,4},{7,5},{8,10},{9,11},{10,... | collective-permute-start | bytes 786440 | tf_op jit(solution)/shard_map/ppermute | solution.py:382
  106.8 9.7 %collective-permute-start.20 = (f32[256,256]{1,0:T(8,128)S(1)}, f32[256,256]{1,0:T(8,128)S(1)}, u32[]{:S(2)}, u32[]{:S(2)}) collective-permute-start(f32[256,256]{1,0:T(8,128)S(1)} %get-tuple-element.184.refs_0_.rest_0_.own), channel_id=1, source_target_pairs={{0,1},{1,0},{2,3},{3,2},{4,5},{5,4},{6,7},{7,6},{8,9},{9,8},{10,11... | collective-permute-start | bytes 786440 | tf_op jit(solution)/shard_map/ppermute | solution.py:385
  107.0 9.5 %collective-permute-start.21 = (f32[256,256]{1,0:T(8,128)S(1)}, f32[256,256]{1,0:T(8,128)S(1)}, u32[]{:S(2)}, u32[]{:S(2)}) collective-permute-start(f32[256,256]{1,0:T(8,128)S(1)} %collective-permute-done.18.refs_1_.rest_1_), channel_id=1, source_target_pairs={{0,4},{1,5},{2,6},{3,7},{4,0},{5,1},{6,2},{7,3},{8,12},{9,13},{10,... | collective-permute-start | bytes 786440 | tf_op jit(solution)/shard_map/ppermute | solution.py:382
  116.7 7.9 %collective-permute-start.22 = (f32[256,256]{1,0:T(8,128)S(1)}, f32[256,256]{1,0:T(8,128)S(1)}, u32[]{:S(2)}, u32[]{:S(2)}) collective-permute-start(f32[256,256]{1,0:T(8,128)S(1)} %collective-permute-done.18.refs_1_.rest_1_), channel_id=1, source_target_pairs={{0,1},{1,0},{2,3},{3,2},{4,5},{5,4},{6,7},{7,6},{8,9},{9,8},{10,11... | collective-permute-start | bytes 786440 | tf_op jit(solution)/shard_map/ppermute | solution.py:385
  116.9 7.8 %collective-permute-start.23 = (f32[256,256]{1,0:T(8,128)S(1)}, f32[256,256]{1,0:T(8,128)S(1)}, u32[]{:S(2)}, u32[]{:S(2)}) collective-permute-start(f32[256,256]{1,0:T(8,128)S(1)} %collective-permute-done.19.refs_2_.rest_2_), channel_id=1, source_target_pairs={{0,1},{1,0},{2,3},{3,2},{4,5},{5,4},{6,7},{7,6},{8,9},{9,8},{10,11... | collective-permute-start | bytes 786440 | tf_op jit(solution)/shard_map/ppermute | solution.py:385
  117.3 7.4 %collective-permute-start.24 = (f32[256,256]{1,0:T(8,128)S(1)}, f32[256,256]{1,0:T(8,128)S(1)}, u32[]{:S(2)}, u32[]{:S(2)}) collective-permute-start(f32[256,256]{1,0:T(8,128)S(1)} %collective-permute-done.21.refs_3_.rest_3_), channel_id=1, source_target_pairs={{0,1},{1,0},{2,3},{3,2},{4,5},{5,4},{6,7},{7,6},{8,9},{9,8},{10,11... | collective-permute-start | bytes 786440 | tf_op jit(solution)/shard_map/ppermute | solution.py:385
  (1 other events, 1.8 us)

commit v18 on v17

--- a/solution.py
+++ b/solution.py
@@ -106,9 +106,9 @@
         copy.start()
     outs = []
     copies = []
-    for k in range(pairs):
-        for way, (out, to) in enumerate(((keep, side), (swap, 1 - side))):
-            slot = 2 * lax.bitwise_xor(pair, k) + to
+    for way, (out, to) in enumerate(((keep, side), (swap, 1 - side))):
+        for k, other in enumerate(pair_order(pairs, to)):
+            slot = 2 * lax.bitwise_xor(pair, other) + to
             copy = pltpu.make_async_copy(
                 tiles.at[slot], out.at[k, pl.ds(0, rows)], arrived.at[way, k]
             )
@@ -142,17 +142,40 @@
         copy.wait()
 
 
+def join_kernel(one, two, out):
+    out[0] = one[...]
+    out[1] = two[...]
+
+
 def pair_kernel(keep, swapped, *outs):
     for k, out in enumerate(outs, 1):
         out[0] = keep[k]
         out[1] = swapped[k]
 
 
+def pair_order(pairs, side):
+    return [0, 1 + side, 2 - side, 3] if pairs == 4 else list(range(pairs))
+
+
+def turned(pairs):
+    return [0, 2, 1, 3] if pairs == 4 else list(range(pairs))
+
+
 def sources(count):
     me = lax.axis_index("blk")
     pair, side = lax.div(me, 2), lax.rem(me, 2)
-    pairs = [2 * lax.bitwise_xor(pair, k) for k in range(count // 2)]
+    pairs = [2 * lax.bitwise_xor(pair, k) for k in pair_order(count // 2, side)]
     return [other + side for other in pairs] + [other + 1 - side for other in pairs]
+
+
+def own_tiles(keep, swap, rows):
+    pairs = keep.shape[0]
+    kept = [keep[k, :rows, :] for k in range(pairs)]
+    return kept + [swap[k, :rows, :] for k in turned(pairs)]
+
+
+def views(refs, places):
+    return [refs[i] if place is None else refs[i].at[place] for i, place in places]
 
 
 def slots_of(keep, swapped, *pairs):
@@ -165,7 +188,7 @@
     pairs, _, columns = keep.shape
     classes = parts.shape[2]
     slots = sources(2 * pairs)
-    tiles = [ref[k, :rows, :].astype(jnp.float32) for ref in (keep, swap) for k in range(pairs)]
+    tiles = [tile.astype(jnp.float32) for tile in own_tiles(keep, swap, rows)]
     lane = lax.broadcasted_iota(jnp.int32, (rows, classes), 1).astype(jnp.float32)
     total = authors * class_prior[...]
     for paper, code in enumerate(code_columns(code_lines(seed_class, train_mask, rows))):
@@ -202,9 +225,10 @@
     next_sum(kernel, summed, class_target, parts)
 
 
-def author_kernel(rows, blocks, summed, class_prior, class_target, *rest):
+def author_kernel(rows, places, summed, class_prior, class_target, *rest):
     *rest, full, parts = rest
-    kernels, held = rest[:blocks], slots_of(*rest[blocks:])
+    count = 1 + max(i for i, _ in places)
+    kernels, held = views(rest, places), slots_of(*rest[count:])
     classes = full.shape[1]
     code_rows = -(-rows // LANES)
     metas = [ref[place, rows:, :].astype(jnp.float32) for ref, place in held]
@@ -235,16 +259,15 @@
 
 
 def paper_kernel(
-    blocks, rows, tile_paper, tile_author, tile_count, keep, swap, summed, class_prior,
+    places, rows, tile_paper, tile_author, tile_count, keep, swap, summed, class_prior,
     class_target, *rest,
 ):
-    kernels, (full, parts, *half) = rest[:blocks], rest[blocks:]
-    pairs, _, columns = keep.shape
+    kernels, (full, parts, *half) = views(rest, places), rest[1 + max(i for i, _ in places) :]
+    columns = keep.shape[2]
     classes = full.shape[1]
     scale_cols = col_scale(summed, class_target)
-    slots = sources(blocks)
-    wide = [ref[k, :rows, :] for ref in (keep, swap) for k in range(pairs)]
-    wide = jnp.concatenate(wide, axis=1)
+    slots = sources(len(kernels))
+    wide = jnp.concatenate(own_tiles(keep, swap, rows), axis=1)
     labels = []
     for ref, slot in zip(kernels, slots):
         start = pl.multiple_of(tile_author[slot] * columns, columns)
@@ -270,8 +293,9 @@
     *kernels, summed, class_target, parts = refs
     scale_cols = col_scale(summed, class_target)
     total = None
-    for ref in kernels:
-        kernel = ref[...].astype(jnp.float32)
+    refs = [(ref, i) for ref in kernels for i in range(ref.shape[0] if ref.ndim == 3 else 1)]
+    for ref, i in refs:
+        kernel = (ref[i] if ref.ndim == 3 else ref[...]).astype(jnp.float32)
         local = jnp.sum(row_scale(kernel, scale_cols) * kernel, axis=0, keepdims=True)
         total = local if total is None else total + local
     spread(total, parts)
@@ -369,57 +393,64 @@
     both = shape((2, rows + META, columns), bf16)
     pairs = call(pair_kernel, (both,) * (blocks // 2 - 1), [VMEM] * 2)(keep, swapped)
     local, *pairs = lax.optimization_barrier((local, *pairs))
-    held = [keep, swapped] + [
-        lax.ppermute(one, "blk", [(i, i ^ (2 * k)) for i in range(blocks)])
-        for k, one in enumerate(pairs, 1)
-    ]
+    count = blocks // 2
+
+    def across_pairs(value, even, odd):
+        hops = [2 * odd if i % 2 else 2 * even for i in range(blocks)]
+        return lax.ppermute(value, "blk", [(i, i ^ hop) for i, hop in enumerate(hops)])
+
+    def to_other(value):
+        return lax.ppermute(value, "blk", [(i, i ^ 1) for i in range(blocks)])
+
+    ways = list(zip(pair_order(count, 0), pair_order(count, 1)))
+    held = [keep, swapped] + [across_pairs(one, *way) for one, way in zip(pairs, ways[1:])]
     summed = exchange(local)
 
     author_out = (shape((authors, classes), f32), parts)
     paper_out = (shape((papers, classes), f32), parts, shape((papers, classes), bf16))
 
-    def across_pairs(value, k):
-        return lax.ppermute(value, "blk", [(i, i ^ (2 * k)) for i in range(blocks)])
-
-    def to_other(value):
-        return lax.ppermute(value, "blk", [(i, i ^ 1) for i in range(blocks)])
-
-    def balance(kernel, sent, local, count, widest):
-        here, there = {0: sent}, {}
+    four = count == 4
+    places = [(i, None) for i in range(blocks)]
+    if four:
+        places = [(0, None), (1, None), (2, 0), (2, 1)]
+        places += [(3 + places[k][0], places[k][1]) for k in turned(count)]
+
+    def balance(kernel, sent, local, steps, widest):
+        here, there, joined = [sent], [], None
         sides = 0
-        for step in range(count):
+        for step in range(steps):
+            moves = []
             if step == 0:
-                moves = [(here, k, across_pairs(sent, k)) for k in (1, 2) if k < blocks // 2]
+                moves = [(sent, *way) for way in ways[1 : 2 if four else 3]]
             elif step == 1:
-                moves = [(there, 0, to_other(sent))]
-                for k in range(3, blocks // 2):
-                    got = across_pairs(here[1], 2) if k == 3 else across_pairs(sent, k)
-                    moves.append((here, k, got))
-            else:
-                moves = [(there, k, to_other(here[k])) for k in here if k not in there]
+                moves = [(joined, *ways[2])] if four else [(sent, *way) for way in ways[3:]]
+            moves = [across_pairs(*move) for move in moves]
+            others = [] if step == 0 else [sent] if step == 1 else here[len(there) :]
+            others = [to_other(one) for one in others]
             if sides:
-                summed = narrow_exchange(local, sides, step + 1 == count and sides == 2)
+                summed = narrow_exchange(local, sides, step + 1 == steps and sides == 2)
             else:
                 summed = exchange(local)
-            summed, *moved = lax.optimization_barrier((summed, *(one for _, _, one in moves)))
-            for (place, k, _), one in zip(moves, moved):
-                place[k] = one
-            if step + 1 < count:
+            summed, *moved = lax.optimization_barrier((summed, *moves, *others))
+            here += moved[: len(moves)]
+            there += moved[len(moves) :]
+            if step + 1 < steps:
                 added, size = [kernel], devices
                 if step > 0:
-                    added = list(here.values())
+                    added = list(here)
                     sides = 2
                     if step > 1 and widest:
-                        added += list(there.values())
+                        added += there
                         sides = 1
                     size = sides * lax.axis_size("grp")
                 local = call(
                     balance_kernel, shape((size, 1, classes), f32), [VMEM] * (len(added) + 2)
                 )(*added, summed, target)
-                local, sent, *moved = lax.optimization_barrier((local, sent, *here.values()))
-                here = dict(zip(here, moved))
-        order = range(blocks // 2)
-        return summed, [here[k] for k in order] + [there[k] for k in order]
+                joined = sent
+                if four and step == 0:
+                    joined = call(join_kernel, shape((2, *sent.shape), sent.dtype), [VMEM] * 2)(*here)
+                local, sent, joined, *here = lax.optimization_barrier((local, sent, joined, *here))
+        return summed, here + there
 
     def last_balance(kernel, local):
         for step in range(ITERS):
@@ -436,17 +467,17 @@
             left = ITERS - 1
         else:
             own, local = call(
-                functools.partial(author_kernel, rows, blocks),
+                functools.partial(author_kernel, rows, places),
                 author_out,
-                [VMEM] * (3 + blocks + len(held)),
+                [VMEM] * (3 + len(kernels) + len(held)),
             )(summed, prior, target, *kernels, *held)
             left = ITERS
         author_summed, kernels = balance(own, own, local, left, True)
         last = repeat + 1 == ROUNDS
         kernel, local, *half = call(
-            functools.partial(paper_kernel, blocks, rows),
+            functools.partial(paper_kernel, places, rows),
             paper_out[:2] if last else paper_out,
-            [SMEM, SMEM, SMEM] + [VMEM] * (5 + blocks),
+            [SMEM, SMEM, SMEM] + [VMEM] * (5 + len(kernels)),
         )(
             tile_paper, tile_author, tile_count, keep, swap, author_summed, prior, target, *kernels
         )

time: 172 us -> 168 us (0.977)
  starting transfers between devices: 12.9 us -> 10.3 us
  blocking collectives: 144 us -> 142 us
    ppermute x12 -> x9, starting transfers between devices: 9.84 us -> 8.04 us  [across_pairs(): lax.ppermute(value, 'blk', [(i, i ^ hop) for i, hop in enumerate(hops)])]
    pallas_call x3 -> x6, Pallas kernels: 4.13 us -> 4.2 us  [the longest x2 2.37 us: on_device(): call(functools.partial(paper_kernel, places, rows), paper_out[:2] if last...]
  transfers between devices with their start and end apart: 25 -> 19, of which waited for: 1 -> 1; matrix products, arithmetic and copies ran while one was open for 0% -> 0% of each run, Pallas kernels for 1% -> 1%
where the time goes in v18:
time: 168 us; the launch traced here: 167 us
  blocking collectives  142 us (85%)
  Pallas kernels  12.6 us (8%)
  starting transfers between devices  10.3 us (6%)
    all_to_all x11, blocking collectives, exchange(): return lax.all_to_all(parts, AXES, split_axis=0, concat_axis=0, tiled=True)  105 us
    all_to_all x5, blocking collectives, narrow_exchange(): lax.all_to_all(parts, AXES, split_axis=0, concat_axis=0, axis_index_group...  37.8 us
    ppermute x9, starting transfers between devices, across_pairs(): lax.ppermute(value, 'blk', [(i, i ^ hop) for i, hop in enumerate(hops)])  8.04 us
  transfers between devices with their start and end apart: 19, of which 1 were waited for; matrix products, arithmetic and copies ran while one was open for 0% of the time, Pallas kernels for 1%

profile of v18, /device:TPU:0, one launch (start us, length us, event | category | flops | bytes accessed | tf_op | source)
XLA Modules:
  0.0 166.9 jit_solution(4412758796706790125)
XLA Ops:
  1.3 1.9 %shard_map.95 = (s32[8]{0:T(128)S(1)}, s32[8]{0:T(128)S(1)}, s32[5,128]{1,0:T(8,128)S(1)}, s32[5,128]{1,0:T(8,128)S(1)}, f32[1,256]{1,0:T(1,128)S(1)}, /*index=5...) custom-call(s32[1]{0:T(128)S(6)} %copy.10.tile_count, ...), custom_call_target="tpu_custom_call" | custom-call | tf_op jit(solution)/shard_map/pallas_call | solution.py:381
  3.8 1.1 shard_map.96
  5.1 2.9 %collective-permute-start.1 = (bf16[2,336,128]{2,1,0:T(8,128)(2,1)S(1)}, bf16[2,336,128]{2,1,0:T(8,128)(2,1)S(1)}, u32[]{:S(2)}, u32[]{:S(2)}) collective-permute-start(bf16[2,336,128]{2,1,0:T(8,128)(2,1)S(1)} %get-tuple-element.97), channel_id=1, source_target_pairs={{0,2},{1,5},{2,0},{3,7},{4,6},{5,1},{6,4},{7,3},{8,10},{9,13},{10,... | collective-permute-start | bytes 516104 | tf_op jit(solution)/shard_map/ppermute | solution.py:400
  8.0 1.5 collective-permute-start.2
  9.5 13.4 %all_to_all.80.summed = f32[32,1,256]{2,1,0:T(1,128)S(1)} all-to-all(f32[32,1,256]{2,1,0:T(1,128)S(1)} %shard_map.96), channel_id=1, replica_groups=mesh['grp'=4,'blk'=8] {'grp','blk'}, dimensions={0} | all-to-all | bytes 65536 | tf_op jit(solution)/shard_map/all_to_all | solution.py:333
  24.3 9.0 %all_to_all.81.refs_1_ = f32[32,1,256]{2,1,0:T(1,128)S(1)} all-to-all(f32[32,1,256]{2,1,0:T(1,128)S(1)} %get-tuple-element.101), channel_id=1, replica_groups=mesh['grp'=4,'blk'=8] {'grp','blk'}, dimensions={0} | all-to-all | bytes 65536 | tf_op jit(solution)/shard_map/all_to_all | solution.py:333
  34.2 9.0 %all_to_all.82.refs_3_ = f32[32,1,256]{2,1,0:T(1,128)S(1)} all-to-all(f32[32,1,256]{2,1,0:T(1,128)S(1)} %shard_map.99), channel_id=1, replica_groups=mesh['grp'=4,'blk'=8] {'grp','blk'}, dimensions={0} | all-to-all | bytes 65536 | tf_op jit(solution)/shard_map/all_to_all | solution.py:333
  44.1 8.0 %all_to_all.83.summed = f32[8,1,256]{2,1,0:T(1,128)S(1)} all-to-all(f32[8,1,256]{2,1,0:T(1,128)S(1)} %shard_map.101), channel_id=1, replica_groups={{0,1,8,9,16,17,24,25},{2,3,10,11,18,19,26,27},{4,5,12,13,20,21,28,29},{..., dimensions={0} | all-to-all | bytes 16384 | tf_op jit(solution)/shard_map/all_to_all | solution.py:345
  52.0 1.2 shard_map.102
  53.8 9.0 %all_to_all.84.refs_1_ = f32[32,1,256]{2,1,0:T(1,128)S(1)} all-to-all(f32[32,1,256]{2,1,0:T(1,128)S(1)} %get-tuple-element.120), channel_id=1, replica_groups=mesh['grp'=4,'blk'=8] {'grp','blk'}, dimensions={0} | all-to-all | bytes 65536 | tf_op jit(solution)/shard_map/all_to_all | solution.py:333
  63.7 10.4 %all_to_all.85.refs_3_ = f32[32,1,256]{2,1,0:T(1,128)S(1)} all-to-all(f32[32,1,256]{2,1,0:T(1,128)S(1)} %shard_map.103), channel_id=1, replica_groups=mesh['grp'=4,'blk'=8] {'grp','blk'}, dimensions={0} | all-to-all | bytes 65536 | tf_op jit(solution)/shard_map/all_to_all | solution.py:333
  75.3 7.2 %all_to_all.86.refs_3_ = f32[8,1,256]{2,1,0:T(1,128)S(1)} all-to-all(f32[8,1,256]{2,1,0:T(1,128)S(1)} %shard_map.105), channel_id=1, replica_groups={{8,9,16,17,0,1,24,25},{10,11,18,19,2,3,26,27},{12,13,20,21,4,5,28,29},{..., dimensions={0} | all-to-all | bytes 16384 | tf_op jit(solution)/shard_map/all_to_all | solution.py:345
  83.1 8.2 %all_to_all.87.summed = f32[8,1,256]{2,1,0:T(1,128)S(1)} all-to-all(f32[8,1,256]{2,1,0:T(1,128)S(1)} %shard_map.106), channel_id=1, replica_groups={{0,1,8,9,16,17,24,25},{2,3,10,11,18,19,26,27},{4,5,12,13,20,21,28,29},{..., dimensions={0} | all-to-all | bytes 16384 | tf_op jit(solution)/shard_map/all_to_all | solution.py:345
  91.2 1.7 %shard_map.107 = (f32[256,256]{1,0:T(8,128)S(1)}, f32[32,1,256]{2,1,0:T(1,128)S(1)}) custom-call(f32[8,1,256]{2,1,0:T(1,128)S(1)} %all_to_all.87.summed, f32[1,256]{1,0:T(1,128)S(1)} %get-tuple-element.91.class_prior, f32[1,256]{1,0:T(1,128)S(1)} %get-tuple-element.96.class_target.refs_2_.refs_4_.refs_7_, ...), custom_call_target="tpu_custom_call" | custom-call | tf_op jit(solution)/shard_map/pallas_call | solution.py:469
  93.5 9.0 %all_to_all.88.refs_1_ = f32[32,1,256]{2,1,0:T(1,128)S(1)} all-to-all(f32[32,1,256]{2,1,0:T(1,128)S(1)} %get-tuple-element.144), channel_id=1, replica_groups=mesh['grp'=4,'blk'=8] {'grp','blk'}, dimensions={0} | all-to-all | bytes 65536 | tf_op jit(solution)/shard_map/all_to_all | solution.py:333
  103.3 9.0 %all_to_all.89.refs_3_ = f32[32,1,256]{2,1,0:T(1,128)S(1)} all-to-all(f32[32,1,256]{2,1,0:T(1,128)S(1)} %shard_map.108), channel_id=1, replica_groups=mesh['grp'=4,'blk'=8] {'grp','blk'}, dimensions={0} | all-to-all | bytes 65536 | tf_op jit(solution)/shard_map/all_to_all | solution.py:333
  113.2 7.2 %all_to_all.90.refs_6_ = f32[8,1,256]{2,1,0:T(1,128)S(1)} all-to-all(f32[8,1,256]{2,1,0:T(1,128)S(1)} %shard_map.110), channel_id=1, replica_groups={{8,9,16,17,0,1,24,25},{10,11,18,19,2,3,26,27},{12,13,20,21,4,5,28,29},{..., dimensions={0} | all-to-all | bytes 16384 | tf_op jit(solution)/shard_map/all_to_all | solution.py:345
  120.9 7.2 %all_to_all.91.summed.author_summed = f32[4,1,256]{2,1,0:T(1,128)S(1)} all-to-all(f32[4,1,256]{2,1,0:T(1,128)S(1)} %shard_map.111), channel_id=1, replica_groups={{8,16,0,24},{9,17,1,25},{10,18,2,26},{11,19,3,27},{12,20,4,28},{13,21,5..., dimensions={0} | all-to-all | bytes 8192 | tf_op jit(solution)/shard_map/all_to_all | solution.py:345
  128.1 1.2 shard_map.112
  129.3 9.0 %all_to_all.92.refs_1_ = f32[32,1,256]{2,1,0:T(1,128)S(1)} all-to-all(f32[32,1,256]{2,1,0:T(1,128)S(1)} %get-tuple-element.167), channel_id=1, replica_groups=mesh['grp'=4,'blk'=8] {'grp','blk'}, dimensions={0} | all-to-all | bytes 65536 | tf_op jit(solution)/shard_map/all_to_all | solution.py:333
  138.5 8.9 %all_to_all.93.refs_1_ = f32[32,1,256]{2,1,0:T(1,128)S(1)} all-to-all(f32[32,1,256]{2,1,0:T(1,128)S(1)} %shard_map.113), channel_id=1, replica_groups=mesh['grp'=4,'blk'=8] {'grp','blk'}, dimensions={0} | all-to-all | bytes 65536 | tf_op jit(solution)/shard_map/all_to_all | solution.py:333
  147.7 8.9 %all_to_all.94.refs_1_ = f32[32,1,256]{2,1,0:T(1,128)S(1)} all-to-all(f32[32,1,256]{2,1,0:T(1,128)S(1)} %shard_map.114), channel_id=1, replica_groups=mesh['grp'=4,'blk'=8] {'grp','blk'}, dimensions={0} | all-to-all | bytes 65536 | tf_op jit(solution)/shard_map/all_to_all | solution.py:333
  156.9 8.9 %all_to_all.95.summed = f32[32,1,256]{2,1,0:T(1,128)S(1)} all-to-all(f32[32,1,256]{2,1,0:T(1,128)S(1)} %shard_map.115), channel_id=1, replica_groups=mesh['grp'=4,'blk'=8] {'grp','blk'}, dimensions={0} | all-to-all | bytes 65536 | tf_op jit(solution)/shard_map/all_to_all | solution.py:333
  165.8 1.1 shard_map.116
  (52 shorter events, 10.5 us)
Async XLA Ops:
  3.2 1.8 %collective-permute-start = (bf16[4,336,128]{2,1,0:T(8,128)(2,1)S(1)}, bf16[4,336,128]{2,1,0:T(8,128)(2,1)S(1)}, u32[]{:S(2)}, u32[]{:S(2)}) collective-permute-start(bf16[4,336,128]{2,1,0:T(8,128)(2,1)S(1)} %get-tuple-element.88.swap), channel_id=1, source_target_pairs={{0,1},{1,0},{2,3},{3,2},{4,5},{5,4},{6,7},{7,6},{8,9},{9,8},{10,11... | collective-permute-start | bytes 1032200 | tf_op jit(solution)/shard_map/ppermute | solution.py:389
  5.1 17.8 %collective-permute-start.1 = (bf16[2,336,128]{2,1,0:T(8,128)(2,1)S(1)}, bf16[2,336,128]{2,1,0:T(8,128)(2,1)S(1)}, u32[]{:S(2)}, u32[]{:S(2)}) collective-permute-start(bf16[2,336,128]{2,1,0:T(8,128)(2,1)S(1)} %get-tuple-element.97), channel_id=1, source_target_pairs={{0,2},{1,5},{2,0},{3,7},{4,6},{5,1},{6,4},{7,3},{8,10},{9,13},{10,... | collective-permute-start | bytes 516104 | tf_op jit(solution)/shard_map/ppermute | solution.py:400
  8.0 14.9 %collective-permute-start.2 = (bf16[2,336,128]{2,1,0:T(8,128)(2,1)S(1)}, bf16[2,336,128]{2,1,0:T(8,128)(2,1)S(1)}, u32[]{:S(2)}, u32[]{:S(2)}) collective-permute-start(bf16[2,336,128]{2,1,0:T(8,128)(2,1)S(1)} %get-tuple-element.98), channel_id=1, source_target_pairs={{0,4},{1,3},{2,6},{3,1},{4,0},{5,7},{6,2},{7,5},{8,12},{9,11},{10,... | collective-permute-start | bytes 516104 | tf_op jit(solution)/shard_map/ppermute | solution.py:400
  9.5 13.4 %collective-permute-start.3 = (bf16[2,336,128]{2,1,0:T(8,128)(2,1)S(1)}, bf16[2,336,128]{2,1,0:T(8,128)(2,1)S(1)}, u32[]{:S(2)}, u32[]{:S(2)}) collective-permute-start(bf16[2,336,128]{2,1,0:T(8,128)(2,1)S(1)} %get-tuple-element.99), channel_id=1, source_target_pairs={{0,6},{1,7},{2,4},{3,5},{4,2},{5,3},{6,0},{7,1},{8,14},{9,15},{10,... | collective-permute-start | bytes 516104 | tf_op jit(solution)/shard_map/ppermute | solution.py:400
  23.7 9.6 %collective-permute-start.4 = (f32[256,256]{1,0:T(8,128)S(1)}, f32[256,256]{1,0:T(8,128)S(1)}, u32[]{:S(2)}, u32[]{:S(2)}) collective-permute-start(f32[256,256]{1,0:T(8,128)S(1)} %get-tuple-element.115.refs_0_.one.rest_0_), channel_id=1, source_target_pairs={{0,2},{1,5},{2,0},{3,7},{4,6},{5,1},{6,4},{7,3},{8,10},{9,13},{10,... | collective-permute-start | bytes 786440 | tf_op jit(solution)/shard_map/ppermute | solution.py:400
  33.5 9.7 %collective-permute-start.5 = (f32[2,256,256]{2,1,0:T(8,128)S(1)}, f32[2,256,256]{2,1,0:T(8,128)S(1)}, u32[]{:S(2)}, u32[]{:S(2)}) collective-permute-start(f32[2,256,256]{2,1,0:T(8,128)S(1)} %shard_map.100), channel_id=1, source_target_pairs={{0,4},{1,3},{2,6},{3,1},{4,0},{5,7},{6,2},{7,5},{8,12},{9,11},{10,... | collective-permute-start | bytes 1572872 | tf_op jit(solution)/shard_map/ppermute | solution.py:400
  34.2 9.0 %collective-permute-start.6 = (f32[256,256]{1,0:T(8,128)S(1)}, f32[256,256]{1,0:T(8,128)S(1)}, u32[]{:S(2)}, u32[]{:S(2)}) collective-permute-start(f32[256,256]{1,0:T(8,128)S(1)} %get-tuple-element.115.refs_0_.one.rest_0_), channel_id=1, source_target_pairs={{0,1},{1,0},{2,3},{3,2},{4,5},{5,4},{6,7},{7,6},{8,9},{9,8},{10,11... | collective-permute-start | bytes 786440 | tf_op jit(solution)/shard_map/ppermute | solution.py:403
  43.5 8.5 %collective-permute-start.8 = (f32[2,256,256]{2,1,0:T(8,128)S(1)}, f32[2,256,256]{2,1,0:T(8,128)S(1)}, u32[]{:S(2)}, u32[]{:S(2)}) collective-permute-start(f32[2,256,256]{2,1,0:T(8,128)S(1)} %collective-permute-done.5.refs_2_.rest_2_), channel_id=1, source_target_pairs={{0,1},{1,0},{2,3},{3,2},{4,5},{5,4},{6,7},{7,6},{8,9},{9,8},{10,11... | collective-permute-start | bytes 1572872 | tf_op jit(solution)/shard_map/ppermute | solution.py:403
  43.7 8.4 %collective-permute-start.7 = (f32[256,256]{1,0:T(8,128)S(1)}, f32[256,256]{1,0:T(8,128)S(1)}, u32[]{:S(2)}, u32[]{:S(2)}) collective-permute-start(f32[256,256]{1,0:T(8,128)S(1)} %collective-permute-done.4.two.refs_1_.rest_1_), channel_id=1, source_target_pairs={{0,1},{1,0},{2,3},{3,2},{4,5},{5,4},{6,7},{7,6},{8,9},{9,8},{10,11... | collective-permute-start | bytes 786440 | tf_op jit(solution)/shard_map/ppermute | solution.py:403
  53.2 9.5 %collective-permute-start.9 = (bf16[640,256]{1,0:T(8,128)(2,1)S(1)}, bf16[640,256]{1,0:T(8,128)(2,1)S(1)}, u32[]{:S(2)}, u32[]{:S(2)}) collective-permute-start(bf16[640,256]{1,0:T(8,128)(2,1)S(1)} %get-tuple-element.137.one.refs_0_.rest_0_), channel_id=1, source_target_pairs={{0,2},{1,5},{2,0},{3,7},{4,6},{5,1},{6,4},{7,3},{8,10},{9,13},{10,... | collective-permute-start | bytes 983048 | tf_op jit(solution)/shard_map/ppermute | solution.py:400
  63.0 11.0 %collective-permute-start.10 = (bf16[2,640,256]{2,1,0:T(8,128)(2,1)S(1)}, bf16[2,640,256]{2,1,0:T(8,128)(2,1)S(1)}, u32[]{:S(2)}, u32[]{:S(2)}) collective-permute-start(bf16[2,640,256]{2,1,0:T(8,128)(2,1)S(1)} %shard_map.104), channel_id=1, source_target_pairs={{0,4},{1,3},{2,6},{3,1},{4,0},{5,7},{6,2},{7,5},{8,12},{9,11},{10,... | collective-permute-start | bytes 1966088 | tf_op jit(solution)/shard_map/ppermute | solution.py:400
  63.7 10.4 %collective-permute-start.11 = (bf16[640,256]{1,0:T(8,128)(2,1)S(1)}, bf16[640,256]{1,0:T(8,128)(2,1)S(1)}, u32[]{:S(2)}, u32[]{:S(2)}) collective-permute-start(bf16[640,256]{1,0:T(8,128)(2,1)S(1)} %get-tuple-element.137.one.refs_0_.rest_0_), channel_id=1, source_target_pairs={{0,1},{1,0},{2,3},{3,2},{4,5},{5,4},{6,7},{7,6},{8,9},{9,8},{10,11... | collective-permute-start | bytes 983048 | tf_op jit(solution)/shard_map/ppermute | solution.py:403
  74.7 7.8 %collective-permute-start.13 = (bf16[2,640,256]{2,1,0:T(8,128)(2,1)S(1)}, bf16[2,640,256]{2,1,0:T(8,128)(2,1)S(1)}, u32[]{:S(2)}, u32[]{:S(2)}) collective-permute-start(bf16[2,640,256]{2,1,0:T(8,128)(2,1)S(1)} %collective-permute-done.10.refs_2_.rest_2_), channel_id=1, source_target_pairs={{0,1},{1,0},{2,3},{3,2},{4,5},{5,4},{6,7},{7,6},{8,9},{9,8},{10,11... | collective-permute-start | bytes 1966088 | tf_op jit(solution)/shard_map/ppermute | solution.py:403
  74.8 7.7 %collective-permute-start.12 = (bf16[640,256]{1,0:T(8,128)(2,1)S(1)}, bf16[640,256]{1,0:T(8,128)(2,1)S(1)}, u32[]{:S(2)}, u32[]{:S(2)}) collective-permute-start(bf16[640,256]{1,0:T(8,128)(2,1)S(1)} %collective-permute-done.9.two.refs_1_.rest_1_), channel_id=1, source_target_pairs={{0,1},{1,0},{2,3},{3,2},{4,5},{5,4},{6,7},{7,6},{8,9},{9,8},{10,11... | collective-permute-start | bytes 983048 | tf_op jit(solution)/shard_map/ppermute | solution.py:403
  92.9 9.5 %collective-permute-start.14 = (f32[256,256]{1,0:T(8,128)S(1)}, f32[256,256]{1,0:T(8,128)S(1)}, u32[]{:S(2)}, u32[]{:S(2)}) collective-permute-start(f32[256,256]{1,0:T(8,128)S(1)} %get-tuple-element.163.refs_0_.one.rest_0_.own), channel_id=1, source_target_pairs={{0,2},{1,5},{2,0},{3,7},{4,6},{5,1},{6,4},{7,3},{8,10},{9,13},{10,... | collective-permute-start | bytes 786440 | tf_op jit(solution)/shard_map/ppermute | solution.py:400
  102.7 9.7 %collective-permute-start.15 = (f32[2,256,256]{2,1,0:T(8,128)S(1)}, f32[2,256,256]{2,1,0:T(8,128)S(1)}, u32[]{:S(2)}, u32[]{:S(2)}) collective-permute-start(f32[2,256,256]{2,1,0:T(8,128)S(1)} %shard_map.109), channel_id=1, source_target_pairs={{0,4},{1,3},{2,6},{3,1},{4,0},{5,7},{6,2},{7,5},{8,12},{9,11},{10,... | collective-permute-start | bytes 1572872 | tf_op jit(solution)/shard_map/ppermute | solution.py:400
  103.3 9.0 %collective-permute-start.16 = (f32[256,256]{1,0:T(8,128)S(1)}, f32[256,256]{1,0:T(8,128)S(1)}, u32[]{:S(2)}, u32[]{:S(2)}) collective-permute-start(f32[256,256]{1,0:T(8,128)S(1)} %get-tuple-element.163.refs_0_.one.rest_0_.own), channel_id=1, source_target_pairs={{0,1},{1,0},{2,3},{3,2},{4,5},{5,4},{6,7},{7,6},{8,9},{9,8},{10,11... | collective-permute-start | bytes 786440 | tf_op jit(solution)/shard_map/ppermute | solution.py:403
  112.7 7.8 %collective-permute-start.18 = (f32[2,256,256]{2,1,0:T(8,128)S(1)}, f32[2,256,256]{2,1,0:T(8,128)S(1)}, u32[]{:S(2)}, u32[]{:S(2)}) collective-permute-start(f32[2,256,256]{2,1,0:T(8,128)S(1)} %collective-permute-done.15.refs_2_.rest_2_), channel_id=1, source_target_pairs={{0,1},{1,0},{2,3},{3,2},{4,5},{5,4},{6,7},{7,6},{8,9},{9,8},{10,11... | collective-permute-start | bytes 1572872 | tf_op jit(solution)/shard_map/ppermute | solution.py:403
  112.8 7.6 %collective-permute-start.17 = (f32[256,256]{1,0:T(8,128)S(1)}, f32[256,256]{1,0:T(8,128)S(1)}, u32[]{:S(2)}, u32[]{:S(2)}) collective-permute-start(f32[256,256]{1,0:T(8,128)S(1)} %collective-permute-done.14.two.refs_1_.rest_1_), channel_id=1, source_target_pairs={{0,1},{1,0},{2,3},{3,2},{4,5},{5,4},{6,7},{7,6},{8,9},{9,8},{10,11... | collective-permute-start | bytes 786440 | tf_op jit(solution)/shard_map/ppermute | solution.py:403

commit v19 on v18

--- a/solution.py
+++ b/solution.py
@@ -242,7 +242,7 @@
         half = kernels[shift][pl.ds(pl.multiple_of(papers[shift] * rows, rows), rows), :]
         scaled = half.astype(jnp.float32) * scale_cols
         share = scaled * (keep_share / jnp.sum(scaled, axis=1, keepdims=True))
-        labels = share + jnp.where(codes[shift] == lane, 1.0 - keep_share, 0.0)
+        labels = jnp.where(codes[shift] == lane, share + (1.0 - keep_share), share)
         parcel = lax.dot_general(
             ref[place, :rows, :],
             labels.astype(jnp.bfloat16),
@@ -339,7 +339,7 @@
     if not upwards:
         planes = sorted(planes, key=lambda i: abs(2 * i + 1 - groups))
     sets = [
-        [i * blocks + first + side for i in planes for side in range(sides)]
+        [i * blocks + first + side for i in planes for side in reversed(range(sides))]
         for first in range(0, blocks, sides)
     ]
     return lax.all_to_all(

time: 168 us -> 167 us (level)
  no operation moved by 1% of the time
where the time goes in v19:
time: 167 us; the launch traced here: 166 us
  blocking collectives  141 us (84%)
  Pallas kernels  12.6 us (8%)
  starting transfers between devices  10.3 us (6%)
    all_to_all x11, blocking collectives, exchange(): return lax.all_to_all(parts, AXES, split_axis=0, concat_axis=0, tiled=True)  105 us
    all_to_all x5, blocking collectives, narrow_exchange(): lax.all_to_all(parts, AXES, split_axis=0, concat_axis=0, axis_index_group...  36.7 us
    ppermute x9, starting transfers between devices, across_pairs(): lax.ppermute(value, 'blk', [(i, i ^ hop) for i, hop in enumerate(hops)])  8.03 us
  transfers between devices with their start and end apart: 19, of which 1 were waited for; matrix products, arithmetic and copies ran while one was open for 0% of the time, Pallas kernels for 1%

profile of v19, /device:TPU:0, one launch (start us, length us, event | category | flops | bytes accessed | tf_op | source)
XLA Modules:
  0.0 165.9 jit_solution(15246405514097914453)
XLA Ops:
  1.3 1.9 %shard_map.95 = (s32[8]{0:T(128)S(1)}, s32[8]{0:T(128)S(1)}, s32[5,128]{1,0:T(8,128)S(1)}, s32[5,128]{1,0:T(8,128)S(1)}, f32[1,256]{1,0:T(1,128)S(1)}, /*index=5...) custom-call(s32[1]{0:T(128)S(6)} %copy.10.tile_count, ...), custom_call_target="tpu_custom_call" | custom-call | tf_op jit(solution)/shard_map/pallas_call | solution.py:381
  3.8 1.1 shard_map.96
  5.1 2.9 %collective-permute-start.1 = (bf16[2,336,128]{2,1,0:T(8,128)(2,1)S(1)}, bf16[2,336,128]{2,1,0:T(8,128)(2,1)S(1)}, u32[]{:S(2)}, u32[]{:S(2)}) collective-permute-start(bf16[2,336,128]{2,1,0:T(8,128)(2,1)S(1)} %get-tuple-element.97), channel_id=1, source_target_pairs={{0,2},{1,5},{2,0},{3,7},{4,6},{5,1},{6,4},{7,3},{8,10},{9,13},{10,... | collective-permute-start | bytes 516104 | tf_op jit(solution)/shard_map/ppermute | solution.py:400
  8.0 1.5 collective-permute-start.2
  9.5 13.4 %all_to_all.80.summed = f32[32,1,256]{2,1,0:T(1,128)S(1)} all-to-all(f32[32,1,256]{2,1,0:T(1,128)S(1)} %shard_map.96), channel_id=1, replica_groups=mesh['grp'=4,'blk'=8] {'grp','blk'}, dimensions={0} | all-to-all | bytes 65536 | tf_op jit(solution)/shard_map/all_to_all | solution.py:333
  24.3 9.0 %all_to_all.81.refs_1_ = f32[32,1,256]{2,1,0:T(1,128)S(1)} all-to-all(f32[32,1,256]{2,1,0:T(1,128)S(1)} %get-tuple-element.101), channel_id=1, replica_groups=mesh['grp'=4,'blk'=8] {'grp','blk'}, dimensions={0} | all-to-all | bytes 65536 | tf_op jit(solution)/shard_map/all_to_all | solution.py:333
  34.2 9.0 %all_to_all.82.refs_3_ = f32[32,1,256]{2,1,0:T(1,128)S(1)} all-to-all(f32[32,1,256]{2,1,0:T(1,128)S(1)} %shard_map.99), channel_id=1, replica_groups=mesh['grp'=4,'blk'=8] {'grp','blk'}, dimensions={0} | all-to-all | bytes 65536 | tf_op jit(solution)/shard_map/all_to_all | solution.py:333
  44.1 7.7 %all_to_all.83.summed = f32[8,1,256]{2,1,0:T(1,128)S(1)} all-to-all(f32[8,1,256]{2,1,0:T(1,128)S(1)} %shard_map.101), channel_id=1, replica_groups={{1,0,9,8,17,16,25,24},{3,2,11,10,19,18,27,26},{5,4,13,12,21,20,29,28},{..., dimensions={0} | all-to-all | bytes 16384 | tf_op jit(solution)/shard_map/all_to_all | solution.py:345
  51.8 1.2 shard_map.102
  53.5 9.0 %all_to_all.84.refs_1_ = f32[32,1,256]{2,1,0:T(1,128)S(1)} all-to-all(f32[32,1,256]{2,1,0:T(1,128)S(1)} %get-tuple-element.120), channel_id=1, replica_groups=mesh['grp'=4,'blk'=8] {'grp','blk'}, dimensions={0} | all-to-all | bytes 65536 | tf_op jit(solution)/shard_map/all_to_all | solution.py:333
  63.4 10.4 %all_to_all.85.refs_3_ = f32[32,1,256]{2,1,0:T(1,128)S(1)} all-to-all(f32[32,1,256]{2,1,0:T(1,128)S(1)} %shard_map.103), channel_id=1, replica_groups=mesh['grp'=4,'blk'=8] {'grp','blk'}, dimensions={0} | all-to-all | bytes 65536 | tf_op jit(solution)/shard_map/all_to_all | solution.py:333
  75.0 7.0 %all_to_all.86.refs_3_ = f32[8,1,256]{2,1,0:T(1,128)S(1)} all-to-all(f32[8,1,256]{2,1,0:T(1,128)S(1)} %shard_map.105), channel_id=1, replica_groups={{9,8,17,16,1,0,25,24},{11,10,19,18,3,2,27,26},{13,12,21,20,5,4,29,28},{..., dimensions={0} | all-to-all | bytes 16384 | tf_op jit(solution)/shard_map/all_to_all | solution.py:345
  82.6 7.9 %all_to_all.87.summed = f32[8,1,256]{2,1,0:T(1,128)S(1)} all-to-all(f32[8,1,256]{2,1,0:T(1,128)S(1)} %shard_map.106), channel_id=1, replica_groups={{1,0,9,8,17,16,25,24},{3,2,11,10,19,18,27,26},{5,4,13,12,21,20,29,28},{..., dimensions={0} | all-to-all | bytes 16384 | tf_op jit(solution)/shard_map/all_to_all | solution.py:345
  90.4 1.7 %shard_map.107 = (f32[256,256]{1,0:T(8,128)S(1)}, f32[32,1,256]{2,1,0:T(1,128)S(1)}) custom-call(f32[8,1,256]{2,1,0:T(1,128)S(1)} %all_to_all.87.summed, f32[1,256]{1,0:T(1,128)S(1)} %get-tuple-element.91.class_prior, f32[1,256]{1,0:T(1,128)S(1)} %get-tuple-element.96.class_target.refs_2_.refs_4_.refs_7_, ...), custom_call_target="tpu_custom_call" | custom-call | tf_op jit(solution)/shard_map/pallas_call | solution.py:469
  92.7 9.0 %all_to_all.88.refs_1_ = f32[32,1,256]{2,1,0:T(1,128)S(1)} all-to-all(f32[32,1,256]{2,1,0:T(1,128)S(1)} %get-tuple-element.144), channel_id=1, replica_groups=mesh['grp'=4,'blk'=8] {'grp','blk'}, dimensions={0} | all-to-all | bytes 65536 | tf_op jit(solution)/shard_map/all_to_all | solution.py:333
  102.6 9.0 %all_to_all.89.refs_3_ = f32[32,1,256]{2,1,0:T(1,128)S(1)} all-to-all(f32[32,1,256]{2,1,0:T(1,128)S(1)} %shard_map.108), channel_id=1, replica_groups=mesh['grp'=4,'blk'=8] {'grp','blk'}, dimensions={0} | all-to-all | bytes 65536 | tf_op jit(solution)/shard_map/all_to_all | solution.py:333
  112.5 7.0 %all_to_all.90.refs_6_ = f32[8,1,256]{2,1,0:T(1,128)S(1)} all-to-all(f32[8,1,256]{2,1,0:T(1,128)S(1)} %shard_map.110), channel_id=1, replica_groups={{9,8,17,16,1,0,25,24},{11,10,19,18,3,2,27,26},{13,12,21,20,5,4,29,28},{..., dimensions={0} | all-to-all | bytes 16384 | tf_op jit(solution)/shard_map/all_to_all | solution.py:345
  119.9 7.2 %all_to_all.91.summed.author_summed = f32[4,1,256]{2,1,0:T(1,128)S(1)} all-to-all(f32[4,1,256]{2,1,0:T(1,128)S(1)} %shard_map.111), channel_id=1, replica_groups={{8,16,0,24},{9,17,1,25},{10,18,2,26},{11,19,3,27},{12,20,4,28},{13,21,5..., dimensions={0} | all-to-all | bytes 8192 | tf_op jit(solution)/shard_map/all_to_all | solution.py:345
  127.1 1.2 shard_map.112
  128.3 9.0 %all_to_all.92.refs_1_ = f32[32,1,256]{2,1,0:T(1,128)S(1)} all-to-all(f32[32,1,256]{2,1,0:T(1,128)S(1)} %get-tuple-element.167), channel_id=1, replica_groups=mesh['grp'=4,'blk'=8] {'grp','blk'}, dimensions={0} | all-to-all | bytes 65536 | tf_op jit(solution)/shard_map/all_to_all | solution.py:333
  137.5 8.9 %all_to_all.93.refs_1_ = f32[32,1,256]{2,1,0:T(1,128)S(1)} all-to-all(f32[32,1,256]{2,1,0:T(1,128)S(1)} %shard_map.113), channel_id=1, replica_groups=mesh['grp'=4,'blk'=8] {'grp','blk'}, dimensions={0} | all-to-all | bytes 65536 | tf_op jit(solution)/shard_map/all_to_all | solution.py:333
  146.7 8.9 %all_to_all.94.refs_1_ = f32[32,1,256]{2,1,0:T(1,128)S(1)} all-to-all(f32[32,1,256]{2,1,0:T(1,128)S(1)} %shard_map.114), channel_id=1, replica_groups=mesh['grp'=4,'blk'=8] {'grp','blk'}, dimensions={0} | all-to-all | bytes 65536 | tf_op jit(solution)/shard_map/all_to_all | solution.py:333
  155.9 8.9 %all_to_all.95.summed = f32[32,1,256]{2,1,0:T(1,128)S(1)} all-to-all(f32[32,1,256]{2,1,0:T(1,128)S(1)} %shard_map.115), channel_id=1, replica_groups=mesh['grp'=4,'blk'=8] {'grp','blk'}, dimensions={0} | all-to-all | bytes 65536 | tf_op jit(solution)/shard_map/all_to_all | solution.py:333
  164.8 1.1 shard_map.116
  (52 shorter events, 10.5 us)
Async XLA Ops:
  3.2 1.8 %collective-permute-start = (bf16[4,336,128]{2,1,0:T(8,128)(2,1)S(1)}, bf16[4,336,128]{2,1,0:T(8,128)(2,1)S(1)}, u32[]{:S(2)}, u32[]{:S(2)}) collective-permute-start(bf16[4,336,128]{2,1,0:T(8,128)(2,1)S(1)} %get-tuple-element.88.swap), channel_id=1, source_target_pairs={{0,1},{1,0},{2,3},{3,2},{4,5},{5,4},{6,7},{7,6},{8,9},{9,8},{10,11... | collective-permute-start | bytes 1032200 | tf_op jit(solution)/shard_map/ppermute | solution.py:389
  5.1 17.8 %collective-permute-start.1 = (bf16[2,336,128]{2,1,0:T(8,128)(2,1)S(1)}, bf16[2,336,128]{2,1,0:T(8,128)(2,1)S(1)}, u32[]{:S(2)}, u32[]{:S(2)}) collective-permute-start(bf16[2,336,128]{2,1,0:T(8,128)(2,1)S(1)} %get-tuple-element.97), channel_id=1, source_target_pairs={{0,2},{1,5},{2,0},{3,7},{4,6},{5,1},{6,4},{7,3},{8,10},{9,13},{10,... | collective-permute-start | bytes 516104 | tf_op jit(solution)/shard_map/ppermute | solution.py:400
  8.0 14.9 %collective-permute-start.2 = (bf16[2,336,128]{2,1,0:T(8,128)(2,1)S(1)}, bf16[2,336,128]{2,1,0:T(8,128)(2,1)S(1)}, u32[]{:S(2)}, u32[]{:S(2)}) collective-permute-start(bf16[2,336,128]{2,1,0:T(8,128)(2,1)S(1)} %get-tuple-element.98), channel_id=1, source_target_pairs={{0,4},{1,3},{2,6},{3,1},{4,0},{5,7},{6,2},{7,5},{8,12},{9,11},{10,... | collective-permute-start | bytes 516104 | tf_op jit(solution)/shard_map/ppermute | solution.py:400
  9.5 13.4 %collective-permute-start.3 = (bf16[2,336,128]{2,1,0:T(8,128)(2,1)S(1)}, bf16[2,336,128]{2,1,0:T(8,128)(2,1)S(1)}, u32[]{:S(2)}, u32[]{:S(2)}) collective-permute-start(bf16[2,336,128]{2,1,0:T(8,128)(2,1)S(1)} %get-tuple-element.99), channel_id=1, source_target_pairs={{0,6},{1,7},{2,4},{3,5},{4,2},{5,3},{6,0},{7,1},{8,14},{9,15},{10,... | collective-permute-start | bytes 516104 | tf_op jit(solution)/shard_map/ppermute | solution.py:400
  23.7 9.6 %collective-permute-start.4 = (f32[256,256]{1,0:T(8,128)S(1)}, f32[256,256]{1,0:T(8,128)S(1)}, u32[]{:S(2)}, u32[]{:S(2)}) collective-permute-start(f32[256,256]{1,0:T(8,128)S(1)} %get-tuple-element.115.refs_0_.one.rest_0_), channel_id=1, source_target_pairs={{0,2},{1,5},{2,0},{3,7},{4,6},{5,1},{6,4},{7,3},{8,10},{9,13},{10,... | collective-permute-start | bytes 786440 | tf_op jit(solution)/shard_map/ppermute | solution.py:400
  33.5 9.7 %collective-permute-start.5 = (f32[2,256,256]{2,1,0:T(8,128)S(1)}, f32[2,256,256]{2,1,0:T(8,128)S(1)}, u32[]{:S(2)}, u32[]{:S(2)}) collective-permute-start(f32[2,256,256]{2,1,0:T(8,128)S(1)} %shard_map.100), channel_id=1, source_target_pairs={{0,4},{1,3},{2,6},{3,1},{4,0},{5,7},{6,2},{7,5},{8,12},{9,11},{10,... | collective-permute-start | bytes 1572872 | tf_op jit(solution)/shard_map/ppermute | solution.py:400
  34.2 9.0 %collective-permute-start.6 = (f32[256,256]{1,0:T(8,128)S(1)}, f32[256,256]{1,0:T(8,128)S(1)}, u32[]{:S(2)}, u32[]{:S(2)}) collective-permute-start(f32[256,256]{1,0:T(8,128)S(1)} %get-tuple-element.115.refs_0_.one.rest_0_), channel_id=1, source_target_pairs={{0,1},{1,0},{2,3},{3,2},{4,5},{5,4},{6,7},{7,6},{8,9},{9,8},{10,11... | collective-permute-start | bytes 786440 | tf_op jit(solution)/shard_map/ppermute | solution.py:403
  43.5 8.3 %collective-permute-start.8 = (f32[2,256,256]{2,1,0:T(8,128)S(1)}, f32[2,256,256]{2,1,0:T(8,128)S(1)}, u32[]{:S(2)}, u32[]{:S(2)}) collective-permute-start(f32[2,256,256]{2,1,0:T(8,128)S(1)} %collective-permute-done.5.refs_2_.rest_2_), channel_id=1, source_target_pairs={{0,1},{1,0},{2,3},{3,2},{4,5},{5,4},{6,7},{7,6},{8,9},{9,8},{10,11... | collective-permute-start | bytes 1572872 | tf_op jit(solution)/shard_map/ppermute | solution.py:403
  43.7 8.1 %collective-permute-start.7 = (f32[256,256]{1,0:T(8,128)S(1)}, f32[256,256]{1,0:T(8,128)S(1)}, u32[]{:S(2)}, u32[]{:S(2)}) collective-permute-start(f32[256,256]{1,0:T(8,128)S(1)} %collective-permute-done.4.two.refs_1_.rest_1_), channel_id=1, source_target_pairs={{0,1},{1,0},{2,3},{3,2},{4,5},{5,4},{6,7},{7,6},{8,9},{9,8},{10,11... | collective-permute-start | bytes 786440 | tf_op jit(solution)/shard_map/ppermute | solution.py:403
  53.0 9.5 %collective-permute-start.9 = (bf16[640,256]{1,0:T(8,128)(2,1)S(1)}, bf16[640,256]{1,0:T(8,128)(2,1)S(1)}, u32[]{:S(2)}, u32[]{:S(2)}) collective-permute-start(bf16[640,256]{1,0:T(8,128)(2,1)S(1)} %get-tuple-element.137.one.refs_0_.rest_0_), channel_id=1, source_target_pairs={{0,2},{1,5},{2,0},{3,7},{4,6},{5,1},{6,4},{7,3},{8,10},{9,13},{10,... | collective-permute-start | bytes 983048 | tf_op jit(solution)/shard_map/ppermute | solution.py:400
  62.8 11.0 %collective-permute-start.10 = (bf16[2,640,256]{2,1,0:T(8,128)(2,1)S(1)}, bf16[2,640,256]{2,1,0:T(8,128)(2,1)S(1)}, u32[]{:S(2)}, u32[]{:S(2)}) collective-permute-start(bf16[2,640,256]{2,1,0:T(8,128)(2,1)S(1)} %shard_map.104), channel_id=1, source_target_pairs={{0,4},{1,3},{2,6},{3,1},{4,0},{5,7},{6,2},{7,5},{8,12},{9,11},{10,... | collective-permute-start | bytes 1966088 | tf_op jit(solution)/shard_map/ppermute | solution.py:400
  63.4 10.4 %collective-permute-start.11 = (bf16[640,256]{1,0:T(8,128)(2,1)S(1)}, bf16[640,256]{1,0:T(8,128)(2,1)S(1)}, u32[]{:S(2)}, u32[]{:S(2)}) collective-permute-start(bf16[640,256]{1,0:T(8,128)(2,1)S(1)} %get-tuple-element.137.one.refs_0_.rest_0_), channel_id=1, source_target_pairs={{0,1},{1,0},{2,3},{3,2},{4,5},{5,4},{6,7},{7,6},{8,9},{9,8},{10,11... | collective-permute-start | bytes 983048 | tf_op jit(solution)/shard_map/ppermute | solution.py:403
  74.4 7.5 %collective-permute-start.13 = (bf16[2,640,256]{2,1,0:T(8,128)(2,1)S(1)}, bf16[2,640,256]{2,1,0:T(8,128)(2,1)S(1)}, u32[]{:S(2)}, u32[]{:S(2)}) collective-permute-start(bf16[2,640,256]{2,1,0:T(8,128)(2,1)S(1)} %collective-permute-done.10.refs_2_.rest_2_), channel_id=1, source_target_pairs={{0,1},{1,0},{2,3},{3,2},{4,5},{5,4},{6,7},{7,6},{8,9},{9,8},{10,11... | collective-permute-start | bytes 1966088 | tf_op jit(solution)/shard_map/ppermute | solution.py:403
  74.6 7.4 %collective-permute-start.12 = (bf16[640,256]{1,0:T(8,128)(2,1)S(1)}, bf16[640,256]{1,0:T(8,128)(2,1)S(1)}, u32[]{:S(2)}, u32[]{:S(2)}) collective-permute-start(bf16[640,256]{1,0:T(8,128)(2,1)S(1)} %collective-permute-done.9.two.refs_1_.rest_1_), channel_id=1, source_target_pairs={{0,1},{1,0},{2,3},{3,2},{4,5},{5,4},{6,7},{7,6},{8,9},{9,8},{10,11... | collective-permute-start | bytes 983048 | tf_op jit(solution)/shard_map/ppermute | solution.py:403
  92.2 9.5 %collective-permute-start.14 = (f32[256,256]{1,0:T(8,128)S(1)}, f32[256,256]{1,0:T(8,128)S(1)}, u32[]{:S(2)}, u32[]{:S(2)}) collective-permute-start(f32[256,256]{1,0:T(8,128)S(1)} %get-tuple-element.163.refs_0_.one.rest_0_.own), channel_id=1, source_target_pairs={{0,2},{1,5},{2,0},{3,7},{4,6},{5,1},{6,4},{7,3},{8,10},{9,13},{10,... | collective-permute-start | bytes 786440 | tf_op jit(solution)/shard_map/ppermute | solution.py:400
  101.9 9.7 %collective-permute-start.15 = (f32[2,256,256]{2,1,0:T(8,128)S(1)}, f32[2,256,256]{2,1,0:T(8,128)S(1)}, u32[]{:S(2)}, u32[]{:S(2)}) collective-permute-start(f32[2,256,256]{2,1,0:T(8,128)S(1)} %shard_map.109), channel_id=1, source_target_pairs={{0,4},{1,3},{2,6},{3,1},{4,0},{5,7},{6,2},{7,5},{8,12},{9,11},{10,... | collective-permute-start | bytes 1572872 | tf_op jit(solution)/shard_map/ppermute | solution.py:400
  102.6 9.0 %collective-permute-start.16 = (f32[256,256]{1,0:T(8,128)S(1)}, f32[256,256]{1,0:T(8,128)S(1)}, u32[]{:S(2)}, u32[]{:S(2)}) collective-permute-start(f32[256,256]{1,0:T(8,128)S(1)} %get-tuple-element.163.refs_0_.one.rest_0_.own), channel_id=1, source_target_pairs={{0,1},{1,0},{2,3},{3,2},{4,5},{5,4},{6,7},{7,6},{8,9},{9,8},{10,11... | collective-permute-start | bytes 786440 | tf_op jit(solution)/shard_map/ppermute | solution.py:403
  111.9 7.5 %collective-permute-start.18 = (f32[2,256,256]{2,1,0:T(8,128)S(1)}, f32[2,256,256]{2,1,0:T(8,128)S(1)}, u32[]{:S(2)}, u32[]{:S(2)}) collective-permute-start(f32[2,256,256]{2,1,0:T(8,128)S(1)} %collective-permute-done.15.refs_2_.rest_2_), channel_id=1, source_target_pairs={{0,1},{1,0},{2,3},{3,2},{4,5},{5,4},{6,7},{7,6},{8,9},{9,8},{10,11... | collective-permute-start | bytes 1572872 | tf_op jit(solution)/shard_map/ppermute | solution.py:403
  112.1 7.4 %collective-permute-start.17 = (f32[256,256]{1,0:T(8,128)S(1)}, f32[256,256]{1,0:T(8,128)S(1)}, u32[]{:S(2)}, u32[]{:S(2)}) collective-permute-start(f32[256,256]{1,0:T(8,128)S(1)} %collective-permute-done.14.two.refs_1_.rest_1_), channel_id=1, source_target_pairs={{0,1},{1,0},{2,3},{3,2},{4,5},{5,4},{6,7},{7,6},{8,9},{9,8},{10,11... | collective-permute-start | bytes 786440 | tf_op jit(solution)/shard_map/ppermute | solution.py:403

commit v20 on v19

--- a/solution.py
+++ b/solution.py
@@ -262,7 +262,7 @@
     places, rows, tile_paper, tile_author, tile_count, keep, swap, summed, class_prior,
     class_target, *rest,
 ):
-    kernels, (full, parts, *half) = views(rest, places), rest[1 + max(i for i, _ in places) :]
+    kernels, (full, parts, half) = views(rest, places), rest[1 + max(i for i, _ in places) :]
     columns = keep.shape[2]
     classes = full.shape[1]
     scale_cols = col_scale(summed, class_target)
@@ -283,8 +283,7 @@
         mass = jnp.dot(wide, jnp.concatenate(chosen, axis=0), preferred_element_type=jnp.float32)
         kernel = mass + class_prior[...]
         full[paper * rows : (paper + 1) * rows, :] = kernel
-        for out in half:
-            out[paper * rows : (paper + 1) * rows, :] = kernel.astype(jnp.bfloat16)
+        half[paper * rows : (paper + 1) * rows, :] = kernel.astype(jnp.bfloat16)
         column = column + jnp.sum(kernel, axis=0, keepdims=True)
     spread(column, parts)
 
@@ -415,7 +414,7 @@
         places = [(0, None), (1, None), (2, 0), (2, 1)]
         places += [(3 + places[k][0], places[k][1]) for k in turned(count)]
 
-    def balance(kernel, sent, local, steps, widest):
+    def balance(kernel, sent, local, steps, widest=False, last=False):
         here, there, joined = [sent], [], None
         sides = 0
         for step in range(steps):
@@ -426,9 +425,10 @@
                 moves = [(joined, *ways[2])] if four else [(sent, *way) for way in ways[3:]]
             moves = [across_pairs(*move) for move in moves]
             others = [] if step == 0 else [sent] if step == 1 else here[len(there) :]
-            others = [to_other(one) for one in others]
+            others = [] if last else [to_other(one) for one in others]
             if sides:
-                summed = narrow_exchange(local, sides, step + 1 == steps and sides == 2)
+                upwards = step + 1 == steps and sides == 2 and not last
+                summed = narrow_exchange(local, sides, upwards)
             else:
                 summed = exchange(local)
             summed, *moved = lax.optimization_barrier((summed, *moves, *others))
@@ -452,13 +452,6 @@
                 local, sent, joined, *here = lax.optimization_barrier((local, sent, joined, *here))
         return summed, here + there
 
-    def last_balance(kernel, local):
-        for step in range(ITERS):
-            summed = exchange(local)
-            if step + 1 < ITERS:
-                local = call(balance_kernel, parts, [VMEM] * 3)(kernel, summed, target)
-        return summed
-
     for repeat in range(ROUNDS):
         if repeat == 0:
             own, local = call(
@@ -472,19 +465,16 @@
                 [VMEM] * (3 + len(kernels) + len(held)),
             )(summed, prior, target, *kernels, *held)
             left = ITERS
-        author_summed, kernels = balance(own, own, local, left, True)
+        author_summed, kernels = balance(own, own, local, left, widest=True)
         last = repeat + 1 == ROUNDS
-        kernel, local, *half = call(
+        kernel, local, half = call(
             functools.partial(paper_kernel, places, rows),
-            paper_out[:2] if last else paper_out,
+            paper_out,
             [SMEM, SMEM, SMEM] + [VMEM] * (5 + len(kernels)),
         )(
             tile_paper, tile_author, tile_count, keep, swap, author_summed, prior, target, *kernels
         )
-        if last:
-            summed = last_balance(kernel, local)
-        else:
-            summed, kernels = balance(kernel, half[0], local, ITERS, False)
+        summed, kernels = balance(kernel, half, local, ITERS, last=last)
     return call(
         functools.partial(final_kernel, rows),
         (shape((papers, classes), f32), shape((authors, classes), f32)),

time: 167 us -> 167 us (level)
    all_to_all x11 -> x9, blocking collectives: 105 us -> 89.1 us  [exchange(): return lax.all_to_all(parts, AXES, split_axis=0, concat_axis=0, tiled=True)]
    all_to_all x5 -> x7, blocking collectives: 36.7 us -> 50.7 us  [narrow_exchange(): lax.all_to_all(parts, AXES, split_axis=0, concat_axis=0, axis_index_group...]
    pallas_call x8 -> x11, Pallas kernels: 2.74 us -> 4.13 us  [balance(): call(balance_kernel, shape((size, 1, classes), f32), [VMEM] * (len(added)...]
    ppermute x9 -> x11, starting transfers between devices: 8.03 us -> 9.21 us  [across_pairs(): lax.ppermute(value, 'blk', [(i, i ^ hop) for i, hop in enumerate(hops)])]
  transfers between devices with their start and end apart: 19 -> 21, of which waited for: 1 -> 1; matrix products, arithmetic and copies ran while one was open for 0% -> 0% of each run, Pallas kernels for 1% -> 1%
where the time goes in v20:
time: 167 us; the launch traced here: 166 us
  blocking collectives  140 us (84%)
  Pallas kernels  13.4 us (8%)
  starting transfers between devices  11.5 us (7%)
    all_to_all x9, blocking collectives, exchange(): return lax.all_to_all(parts, AXES, split_axis=0, concat_axis=0, tiled=True)  89.1 us
    all_to_all x7, blocking collectives, narrow_exchange(): lax.all_to_all(parts, AXES, split_axis=0, concat_axis=0, axis_index_group...  50.7 us
    ppermute x11, starting transfers between devices, across_pairs(): lax.ppermute(value, 'blk', [(i, i ^ hop) for i, hop in enumerate(hops)])  9.21 us
    pallas_call x11, Pallas kernels, balance(): call(balance_kernel, shape((size, 1, classes), f32), [VMEM] * (len(added)...  4.13 us
  transfers between devices with their start and end apart: 21, of which 1 were waited for; matrix products, arithmetic and copies ran while one was open for 0% of the time, Pallas kernels for 1%

profile of v20, /device:TPU:0, one launch (start us, length us, event | category | flops | bytes accessed | tf_op | source)
XLA Modules:
  0.0 166.3 jit_solution(7238809712596971981)
XLA Ops:
  1.3 1.9 %shard_map.95 = (s32[8]{0:T(128)S(1)}, s32[8]{0:T(128)S(1)}, s32[5,128]{1,0:T(8,128)S(1)}, s32[5,128]{1,0:T(8,128)S(1)}, f32[1,256]{1,0:T(1,128)S(1)}, /*index=5...) custom-call(s32[1]{0:T(128)S(6)} %copy.10.tile_count, ...), custom_call_target="tpu_custom_call" | custom-call | tf_op jit(solution)/shard_map/pallas_call | solution.py:380
  3.8 1.1 shard_map.96
  5.1 2.9 %collective-permute-start.1 = (bf16[2,336,128]{2,1,0:T(8,128)(2,1)S(1)}, bf16[2,336,128]{2,1,0:T(8,128)(2,1)S(1)}, u32[]{:S(2)}, u32[]{:S(2)}) collective-permute-start(bf16[2,336,128]{2,1,0:T(8,128)(2,1)S(1)} %get-tuple-element.111), channel_id=1, source_target_pairs={{0,2},{1,5},{2,0},{3,7},{4,6},{5,1},{6,4},{7,3},{8,10},{9,13},{10,... | collective-permute-start | bytes 516104 | tf_op jit(solution)/shard_map/ppermute | solution.py:399
  8.0 1.5 collective-permute-start.2
  9.5 13.4 %all_to_all.80.summed = f32[32,1,256]{2,1,0:T(1,128)S(1)} all-to-all(f32[32,1,256]{2,1,0:T(1,128)S(1)} %shard_map.96), channel_id=1, replica_groups=mesh['grp'=4,'blk'=8] {'grp','blk'}, dimensions={0} | all-to-all | bytes 65536 | tf_op jit(solution)/shard_map/all_to_all | solution.py:332
  24.3 9.0 %all_to_all.81.refs_1_ = f32[32,1,256]{2,1,0:T(1,128)S(1)} all-to-all(f32[32,1,256]{2,1,0:T(1,128)S(1)} %get-tuple-element.115), channel_id=1, replica_groups=mesh['grp'=4,'blk'=8] {'grp','blk'}, dimensions={0} | all-to-all | bytes 65536 | tf_op jit(solution)/shard_map/all_to_all | solution.py:332
  34.2 9.0 %all_to_all.82.refs_3_ = f32[32,1,256]{2,1,0:T(1,128)S(1)} all-to-all(f32[32,1,256]{2,1,0:T(1,128)S(1)} %shard_map.99), channel_id=1, replica_groups=mesh['grp'=4,'blk'=8] {'grp','blk'}, dimensions={0} | all-to-all | bytes 65536 | tf_op jit(solution)/shard_map/all_to_all | solution.py:332
  44.1 7.7 %all_to_all.83.summed = f32[8,1,256]{2,1,0:T(1,128)S(1)} all-to-all(f32[8,1,256]{2,1,0:T(1,128)S(1)} %shard_map.101), channel_id=1, replica_groups={{1,0,9,8,17,16,25,24},{3,2,11,10,19,18,27,26},{5,4,13,12,21,20,29,28},{..., dimensions={0} | all-to-all | bytes 16384 | tf_op jit(solution)/shard_map/all_to_all | solution.py:344
  51.8 1.2 shard_map.102
  53.5 9.0 %all_to_all.84.refs_1_ = f32[32,1,256]{2,1,0:T(1,128)S(1)} all-to-all(f32[32,1,256]{2,1,0:T(1,128)S(1)} %get-tuple-element.134), channel_id=1, replica_groups=mesh['grp'=4,'blk'=8] {'grp','blk'}, dimensions={0} | all-to-all | bytes 65536 | tf_op jit(solution)/shard_map/all_to_all | solution.py:332
  63.4 10.4 %all_to_all.85.refs_3_ = f32[32,1,256]{2,1,0:T(1,128)S(1)} all-to-all(f32[32,1,256]{2,1,0:T(1,128)S(1)} %shard_map.103), channel_id=1, replica_groups=mesh['grp'=4,'blk'=8] {'grp','blk'}, dimensions={0} | all-to-all | bytes 65536 | tf_op jit(solution)/shard_map/all_to_all | solution.py:332
  75.0 7.0 %all_to_all.86.refs_3_ = f32[8,1,256]{2,1,0:T(1,128)S(1)} all-to-all(f32[8,1,256]{2,1,0:T(1,128)S(1)} %shard_map.105), channel_id=1, replica_groups={{9,8,17,16,1,0,25,24},{11,10,19,18,3,2,27,26},{13,12,21,20,5,4,29,28},{..., dimensions={0} | all-to-all | bytes 16384 | tf_op jit(solution)/shard_map/all_to_all | solution.py:344
  82.6 7.9 %all_to_all.87.summed = f32[8,1,256]{2,1,0:T(1,128)S(1)} all-to-all(f32[8,1,256]{2,1,0:T(1,128)S(1)} %shard_map.106), channel_id=1, replica_groups={{1,0,9,8,17,16,25,24},{3,2,11,10,19,18,27,26},{5,4,13,12,21,20,29,28},{..., dimensions={0} | all-to-all | bytes 16384 | tf_op jit(solution)/shard_map/all_to_all | solution.py:344
  90.4 1.7 %shard_map.107 = (f32[256,256]{1,0:T(8,128)S(1)}, f32[32,1,256]{2,1,0:T(1,128)S(1)}) custom-call(f32[8,1,256]{2,1,0:T(1,128)S(1)} %all_to_all.87.summed, f32[1,256]{1,0:T(1,128)S(1)} %get-tuple-element.105.class_prior, f32[1,256]{1,0:T(1,128)S(1)} %get-tuple-element.110.class_target.refs_2_.refs_4_.refs_7_, ...), custom_call_target="tpu_custom_call" | custom-call | tf_op jit(solution)/shard_map/pallas_call | solution.py:462
  92.7 9.0 %all_to_all.88.refs_1_ = f32[32,1,256]{2,1,0:T(1,128)S(1)} all-to-all(f32[32,1,256]{2,1,0:T(1,128)S(1)} %get-tuple-element.158), channel_id=1, replica_groups=mesh['grp'=4,'blk'=8] {'grp','blk'}, dimensions={0} | all-to-all | bytes 65536 | tf_op jit(solution)/shard_map/all_to_all | solution.py:332
  102.6 9.0 %all_to_all.89.refs_3_ = f32[32,1,256]{2,1,0:T(1,128)S(1)} all-to-all(f32[32,1,256]{2,1,0:T(1,128)S(1)} %shard_map.108), channel_id=1, replica_groups=mesh['grp'=4,'blk'=8] {'grp','blk'}, dimensions={0} | all-to-all | bytes 65536 | tf_op jit(solution)/shard_map/all_to_all | solution.py:332
  112.5 7.0 %all_to_all.90.refs_6_ = f32[8,1,256]{2,1,0:T(1,128)S(1)} all-to-all(f32[8,1,256]{2,1,0:T(1,128)S(1)} %shard_map.110), channel_id=1, replica_groups={{9,8,17,16,1,0,25,24},{11,10,19,18,3,2,27,26},{13,12,21,20,5,4,29,28},{..., dimensions={0} | all-to-all | bytes 16384 | tf_op jit(solution)/shard_map/all_to_all | solution.py:344
  119.9 7.2 %all_to_all.91.summed.author_summed = f32[4,1,256]{2,1,0:T(1,128)S(1)} all-to-all(f32[4,1,256]{2,1,0:T(1,128)S(1)} %shard_map.111), channel_id=1, replica_groups={{8,16,0,24},{9,17,1,25},{10,18,2,26},{11,19,3,27},{12,20,4,28},{13,21,5..., dimensions={0} | all-to-all | bytes 8192 | tf_op jit(solution)/shard_map/all_to_all | solution.py:344
  127.1 1.2 shard_map.112
  128.9 9.8 %all_to_all.92.refs_1_ = f32[32,1,256]{2,1,0:T(1,128)S(1)} all-to-all(f32[32,1,256]{2,1,0:T(1,128)S(1)} %get-tuple-element.181), channel_id=1, replica_groups=mesh['grp'=4,'blk'=8] {'grp','blk'}, dimensions={0} | all-to-all | bytes 65536 | tf_op jit(solution)/shard_map/all_to_all | solution.py:332
  139.6 10.4 %all_to_all.93.refs_3_ = f32[32,1,256]{2,1,0:T(1,128)S(1)} all-to-all(f32[32,1,256]{2,1,0:T(1,128)S(1)} %shard_map.113), channel_id=1, replica_groups=mesh['grp'=4,'blk'=8] {'grp','blk'}, dimensions={0} | all-to-all | bytes 65536 | tf_op jit(solution)/shard_map/all_to_all | solution.py:332
  150.6 7.0 %all_to_all.94.refs_3_ = f32[8,1,256]{2,1,0:T(1,128)S(1)} all-to-all(f32[8,1,256]{2,1,0:T(1,128)S(1)} %shard_map.115), channel_id=1, replica_groups={{9,8,17,16,1,0,25,24},{11,10,19,18,3,2,27,26},{13,12,21,20,5,4,29,28},{..., dimensions={0} | all-to-all | bytes 16384 | tf_op jit(solution)/shard_map/all_to_all | solution.py:344
  158.2 7.0 %all_to_all.95.summed = f32[8,1,256]{2,1,0:T(1,128)S(1)} all-to-all(f32[8,1,256]{2,1,0:T(1,128)S(1)} %shard_map.116), channel_id=1, replica_groups={{9,8,17,16,1,0,25,24},{11,10,19,18,3,2,27,26},{13,12,21,20,5,4,29,28},{..., dimensions={0} | all-to-all | bytes 16384 | tf_op jit(solution)/shard_map/all_to_all | solution.py:344
  165.2 1.1 shard_map.117
  (57 shorter events, 12.4 us)
Async XLA Ops:
  3.2 1.8 %collective-permute-start = (bf16[4,336,128]{2,1,0:T(8,128)(2,1)S(1)}, bf16[4,336,128]{2,1,0:T(8,128)(2,1)S(1)}, u32[]{:S(2)}, u32[]{:S(2)}) collective-permute-start(bf16[4,336,128]{2,1,0:T(8,128)(2,1)S(1)} %get-tuple-element.102.swap), channel_id=1, source_target_pairs={{0,1},{1,0},{2,3},{3,2},{4,5},{5,4},{6,7},{7,6},{8,9},{9,8},{10,11... | collective-permute-start | bytes 1032200 | tf_op jit(solution)/shard_map/ppermute | solution.py:388
  5.1 17.8 %collective-permute-start.1 = (bf16[2,336,128]{2,1,0:T(8,128)(2,1)S(1)}, bf16[2,336,128]{2,1,0:T(8,128)(2,1)S(1)}, u32[]{:S(2)}, u32[]{:S(2)}) collective-permute-start(bf16[2,336,128]{2,1,0:T(8,128)(2,1)S(1)} %get-tuple-element.111), channel_id=1, source_target_pairs={{0,2},{1,5},{2,0},{3,7},{4,6},{5,1},{6,4},{7,3},{8,10},{9,13},{10,... | collective-permute-start | bytes 516104 | tf_op jit(solution)/shard_map/ppermute | solution.py:399
  8.0 14.9 %collective-permute-start.2 = (bf16[2,336,128]{2,1,0:T(8,128)(2,1)S(1)}, bf16[2,336,128]{2,1,0:T(8,128)(2,1)S(1)}, u32[]{:S(2)}, u32[]{:S(2)}) collective-permute-start(bf16[2,336,128]{2,1,0:T(8,128)(2,1)S(1)} %get-tuple-element.112), channel_id=1, source_target_pairs={{0,4},{1,3},{2,6},{3,1},{4,0},{5,7},{6,2},{7,5},{8,12},{9,11},{10,... | collective-permute-start | bytes 516104 | tf_op jit(solution)/shard_map/ppermute | solution.py:399
  9.5 13.4 %collective-permute-start.3 = (bf16[2,336,128]{2,1,0:T(8,128)(2,1)S(1)}, bf16[2,336,128]{2,1,0:T(8,128)(2,1)S(1)}, u32[]{:S(2)}, u32[]{:S(2)}) collective-permute-start(bf16[2,336,128]{2,1,0:T(8,128)(2,1)S(1)} %get-tuple-element.113), channel_id=1, source_target_pairs={{0,6},{1,7},{2,4},{3,5},{4,2},{5,3},{6,0},{7,1},{8,14},{9,15},{10,... | collective-permute-start | bytes 516104 | tf_op jit(solution)/shard_map/ppermute | solution.py:399
  23.7 9.6 %collective-permute-start.4 = (f32[256,256]{1,0:T(8,128)S(1)}, f32[256,256]{1,0:T(8,128)S(1)}, u32[]{:S(2)}, u32[]{:S(2)}) collective-permute-start(f32[256,256]{1,0:T(8,128)S(1)} %get-tuple-element.129.refs_0_.one.rest_0_), channel_id=1, source_target_pairs={{0,2},{1,5},{2,0},{3,7},{4,6},{5,1},{6,4},{7,3},{8,10},{9,13},{10,... | collective-permute-start | bytes 786440 | tf_op jit(solution)/shard_map/ppermute | solution.py:399
  33.5 9.7 %collective-permute-start.5 = (f32[2,256,256]{2,1,0:T(8,128)S(1)}, f32[2,256,256]{2,1,0:T(8,128)S(1)}, u32[]{:S(2)}, u32[]{:S(2)}) collective-permute-start(f32[2,256,256]{2,1,0:T(8,128)S(1)} %shard_map.100), channel_id=1, source_target_pairs={{0,4},{1,3},{2,6},{3,1},{4,0},{5,7},{6,2},{7,5},{8,12},{9,11},{10,... | collective-permute-start | bytes 1572872 | tf_op jit(solution)/shard_map/ppermute | solution.py:399
  34.2 9.0 %collective-permute-start.6 = (f32[256,256]{1,0:T(8,128)S(1)}, f32[256,256]{1,0:T(8,128)S(1)}, u32[]{:S(2)}, u32[]{:S(2)}) collective-permute-start(f32[256,256]{1,0:T(8,128)S(1)} %get-tuple-element.129.refs_0_.one.rest_0_), channel_id=1, source_target_pairs={{0,1},{1,0},{2,3},{3,2},{4,5},{5,4},{6,7},{7,6},{8,9},{9,8},{10,11... | collective-permute-start | bytes 786440 | tf_op jit(solution)/shard_map/ppermute | solution.py:402
  43.5 8.3 %collective-permute-start.8 = (f32[2,256,256]{2,1,0:T(8,128)S(1)}, f32[2,256,256]{2,1,0:T(8,128)S(1)}, u32[]{:S(2)}, u32[]{:S(2)}) collective-permute-start(f32[2,256,256]{2,1,0:T(8,128)S(1)} %collective-permute-done.5.refs_2_.rest_2_), channel_id=1, source_target_pairs={{0,1},{1,0},{2,3},{3,2},{4,5},{5,4},{6,7},{7,6},{8,9},{9,8},{10,11... | collective-permute-start | bytes 1572872 | tf_op jit(solution)/shard_map/ppermute | solution.py:402
  43.7 8.1 %collective-permute-start.7 = (f32[256,256]{1,0:T(8,128)S(1)}, f32[256,256]{1,0:T(8,128)S(1)}, u32[]{:S(2)}, u32[]{:S(2)}) collective-permute-start(f32[256,256]{1,0:T(8,128)S(1)} %collective-permute-done.4.two.refs_1_.rest_1_), channel_id=1, source_target_pairs={{0,1},{1,0},{2,3},{3,2},{4,5},{5,4},{6,7},{7,6},{8,9},{9,8},{10,11... | collective-permute-start | bytes 786440 | tf_op jit(solution)/shard_map/ppermute | solution.py:402
  53.0 9.5 %collective-permute-start.9 = (bf16[640,256]{1,0:T(8,128)(2,1)S(1)}, bf16[640,256]{1,0:T(8,128)(2,1)S(1)}, u32[]{:S(2)}, u32[]{:S(2)}) collective-permute-start(bf16[640,256]{1,0:T(8,128)(2,1)S(1)} %get-tuple-element.151.one.refs_0_.rest_0_), channel_id=1, source_target_pairs={{0,2},{1,5},{2,0},{3,7},{4,6},{5,1},{6,4},{7,3},{8,10},{9,13},{10,... | collective-permute-start | bytes 983048 | tf_op jit(solution)/shard_map/ppermute | solution.py:399
  62.8 11.0 %collective-permute-start.10 = (bf16[2,640,256]{2,1,0:T(8,128)(2,1)S(1)}, bf16[2,640,256]{2,1,0:T(8,128)(2,1)S(1)}, u32[]{:S(2)}, u32[]{:S(2)}) collective-permute-start(bf16[2,640,256]{2,1,0:T(8,128)(2,1)S(1)} %shard_map.104), channel_id=1, source_target_pairs={{0,4},{1,3},{2,6},{3,1},{4,0},{5,7},{6,2},{7,5},{8,12},{9,11},{10,... | collective-permute-start | bytes 1966088 | tf_op jit(solution)/shard_map/ppermute | solution.py:399
  63.4 10.4 %collective-permute-start.11 = (bf16[640,256]{1,0:T(8,128)(2,1)S(1)}, bf16[640,256]{1,0:T(8,128)(2,1)S(1)}, u32[]{:S(2)}, u32[]{:S(2)}) collective-permute-start(bf16[640,256]{1,0:T(8,128)(2,1)S(1)} %get-tuple-element.151.one.refs_0_.rest_0_), channel_id=1, source_target_pairs={{0,1},{1,0},{2,3},{3,2},{4,5},{5,4},{6,7},{7,6},{8,9},{9,8},{10,11... | collective-permute-start | bytes 983048 | tf_op jit(solution)/shard_map/ppermute | solution.py:402
  74.4 7.5 %collective-permute-start.13 = (bf16[2,640,256]{2,1,0:T(8,128)(2,1)S(1)}, bf16[2,640,256]{2,1,0:T(8,128)(2,1)S(1)}, u32[]{:S(2)}, u32[]{:S(2)}) collective-permute-start(bf16[2,640,256]{2,1,0:T(8,128)(2,1)S(1)} %collective-permute-done.10.refs_2_.rest_2_), channel_id=1, source_target_pairs={{0,1},{1,0},{2,3},{3,2},{4,5},{5,4},{6,7},{7,6},{8,9},{9,8},{10,11... | collective-permute-start | bytes 1966088 | tf_op jit(solution)/shard_map/ppermute | solution.py:402
  74.6 7.4 %collective-permute-start.12 = (bf16[640,256]{1,0:T(8,128)(2,1)S(1)}, bf16[640,256]{1,0:T(8,128)(2,1)S(1)}, u32[]{:S(2)}, u32[]{:S(2)}) collective-permute-start(bf16[640,256]{1,0:T(8,128)(2,1)S(1)} %collective-permute-done.9.two.refs_1_.rest_1_), channel_id=1, source_target_pairs={{0,1},{1,0},{2,3},{3,2},{4,5},{5,4},{6,7},{7,6},{8,9},{9,8},{10,11... | collective-permute-start | bytes 983048 | tf_op jit(solution)/shard_map/ppermute | solution.py:402
  92.2 9.5 %collective-permute-start.14 = (f32[256,256]{1,0:T(8,128)S(1)}, f32[256,256]{1,0:T(8,128)S(1)}, u32[]{:S(2)}, u32[]{:S(2)}) collective-permute-start(f32[256,256]{1,0:T(8,128)S(1)} %get-tuple-element.177.refs_0_.one.rest_0_.own), channel_id=1, source_target_pairs={{0,2},{1,5},{2,0},{3,7},{4,6},{5,1},{6,4},{7,3},{8,10},{9,13},{10,... | collective-permute-start | bytes 786440 | tf_op jit(solution)/shard_map/ppermute | solution.py:399
  101.9 9.7 %collective-permute-start.15 = (f32[2,256,256]{2,1,0:T(8,128)S(1)}, f32[2,256,256]{2,1,0:T(8,128)S(1)}, u32[]{:S(2)}, u32[]{:S(2)}) collective-permute-start(f32[2,256,256]{2,1,0:T(8,128)S(1)} %shard_map.109), channel_id=1, source_target_pairs={{0,4},{1,3},{2,6},{3,1},{4,0},{5,7},{6,2},{7,5},{8,12},{9,11},{10,... | collective-permute-start | bytes 1572872 | tf_op jit(solution)/shard_map/ppermute | solution.py:399
  102.6 9.0 %collective-permute-start.16 = (f32[256,256]{1,0:T(8,128)S(1)}, f32[256,256]{1,0:T(8,128)S(1)}, u32[]{:S(2)}, u32[]{:S(2)}) collective-permute-start(f32[256,256]{1,0:T(8,128)S(1)} %get-tuple-element.177.refs_0_.one.rest_0_.own), channel_id=1, source_target_pairs={{0,1},{1,0},{2,3},{3,2},{4,5},{5,4},{6,7},{7,6},{8,9},{9,8},{10,11... | collective-permute-start | bytes 786440 | tf_op jit(solution)/shard_map/ppermute | solution.py:402
  111.9 7.5 %collective-permute-start.18 = (f32[2,256,256]{2,1,0:T(8,128)S(1)}, f32[2,256,256]{2,1,0:T(8,128)S(1)}, u32[]{:S(2)}, u32[]{:S(2)}) collective-permute-start(f32[2,256,256]{2,1,0:T(8,128)S(1)} %collective-permute-done.15.refs_2_.rest_2_), channel_id=1, source_target_pairs={{0,1},{1,0},{2,3},{3,2},{4,5},{5,4},{6,7},{7,6},{8,9},{9,8},{10,11... | collective-permute-start | bytes 1572872 | tf_op jit(solution)/shard_map/ppermute | solution.py:402
  112.1 7.4 %collective-permute-start.17 = (f32[256,256]{1,0:T(8,128)S(1)}, f32[256,256]{1,0:T(8,128)S(1)}, u32[]{:S(2)}, u32[]{:S(2)}) collective-permute-start(f32[256,256]{1,0:T(8,128)S(1)} %collective-permute-done.14.two.refs_1_.rest_1_), channel_id=1, source_target_pairs={{0,1},{1,0},{2,3},{3,2},{4,5},{5,4},{6,7},{7,6},{8,9},{9,8},{10,11... | collective-permute-start | bytes 786440 | tf_op jit(solution)/shard_map/ppermute | solution.py:402
  128.3 10.4 %collective-permute-start.19 = (bf16[640,256]{1,0:T(8,128)(2,1)S(1)}, bf16[640,256]{1,0:T(8,128)(2,1)S(1)}, u32[]{:S(2)}, u32[]{:S(2)}) collective-permute-start(bf16[640,256]{1,0:T(8,128)(2,1)S(1)} %get-tuple-element.191.one.refs_0_), channel_id=1, source_target_pairs={{0,2},{1,5},{2,0},{3,7},{4,6},{5,1},{6,4},{7,3},{8,10},{9,13},{10,... | collective-permute-start | bytes 983048 | tf_op jit(solution)/shard_map/ppermute | solution.py:399
  139.0 11.0 %collective-permute-start.20 = (bf16[2,640,256]{2,1,0:T(8,128)(2,1)S(1)}, bf16[2,640,256]{2,1,0:T(8,128)(2,1)S(1)}, u32[]{:S(2)}, u32[]{:S(2)}) collective-permute-start(bf16[2,640,256]{2,1,0:T(8,128)(2,1)S(1)} %shard_map.114), channel_id=1, source_target_pairs={{0,4},{1,3},{2,6},{3,1},{4,0},{5,7},{6,2},{7,5},{8,12},{9,11},{10,... | collective-permute-start | bytes 1966088 | tf_op jit(solution)/shard_map/ppermute | solution.py:399

commit v21 on v19

--- a/solution.py
+++ b/solution.py
@@ -142,9 +142,18 @@
         copy.wait()
 
 
-def join_kernel(one, two, out):
-    out[0] = one[...]
-    out[1] = two[...]
+def pieces(refs):
+    return [(ref, i) for ref in refs for i in range(ref.shape[0] if ref.ndim == 3 else 1)]
+
+
+def piece(ref, i):
+    return ref[i] if ref.ndim == 3 else ref[...]
+
+
+def join_kernel(*refs):
+    *ins, out = refs
+    for place, one in enumerate(pieces(ins)):
+        out[place] = piece(*one)
 
 
 def pair_kernel(keep, swapped, *outs):
@@ -293,9 +302,8 @@
     *kernels, summed, class_target, parts = refs
     scale_cols = col_scale(summed, class_target)
     total = None
-    refs = [(ref, i) for ref in kernels for i in range(ref.shape[0] if ref.ndim == 3 else 1)]
-    for ref, i in refs:
-        kernel = (ref[i] if ref.ndim == 3 else ref[...]).astype(jnp.float32)
+    for one in pieces(kernels):
+        kernel = piece(*one).astype(jnp.float32)
         local = jnp.sum(row_scale(kernel, scale_cols) * kernel, axis=0, keepdims=True)
         total = local if total is None else total + local
     spread(total, parts)
@@ -413,7 +421,7 @@
     places = [(i, None) for i in range(blocks)]
     if four:
         places = [(0, None), (1, None), (2, 0), (2, 1)]
-        places += [(3 + places[k][0], places[k][1]) for k in turned(count)]
+        places += [(3, k) for k in turned(count)]
 
     def balance(kernel, sent, local, steps, widest):
         here, there, joined = [sent], [], None
@@ -426,6 +434,8 @@
                 moves = [(joined, *ways[2])] if four else [(sent, *way) for way in ways[3:]]
             moves = [across_pairs(*move) for move in moves]
             others = [] if step == 0 else [sent] if step == 1 else here[len(there) :]
+            if four:
+                others = [joined] if step == 2 else []
             others = [to_other(one) for one in others]
             if sides:
                 summed = narrow_exchange(local, sides, step + 1 == steps and sides == 2)
@@ -447,8 +457,10 @@
                     balance_kernel, shape((size, 1, classes), f32), [VMEM] * (len(added) + 2)
                 )(*added, summed, target)
                 joined = sent
-                if four and step == 0:
-                    joined = call(join_kernel, shape((2, *sent.shape), sent.dtype), [VMEM] * 2)(*here)
+                if four and step < 2:
+                    joined = call(
+                        join_kernel, shape((2 * step + 2, *sent.shape), sent.dtype), [VMEM] * len(here)
+                    )(*here)
                 local, sent, joined, *here = lax.optimization_barrier((local, sent, joined, *here))
         return summed, here + there
 

time: 167 us -> 166 us (level)
  transfers between devices with their start and end apart: 19 -> 13, of which waited for: 1 -> 1; matrix products, arithmetic and copies ran while one was open for 0% -> 0% of each run, Pallas kernels for 1% -> 1%
where the time goes in v21:
time: 166 us; the launch traced here: 165 us
  blocking collectives  142 us (86%)
  Pallas kernels  12.8 us (8%)
  starting transfers between devices  8.9 us (5%)
    all_to_all x11, blocking collectives, exchange(): return lax.all_to_all(parts, AXES, split_axis=0, concat_axis=0, tiled=True)  105 us
    all_to_all x5, blocking collectives, narrow_exchange(): lax.all_to_all(parts, AXES, split_axis=0, concat_axis=0, axis_index_group...  37.5 us
    ppermute x9, starting transfers between devices, across_pairs(): lax.ppermute(value, 'blk', [(i, i ^ hop) for i, hop in enumerate(hops)])  8.01 us
  transfers between devices with their start and end apart: 13, of which 1 were waited for; matrix products, arithmetic and copies ran while one was open for 0% of the time, Pallas kernels for 1%

profile of v21, /device:TPU:0, one launch (start us, length us, event | category | flops | bytes accessed | tf_op | source)
XLA Modules:
  0.0 165.4 jit_solution(2419996922727835573)
XLA Ops:
  1.3 1.9 %shard_map.95 = (s32[8]{0:T(128)S(1)}, s32[8]{0:T(128)S(1)}, s32[5,128]{1,0:T(8,128)S(1)}, s32[5,128]{1,0:T(8,128)S(1)}, f32[1,256]{1,0:T(1,128)S(1)}, /*index=5...) custom-call(s32[1]{0:T(128)S(6)} %copy.10.tile_count, ...), custom_call_target="tpu_custom_call" | custom-call | tf_op jit(solution)/shard_map/pallas_call | solution.py:389
  3.8 1.1 shard_map.96
  5.1 2.9 %collective-permute-start.1 = (bf16[2,336,128]{2,1,0:T(8,128)(2,1)S(1)}, bf16[2,336,128]{2,1,0:T(8,128)(2,1)S(1)}, u32[]{:S(2)}, u32[]{:S(2)}) collective-permute-start(bf16[2,336,128]{2,1,0:T(8,128)(2,1)S(1)} %get-tuple-element.91), channel_id=1, source_target_pairs={{0,2},{1,5},{2,0},{3,7},{4,6},{5,1},{6,4},{7,3},{8,10},{9,13},{10,... | collective-permute-start | bytes 516104 | tf_op jit(solution)/shard_map/ppermute | solution.py:408
  8.0 1.5 collective-permute-start.2
  9.5 13.4 %all_to_all.80.summed = f32[32,1,256]{2,1,0:T(1,128)S(1)} all-to-all(f32[32,1,256]{2,1,0:T(1,128)S(1)} %shard_map.96), channel_id=1, replica_groups=mesh['grp'=4,'blk'=8] {'grp','blk'}, dimensions={0} | all-to-all | bytes 65536 | tf_op jit(solution)/shard_map/all_to_all | solution.py:341
  24.3 9.0 %all_to_all.81.refs_1_ = f32[32,1,256]{2,1,0:T(1,128)S(1)} all-to-all(f32[32,1,256]{2,1,0:T(1,128)S(1)} %get-tuple-element.95), channel_id=1, replica_groups=mesh['grp'=4,'blk'=8] {'grp','blk'}, dimensions={0} | all-to-all | bytes 65536 | tf_op jit(solution)/shard_map/all_to_all | solution.py:341
  34.2 9.0 %all_to_all.82.refs_3_ = f32[32,1,256]{2,1,0:T(1,128)S(1)} all-to-all(f32[32,1,256]{2,1,0:T(1,128)S(1)} %shard_map.99), channel_id=1, replica_groups=mesh['grp'=4,'blk'=8] {'grp','blk'}, dimensions={0} | all-to-all | bytes 65536 | tf_op jit(solution)/shard_map/all_to_all | solution.py:341
  43.6 8.0 %all_to_all.83.summed = f32[8,1,256]{2,1,0:T(1,128)S(1)} all-to-all(f32[8,1,256]{2,1,0:T(1,128)S(1)} %shard_map.101), channel_id=1, replica_groups={{1,0,9,8,17,16,25,24},{3,2,11,10,19,18,27,26},{5,4,13,12,21,20,29,28},{..., dimensions={0} | all-to-all | bytes 16384 | tf_op jit(solution)/shard_map/all_to_all | solution.py:353
  51.7 1.2 shard_map.103
  53.4 9.0 %all_to_all.84.refs_1_ = f32[32,1,256]{2,1,0:T(1,128)S(1)} all-to-all(f32[32,1,256]{2,1,0:T(1,128)S(1)} %get-tuple-element.112), channel_id=1, replica_groups=mesh['grp'=4,'blk'=8] {'grp','blk'}, dimensions={0} | all-to-all | bytes 65536 | tf_op jit(solution)/shard_map/all_to_all | solution.py:341
  63.3 10.4 %all_to_all.85.refs_3_ = f32[32,1,256]{2,1,0:T(1,128)S(1)} all-to-all(f32[32,1,256]{2,1,0:T(1,128)S(1)} %shard_map.104), channel_id=1, replica_groups=mesh['grp'=4,'blk'=8] {'grp','blk'}, dimensions={0} | all-to-all | bytes 65536 | tf_op jit(solution)/shard_map/all_to_all | solution.py:341
  74.6 7.1 %all_to_all.86.refs_3_ = f32[8,1,256]{2,1,0:T(1,128)S(1)} all-to-all(f32[8,1,256]{2,1,0:T(1,128)S(1)} %shard_map.106), channel_id=1, replica_groups={{9,8,17,16,1,0,25,24},{11,10,19,18,3,2,27,26},{13,12,21,20,5,4,29,28},{..., dimensions={0} | all-to-all | bytes 16384 | tf_op jit(solution)/shard_map/all_to_all | solution.py:353
  82.3 7.9 %all_to_all.87.summed = f32[8,1,256]{2,1,0:T(1,128)S(1)} all-to-all(f32[8,1,256]{2,1,0:T(1,128)S(1)} %shard_map.108), channel_id=1, replica_groups={{1,0,9,8,17,16,25,24},{3,2,11,10,19,18,27,26},{5,4,13,12,21,20,29,28},{..., dimensions={0} | all-to-all | bytes 16384 | tf_op jit(solution)/shard_map/all_to_all | solution.py:353
  90.2 1.7 %shard_map.109 = (f32[256,256]{1,0:T(8,128)S(1)}, f32[32,1,256]{2,1,0:T(1,128)S(1)}) custom-call(f32[8,1,256]{2,1,0:T(1,128)S(1)} %all_to_all.87.summed, f32[1,256]{1,0:T(1,128)S(1)} %get-tuple-element.85.class_prior, f32[1,256]{1,0:T(1,128)S(1)} %get-tuple-element.90.class_target.refs_2_.refs_4_.refs_5_, ...), custom_call_target="tpu_custom_call" | custom-call | tf_op jit(solution)/shard_map/pallas_call | solution.py:481
  92.5 9.0 %all_to_all.88.refs_1_ = f32[32,1,256]{2,1,0:T(1,128)S(1)} all-to-all(f32[32,1,256]{2,1,0:T(1,128)S(1)} %get-tuple-element.134), channel_id=1, replica_groups=mesh['grp'=4,'blk'=8] {'grp','blk'}, dimensions={0} | all-to-all | bytes 65536 | tf_op jit(solution)/shard_map/all_to_all | solution.py:341
  102.3 9.0 %all_to_all.89.refs_3_ = f32[32,1,256]{2,1,0:T(1,128)S(1)} all-to-all(f32[32,1,256]{2,1,0:T(1,128)S(1)} %shard_map.110), channel_id=1, replica_groups=mesh['grp'=4,'blk'=8] {'grp','blk'}, dimensions={0} | all-to-all | bytes 65536 | tf_op jit(solution)/shard_map/all_to_all | solution.py:341
  111.8 7.2 %all_to_all.90.refs_4_ = f32[8,1,256]{2,1,0:T(1,128)S(1)} all-to-all(f32[8,1,256]{2,1,0:T(1,128)S(1)} %shard_map.112), channel_id=1, replica_groups={{9,8,17,16,1,0,25,24},{11,10,19,18,3,2,27,26},{13,12,21,20,5,4,29,28},{..., dimensions={0} | all-to-all | bytes 16384 | tf_op jit(solution)/shard_map/all_to_all | solution.py:353
  119.3 7.2 %all_to_all.91.summed.author_summed = f32[4,1,256]{2,1,0:T(1,128)S(1)} all-to-all(f32[4,1,256]{2,1,0:T(1,128)S(1)} %shard_map.114), channel_id=1, replica_groups={{8,16,0,24},{9,17,1,25},{10,18,2,26},{11,19,3,27},{12,20,4,28},{13,21,5..., dimensions={0} | all-to-all | bytes 8192 | tf_op jit(solution)/shard_map/all_to_all | solution.py:353
  126.6 1.2 shard_map.115
  127.8 9.0 %all_to_all.92.refs_1_ = f32[32,1,256]{2,1,0:T(1,128)S(1)} all-to-all(f32[32,1,256]{2,1,0:T(1,128)S(1)} %get-tuple-element.155), channel_id=1, replica_groups=mesh['grp'=4,'blk'=8] {'grp','blk'}, dimensions={0} | all-to-all | bytes 65536 | tf_op jit(solution)/shard_map/all_to_all | solution.py:341
  137.0 8.9 %all_to_all.93.refs_1_ = f32[32,1,256]{2,1,0:T(1,128)S(1)} all-to-all(f32[32,1,256]{2,1,0:T(1,128)S(1)} %shard_map.116), channel_id=1, replica_groups=mesh['grp'=4,'blk'=8] {'grp','blk'}, dimensions={0} | all-to-all | bytes 65536 | tf_op jit(solution)/shard_map/all_to_all | solution.py:341
  146.1 8.9 %all_to_all.94.refs_1_ = f32[32,1,256]{2,1,0:T(1,128)S(1)} all-to-all(f32[32,1,256]{2,1,0:T(1,128)S(1)} %shard_map.117), channel_id=1, replica_groups=mesh['grp'=4,'blk'=8] {'grp','blk'}, dimensions={0} | all-to-all | bytes 65536 | tf_op jit(solution)/shard_map/all_to_all | solution.py:341
  155.3 8.9 %all_to_all.95.summed = f32[32,1,256]{2,1,0:T(1,128)S(1)} all-to-all(f32[32,1,256]{2,1,0:T(1,128)S(1)} %shard_map.118), channel_id=1, replica_groups=mesh['grp'=4,'blk'=8] {'grp','blk'}, dimensions={0} | all-to-all | bytes 65536 | tf_op jit(solution)/shard_map/all_to_all | solution.py:341
  164.3 1.1 shard_map.119
  (43 shorter events, 9.3 us)
Async XLA Ops:
  3.2 1.8 %collective-permute-start = (bf16[4,336,128]{2,1,0:T(8,128)(2,1)S(1)}, bf16[4,336,128]{2,1,0:T(8,128)(2,1)S(1)}, u32[]{:S(2)}, u32[]{:S(2)}) collective-permute-start(bf16[4,336,128]{2,1,0:T(8,128)(2,1)S(1)} %get-tuple-element.82.swap), channel_id=1, source_target_pairs={{0,1},{1,0},{2,3},{3,2},{4,5},{5,4},{6,7},{7,6},{8,9},{9,8},{10,11... | collective-permute-start | bytes 1032200 | tf_op jit(solution)/shard_map/ppermute | solution.py:397
  5.1 17.8 %collective-permute-start.1 = (bf16[2,336,128]{2,1,0:T(8,128)(2,1)S(1)}, bf16[2,336,128]{2,1,0:T(8,128)(2,1)S(1)}, u32[]{:S(2)}, u32[]{:S(2)}) collective-permute-start(bf16[2,336,128]{2,1,0:T(8,128)(2,1)S(1)} %get-tuple-element.91), channel_id=1, source_target_pairs={{0,2},{1,5},{2,0},{3,7},{4,6},{5,1},{6,4},{7,3},{8,10},{9,13},{10,... | collective-permute-start | bytes 516104 | tf_op jit(solution)/shard_map/ppermute | solution.py:408
  8.0 14.9 %collective-permute-start.2 = (bf16[2,336,128]{2,1,0:T(8,128)(2,1)S(1)}, bf16[2,336,128]{2,1,0:T(8,128)(2,1)S(1)}, u32[]{:S(2)}, u32[]{:S(2)}) collective-permute-start(bf16[2,336,128]{2,1,0:T(8,128)(2,1)S(1)} %get-tuple-element.92), channel_id=1, source_target_pairs={{0,4},{1,3},{2,6},{3,1},{4,0},{5,7},{6,2},{7,5},{8,12},{9,11},{10,... | collective-permute-start | bytes 516104 | tf_op jit(solution)/shard_map/ppermute | solution.py:408
  9.5 13.4 %collective-permute-start.3 = (bf16[2,336,128]{2,1,0:T(8,128)(2,1)S(1)}, bf16[2,336,128]{2,1,0:T(8,128)(2,1)S(1)}, u32[]{:S(2)}, u32[]{:S(2)}) collective-permute-start(bf16[2,336,128]{2,1,0:T(8,128)(2,1)S(1)} %get-tuple-element.93), channel_id=1, source_target_pairs={{0,6},{1,7},{2,4},{3,5},{4,2},{5,3},{6,0},{7,1},{8,14},{9,15},{10,... | collective-permute-start | bytes 516104 | tf_op jit(solution)/shard_map/ppermute | solution.py:408
  23.7 9.6 %collective-permute-start.4 = (f32[256,256]{1,0:T(8,128)S(1)}, f32[256,256]{1,0:T(8,128)S(1)}, u32[]{:S(2)}, u32[]{:S(2)}) collective-permute-start(f32[256,256]{1,0:T(8,128)S(1)} %get-tuple-element.107.refs_0_.rest_0_), channel_id=1, source_target_pairs={{0,2},{1,5},{2,0},{3,7},{4,6},{5,1},{6,4},{7,3},{8,10},{9,13},{10,... | collective-permute-start | bytes 786440 | tf_op jit(solution)/shard_map/ppermute | solution.py:408
  33.5 9.6 %collective-permute-start.5 = (f32[2,256,256]{2,1,0:T(8,128)S(1)}, f32[2,256,256]{2,1,0:T(8,128)S(1)}, u32[]{:S(2)}, u32[]{:S(2)}) collective-permute-start(f32[2,256,256]{2,1,0:T(8,128)S(1)} %shard_map.100), channel_id=1, source_target_pairs={{0,4},{1,3},{2,6},{3,1},{4,0},{5,7},{6,2},{7,5},{8,12},{9,11},{10,... | collective-permute-start | bytes 1572872 | tf_op jit(solution)/shard_map/ppermute | solution.py:408
  43.5 8.2 %collective-permute-start.6 = (f32[4,256,256]{2,1,0:T(8,128)S(1)}, f32[4,256,256]{2,1,0:T(8,128)S(1)}, u32[]{:S(2)}, u32[]{:S(2)}) collective-permute-start(f32[4,256,256]{2,1,0:T(8,128)S(1)} %shard_map.102), channel_id=1, source_target_pairs={{0,1},{1,0},{2,3},{3,2},{4,5},{5,4},{6,7},{7,6},{8,9},{9,8},{10,11... | collective-permute-start | bytes 3145736 | tf_op jit(solution)/shard_map/ppermute | solution.py:411
  52.9 9.5 %collective-permute-start.7 = (bf16[640,256]{1,0:T(8,128)(2,1)S(1)}, bf16[640,256]{1,0:T(8,128)(2,1)S(1)}, u32[]{:S(2)}, u32[]{:S(2)}) collective-permute-start(bf16[640,256]{1,0:T(8,128)(2,1)S(1)} %get-tuple-element.129.refs_0_.rest_0_), channel_id=1, source_target_pairs={{0,2},{1,5},{2,0},{3,7},{4,6},{5,1},{6,4},{7,3},{8,10},{9,13},{10,... | collective-permute-start | bytes 983048 | tf_op jit(solution)/shard_map/ppermute | solution.py:408
  62.7 11.0 %collective-permute-start.8 = (bf16[2,640,256]{2,1,0:T(8,128)(2,1)S(1)}, bf16[2,640,256]{2,1,0:T(8,128)(2,1)S(1)}, u32[]{:S(2)}, u32[]{:S(2)}) collective-permute-start(bf16[2,640,256]{2,1,0:T(8,128)(2,1)S(1)} %shard_map.105), channel_id=1, source_target_pairs={{0,4},{1,3},{2,6},{3,1},{4,0},{5,7},{6,2},{7,5},{8,12},{9,11},{10,... | collective-permute-start | bytes 1966088 | tf_op jit(solution)/shard_map/ppermute | solution.py:408
  74.4 7.3 %collective-permute-start.9 = (bf16[4,640,256]{2,1,0:T(8,128)(2,1)S(1)}, bf16[4,640,256]{2,1,0:T(8,128)(2,1)S(1)}, u32[]{:S(2)}, u32[]{:S(2)}) collective-permute-start(bf16[4,640,256]{2,1,0:T(8,128)(2,1)S(1)} %shard_map.107), channel_id=1, source_target_pairs={{0,1},{1,0},{2,3},{3,2},{4,5},{5,4},{6,7},{7,6},{8,9},{9,8},{10,11... | collective-permute-start | bytes 3932168 | tf_op jit(solution)/shard_map/ppermute | solution.py:411
  91.9 9.5 %collective-permute-start.10 = (f32[256,256]{1,0:T(8,128)S(1)}, f32[256,256]{1,0:T(8,128)S(1)}, u32[]{:S(2)}, u32[]{:S(2)}) collective-permute-start(f32[256,256]{1,0:T(8,128)S(1)} %get-tuple-element.151.refs_0_.rest_0_.own), channel_id=1, source_target_pairs={{0,2},{1,5},{2,0},{3,7},{4,6},{5,1},{6,4},{7,3},{8,10},{9,13},{10,... | collective-permute-start | bytes 786440 | tf_op jit(solution)/shard_map/ppermute | solution.py:408
  101.7 9.6 %collective-permute-start.11 = (f32[2,256,256]{2,1,0:T(8,128)S(1)}, f32[2,256,256]{2,1,0:T(8,128)S(1)}, u32[]{:S(2)}, u32[]{:S(2)}) collective-permute-start(f32[2,256,256]{2,1,0:T(8,128)S(1)} %shard_map.111), channel_id=1, source_target_pairs={{0,4},{1,3},{2,6},{3,1},{4,0},{5,7},{6,2},{7,5},{8,12},{9,11},{10,... | collective-permute-start | bytes 1572872 | tf_op jit(solution)/shard_map/ppermute | solution.py:408
  111.7 7.3 %collective-permute-start.12 = (f32[4,256,256]{2,1,0:T(8,128)S(1)}, f32[4,256,256]{2,1,0:T(8,128)S(1)}, u32[]{:S(2)}, u32[]{:S(2)}) collective-permute-start(f32[4,256,256]{2,1,0:T(8,128)S(1)} %shard_map.113), channel_id=1, source_target_pairs={{0,1},{1,0},{2,3},{3,2},{4,5},{5,4},{6,7},{7,6},{8,9},{9,8},{10,11... | collective-permute-start | bytes 3145736 | tf_op jit(solution)/shard_map/ppermute | solution.py:411

commit v22 on v21

--- a/solution.py
+++ b/solution.py
@@ -341,15 +341,12 @@
     return lax.all_to_all(parts, AXES, split_axis=0, concat_axis=0, tiled=True)
 
 
-def narrow_exchange(parts, sides, upwards):
+def narrow_exchange(parts, corners, upwards):
     groups, blocks = lax.axis_size("grp"), lax.axis_size("blk")
     planes = range(groups)
     if not upwards:
         planes = sorted(planes, key=lambda i: abs(2 * i + 1 - groups))
-    sets = [
-        [i * blocks + first + side for i in planes for side in reversed(range(sides))]
-        for first in range(0, blocks, sides)
-    ]
+    sets = [[i * blocks + corner for i in planes for corner in one] for one in corners]
     return lax.all_to_all(
         parts, AXES, split_axis=0, concat_axis=0, axis_index_groups=sets, tiled=True
     )
@@ -423,9 +420,13 @@
         places = [(0, None), (1, None), (2, 0), (2, 1)]
         places += [(3, k) for k in turned(count)]
 
+    alone = [[i] for i in range(blocks)]
+    in_pair = [[i + 1, i] for i in range(0, blocks, 2)]
+    in_cross = [[1, 3, 0, 4], [7, 5, 6, 2]]
+
     def balance(kernel, sent, local, steps, widest):
         here, there, joined = [sent], [], None
-        sides = 0
+        corners = None
         for step in range(steps):
             moves = []
             if step == 0:
@@ -437,8 +438,9 @@
             if four:
                 others = [joined] if step == 2 else []
             others = [to_other(one) for one in others]
-            if sides:
-                summed = narrow_exchange(local, sides, step + 1 == steps and sides == 2)
+            if corners:
+                upwards = step + 1 == steps and corners == in_pair
+                summed = narrow_exchange(local, corners, upwards)
             else:
                 summed = exchange(local)
             summed, *moved = lax.optimization_barrier((summed, *moves, *others))
@@ -446,13 +448,13 @@
             there += moved[len(moves) :]
             if step + 1 < steps:
                 added, size = [kernel], devices
-                if step > 0:
+                if step > 0 or four:
                     added = list(here)
-                    sides = 2
+                    corners = in_pair if step > 0 else in_cross
                     if step > 1 and widest:
                         added += there
-                        sides = 1
-                    size = sides * lax.axis_size("grp")
+                        corners = alone
+                    size = len(corners[0]) * lax.axis_size("grp")
                 local = call(
                     balance_kernel, shape((size, 1, classes), f32), [VMEM] * (len(added) + 2)
                 )(*added, summed, target)

time: 166 us -> 167 us (level)
    all_to_all x11 -> x8, blocking collectives: 105 us -> 76.5 us  [exchange(): return lax.all_to_all(parts, AXES, split_axis=0, concat_axis=0, tiled=True)]
    all_to_all x5 -> x8, blocking collectives: 37.5 us -> 65.3 us  [narrow_exchange(): lax.all_to_all(parts, AXES, split_axis=0, concat_axis=0, axis_index_group...]
where the time goes in v22:
time: 167 us
  blocking collectives  142 us (85%)
  Pallas kernels  13.8 us (8%)
  starting transfers between devices  9.4 us (6%)
    all_to_all x8, blocking collectives, exchange(): return lax.all_to_all(parts, AXES, split_axis=0, concat_axis=0, tiled=True)  76.5 us
    all_to_all x8, blocking collectives, narrow_exchange(): lax.all_to_all(parts, AXES, split_axis=0, concat_axis=0, axis_index_group...  65.3 us
    ppermute x9, starting transfers between devices, across_pairs(): lax.ppermute(value, 'blk', [(i, i ^ hop) for i, hop in enumerate(hops)])  8.62 us
  transfers between devices with their start and end apart: 13, of which 1 were waited for; matrix products, arithmetic and copies ran while one was open for 0% of the time, Pallas kernels for 1%

profile of v22, /device:TPU:0, one launch (start us, length us, event | category | flops | bytes accessed | tf_op | source)
XLA Modules:
  0.0 166.7 jit_solution(300721524533321357)
XLA Ops:
  1.3 1.9 %shard_map.95 = (s32[8]{0:T(128)S(1)}, s32[8]{0:T(128)S(1)}, s32[5,128]{1,0:T(8,128)S(1)}, s32[5,128]{1,0:T(8,128)S(1)}, f32[1,256]{1,0:T(1,128)S(1)}, /*index=5...) custom-call(s32[1]{0:T(128)S(6)} %copy.10.tile_count, ...), custom_call_target="tpu_custom_call" | custom-call | tf_op jit(solution)/shard_map/pallas_call | solution.py:386
  3.8 1.1 shard_map.96
  5.1 2.9 %collective-permute-start.1 = (bf16[2,336,128]{2,1,0:T(8,128)(2,1)S(1)}, bf16[2,336,128]{2,1,0:T(8,128)(2,1)S(1)}, u32[]{:S(2)}, u32[]{:S(2)}) collective-permute-start(bf16[2,336,128]{2,1,0:T(8,128)(2,1)S(1)} %get-tuple-element.90), channel_id=1, source_target_pairs={{0,2},{1,5},{2,0},{3,7},{4,6},{5,1},{6,4},{7,3},{8,10},{9,13},{10,... | collective-permute-start | bytes 516104 | tf_op jit(solution)/shard_map/ppermute | solution.py:405
  8.0 1.5 collective-permute-start.2
  9.5 13.4 %all_to_all.80.summed = f32[32,1,256]{2,1,0:T(1,128)S(1)} all-to-all(f32[32,1,256]{2,1,0:T(1,128)S(1)} %shard_map.96), channel_id=1, replica_groups=mesh['grp'=4,'blk'=8] {'grp','blk'}, dimensions={0} | all-to-all | bytes 65536 | tf_op jit(solution)/shard_map/all_to_all | solution.py:341
  24.3 9.0 %all_to_all.81.refs_2_ = f32[32,1,256]{2,1,0:T(1,128)S(1)} all-to-all(f32[32,1,256]{2,1,0:T(1,128)S(1)} %get-tuple-element.94), channel_id=1, replica_groups=mesh['grp'=4,'blk'=8] {'grp','blk'}, dimensions={0} | all-to-all | bytes 65536 | tf_op jit(solution)/shard_map/all_to_all | solution.py:341
  34.2 8.8 %all_to_all.82.refs_3_ = f32[16,1,256]{2,1,0:T(1,128)S(1)} all-to-all(f32[16,1,256]{2,1,0:T(1,128)S(1)} %shard_map.99), channel_id=1, replica_groups={{9,11,8,12,17,19,16,20,1,3,0,4,25,27,24,28},{15,13,14,10,23,21,22,18,7,..., dimensions={0} | all-to-all | bytes 32768 | tf_op jit(solution)/shard_map/all_to_all | solution.py:350
  43.4 8.1 %all_to_all.83.summed = f32[8,1,256]{2,1,0:T(1,128)S(1)} all-to-all(f32[8,1,256]{2,1,0:T(1,128)S(1)} %shard_map.101), channel_id=1, replica_groups={{1,0,9,8,17,16,25,24},{3,2,11,10,19,18,27,26},{5,4,13,12,21,20,29,28},{..., dimensions={0} | all-to-all | bytes 16384 | tf_op jit(solution)/shard_map/all_to_all | solution.py:350
  51.5 2.0 %shard_map.103 = (f32[640,256]{1,0:T(8,128)}, f32[32,1,256]{2,1,0:T(1,128)S(1)}, bf16[640,256]{1,0:T(8,128)(2,1)S(1)}) custom-call(s32[8]{0:T(128)S(1)} %get-tuple-element.78.tile_paper, s32[8]{0:T(128)S(1)} %get-tuple-element.79.tile_author, s32[1]{0:T(128)S(6)} %copy.10.tile_count, bf16[4,336,128]{2,1,0:T(8,128)(2,1)S(1)} %get-tuple-element.80.keep.rest_0_.rest_4_, ...), custom_call_target="tpu_custom_call" | custom-call | tf_op jit(solution)/shard_map/pallas_call | solution.py:491
  54.6 8.9 %all_to_all.84.refs_2_ = f32[32,1,256]{2,1,0:T(1,128)S(1)} all-to-all(f32[32,1,256]{2,1,0:T(1,128)S(1)} %get-tuple-element.111), channel_id=1, replica_groups=mesh['grp'=4,'blk'=8] {'grp','blk'}, dimensions={0} | all-to-all | bytes 65536 | tf_op jit(solution)/shard_map/all_to_all | solution.py:341
  64.6 10.1 %all_to_all.85.refs_3_ = f32[16,1,256]{2,1,0:T(1,128)S(1)} all-to-all(f32[16,1,256]{2,1,0:T(1,128)S(1)} %shard_map.104), channel_id=1, replica_groups={{9,11,8,12,17,19,16,20,1,3,0,4,25,27,24,28},{15,13,14,10,23,21,22,18,7,..., dimensions={0} | all-to-all | bytes 32768 | tf_op jit(solution)/shard_map/all_to_all | solution.py:350
  75.5 7.1 %all_to_all.86.refs_3_ = f32[8,1,256]{2,1,0:T(1,128)S(1)} all-to-all(f32[8,1,256]{2,1,0:T(1,128)S(1)} %shard_map.106), channel_id=1, replica_groups={{9,8,17,16,1,0,25,24},{11,10,19,18,3,2,27,26},{13,12,21,20,5,4,29,28},{..., dimensions={0} | all-to-all | bytes 16384 | tf_op jit(solution)/shard_map/all_to_all | solution.py:350
  83.2 7.9 %all_to_all.87.summed = f32[8,1,256]{2,1,0:T(1,128)S(1)} all-to-all(f32[8,1,256]{2,1,0:T(1,128)S(1)} %shard_map.108), channel_id=1, replica_groups={{1,0,9,8,17,16,25,24},{3,2,11,10,19,18,27,26},{5,4,13,12,21,20,29,28},{..., dimensions={0} | all-to-all | bytes 16384 | tf_op jit(solution)/shard_map/all_to_all | solution.py:350
  91.1 1.7 %shard_map.109 = (f32[256,256]{1,0:T(8,128)S(1)}, f32[32,1,256]{2,1,0:T(1,128)S(1)}) custom-call(f32[8,1,256]{2,1,0:T(1,128)S(1)} %all_to_all.87.summed, f32[1,256]{1,0:T(1,128)S(1)} %get-tuple-element.84.class_prior, f32[1,256]{1,0:T(1,128)S(1)} %get-tuple-element.89.class_target.refs_3_.refs_4_.refs_5_.refs_2_, ...), custom_call_target="tpu_custom_call" | custom-call | tf_op jit(solution)/shard_map/pallas_call | solution.py:483
  93.5 9.0 %all_to_all.88.refs_2_ = f32[32,1,256]{2,1,0:T(1,128)S(1)} all-to-all(f32[32,1,256]{2,1,0:T(1,128)S(1)} %get-tuple-element.132), channel_id=1, replica_groups=mesh['grp'=4,'blk'=8] {'grp','blk'}, dimensions={0} | all-to-all | bytes 65536 | tf_op jit(solution)/shard_map/all_to_all | solution.py:341
  103.4 8.8 %all_to_all.89.refs_3_ = f32[16,1,256]{2,1,0:T(1,128)S(1)} all-to-all(f32[16,1,256]{2,1,0:T(1,128)S(1)} %shard_map.110), channel_id=1, replica_groups={{9,11,8,12,17,19,16,20,1,3,0,4,25,27,24,28},{15,13,14,10,23,21,22,18,7,..., dimensions={0} | all-to-all | bytes 32768 | tf_op jit(solution)/shard_map/all_to_all | solution.py:350
  112.6 7.1 %all_to_all.90.refs_4_ = f32[8,1,256]{2,1,0:T(1,128)S(1)} all-to-all(f32[8,1,256]{2,1,0:T(1,128)S(1)} %shard_map.112), channel_id=1, replica_groups={{9,8,17,16,1,0,25,24},{11,10,19,18,3,2,27,26},{13,12,21,20,5,4,29,28},{..., dimensions={0} | all-to-all | bytes 16384 | tf_op jit(solution)/shard_map/all_to_all | solution.py:350
  120.2 7.2 %all_to_all.91.summed.author_summed = f32[4,1,256]{2,1,0:T(1,128)S(1)} all-to-all(f32[4,1,256]{2,1,0:T(1,128)S(1)} %shard_map.114), channel_id=1, replica_groups={{8,16,0,24},{9,17,1,25},{10,18,2,26},{11,19,3,27},{12,20,4,28},{13,21,5..., dimensions={0} | all-to-all | bytes 8192 | tf_op jit(solution)/shard_map/all_to_all | solution.py:350
  127.4 1.2 shard_map.115
  128.6 9.4 %all_to_all.92.refs_1_ = f32[32,1,256]{2,1,0:T(1,128)S(1)} all-to-all(f32[32,1,256]{2,1,0:T(1,128)S(1)} %get-tuple-element.153), channel_id=1, replica_groups=mesh['grp'=4,'blk'=8] {'grp','blk'}, dimensions={0} | all-to-all | bytes 65536 | tf_op jit(solution)/shard_map/all_to_all | solution.py:341
  138.2 8.9 %all_to_all.93.refs_1_ = f32[32,1,256]{2,1,0:T(1,128)S(1)} all-to-all(f32[32,1,256]{2,1,0:T(1,128)S(1)} %shard_map.116), channel_id=1, replica_groups=mesh['grp'=4,'blk'=8] {'grp','blk'}, dimensions={0} | all-to-all | bytes 65536 | tf_op jit(solution)/shard_map/all_to_all | solution.py:341
  147.4 8.9 %all_to_all.94.refs_1_ = f32[32,1,256]{2,1,0:T(1,128)S(1)} all-to-all(f32[32,1,256]{2,1,0:T(1,128)S(1)} %shard_map.117), channel_id=1, replica_groups=mesh['grp'=4,'blk'=8] {'grp','blk'}, dimensions={0} | all-to-all | bytes 65536 | tf_op jit(solution)/shard_map/all_to_all | solution.py:341
  156.6 8.9 %all_to_all.95.summed = f32[32,1,256]{2,1,0:T(1,128)S(1)} all-to-all(f32[32,1,256]{2,1,0:T(1,128)S(1)} %shard_map.118), channel_id=1, replica_groups=mesh['grp'=4,'blk'=8] {'grp','blk'}, dimensions={0} | all-to-all | bytes 65536 | tf_op jit(solution)/shard_map/all_to_all | solution.py:341
  165.6 1.1 shard_map.119
  (43 shorter events, 9.9 us)
Async XLA Ops:
  3.2 1.8 %collective-permute-start = (bf16[4,336,128]{2,1,0:T(8,128)(2,1)S(1)}, bf16[4,336,128]{2,1,0:T(8,128)(2,1)S(1)}, u32[]{:S(2)}, u32[]{:S(2)}) collective-permute-start(bf16[4,336,128]{2,1,0:T(8,128)(2,1)S(1)} %get-tuple-element.81.swap), channel_id=1, source_target_pairs={{0,1},{1,0},{2,3},{3,2},{4,5},{5,4},{6,7},{7,6},{8,9},{9,8},{10,11... | collective-permute-start | bytes 1032200 | tf_op jit(solution)/shard_map/ppermute | solution.py:394
  5.1 17.8 %collective-permute-start.1 = (bf16[2,336,128]{2,1,0:T(8,128)(2,1)S(1)}, bf16[2,336,128]{2,1,0:T(8,128)(2,1)S(1)}, u32[]{:S(2)}, u32[]{:S(2)}) collective-permute-start(bf16[2,336,128]{2,1,0:T(8,128)(2,1)S(1)} %get-tuple-element.90), channel_id=1, source_target_pairs={{0,2},{1,5},{2,0},{3,7},{4,6},{5,1},{6,4},{7,3},{8,10},{9,13},{10,... | collective-permute-start | bytes 516104 | tf_op jit(solution)/shard_map/ppermute | solution.py:405
  8.0 14.9 %collective-permute-start.2 = (bf16[2,336,128]{2,1,0:T(8,128)(2,1)S(1)}, bf16[2,336,128]{2,1,0:T(8,128)(2,1)S(1)}, u32[]{:S(2)}, u32[]{:S(2)}) collective-permute-start(bf16[2,336,128]{2,1,0:T(8,128)(2,1)S(1)} %get-tuple-element.91), channel_id=1, source_target_pairs={{0,4},{1,3},{2,6},{3,1},{4,0},{5,7},{6,2},{7,5},{8,12},{9,11},{10,... | collective-permute-start | bytes 516104 | tf_op jit(solution)/shard_map/ppermute | solution.py:405
  9.5 13.4 %collective-permute-start.3 = (bf16[2,336,128]{2,1,0:T(8,128)(2,1)S(1)}, bf16[2,336,128]{2,1,0:T(8,128)(2,1)S(1)}, u32[]{:S(2)}, u32[]{:S(2)}) collective-permute-start(bf16[2,336,128]{2,1,0:T(8,128)(2,1)S(1)} %get-tuple-element.92), channel_id=1, source_target_pairs={{0,6},{1,7},{2,4},{3,5},{4,2},{5,3},{6,0},{7,1},{8,14},{9,15},{10,... | collective-permute-start | bytes 516104 | tf_op jit(solution)/shard_map/ppermute | solution.py:405
  23.7 9.6 %collective-permute-start.4 = (f32[256,256]{1,0:T(8,128)S(1)}, f32[256,256]{1,0:T(8,128)S(1)}, u32[]{:S(2)}, u32[]{:S(2)}) collective-permute-start(f32[256,256]{1,0:T(8,128)S(1)} %get-tuple-element.106.refs_0_.rest_0_), channel_id=1, source_target_pairs={{0,2},{1,5},{2,0},{3,7},{4,6},{5,1},{6,4},{7,3},{8,10},{9,13},{10,... | collective-permute-start | bytes 786440 | tf_op jit(solution)/shard_map/ppermute | solution.py:405
  33.6 9.5 %collective-permute-start.5 = (f32[2,256,256]{2,1,0:T(8,128)S(1)}, f32[2,256,256]{2,1,0:T(8,128)S(1)}, u32[]{:S(2)}, u32[]{:S(2)}) collective-permute-start(f32[2,256,256]{2,1,0:T(8,128)S(1)} %shard_map.100), channel_id=1, source_target_pairs={{0,4},{1,3},{2,6},{3,1},{4,0},{5,7},{6,2},{7,5},{8,12},{9,11},{10,... | collective-permute-start | bytes 1572872 | tf_op jit(solution)/shard_map/ppermute | solution.py:405
  43.4 8.2 %collective-permute-start.6 = (f32[4,256,256]{2,1,0:T(8,128)S(1)}, f32[4,256,256]{2,1,0:T(8,128)S(1)}, u32[]{:S(2)}, u32[]{:S(2)}) collective-permute-start(f32[4,256,256]{2,1,0:T(8,128)S(1)} %shard_map.102), channel_id=1, source_target_pairs={{0,1},{1,0},{2,3},{3,2},{4,5},{5,4},{6,7},{7,6},{8,9},{9,8},{10,11... | collective-permute-start | bytes 3145736 | tf_op jit(solution)/shard_map/ppermute | solution.py:408
  53.5 10.0 %collective-permute-start.7 = (bf16[640,256]{1,0:T(8,128)(2,1)S(1)}, bf16[640,256]{1,0:T(8,128)(2,1)S(1)}, u32[]{:S(2)}, u32[]{:S(2)}) collective-permute-start(bf16[640,256]{1,0:T(8,128)(2,1)S(1)} %get-tuple-element.127.refs_0_.rest_0_), channel_id=1, source_target_pairs={{0,2},{1,5},{2,0},{3,7},{4,6},{5,1},{6,4},{7,3},{8,10},{9,13},{10,... | collective-permute-start | bytes 983048 | tf_op jit(solution)/shard_map/ppermute | solution.py:405
  63.9 10.8 %collective-permute-start.8 = (bf16[2,640,256]{2,1,0:T(8,128)(2,1)S(1)}, bf16[2,640,256]{2,1,0:T(8,128)(2,1)S(1)}, u32[]{:S(2)}, u32[]{:S(2)}) collective-permute-start(bf16[2,640,256]{2,1,0:T(8,128)(2,1)S(1)} %shard_map.105), channel_id=1, source_target_pairs={{0,4},{1,3},{2,6},{3,1},{4,0},{5,7},{6,2},{7,5},{8,12},{9,11},{10,... | collective-permute-start | bytes 1966088 | tf_op jit(solution)/shard_map/ppermute | solution.py:405
  75.4 7.3 %collective-permute-start.9 = (bf16[4,640,256]{2,1,0:T(8,128)(2,1)S(1)}, bf16[4,640,256]{2,1,0:T(8,128)(2,1)S(1)}, u32[]{:S(2)}, u32[]{:S(2)}) collective-permute-start(bf16[4,640,256]{2,1,0:T(8,128)(2,1)S(1)} %shard_map.107), channel_id=1, source_target_pairs={{0,1},{1,0},{2,3},{3,2},{4,5},{5,4},{6,7},{7,6},{8,9},{9,8},{10,11... | collective-permute-start | bytes 3932168 | tf_op jit(solution)/shard_map/ppermute | solution.py:408
  92.8 9.6 %collective-permute-start.10 = (f32[256,256]{1,0:T(8,128)S(1)}, f32[256,256]{1,0:T(8,128)S(1)}, u32[]{:S(2)}, u32[]{:S(2)}) collective-permute-start(f32[256,256]{1,0:T(8,128)S(1)} %get-tuple-element.149.refs_0_.rest_0_.own), channel_id=1, source_target_pairs={{0,2},{1,5},{2,0},{3,7},{4,6},{5,1},{6,4},{7,3},{8,10},{9,13},{10,... | collective-permute-start | bytes 786440 | tf_op jit(solution)/shard_map/ppermute | solution.py:405
  102.7 9.5 %collective-permute-start.11 = (f32[2,256,256]{2,1,0:T(8,128)S(1)}, f32[2,256,256]{2,1,0:T(8,128)S(1)}, u32[]{:S(2)}, u32[]{:S(2)}) collective-permute-start(f32[2,256,256]{2,1,0:T(8,128)S(1)} %shard_map.111), channel_id=1, source_target_pairs={{0,4},{1,3},{2,6},{3,1},{4,0},{5,7},{6,2},{7,5},{8,12},{9,11},{10,... | collective-permute-start | bytes 1572872 | tf_op jit(solution)/shard_map/ppermute | solution.py:405
  112.6 7.2 %collective-permute-start.12 = (f32[4,256,256]{2,1,0:T(8,128)S(1)}, f32[4,256,256]{2,1,0:T(8,128)S(1)}, u32[]{:S(2)}, u32[]{:S(2)}) collective-permute-start(f32[4,256,256]{2,1,0:T(8,128)S(1)} %shard_map.113), channel_id=1, source_target_pairs={{0,1},{1,0},{2,3},{3,2},{4,5},{5,4},{6,7},{7,6},{8,9},{9,8},{10,11... | collective-permute-start | bytes 3145736 | tf_op jit(solution)/shard_map/ppermute | solution.py:408

commit v23 on v21

--- a/solution.py
+++ b/solution.py
@@ -24,13 +24,14 @@
 def call(kernel, out_shape, in_specs, scratch_shapes=(), out_specs=None):
     if out_specs is None:
         out_specs = jax.tree.map(lambda _: VMEM, out_shape)
+    room = 20 if lax.axis_size("blk") <= 8 else 48
     return pl.pallas_call(
         kernel,
         out_shape=out_shape,
         in_specs=in_specs,
         out_specs=out_specs,
         scratch_shapes=list(scratch_shapes),
-        compiler_params=pltpu.CompilerParams(vmem_limit_bytes=48 * 1024 * 1024),
+        compiler_params=pltpu.CompilerParams(vmem_limit_bytes=room * 1024 * 1024),
     )
 
 
@@ -271,7 +272,7 @@
     places, rows, tile_paper, tile_author, tile_count, keep, swap, summed, class_prior,
     class_target, *rest,
 ):
-    kernels, (full, parts, *half) = views(rest, places), rest[1 + max(i for i, _ in places) :]
+    kernels, (full, parts) = views(rest, places), rest[1 + max(i for i, _ in places) :]
     columns = keep.shape[2]
     classes = full.shape[1]
     scale_cols = col_scale(summed, class_target)
@@ -292,8 +293,6 @@
         mass = jnp.dot(wide, jnp.concatenate(chosen, axis=0), preferred_element_type=jnp.float32)
         kernel = mass + class_prior[...]
         full[paper * rows : (paper + 1) * rows, :] = kernel
-        for out in half:
-            out[paper * rows : (paper + 1) * rows, :] = kernel.astype(jnp.bfloat16)
         column = column + jnp.sum(kernel, axis=0, keepdims=True)
     spread(column, parts)
 
@@ -415,27 +414,35 @@
     summed = exchange(local)
 
     author_out = (shape((authors, classes), f32), parts)
-    paper_out = (shape((papers, classes), f32), parts, shape((papers, classes), bf16))
+    paper_out = (shape((papers, classes), f32), parts)
 
     four = count == 4
     places = [(i, None) for i in range(blocks)]
     if four:
         places = [(0, None), (1, None), (2, 0), (2, 1)]
         places += [(3, k) for k in turned(count)]
-
-    def balance(kernel, sent, local, steps, widest):
+    paper_places = [(i, None) for i in range(count)]
+    paper_places += [(count, k) if four else (count + k, None) for k in turned(count)]
+
+    def balance(kernel, local, steps, authors):
+        sent = kernel
         here, there, joined = [sent], [], None
+        full = 1 if authors or not four else 2
         sides = 0
         for step in range(steps):
             moves = []
             if step == 0:
                 moves = [(sent, *way) for way in ways[1 : 2 if four else 3]]
             elif step == 1:
-                moves = [(joined, *ways[2])] if four else [(sent, *way) for way in ways[3:]]
+                moves = [(sent, *way) for way in ways[3:]]
+                if four:
+                    moves = [(joined if authors else sent, *ways[2])]
+            elif step == full:
+                moves = [(here[1], *ways[2])]
             moves = [across_pairs(*move) for move in moves]
             others = [] if step == 0 else [sent] if step == 1 else here[len(there) :]
             if four:
-                others = [joined] if step == 2 else []
+                others = [joined] if step == full + 1 else []
             others = [to_other(one) for one in others]
             if sides:
                 summed = narrow_exchange(local, sides, step + 1 == steps and sides == 2)
@@ -446,10 +453,10 @@
             there += moved[len(moves) :]
             if step + 1 < steps:
                 added, size = [kernel], devices
-                if step > 0:
+                if step >= full:
                     added = list(here)
                     sides = 2
-                    if step > 1 and widest:
+                    if step > 1 and authors:
                         added += there
                         sides = 1
                     size = sides * lax.axis_size("grp")
@@ -457,9 +464,10 @@
                     balance_kernel, shape((size, 1, classes), f32), [VMEM] * (len(added) + 2)
                 )(*added, summed, target)
                 joined = sent
-                if four and step < 2:
+                if four and (step == full or authors and step == 0):
+                    size = 4 if step == full else 2
                     joined = call(
-                        join_kernel, shape((2 * step + 2, *sent.shape), sent.dtype), [VMEM] * len(here)
+                        join_kernel, shape((size, *sent.shape), sent.dtype), [VMEM] * len(here)
                     )(*here)
                 local, sent, joined, *here = lax.optimization_barrier((local, sent, joined, *here))
         return summed, here + there
@@ -479,16 +487,16 @@
             left = ITERS - 1
         else:
             own, local = call(
-                functools.partial(author_kernel, rows, places),
+                functools.partial(author_kernel, rows, paper_places),
                 author_out,
                 [VMEM] * (3 + len(kernels) + len(held)),
             )(summed, prior, target, *kernels, *held)
             left = ITERS
-        author_summed, kernels = balance(own, own, local, left, True)
+        author_summed, kernels = balance(own, local, left, True)
         last = repeat + 1 == ROUNDS
-        kernel, local, *half = call(
+        kernel, local = call(
             functools.partial(paper_kernel, places, rows),
-            paper_out[:2] if last else paper_out,
+            paper_out,
             [SMEM, SMEM, SMEM] + [VMEM] * (5 + len(kernels)),
         )(
             tile_paper, tile_author, tile_count, keep, swap, author_summed, prior, target, *kernels
@@ -496,7 +504,7 @@
         if last:
             summed = last_balance(kernel, local)
         else:
-            summed, kernels = balance(kernel, half[0], local, ITERS, False)
+            summed, kernels = balance(kernel, local, ITERS, False)
     return call(
         functools.partial(final_kernel, rows),
         (shape((papers, classes), f32), shape((authors, classes), f32)),

time: 166 us -> 172 us (1.036)
  blocking collectives: 142 us -> 146 us
  starting transfers between devices: 8.9 us -> 11.4 us
    all_to_all x11 -> x12, blocking collectives: 105 us -> 115 us  [exchange(): return lax.all_to_all(parts, AXES, split_axis=0, concat_axis=0, tiled=True)]
    all_to_all x5 -> x4, blocking collectives: 37.5 us -> 30.5 us  [narrow_exchange(): lax.all_to_all(parts, AXES, split_axis=0, concat_axis=0, axis_index_group...]
    ppermute x9 -> x10, starting transfers between devices: 8.01 us -> 10.5 us  [across_pairs(): lax.ppermute(value, 'blk', [(i, i ^ hop) for i, hop in enumerate(hops)])]
    pallas_call x9 -> x8, Pallas kernels: 4.43 us -> 4.47 us  [the longest x2 2.39 us: on_device(): call(functools.partial(paper_kernel, places, rows), paper_out, [SMEM, SME...]
  transfers between devices with their start and end apart: 13 -> 14, of which waited for: 1 -> 1; matrix products, arithmetic and copies ran while one was open for 0% -> 0% of each run, Pallas kernels for 1% -> 1%
where the time goes in v23:
time: 172 us; the launch traced here: 171 us
  blocking collectives  146 us (85%)
  Pallas kernels  12.5 us (7%)
  starting transfers between devices  11.4 us (7%)
    all_to_all x12, blocking collectives, exchange(): return lax.all_to_all(parts, AXES, split_axis=0, concat_axis=0, tiled=True)  115 us
    all_to_all x4, blocking collectives, narrow_exchange(): lax.all_to_all(parts, AXES, split_axis=0, concat_axis=0, axis_index_group...  30.5 us
    ppermute x10, starting transfers between devices, across_pairs(): lax.ppermute(value, 'blk', [(i, i ^ hop) for i, hop in enumerate(hops)])  10.5 us
  transfers between devices with their start and end apart: 14, of which 1 were waited for; matrix products, arithmetic and copies ran while one was open for 0% of the time, Pallas kernels for 1%

profile of v23, /device:TPU:0, one launch (start us, length us, event | category | flops | bytes accessed | tf_op | source)
XLA Modules:
  0.0 171.4 jit_solution(13911404158169325292)
XLA Ops:
  1.3 1.9 %shard_map.95 = (s32[8]{0:T(128)S(1)}, s32[8]{0:T(128)S(1)}, s32[5,128]{1,0:T(8,128)S(1)}, s32[5,128]{1,0:T(8,128)S(1)}, f32[1,256]{1,0:T(1,128)S(1)}, /*index=5...) custom-call(s32[1]{0:T(128)S(6)} %copy.10.tile_count, ...), custom_call_target="tpu_custom_call" | custom-call | tf_op jit(solution)/shard_map/pallas_call | solution.py:388
  5.1 2.9 %collective-permute-start.1 = (bf16[2,336,128]{2,1,0:T(8,128)(2,1)S(1)}, bf16[2,336,128]{2,1,0:T(8,128)(2,1)S(1)}, u32[]{:S(2)}, u32[]{:S(2)}) collective-permute-start(bf16[2,336,128]{2,1,0:T(8,128)(2,1)S(1)} %get-tuple-element.93), channel_id=1, source_target_pairs={{0,2},{1,5},{2,0},{3,7},{4,6},{5,1},{6,4},{7,3},{8,10},{9,13},{10,... | collective-permute-start | bytes 516104 | tf_op jit(solution)/shard_map/ppermute | solution.py:407
  8.0 1.5 collective-permute-start.2
  9.5 13.4 %all_to_all.80.summed = f32[32,1,256]{2,1,0:T(1,128)S(1)} all-to-all(f32[32,1,256]{2,1,0:T(1,128)S(1)} %shard_map.96), channel_id=1, replica_groups=mesh['grp'=4,'blk'=8] {'grp','blk'}, dimensions={0} | all-to-all | bytes 65536 | tf_op jit(solution)/shard_map/all_to_all | solution.py:340
  24.3 9.0 %all_to_all.81.refs_1_ = f32[32,1,256]{2,1,0:T(1,128)S(1)} all-to-all(f32[32,1,256]{2,1,0:T(1,128)S(1)} %get-tuple-element.97), channel_id=1, replica_groups=mesh['grp'=4,'blk'=8] {'grp','blk'}, dimensions={0} | all-to-all | bytes 65536 | tf_op jit(solution)/shard_map/all_to_all | solution.py:340
  34.2 9.0 %all_to_all.82.refs_3_ = f32[32,1,256]{2,1,0:T(1,128)S(1)} all-to-all(f32[32,1,256]{2,1,0:T(1,128)S(1)} %shard_map.99), channel_id=1, replica_groups=mesh['grp'=4,'blk'=8] {'grp','blk'}, dimensions={0} | all-to-all | bytes 65536 | tf_op jit(solution)/shard_map/all_to_all | solution.py:340
  43.6 8.0 %all_to_all.83.summed = f32[8,1,256]{2,1,0:T(1,128)S(1)} all-to-all(f32[8,1,256]{2,1,0:T(1,128)S(1)} %shard_map.101), channel_id=1, replica_groups={{1,0,9,8,17,16,25,24},{3,2,11,10,19,18,27,26},{5,4,13,12,21,20,29,28},{..., dimensions={0} | all-to-all | bytes 16384 | tf_op jit(solution)/shard_map/all_to_all | solution.py:352
  51.7 1.2 shard_map.103
  53.4 10.5 %all_to_all.84.refs_1_ = f32[32,1,256]{2,1,0:T(1,128)S(1)} all-to-all(f32[32,1,256]{2,1,0:T(1,128)S(1)} %get-tuple-element.114), channel_id=1, replica_groups=mesh['grp'=4,'blk'=8] {'grp','blk'}, dimensions={0} | all-to-all | bytes 65536 | tf_op jit(solution)/shard_map/all_to_all | solution.py:340
  64.1 1.5 collective-permute-start.8
  65.6 9.5 %all_to_all.85.refs_1_ = f32[32,1,256]{2,1,0:T(1,128)S(1)} all-to-all(f32[32,1,256]{2,1,0:T(1,128)S(1)} %shard_map.104), channel_id=1, replica_groups=mesh['grp'=4,'blk'=8] {'grp','blk'}, dimensions={0} | all-to-all | bytes 65536 | tf_op jit(solution)/shard_map/all_to_all | solution.py:340
  75.4 1.5 collective-permute-start.9
  76.9 9.5 %all_to_all.86.refs_4_ = f32[32,1,256]{2,1,0:T(1,128)S(1)} all-to-all(f32[32,1,256]{2,1,0:T(1,128)S(1)} %shard_map.105), channel_id=1, replica_groups=mesh['grp'=4,'blk'=8] {'grp','blk'}, dimensions={0} | all-to-all | bytes 65536 | tf_op jit(solution)/shard_map/all_to_all | solution.py:340
  87.2 8.1 %all_to_all.87.summed = f32[8,1,256]{2,1,0:T(1,128)S(1)} all-to-all(f32[8,1,256]{2,1,0:T(1,128)S(1)} %shard_map.106), channel_id=1, replica_groups={{1,0,9,8,17,16,25,24},{3,2,11,10,19,18,27,26},{5,4,13,12,21,20,29,28},{..., dimensions={0} | all-to-all | bytes 16384 | tf_op jit(solution)/shard_map/all_to_all | solution.py:352
  95.3 1.7 shard_map.108
  97.7 9.7 %all_to_all.88.refs_1_ = f32[32,1,256]{2,1,0:T(1,128)S(1)} all-to-all(f32[32,1,256]{2,1,0:T(1,128)S(1)} %get-tuple-element.138), channel_id=1, replica_groups=mesh['grp'=4,'blk'=8] {'grp','blk'}, dimensions={0} | all-to-all | bytes 65536 | tf_op jit(solution)/shard_map/all_to_all | solution.py:340
  108.3 9.0 %all_to_all.89.refs_3_ = f32[32,1,256]{2,1,0:T(1,128)S(1)} all-to-all(f32[32,1,256]{2,1,0:T(1,128)S(1)} %shard_map.109), channel_id=1, replica_groups=mesh['grp'=4,'blk'=8] {'grp','blk'}, dimensions={0} | all-to-all | bytes 65536 | tf_op jit(solution)/shard_map/all_to_all | solution.py:340
  117.7 7.2 %all_to_all.90.refs_4_ = f32[8,1,256]{2,1,0:T(1,128)S(1)} all-to-all(f32[8,1,256]{2,1,0:T(1,128)S(1)} %shard_map.111), channel_id=1, replica_groups={{9,8,17,16,1,0,25,24},{11,10,19,18,3,2,27,26},{13,12,21,20,5,4,29,28},{..., dimensions={0} | all-to-all | bytes 16384 | tf_op jit(solution)/shard_map/all_to_all | solution.py:352
  125.3 7.2 %all_to_all.91.summed.author_summed = f32[4,1,256]{2,1,0:T(1,128)S(1)} all-to-all(f32[4,1,256]{2,1,0:T(1,128)S(1)} %shard_map.113), channel_id=1, replica_groups={{8,16,0,24},{9,17,1,25},{10,18,2,26},{11,19,3,27},{12,20,4,28},{13,21,5..., dimensions={0} | all-to-all | bytes 8192 | tf_op jit(solution)/shard_map/all_to_all | solution.py:352
  132.5 1.2 shard_map.114
  133.7 9.0 %all_to_all.92.refs_1_ = f32[32,1,256]{2,1,0:T(1,128)S(1)} all-to-all(f32[32,1,256]{2,1,0:T(1,128)S(1)} %get-tuple-element.159), channel_id=1, replica_groups=mesh['grp'=4,'blk'=8] {'grp','blk'}, dimensions={0} | all-to-all | bytes 65536 | tf_op jit(solution)/shard_map/all_to_all | solution.py:340
  142.9 8.9 %all_to_all.93.refs_1_ = f32[32,1,256]{2,1,0:T(1,128)S(1)} all-to-all(f32[32,1,256]{2,1,0:T(1,128)S(1)} %shard_map.115), channel_id=1, replica_groups=mesh['grp'=4,'blk'=8] {'grp','blk'}, dimensions={0} | all-to-all | bytes 65536 | tf_op jit(solution)/shard_map/all_to_all | solution.py:340
  152.1 8.9 %all_to_all.94.refs_1_ = f32[32,1,256]{2,1,0:T(1,128)S(1)} all-to-all(f32[32,1,256]{2,1,0:T(1,128)S(1)} %shard_map.116), channel_id=1, replica_groups=mesh['grp'=4,'blk'=8] {'grp','blk'}, dimensions={0} | all-to-all | bytes 65536 | tf_op jit(solution)/shard_map/all_to_all | solution.py:340
  161.3 8.9 %all_to_all.95.summed = f32[32,1,256]{2,1,0:T(1,128)S(1)} all-to-all(f32[32,1,256]{2,1,0:T(1,128)S(1)} %shard_map.117), channel_id=1, replica_groups=mesh['grp'=4,'blk'=8] {'grp','blk'}, dimensions={0} | all-to-all | bytes 65536 | tf_op jit(solution)/shard_map/all_to_all | solution.py:340
  (44 shorter events, 10.6 us)
Async XLA Ops:
  3.2 1.8 %collective-permute-start = (bf16[4,336,128]{2,1,0:T(8,128)(2,1)S(1)}, bf16[4,336,128]{2,1,0:T(8,128)(2,1)S(1)}, u32[]{:S(2)}, u32[]{:S(2)}) collective-permute-start(bf16[4,336,128]{2,1,0:T(8,128)(2,1)S(1)} %get-tuple-element.84.swap), channel_id=1, source_target_pairs={{0,1},{1,0},{2,3},{3,2},{4,5},{5,4},{6,7},{7,6},{8,9},{9,8},{10,11... | collective-permute-start | bytes 1032200 | tf_op jit(solution)/shard_map/ppermute | solution.py:396
  5.1 17.8 %collective-permute-start.1 = (bf16[2,336,128]{2,1,0:T(8,128)(2,1)S(1)}, bf16[2,336,128]{2,1,0:T(8,128)(2,1)S(1)}, u32[]{:S(2)}, u32[]{:S(2)}) collective-permute-start(bf16[2,336,128]{2,1,0:T(8,128)(2,1)S(1)} %get-tuple-element.93), channel_id=1, source_target_pairs={{0,2},{1,5},{2,0},{3,7},{4,6},{5,1},{6,4},{7,3},{8,10},{9,13},{10,... | collective-permute-start | bytes 516104 | tf_op jit(solution)/shard_map/ppermute | solution.py:407
  8.0 14.9 %collective-permute-start.2 = (bf16[2,336,128]{2,1,0:T(8,128)(2,1)S(1)}, bf16[2,336,128]{2,1,0:T(8,128)(2,1)S(1)}, u32[]{:S(2)}, u32[]{:S(2)}) collective-permute-start(bf16[2,336,128]{2,1,0:T(8,128)(2,1)S(1)} %get-tuple-element.94), channel_id=1, source_target_pairs={{0,4},{1,3},{2,6},{3,1},{4,0},{5,7},{6,2},{7,5},{8,12},{9,11},{10,... | collective-permute-start | bytes 516104 | tf_op jit(solution)/shard_map/ppermute | solution.py:407
  9.5 13.4 %collective-permute-start.3 = (bf16[2,336,128]{2,1,0:T(8,128)(2,1)S(1)}, bf16[2,336,128]{2,1,0:T(8,128)(2,1)S(1)}, u32[]{:S(2)}, u32[]{:S(2)}) collective-permute-start(bf16[2,336,128]{2,1,0:T(8,128)(2,1)S(1)} %get-tuple-element.95), channel_id=1, source_target_pairs={{0,6},{1,7},{2,4},{3,5},{4,2},{5,3},{6,0},{7,1},{8,14},{9,15},{10,... | collective-permute-start | bytes 516104 | tf_op jit(solution)/shard_map/ppermute | solution.py:407
  23.7 9.6 %collective-permute-start.4 = (f32[256,256]{1,0:T(8,128)S(1)}, f32[256,256]{1,0:T(8,128)S(1)}, u32[]{:S(2)}, u32[]{:S(2)}) collective-permute-start(f32[256,256]{1,0:T(8,128)S(1)} %get-tuple-element.109.refs_0_.rest_0_), channel_id=1, source_target_pairs={{0,2},{1,5},{2,0},{3,7},{4,6},{5,1},{6,4},{7,3},{8,10},{9,13},{10,... | collective-permute-start | bytes 786440 | tf_op jit(solution)/shard_map/ppermute | solution.py:407
  33.5 9.6 %collective-permute-start.5 = (f32[2,256,256]{2,1,0:T(8,128)S(1)}, f32[2,256,256]{2,1,0:T(8,128)S(1)}, u32[]{:S(2)}, u32[]{:S(2)}) collective-permute-start(f32[2,256,256]{2,1,0:T(8,128)S(1)} %shard_map.100), channel_id=1, source_target_pairs={{0,4},{1,3},{2,6},{3,1},{4,0},{5,7},{6,2},{7,5},{8,12},{9,11},{10,... | collective-permute-start | bytes 1572872 | tf_op jit(solution)/shard_map/ppermute | solution.py:407
  43.5 8.2 %collective-permute-start.6 = (f32[4,256,256]{2,1,0:T(8,128)S(1)}, f32[4,256,256]{2,1,0:T(8,128)S(1)}, u32[]{:S(2)}, u32[]{:S(2)}) collective-permute-start(f32[4,256,256]{2,1,0:T(8,128)S(1)} %shard_map.102), channel_id=1, source_target_pairs={{0,1},{1,0},{2,3},{3,2},{4,5},{5,4},{6,7},{7,6},{8,9},{9,8},{10,11... | collective-permute-start | bytes 3145736 | tf_op jit(solution)/shard_map/ppermute | solution.py:410
  52.9 11.0 %collective-permute-start.7 = (f32[640,256]{1,0:T(8,128)S(1)}, f32[640,256]{1,0:T(8,128)S(1)}, u32[]{:S(2)}, u32[]{:S(2)}) collective-permute-start(f32[640,256]{1,0:T(8,128)S(1)} %get-tuple-element.132.refs_0_.rest_0_), channel_id=1, source_target_pairs={{0,2},{1,5},{2,0},{3,7},{4,6},{5,1},{6,4},{7,3},{8,10},{9,13},{10,... | collective-permute-start | bytes 1966088 | tf_op jit(solution)/shard_map/ppermute | solution.py:407
  64.1 11.0 %collective-permute-start.8 = (f32[640,256]{1,0:T(8,128)S(1)}, f32[640,256]{1,0:T(8,128)S(1)}, u32[]{:S(2)}, u32[]{:S(2)}) collective-permute-start(f32[640,256]{1,0:T(8,128)S(1)} %get-tuple-element.132.refs_0_.rest_0_), channel_id=1, source_target_pairs={{0,4},{1,3},{2,6},{3,1},{4,0},{5,7},{6,2},{7,5},{8,12},{9,11},{10,... | collective-permute-start | bytes 1966088 | tf_op jit(solution)/shard_map/ppermute | solution.py:407
  75.4 11.0 %collective-permute-start.9 = (f32[640,256]{1,0:T(8,128)S(1)}, f32[640,256]{1,0:T(8,128)S(1)}, u32[]{:S(2)}, u32[]{:S(2)}) collective-permute-start(f32[640,256]{1,0:T(8,128)S(1)} %collective-permute-done.7.refs_1_.rest_1_), channel_id=1, source_target_pairs={{0,4},{1,3},{2,6},{3,1},{4,0},{5,7},{6,2},{7,5},{8,12},{9,11},{10,... | collective-permute-start | bytes 1966088 | tf_op jit(solution)/shard_map/ppermute | solution.py:407
  87.1 8.2 %collective-permute-start.10 = (f32[4,640,256]{2,1,0:T(8,128)S(1)}, f32[4,640,256]{2,1,0:T(8,128)S(1)}, u32[]{:S(2)}, u32[]{:S(2)}) collective-permute-start(f32[4,640,256]{2,1,0:T(8,128)S(1)} %shard_map.107), channel_id=1, source_target_pairs={{0,1},{1,0},{2,3},{3,2},{4,5},{5,4},{6,7},{7,6},{8,9},{9,8},{10,11... | collective-permute-start | bytes 7864328 | tf_op jit(solution)/shard_map/ppermute | solution.py:410
  97.0 10.4 %collective-permute-start.11 = (f32[256,256]{1,0:T(8,128)S(1)}, f32[256,256]{1,0:T(8,128)S(1)}, u32[]{:S(2)}, u32[]{:S(2)}) collective-permute-start(f32[256,256]{1,0:T(8,128)S(1)} %get-tuple-element.155.refs_0_.rest_0_.own), channel_id=1, source_target_pairs={{0,2},{1,5},{2,0},{3,7},{4,6},{5,1},{6,4},{7,3},{8,10},{9,13},{10,... | collective-permute-start | bytes 786440 | tf_op jit(solution)/shard_map/ppermute | solution.py:407
  107.6 9.6 %collective-permute-start.12 = (f32[2,256,256]{2,1,0:T(8,128)S(1)}, f32[2,256,256]{2,1,0:T(8,128)S(1)}, u32[]{:S(2)}, u32[]{:S(2)}) collective-permute-start(f32[2,256,256]{2,1,0:T(8,128)S(1)} %shard_map.110), channel_id=1, source_target_pairs={{0,4},{1,3},{2,6},{3,1},{4,0},{5,7},{6,2},{7,5},{8,12},{9,11},{10,... | collective-permute-start | bytes 1572872 | tf_op jit(solution)/shard_map/ppermute | solution.py:407
  117.6 7.3 %collective-permute-start.13 = (f32[4,256,256]{2,1,0:T(8,128)S(1)}, f32[4,256,256]{2,1,0:T(8,128)S(1)}, u32[]{:S(2)}, u32[]{:S(2)}) collective-permute-start(f32[4,256,256]{2,1,0:T(8,128)S(1)} %shard_map.112), channel_id=1, source_target_pairs={{0,1},{1,0},{2,3},{3,2},{4,5},{5,4},{6,7},{7,6},{8,9},{9,8},{10,11... | collective-permute-start | bytes 3145736 | tf_op jit(solution)/shard_map/ppermute | solution.py:410

commit v24 on v22

--- a/solution.py
+++ b/solution.py
@@ -24,13 +24,14 @@
 def call(kernel, out_shape, in_specs, scratch_shapes=(), out_specs=None):
     if out_specs is None:
         out_specs = jax.tree.map(lambda _: VMEM, out_shape)
+    room = 20 if lax.axis_size("blk") <= 8 else 48
     return pl.pallas_call(
         kernel,
         out_shape=out_shape,
         in_specs=in_specs,
         out_specs=out_specs,
         scratch_shapes=list(scratch_shapes),
-        compiler_params=pltpu.CompilerParams(vmem_limit_bytes=48 * 1024 * 1024),
+        compiler_params=pltpu.CompilerParams(vmem_limit_bytes=room * 1024 * 1024),
     )
 
 
@@ -448,7 +449,7 @@
             there += moved[len(moves) :]
             if step + 1 < steps:
                 added, size = [kernel], devices
-                if step > 0 or four:
+                if step > 0 or four and widest:
                     added = list(here)
                     corners = in_pair if step > 0 else in_cross
                     if step > 1 and widest:

time: 167 us -> 167 us (level)
    all_to_all x8 -> x9, blocking collectives: 76.5 us -> 86.9 us  [exchange(): return lax.all_to_all(parts, AXES, split_axis=0, concat_axis=0, tiled=True)]
    all_to_all x8 -> x7, blocking collectives: 65.3 us -> 55.1 us  [narrow_exchange(): lax.all_to_all(parts, AXES, split_axis=0, concat_axis=0, axis_index_group...]
where the time goes in v24:
time: 167 us; the launch traced here: 166 us
  blocking collectives  142 us (85%)
  Pallas kernels  12.9 us (8%)
  starting transfers between devices  9.4 us (6%)
    all_to_all x9, blocking collectives, exchange(): return lax.all_to_all(parts, AXES, split_axis=0, concat_axis=0, tiled=True)  86.9 us
    all_to_all x7, blocking collectives, narrow_exchange(): lax.all_to_all(parts, AXES, split_axis=0, concat_axis=0, axis_index_group...  55.1 us
    ppermute x9, starting transfers between devices, across_pairs(): lax.ppermute(value, 'blk', [(i, i ^ hop) for i, hop in enumerate(hops)])  8.62 us
  transfers between devices with their start and end apart: 13, of which 1 were waited for; matrix products, arithmetic and copies ran while one was open for 0% of the time, Pallas kernels for 1%

profile of v24, /device:TPU:0, one launch (start us, length us, event | category | flops | bytes accessed | tf_op | source)
XLA Modules:
  0.0 166.0 jit_solution(9585379548728958801)
XLA Ops:
  1.3 1.9 %shard_map.95 = (s32[8]{0:T(128)S(1)}, s32[8]{0:T(128)S(1)}, s32[5,128]{1,0:T(8,128)S(1)}, s32[5,128]{1,0:T(8,128)S(1)}, f32[1,256]{1,0:T(1,128)S(1)}, /*index=5...) custom-call(s32[1]{0:T(128)S(6)} %copy.10.tile_count, ...), custom_call_target="tpu_custom_call" | custom-call | tf_op jit(solution)/shard_map/pallas_call | solution.py:387
  5.1 2.9 %collective-permute-start.1 = (bf16[2,336,128]{2,1,0:T(8,128)(2,1)S(1)}, bf16[2,336,128]{2,1,0:T(8,128)(2,1)S(1)}, u32[]{:S(2)}, u32[]{:S(2)}) collective-permute-start(bf16[2,336,128]{2,1,0:T(8,128)(2,1)S(1)} %get-tuple-element.91), channel_id=1, source_target_pairs={{0,2},{1,5},{2,0},{3,7},{4,6},{5,1},{6,4},{7,3},{8,10},{9,13},{10,... | collective-permute-start | bytes 516104 | tf_op jit(solution)/shard_map/ppermute | solution.py:406
  8.0 1.5 collective-permute-start.2
  9.5 13.4 %all_to_all.80.summed = f32[32,1,256]{2,1,0:T(1,128)S(1)} all-to-all(f32[32,1,256]{2,1,0:T(1,128)S(1)} %shard_map.96), channel_id=1, replica_groups=mesh['grp'=4,'blk'=8] {'grp','blk'}, dimensions={0} | all-to-all | bytes 65536 | tf_op jit(solution)/shard_map/all_to_all | solution.py:342
  24.3 9.0 %all_to_all.81.refs_2_ = f32[32,1,256]{2,1,0:T(1,128)S(1)} all-to-all(f32[32,1,256]{2,1,0:T(1,128)S(1)} %get-tuple-element.95), channel_id=1, replica_groups=mesh['grp'=4,'blk'=8] {'grp','blk'}, dimensions={0} | all-to-all | bytes 65536 | tf_op jit(solution)/shard_map/all_to_all | solution.py:342
  34.2 8.8 %all_to_all.82.refs_3_ = f32[16,1,256]{2,1,0:T(1,128)S(1)} all-to-all(f32[16,1,256]{2,1,0:T(1,128)S(1)} %shard_map.99), channel_id=1, replica_groups={{9,11,8,12,17,19,16,20,1,3,0,4,25,27,24,28},{15,13,14,10,23,21,22,18,7,..., dimensions={0} | all-to-all | bytes 32768 | tf_op jit(solution)/shard_map/all_to_all | solution.py:351
  43.4 8.1 %all_to_all.83.summed = f32[8,1,256]{2,1,0:T(1,128)S(1)} all-to-all(f32[8,1,256]{2,1,0:T(1,128)S(1)} %shard_map.101), channel_id=1, replica_groups={{1,0,9,8,17,16,25,24},{3,2,11,10,19,18,27,26},{5,4,13,12,21,20,29,28},{..., dimensions={0} | all-to-all | bytes 16384 | tf_op jit(solution)/shard_map/all_to_all | solution.py:351
  51.5 1.2 shard_map.103
  52.7 1.1 collective-permute-start.7
  53.9 8.9 %all_to_all.84.refs_1_ = f32[32,1,256]{2,1,0:T(1,128)S(1)} all-to-all(f32[32,1,256]{2,1,0:T(1,128)S(1)} %get-tuple-element.112), channel_id=1, replica_groups=mesh['grp'=4,'blk'=8] {'grp','blk'}, dimensions={0} | all-to-all | bytes 65536 | tf_op jit(solution)/shard_map/all_to_all | solution.py:342
  63.7 10.4 %all_to_all.85.refs_3_ = f32[32,1,256]{2,1,0:T(1,128)S(1)} all-to-all(f32[32,1,256]{2,1,0:T(1,128)S(1)} %shard_map.104), channel_id=1, replica_groups=mesh['grp'=4,'blk'=8] {'grp','blk'}, dimensions={0} | all-to-all | bytes 65536 | tf_op jit(solution)/shard_map/all_to_all | solution.py:342
  74.9 7.1 %all_to_all.86.refs_3_ = f32[8,1,256]{2,1,0:T(1,128)S(1)} all-to-all(f32[8,1,256]{2,1,0:T(1,128)S(1)} %shard_map.106), channel_id=1, replica_groups={{9,8,17,16,1,0,25,24},{11,10,19,18,3,2,27,26},{13,12,21,20,5,4,29,28},{..., dimensions={0} | all-to-all | bytes 16384 | tf_op jit(solution)/shard_map/all_to_all | solution.py:351
  82.7 7.9 %all_to_all.87.summed = f32[8,1,256]{2,1,0:T(1,128)S(1)} all-to-all(f32[8,1,256]{2,1,0:T(1,128)S(1)} %shard_map.108), channel_id=1, replica_groups={{1,0,9,8,17,16,25,24},{3,2,11,10,19,18,27,26},{5,4,13,12,21,20,29,28},{..., dimensions={0} | all-to-all | bytes 16384 | tf_op jit(solution)/shard_map/all_to_all | solution.py:351
  90.5 1.7 %shard_map.109 = (f32[256,256]{1,0:T(8,128)S(1)}, f32[32,1,256]{2,1,0:T(1,128)S(1)}) custom-call(f32[8,1,256]{2,1,0:T(1,128)S(1)} %all_to_all.87.summed, f32[1,256]{1,0:T(1,128)S(1)} %get-tuple-element.85.class_prior, f32[1,256]{1,0:T(1,128)S(1)} %get-tuple-element.90.class_target.refs_3_.refs_4_.refs_2_.refs_5_, ...), custom_call_target="tpu_custom_call" | custom-call | tf_op jit(solution)/shard_map/pallas_call | solution.py:484
  92.8 9.0 %all_to_all.88.refs_2_ = f32[32,1,256]{2,1,0:T(1,128)S(1)} all-to-all(f32[32,1,256]{2,1,0:T(1,128)S(1)} %get-tuple-element.134), channel_id=1, replica_groups=mesh['grp'=4,'blk'=8] {'grp','blk'}, dimensions={0} | all-to-all | bytes 65536 | tf_op jit(solution)/shard_map/all_to_all | solution.py:342
  102.7 8.8 %all_to_all.89.refs_3_ = f32[16,1,256]{2,1,0:T(1,128)S(1)} all-to-all(f32[16,1,256]{2,1,0:T(1,128)S(1)} %shard_map.110), channel_id=1, replica_groups={{9,11,8,12,17,19,16,20,1,3,0,4,25,27,24,28},{15,13,14,10,23,21,22,18,7,..., dimensions={0} | all-to-all | bytes 32768 | tf_op jit(solution)/shard_map/all_to_all | solution.py:351
  112.0 7.1 %all_to_all.90.refs_4_ = f32[8,1,256]{2,1,0:T(1,128)S(1)} all-to-all(f32[8,1,256]{2,1,0:T(1,128)S(1)} %shard_map.112), channel_id=1, replica_groups={{9,8,17,16,1,0,25,24},{11,10,19,18,3,2,27,26},{13,12,21,20,5,4,29,28},{..., dimensions={0} | all-to-all | bytes 16384 | tf_op jit(solution)/shard_map/all_to_all | solution.py:351
  119.5 7.2 %all_to_all.91.summed.author_summed = f32[4,1,256]{2,1,0:T(1,128)S(1)} all-to-all(f32[4,1,256]{2,1,0:T(1,128)S(1)} %shard_map.114), channel_id=1, replica_groups={{8,16,0,24},{9,17,1,25},{10,18,2,26},{11,19,3,27},{12,20,4,28},{13,21,5..., dimensions={0} | all-to-all | bytes 8192 | tf_op jit(solution)/shard_map/all_to_all | solution.py:351
  126.7 1.2 shard_map.115
  127.9 9.4 %all_to_all.92.refs_1_ = f32[32,1,256]{2,1,0:T(1,128)S(1)} all-to-all(f32[32,1,256]{2,1,0:T(1,128)S(1)} %get-tuple-element.155), channel_id=1, replica_groups=mesh['grp'=4,'blk'=8] {'grp','blk'}, dimensions={0} | all-to-all | bytes 65536 | tf_op jit(solution)/shard_map/all_to_all | solution.py:342
  137.6 8.9 %all_to_all.93.refs_1_ = f32[32,1,256]{2,1,0:T(1,128)S(1)} all-to-all(f32[32,1,256]{2,1,0:T(1,128)S(1)} %shard_map.116), channel_id=1, replica_groups=mesh['grp'=4,'blk'=8] {'grp','blk'}, dimensions={0} | all-to-all | bytes 65536 | tf_op jit(solution)/shard_map/all_to_all | solution.py:342
  146.8 8.9 %all_to_all.94.refs_1_ = f32[32,1,256]{2,1,0:T(1,128)S(1)} all-to-all(f32[32,1,256]{2,1,0:T(1,128)S(1)} %shard_map.117), channel_id=1, replica_groups=mesh['grp'=4,'blk'=8] {'grp','blk'}, dimensions={0} | all-to-all | bytes 65536 | tf_op jit(solution)/shard_map/all_to_all | solution.py:342
  155.9 8.9 %all_to_all.95.summed = f32[32,1,256]{2,1,0:T(1,128)S(1)} all-to-all(f32[32,1,256]{2,1,0:T(1,128)S(1)} %shard_map.118), channel_id=1, replica_groups=mesh['grp'=4,'blk'=8] {'grp','blk'}, dimensions={0} | all-to-all | bytes 65536 | tf_op jit(solution)/shard_map/all_to_all | solution.py:342
  164.9 1.1 shard_map.119
  (43 shorter events, 9.7 us)
Async XLA Ops:
  3.2 1.8 %collective-permute-start = (bf16[4,336,128]{2,1,0:T(8,128)(2,1)S(1)}, bf16[4,336,128]{2,1,0:T(8,128)(2,1)S(1)}, u32[]{:S(2)}, u32[]{:S(2)}) collective-permute-start(bf16[4,336,128]{2,1,0:T(8,128)(2,1)S(1)} %get-tuple-element.82.swap), channel_id=1, source_target_pairs={{0,1},{1,0},{2,3},{3,2},{4,5},{5,4},{6,7},{7,6},{8,9},{9,8},{10,11... | collective-permute-start | bytes 1032200 | tf_op jit(solution)/shard_map/ppermute | solution.py:395
  5.1 17.8 %collective-permute-start.1 = (bf16[2,336,128]{2,1,0:T(8,128)(2,1)S(1)}, bf16[2,336,128]{2,1,0:T(8,128)(2,1)S(1)}, u32[]{:S(2)}, u32[]{:S(2)}) collective-permute-start(bf16[2,336,128]{2,1,0:T(8,128)(2,1)S(1)} %get-tuple-element.91), channel_id=1, source_target_pairs={{0,2},{1,5},{2,0},{3,7},{4,6},{5,1},{6,4},{7,3},{8,10},{9,13},{10,... | collective-permute-start | bytes 516104 | tf_op jit(solution)/shard_map/ppermute | solution.py:406
  8.0 14.9 %collective-permute-start.2 = (bf16[2,336,128]{2,1,0:T(8,128)(2,1)S(1)}, bf16[2,336,128]{2,1,0:T(8,128)(2,1)S(1)}, u32[]{:S(2)}, u32[]{:S(2)}) collective-permute-start(bf16[2,336,128]{2,1,0:T(8,128)(2,1)S(1)} %get-tuple-element.92), channel_id=1, source_target_pairs={{0,4},{1,3},{2,6},{3,1},{4,0},{5,7},{6,2},{7,5},{8,12},{9,11},{10,... | collective-permute-start | bytes 516104 | tf_op jit(solution)/shard_map/ppermute | solution.py:406
  9.5 13.4 %collective-permute-start.3 = (bf16[2,336,128]{2,1,0:T(8,128)(2,1)S(1)}, bf16[2,336,128]{2,1,0:T(8,128)(2,1)S(1)}, u32[]{:S(2)}, u32[]{:S(2)}) collective-permute-start(bf16[2,336,128]{2,1,0:T(8,128)(2,1)S(1)} %get-tuple-element.93), channel_id=1, source_target_pairs={{0,6},{1,7},{2,4},{3,5},{4,2},{5,3},{6,0},{7,1},{8,14},{9,15},{10,... | collective-permute-start | bytes 516104 | tf_op jit(solution)/shard_map/ppermute | solution.py:406
  23.7 9.6 %collective-permute-start.4 = (f32[256,256]{1,0:T(8,128)S(1)}, f32[256,256]{1,0:T(8,128)S(1)}, u32[]{:S(2)}, u32[]{:S(2)}) collective-permute-start(f32[256,256]{1,0:T(8,128)S(1)} %get-tuple-element.107.refs_0_.rest_0_), channel_id=1, source_target_pairs={{0,2},{1,5},{2,0},{3,7},{4,6},{5,1},{6,4},{7,3},{8,10},{9,13},{10,... | collective-permute-start | bytes 786440 | tf_op jit(solution)/shard_map/ppermute | solution.py:406
  33.6 9.5 %collective-permute-start.5 = (f32[2,256,256]{2,1,0:T(8,128)S(1)}, f32[2,256,256]{2,1,0:T(8,128)S(1)}, u32[]{:S(2)}, u32[]{:S(2)}) collective-permute-start(f32[2,256,256]{2,1,0:T(8,128)S(1)} %shard_map.100), channel_id=1, source_target_pairs={{0,4},{1,3},{2,6},{3,1},{4,0},{5,7},{6,2},{7,5},{8,12},{9,11},{10,... | collective-permute-start | bytes 1572872 | tf_op jit(solution)/shard_map/ppermute | solution.py:406
  43.4 8.2 %collective-permute-start.6 = (f32[4,256,256]{2,1,0:T(8,128)S(1)}, f32[4,256,256]{2,1,0:T(8,128)S(1)}, u32[]{:S(2)}, u32[]{:S(2)}) collective-permute-start(f32[4,256,256]{2,1,0:T(8,128)S(1)} %shard_map.102), channel_id=1, source_target_pairs={{0,1},{1,0},{2,3},{3,2},{4,5},{5,4},{6,7},{7,6},{8,9},{9,8},{10,11... | collective-permute-start | bytes 3145736 | tf_op jit(solution)/shard_map/ppermute | solution.py:409
  52.7 10.1 %collective-permute-start.7 = (bf16[640,256]{1,0:T(8,128)(2,1)S(1)}, bf16[640,256]{1,0:T(8,128)(2,1)S(1)}, u32[]{:S(2)}, u32[]{:S(2)}) collective-permute-start(bf16[640,256]{1,0:T(8,128)(2,1)S(1)} %get-tuple-element.129.refs_0_.rest_0_), channel_id=1, source_target_pairs={{0,2},{1,5},{2,0},{3,7},{4,6},{5,1},{6,4},{7,3},{8,10},{9,13},{10,... | collective-permute-start | bytes 983048 | tf_op jit(solution)/shard_map/ppermute | solution.py:406
  63.1 11.0 %collective-permute-start.8 = (bf16[2,640,256]{2,1,0:T(8,128)(2,1)S(1)}, bf16[2,640,256]{2,1,0:T(8,128)(2,1)S(1)}, u32[]{:S(2)}, u32[]{:S(2)}) collective-permute-start(bf16[2,640,256]{2,1,0:T(8,128)(2,1)S(1)} %shard_map.105), channel_id=1, source_target_pairs={{0,4},{1,3},{2,6},{3,1},{4,0},{5,7},{6,2},{7,5},{8,12},{9,11},{10,... | collective-permute-start | bytes 1966088 | tf_op jit(solution)/shard_map/ppermute | solution.py:406
  74.8 7.3 %collective-permute-start.9 = (bf16[4,640,256]{2,1,0:T(8,128)(2,1)S(1)}, bf16[4,640,256]{2,1,0:T(8,128)(2,1)S(1)}, u32[]{:S(2)}, u32[]{:S(2)}) collective-permute-start(bf16[4,640,256]{2,1,0:T(8,128)(2,1)S(1)} %shard_map.107), channel_id=1, source_target_pairs={{0,1},{1,0},{2,3},{3,2},{4,5},{5,4},{6,7},{7,6},{8,9},{9,8},{10,11... | collective-permute-start | bytes 3932168 | tf_op jit(solution)/shard_map/ppermute | solution.py:409
  92.3 9.5 %collective-permute-start.10 = (f32[256,256]{1,0:T(8,128)S(1)}, f32[256,256]{1,0:T(8,128)S(1)}, u32[]{:S(2)}, u32[]{:S(2)}) collective-permute-start(f32[256,256]{1,0:T(8,128)S(1)} %get-tuple-element.151.refs_0_.rest_0_.own), channel_id=1, source_target_pairs={{0,2},{1,5},{2,0},{3,7},{4,6},{5,1},{6,4},{7,3},{8,10},{9,13},{10,... | collective-permute-start | bytes 786440 | tf_op jit(solution)/shard_map/ppermute | solution.py:406
  102.1 9.5 %collective-permute-start.11 = (f32[2,256,256]{2,1,0:T(8,128)S(1)}, f32[2,256,256]{2,1,0:T(8,128)S(1)}, u32[]{:S(2)}, u32[]{:S(2)}) collective-permute-start(f32[2,256,256]{2,1,0:T(8,128)S(1)} %shard_map.111), channel_id=1, source_target_pairs={{0,4},{1,3},{2,6},{3,1},{4,0},{5,7},{6,2},{7,5},{8,12},{9,11},{10,... | collective-permute-start | bytes 1572872 | tf_op jit(solution)/shard_map/ppermute | solution.py:406
  111.9 7.2 %collective-permute-start.12 = (f32[4,256,256]{2,1,0:T(8,128)S(1)}, f32[4,256,256]{2,1,0:T(8,128)S(1)}, u32[]{:S(2)}, u32[]{:S(2)}) collective-permute-start(f32[4,256,256]{2,1,0:T(8,128)S(1)} %shard_map.113), channel_id=1, source_target_pairs={{0,1},{1,0},{2,3},{3,2},{4,5},{5,4},{6,7},{7,6},{8,9},{9,8},{10,11... | collective-permute-start | bytes 3145736 | tf_op jit(solution)/shard_map/ppermute | solution.py:409

commit v25 on v21

--- a/solution.py
+++ b/solution.py
@@ -453,15 +453,19 @@
                         added += there
                         sides = 1
                     size = sides * lax.axis_size("grp")
-                local = call(
-                    balance_kernel, shape((size, 1, classes), f32), [VMEM] * (len(added) + 2)
-                )(*added, summed, target)
                 joined = sent
                 if four and step < 2:
                     joined = call(
                         join_kernel, shape((2 * step + 2, *sent.shape), sent.dtype), [VMEM] * len(here)
                     )(*here)
-                local, sent, joined, *here = lax.optimization_barrier((local, sent, joined, *here))
+                    joined, summed = lax.optimization_barrier((joined, summed))
+                local = call(
+                    balance_kernel, shape((size, 1, classes), f32), [VMEM] * (len(added) + 2)
+                )(*added, summed, target)
+                if four:
+                    local, sent, *here = lax.optimization_barrier((local, sent, *here))
+                else:
+                    local, sent, joined, *here = lax.optimization_barrier((local, sent, joined, *here))
         return summed, here + there
 
     def last_balance(kernel, local):

time: 166 us -> 166 us (level)
  transfers between devices with their start and end apart: 13 -> 13, of which waited for: 1 -> 1; matrix products, arithmetic and copies ran while one was open for 0% -> 0% of each run, Pallas kernels for 1% -> 2%
where the time goes in v25:
time: 166 us; the launch traced here: 165 us
  blocking collectives  142 us (86%)
  Pallas kernels  12.8 us (8%)
  starting transfers between devices  9.02 us (5%)
    all_to_all x11, blocking collectives, exchange(): return lax.all_to_all(parts, AXES, split_axis=0, concat_axis=0, tiled=True)  104 us
    all_to_all x5, blocking collectives, narrow_exchange(): lax.all_to_all(parts, AXES, split_axis=0, concat_axis=0, axis_index_group...  37.4 us
    ppermute x9, starting transfers between devices, across_pairs(): lax.ppermute(value, 'blk', [(i, i ^ hop) for i, hop in enumerate(hops)])  8.02 us
  transfers between devices with their start and end apart: 13, of which 1 were waited for; matrix products, arithmetic and copies ran while one was open for 0% of the time, Pallas kernels for 2%

profile of v25, /device:TPU:0, one launch (start us, length us, event | category | flops | bytes accessed | tf_op | source)
XLA Modules:
  0.0 165.1 jit_solution(16477232196999119786)
XLA Ops:
  1.3 1.9 %shard_map.95 = (s32[8]{0:T(128)S(1)}, s32[8]{0:T(128)S(1)}, s32[5,128]{1,0:T(8,128)S(1)}, s32[5,128]{1,0:T(8,128)S(1)}, f32[1,256]{1,0:T(1,128)S(1)}, /*index=5...) custom-call(s32[1]{0:T(128)S(6)} %copy.10.tile_count, ...), custom_call_target="tpu_custom_call" | custom-call | tf_op jit(solution)/shard_map/pallas_call | solution.py:389
  3.8 1.1 shard_map.96
  5.1 2.9 %collective-permute-start.1 = (bf16[2,336,128]{2,1,0:T(8,128)(2,1)S(1)}, bf16[2,336,128]{2,1,0:T(8,128)(2,1)S(1)}, u32[]{:S(2)}, u32[]{:S(2)}) collective-permute-start(bf16[2,336,128]{2,1,0:T(8,128)(2,1)S(1)} %get-tuple-element.97), channel_id=1, source_target_pairs={{0,2},{1,5},{2,0},{3,7},{4,6},{5,1},{6,4},{7,3},{8,10},{9,13},{10,... | collective-permute-start | bytes 516104 | tf_op jit(solution)/shard_map/ppermute | solution.py:408
  8.0 1.5 collective-permute-start.2
  9.5 13.4 %all_to_all.80.summed = f32[32,1,256]{2,1,0:T(1,128)S(1)} all-to-all(f32[32,1,256]{2,1,0:T(1,128)S(1)} %shard_map.96), channel_id=1, replica_groups=mesh['grp'=4,'blk'=8] {'grp','blk'}, dimensions={0} | all-to-all | bytes 65536 | tf_op jit(solution)/shard_map/all_to_all | solution.py:341
  24.3 9.0 %all_to_all.81.refs_1_ = f32[32,1,256]{2,1,0:T(1,128)S(1)} all-to-all(f32[32,1,256]{2,1,0:T(1,128)S(1)} %get-tuple-element.101), channel_id=1, replica_groups=mesh['grp'=4,'blk'=8] {'grp','blk'}, dimensions={0} | all-to-all | bytes 65536 | tf_op jit(solution)/shard_map/all_to_all | solution.py:341
  34.2 9.0 %all_to_all.82.refs_3_ = f32[32,1,256]{2,1,0:T(1,128)S(1)} all-to-all(f32[32,1,256]{2,1,0:T(1,128)S(1)} %shard_map.100), channel_id=1, replica_groups=mesh['grp'=4,'blk'=8] {'grp','blk'}, dimensions={0} | all-to-all | bytes 65536 | tf_op jit(solution)/shard_map/all_to_all | solution.py:341
  43.6 8.0 %all_to_all.83.summed = f32[8,1,256]{2,1,0:T(1,128)S(1)} all-to-all(f32[8,1,256]{2,1,0:T(1,128)S(1)} %shard_map.102), channel_id=1, replica_groups={{1,0,9,8,17,16,25,24},{3,2,11,10,19,18,27,26},{5,4,13,12,21,20,29,28},{..., dimensions={0} | all-to-all | bytes 16384 | tf_op jit(solution)/shard_map/all_to_all | solution.py:353
  51.6 1.2 shard_map.103
  53.4 9.0 %all_to_all.84.refs_1_ = f32[32,1,256]{2,1,0:T(1,128)S(1)} all-to-all(f32[32,1,256]{2,1,0:T(1,128)S(1)} %get-tuple-element.121), channel_id=1, replica_groups=mesh['grp'=4,'blk'=8] {'grp','blk'}, dimensions={0} | all-to-all | bytes 65536 | tf_op jit(solution)/shard_map/all_to_all | solution.py:341
  63.3 10.2 %all_to_all.85.refs_3_ = f32[32,1,256]{2,1,0:T(1,128)S(1)} all-to-all(f32[32,1,256]{2,1,0:T(1,128)S(1)} %shard_map.105), channel_id=1, replica_groups=mesh['grp'=4,'blk'=8] {'grp','blk'}, dimensions={0} | all-to-all | bytes 65536 | tf_op jit(solution)/shard_map/all_to_all | solution.py:341
  74.3 7.2 %all_to_all.86.refs_3_ = f32[8,1,256]{2,1,0:T(1,128)S(1)} all-to-all(f32[8,1,256]{2,1,0:T(1,128)S(1)} %shard_map.107), channel_id=1, replica_groups={{9,8,17,16,1,0,25,24},{11,10,19,18,3,2,27,26},{13,12,21,20,5,4,29,28},{..., dimensions={0} | all-to-all | bytes 16384 | tf_op jit(solution)/shard_map/all_to_all | solution.py:353
  82.0 7.9 %all_to_all.87.summed = f32[8,1,256]{2,1,0:T(1,128)S(1)} all-to-all(f32[8,1,256]{2,1,0:T(1,128)S(1)} %shard_map.108), channel_id=1, replica_groups={{1,0,9,8,17,16,25,24},{3,2,11,10,19,18,27,26},{5,4,13,12,21,20,29,28},{..., dimensions={0} | all-to-all | bytes 16384 | tf_op jit(solution)/shard_map/all_to_all | solution.py:353
  89.9 1.7 %shard_map.109 = (f32[256,256]{1,0:T(8,128)S(1)}, f32[32,1,256]{2,1,0:T(1,128)S(1)}) custom-call(f32[8,1,256]{2,1,0:T(1,128)S(1)} %all_to_all.87.summed, f32[1,256]{1,0:T(1,128)S(1)} %get-tuple-element.91.class_prior, f32[1,256]{1,0:T(1,128)S(1)} %get-tuple-element.96.class_target.refs_2_.refs_4_.refs_5_, ...), custom_call_target="tpu_custom_call" | custom-call | tf_op jit(solution)/shard_map/pallas_call | solution.py:485
  92.2 9.0 %all_to_all.88.refs_1_ = f32[32,1,256]{2,1,0:T(1,128)S(1)} all-to-all(f32[32,1,256]{2,1,0:T(1,128)S(1)} %get-tuple-element.144), channel_id=1, replica_groups=mesh['grp'=4,'blk'=8] {'grp','blk'}, dimensions={0} | all-to-all | bytes 65536 | tf_op jit(solution)/shard_map/all_to_all | solution.py:341
  102.0 9.0 %all_to_all.89.refs_3_ = f32[32,1,256]{2,1,0:T(1,128)S(1)} all-to-all(f32[32,1,256]{2,1,0:T(1,128)S(1)} %shard_map.111), channel_id=1, replica_groups=mesh['grp'=4,'blk'=8] {'grp','blk'}, dimensions={0} | all-to-all | bytes 65536 | tf_op jit(solution)/shard_map/all_to_all | solution.py:341
  111.5 7.1 %all_to_all.90.refs_4_ = f32[8,1,256]{2,1,0:T(1,128)S(1)} all-to-all(f32[8,1,256]{2,1,0:T(1,128)S(1)} %shard_map.113), channel_id=1, replica_groups={{9,8,17,16,1,0,25,24},{11,10,19,18,3,2,27,26},{13,12,21,20,5,4,29,28},{..., dimensions={0} | all-to-all | bytes 16384 | tf_op jit(solution)/shard_map/all_to_all | solution.py:353
  119.0 7.2 %all_to_all.91.summed.author_summed = f32[4,1,256]{2,1,0:T(1,128)S(1)} all-to-all(f32[4,1,256]{2,1,0:T(1,128)S(1)} %shard_map.114), channel_id=1, replica_groups={{8,16,0,24},{9,17,1,25},{10,18,2,26},{11,19,3,27},{12,20,4,28},{13,21,5..., dimensions={0} | all-to-all | bytes 8192 | tf_op jit(solution)/shard_map/all_to_all | solution.py:353
  126.3 1.2 shard_map.115
  127.4 9.0 %all_to_all.92.refs_1_ = f32[32,1,256]{2,1,0:T(1,128)S(1)} all-to-all(f32[32,1,256]{2,1,0:T(1,128)S(1)} %get-tuple-element.167), channel_id=1, replica_groups=mesh['grp'=4,'blk'=8] {'grp','blk'}, dimensions={0} | all-to-all | bytes 65536 | tf_op jit(solution)/shard_map/all_to_all | solution.py:341
  136.7 8.9 %all_to_all.93.refs_1_ = f32[32,1,256]{2,1,0:T(1,128)S(1)} all-to-all(f32[32,1,256]{2,1,0:T(1,128)S(1)} %shard_map.116), channel_id=1, replica_groups=mesh['grp'=4,'blk'=8] {'grp','blk'}, dimensions={0} | all-to-all | bytes 65536 | tf_op jit(solution)/shard_map/all_to_all | solution.py:341
  145.8 8.9 %all_to_all.94.refs_1_ = f32[32,1,256]{2,1,0:T(1,128)S(1)} all-to-all(f32[32,1,256]{2,1,0:T(1,128)S(1)} %shard_map.117), channel_id=1, replica_groups=mesh['grp'=4,'blk'=8] {'grp','blk'}, dimensions={0} | all-to-all | bytes 65536 | tf_op jit(solution)/shard_map/all_to_all | solution.py:341
  155.0 8.9 %all_to_all.95.summed = f32[32,1,256]{2,1,0:T(1,128)S(1)} all-to-all(f32[32,1,256]{2,1,0:T(1,128)S(1)} %shard_map.118), channel_id=1, replica_groups=mesh['grp'=4,'blk'=8] {'grp','blk'}, dimensions={0} | all-to-all | bytes 65536 | tf_op jit(solution)/shard_map/all_to_all | solution.py:341
  164.0 1.1 shard_map.119
  (43 shorter events, 9.4 us)
Async XLA Ops:
  3.2 1.8 %collective-permute-start = (bf16[4,336,128]{2,1,0:T(8,128)(2,1)S(1)}, bf16[4,336,128]{2,1,0:T(8,128)(2,1)S(1)}, u32[]{:S(2)}, u32[]{:S(2)}) collective-permute-start(bf16[4,336,128]{2,1,0:T(8,128)(2,1)S(1)} %get-tuple-element.88.swap), channel_id=1, source_target_pairs={{0,1},{1,0},{2,3},{3,2},{4,5},{5,4},{6,7},{7,6},{8,9},{9,8},{10,11... | collective-permute-start | bytes 1032200 | tf_op jit(solution)/shard_map/ppermute | solution.py:397
  5.1 17.8 %collective-permute-start.1 = (bf16[2,336,128]{2,1,0:T(8,128)(2,1)S(1)}, bf16[2,336,128]{2,1,0:T(8,128)(2,1)S(1)}, u32[]{:S(2)}, u32[]{:S(2)}) collective-permute-start(bf16[2,336,128]{2,1,0:T(8,128)(2,1)S(1)} %get-tuple-element.97), channel_id=1, source_target_pairs={{0,2},{1,5},{2,0},{3,7},{4,6},{5,1},{6,4},{7,3},{8,10},{9,13},{10,... | collective-permute-start | bytes 516104 | tf_op jit(solution)/shard_map/ppermute | solution.py:408
  8.0 14.9 %collective-permute-start.2 = (bf16[2,336,128]{2,1,0:T(8,128)(2,1)S(1)}, bf16[2,336,128]{2,1,0:T(8,128)(2,1)S(1)}, u32[]{:S(2)}, u32[]{:S(2)}) collective-permute-start(bf16[2,336,128]{2,1,0:T(8,128)(2,1)S(1)} %get-tuple-element.98), channel_id=1, source_target_pairs={{0,4},{1,3},{2,6},{3,1},{4,0},{5,7},{6,2},{7,5},{8,12},{9,11},{10,... | collective-permute-start | bytes 516104 | tf_op jit(solution)/shard_map/ppermute | solution.py:408
  9.5 13.4 %collective-permute-start.3 = (bf16[2,336,128]{2,1,0:T(8,128)(2,1)S(1)}, bf16[2,336,128]{2,1,0:T(8,128)(2,1)S(1)}, u32[]{:S(2)}, u32[]{:S(2)}) collective-permute-start(bf16[2,336,128]{2,1,0:T(8,128)(2,1)S(1)} %get-tuple-element.99), channel_id=1, source_target_pairs={{0,6},{1,7},{2,4},{3,5},{4,2},{5,3},{6,0},{7,1},{8,14},{9,15},{10,... | collective-permute-start | bytes 516104 | tf_op jit(solution)/shard_map/ppermute | solution.py:408
  23.7 9.6 %collective-permute-start.4 = (f32[256,256]{1,0:T(8,128)S(1)}, f32[256,256]{1,0:T(8,128)S(1)}, u32[]{:S(2)}, u32[]{:S(2)}) collective-permute-start(f32[256,256]{1,0:T(8,128)S(1)} %get-tuple-element.115.refs_0_.rest_0_), channel_id=1, source_target_pairs={{0,2},{1,5},{2,0},{3,7},{4,6},{5,1},{6,4},{7,3},{8,10},{9,13},{10,... | collective-permute-start | bytes 786440 | tf_op jit(solution)/shard_map/ppermute | solution.py:408
  33.3 9.8 %collective-permute-start.5 = (f32[2,256,256]{2,1,0:T(8,128)S(1)}, f32[2,256,256]{2,1,0:T(8,128)S(1)}, u32[]{:S(2)}, u32[]{:S(2)}) collective-permute-start(f32[2,256,256]{2,1,0:T(8,128)S(1)} %shard_map.99), channel_id=1, source_target_pairs={{0,4},{1,3},{2,6},{3,1},{4,0},{5,7},{6,2},{7,5},{8,12},{9,11},{10,... | collective-permute-start | bytes 1572872 | tf_op jit(solution)/shard_map/ppermute | solution.py:408
  43.2 8.5 %collective-permute-start.6 = (f32[4,256,256]{2,1,0:T(8,128)S(1)}, f32[4,256,256]{2,1,0:T(8,128)S(1)}, u32[]{:S(2)}, u32[]{:S(2)}) collective-permute-start(f32[4,256,256]{2,1,0:T(8,128)S(1)} %shard_map.101), channel_id=1, source_target_pairs={{0,1},{1,0},{2,3},{3,2},{4,5},{5,4},{6,7},{7,6},{8,9},{9,8},{10,11... | collective-permute-start | bytes 3145736 | tf_op jit(solution)/shard_map/ppermute | solution.py:411
  52.8 9.5 %collective-permute-start.7 = (bf16[640,256]{1,0:T(8,128)(2,1)S(1)}, bf16[640,256]{1,0:T(8,128)(2,1)S(1)}, u32[]{:S(2)}, u32[]{:S(2)}) collective-permute-start(bf16[640,256]{1,0:T(8,128)(2,1)S(1)} %get-tuple-element.139.refs_0_.rest_0_), channel_id=1, source_target_pairs={{0,2},{1,5},{2,0},{3,7},{4,6},{5,1},{6,4},{7,3},{8,10},{9,13},{10,... | collective-permute-start | bytes 983048 | tf_op jit(solution)/shard_map/ppermute | solution.py:408
  62.4 11.0 %collective-permute-start.8 = (bf16[2,640,256]{2,1,0:T(8,128)(2,1)S(1)}, bf16[2,640,256]{2,1,0:T(8,128)(2,1)S(1)}, u32[]{:S(2)}, u32[]{:S(2)}) collective-permute-start(bf16[2,640,256]{2,1,0:T(8,128)(2,1)S(1)} %shard_map.104), channel_id=1, source_target_pairs={{0,4},{1,3},{2,6},{3,1},{4,0},{5,7},{6,2},{7,5},{8,12},{9,11},{10,... | collective-permute-start | bytes 1966088 | tf_op jit(solution)/shard_map/ppermute | solution.py:408
  73.6 7.9 %collective-permute-start.9 = (bf16[4,640,256]{2,1,0:T(8,128)(2,1)S(1)}, bf16[4,640,256]{2,1,0:T(8,128)(2,1)S(1)}, u32[]{:S(2)}, u32[]{:S(2)}) collective-permute-start(bf16[4,640,256]{2,1,0:T(8,128)(2,1)S(1)} %shard_map.106), channel_id=1, source_target_pairs={{0,1},{1,0},{2,3},{3,2},{4,5},{5,4},{6,7},{7,6},{8,9},{9,8},{10,11... | collective-permute-start | bytes 3932168 | tf_op jit(solution)/shard_map/ppermute | solution.py:411
  91.6 9.5 %collective-permute-start.10 = (f32[256,256]{1,0:T(8,128)S(1)}, f32[256,256]{1,0:T(8,128)S(1)}, u32[]{:S(2)}, u32[]{:S(2)}) collective-permute-start(f32[256,256]{1,0:T(8,128)S(1)} %get-tuple-element.163.refs_0_.rest_0_.own), channel_id=1, source_target_pairs={{0,2},{1,5},{2,0},{3,7},{4,6},{5,1},{6,4},{7,3},{8,10},{9,13},{10,... | collective-permute-start | bytes 786440 | tf_op jit(solution)/shard_map/ppermute | solution.py:408
  101.2 9.8 %collective-permute-start.11 = (f32[2,256,256]{2,1,0:T(8,128)S(1)}, f32[2,256,256]{2,1,0:T(8,128)S(1)}, u32[]{:S(2)}, u32[]{:S(2)}) collective-permute-start(f32[2,256,256]{2,1,0:T(8,128)S(1)} %shard_map.110), channel_id=1, source_target_pairs={{0,4},{1,3},{2,6},{3,1},{4,0},{5,7},{6,2},{7,5},{8,12},{9,11},{10,... | collective-permute-start | bytes 1572872 | tf_op jit(solution)/shard_map/ppermute | solution.py:408
  111.1 7.6 %collective-permute-start.12 = (f32[4,256,256]{2,1,0:T(8,128)S(1)}, f32[4,256,256]{2,1,0:T(8,128)S(1)}, u32[]{:S(2)}, u32[]{:S(2)}) collective-permute-start(f32[4,256,256]{2,1,0:T(8,128)S(1)} %shard_map.112), channel_id=1, source_target_pairs={{0,1},{1,0},{2,3},{3,2},{4,5},{5,4},{6,7},{7,6},{8,9},{9,8},{10,11... | collective-permute-start | bytes 3145736 | tf_op jit(solution)/shard_map/ppermute | solution.py:411

commit v26 on v25

--- a/solution.py
+++ b/solution.py
@@ -423,7 +423,7 @@
         places = [(0, None), (1, None), (2, 0), (2, 1)]
         places += [(3, k) for k in turned(count)]
 
-    def balance(kernel, sent, local, steps, widest):
+    def balance(kernel, sent, local, steps, calm):
         here, there, joined = [sent], [], None
         sides = 0
         for step in range(steps):
@@ -438,7 +438,7 @@
                 others = [joined] if step == 2 else []
             others = [to_other(one) for one in others]
             if sides:
-                summed = narrow_exchange(local, sides, step + 1 == steps and sides == 2)
+                summed = narrow_exchange(local, sides, step + 1 == steps and not calm)
             else:
                 summed = exchange(local)
             summed, *moved = lax.optimization_barrier((summed, *moves, *others))
@@ -449,9 +449,6 @@
                 if step > 0:
                     added = list(here)
                     sides = 2
-                    if step > 1 and widest:
-                        added += there
-                        sides = 1
                     size = sides * lax.axis_size("grp")
                 joined = sent
                 if four and step < 2:
@@ -488,7 +485,7 @@
                 [VMEM] * (3 + len(kernels) + len(held)),
             )(summed, prior, target, *kernels, *held)
             left = ITERS
-        author_summed, kernels = balance(own, own, local, left, True)
+        author_summed, kernels = balance(own, own, local, left, repeat + 1 == ROUNDS)
         last = repeat + 1 == ROUNDS
         kernel, local, *half = call(
             functools.partial(paper_kernel, places, rows),

time: 166 us -> 165 us (level)
  no operation moved by 1% of the time
where the time goes in v26:
time: 165 us
  blocking collectives  141 us (85%)
  Pallas kernels  12.7 us (8%)
  starting transfers between devices  9.03 us (5%)
    all_to_all x11, blocking collectives, exchange(): return lax.all_to_all(parts, AXES, split_axis=0, concat_axis=0, tiled=True)  104 us
    all_to_all x5, blocking collectives, narrow_exchange(): lax.all_to_all(parts, AXES, split_axis=0, concat_axis=0, axis_index_group...  37.1 us
    ppermute x9, starting transfers between devices, across_pairs(): lax.ppermute(value, 'blk', [(i, i ^ hop) for i, hop in enumerate(hops)])  8.03 us
  transfers between devices with their start and end apart: 13, of which 1 were waited for; matrix products, arithmetic and copies ran while one was open for 0% of the time, Pallas kernels for 2%

profile of v26, /device:TPU:0, one launch (start us, length us, event | category | flops | bytes accessed | tf_op | source)
XLA Modules:
  0.0 164.7 jit_solution(5733369332873010374)
XLA Ops:
  1.3 1.9 %shard_map.95 = (s32[8]{0:T(128)S(1)}, s32[8]{0:T(128)S(1)}, s32[5,128]{1,0:T(8,128)S(1)}, s32[5,128]{1,0:T(8,128)S(1)}, f32[1,256]{1,0:T(1,128)S(1)}, /*index=5...) custom-call(s32[1]{0:T(128)S(6)} %copy.10.tile_count, ...), custom_call_target="tpu_custom_call" | custom-call | tf_op jit(solution)/shard_map/pallas_call | solution.py:389
  3.8 1.1 shard_map.96
  5.1 2.9 %collective-permute-start.1 = (bf16[2,336,128]{2,1,0:T(8,128)(2,1)S(1)}, bf16[2,336,128]{2,1,0:T(8,128)(2,1)S(1)}, u32[]{:S(2)}, u32[]{:S(2)}) collective-permute-start(bf16[2,336,128]{2,1,0:T(8,128)(2,1)S(1)} %get-tuple-element.97), channel_id=1, source_target_pairs={{0,2},{1,5},{2,0},{3,7},{4,6},{5,1},{6,4},{7,3},{8,10},{9,13},{10,... | collective-permute-start | bytes 516104 | tf_op jit(solution)/shard_map/ppermute | solution.py:408
  8.0 1.5 collective-permute-start.2
  9.5 13.4 %all_to_all.80.summed = f32[32,1,256]{2,1,0:T(1,128)S(1)} all-to-all(f32[32,1,256]{2,1,0:T(1,128)S(1)} %shard_map.96), channel_id=1, replica_groups=mesh['grp'=4,'blk'=8] {'grp','blk'}, dimensions={0} | all-to-all | bytes 65536 | tf_op jit(solution)/shard_map/all_to_all | solution.py:341
  24.3 9.0 %all_to_all.81.refs_1_ = f32[32,1,256]{2,1,0:T(1,128)S(1)} all-to-all(f32[32,1,256]{2,1,0:T(1,128)S(1)} %get-tuple-element.101), channel_id=1, replica_groups=mesh['grp'=4,'blk'=8] {'grp','blk'}, dimensions={0} | all-to-all | bytes 65536 | tf_op jit(solution)/shard_map/all_to_all | solution.py:341
  34.2 9.0 %all_to_all.82.refs_3_ = f32[32,1,256]{2,1,0:T(1,128)S(1)} all-to-all(f32[32,1,256]{2,1,0:T(1,128)S(1)} %shard_map.100), channel_id=1, replica_groups=mesh['grp'=4,'blk'=8] {'grp','blk'}, dimensions={0} | all-to-all | bytes 65536 | tf_op jit(solution)/shard_map/all_to_all | solution.py:341
  43.6 8.0 %all_to_all.83.summed = f32[8,1,256]{2,1,0:T(1,128)S(1)} all-to-all(f32[8,1,256]{2,1,0:T(1,128)S(1)} %shard_map.102), channel_id=1, replica_groups={{1,0,9,8,17,16,25,24},{3,2,11,10,19,18,27,26},{5,4,13,12,21,20,29,28},{..., dimensions={0} | all-to-all | bytes 16384 | tf_op jit(solution)/shard_map/all_to_all | solution.py:353
  51.6 1.2 shard_map.103
  53.4 9.0 %all_to_all.84.refs_1_ = f32[32,1,256]{2,1,0:T(1,128)S(1)} all-to-all(f32[32,1,256]{2,1,0:T(1,128)S(1)} %get-tuple-element.121), channel_id=1, replica_groups=mesh['grp'=4,'blk'=8] {'grp','blk'}, dimensions={0} | all-to-all | bytes 65536 | tf_op jit(solution)/shard_map/all_to_all | solution.py:341
  63.3 10.2 %all_to_all.85.refs_3_ = f32[32,1,256]{2,1,0:T(1,128)S(1)} all-to-all(f32[32,1,256]{2,1,0:T(1,128)S(1)} %shard_map.105), channel_id=1, replica_groups=mesh['grp'=4,'blk'=8] {'grp','blk'}, dimensions={0} | all-to-all | bytes 65536 | tf_op jit(solution)/shard_map/all_to_all | solution.py:341
  74.3 7.2 %all_to_all.86.refs_3_ = f32[8,1,256]{2,1,0:T(1,128)S(1)} all-to-all(f32[8,1,256]{2,1,0:T(1,128)S(1)} %shard_map.107), channel_id=1, replica_groups={{9,8,17,16,1,0,25,24},{11,10,19,18,3,2,27,26},{13,12,21,20,5,4,29,28},{..., dimensions={0} | all-to-all | bytes 16384 | tf_op jit(solution)/shard_map/all_to_all | solution.py:353
  82.0 7.9 %all_to_all.87.summed = f32[8,1,256]{2,1,0:T(1,128)S(1)} all-to-all(f32[8,1,256]{2,1,0:T(1,128)S(1)} %shard_map.108), channel_id=1, replica_groups={{1,0,9,8,17,16,25,24},{3,2,11,10,19,18,27,26},{5,4,13,12,21,20,29,28},{..., dimensions={0} | all-to-all | bytes 16384 | tf_op jit(solution)/shard_map/all_to_all | solution.py:353
  89.9 1.7 %shard_map.109 = (f32[256,256]{1,0:T(8,128)S(1)}, f32[32,1,256]{2,1,0:T(1,128)S(1)}) custom-call(f32[8,1,256]{2,1,0:T(1,128)S(1)} %all_to_all.87.summed, f32[1,256]{1,0:T(1,128)S(1)} %get-tuple-element.91.class_prior, f32[1,256]{1,0:T(1,128)S(1)} %get-tuple-element.96.class_target.refs_2_.refs_4_, bf16[640,256]{1,0:T(8,128)(2,1)S(1)} %get-tuple-element.139.refs_0_.rest_0_, ...), custom_call_target="tpu_custom_call" | custom-call | tf_op jit(solution)/shard_map/pallas_call | solution.py:482
  92.2 9.0 %all_to_all.88.refs_1_ = f32[32,1,256]{2,1,0:T(1,128)S(1)} all-to-all(f32[32,1,256]{2,1,0:T(1,128)S(1)} %get-tuple-element.144), channel_id=1, replica_groups=mesh['grp'=4,'blk'=8] {'grp','blk'}, dimensions={0} | all-to-all | bytes 65536 | tf_op jit(solution)/shard_map/all_to_all | solution.py:341
  102.0 9.0 %all_to_all.89.refs_3_ = f32[32,1,256]{2,1,0:T(1,128)S(1)} all-to-all(f32[32,1,256]{2,1,0:T(1,128)S(1)} %shard_map.111), channel_id=1, replica_groups=mesh['grp'=4,'blk'=8] {'grp','blk'}, dimensions={0} | all-to-all | bytes 65536 | tf_op jit(solution)/shard_map/all_to_all | solution.py:341
  111.5 7.1 %all_to_all.90.refs_3_ = f32[8,1,256]{2,1,0:T(1,128)S(1)} all-to-all(f32[8,1,256]{2,1,0:T(1,128)S(1)} %shard_map.113), channel_id=1, replica_groups={{9,8,17,16,1,0,25,24},{11,10,19,18,3,2,27,26},{13,12,21,20,5,4,29,28},{..., dimensions={0} | all-to-all | bytes 16384 | tf_op jit(solution)/shard_map/all_to_all | solution.py:353
  118.9 7.0 %all_to_all.91.summed.author_summed = f32[8,1,256]{2,1,0:T(1,128)S(1)} all-to-all(f32[8,1,256]{2,1,0:T(1,128)S(1)} %shard_map.114), channel_id=1, replica_groups={{9,8,17,16,1,0,25,24},{11,10,19,18,3,2,27,26},{13,12,21,20,5,4,29,28},{..., dimensions={0} | all-to-all | bytes 16384 | tf_op jit(solution)/shard_map/all_to_all | solution.py:353
  125.9 1.2 shard_map.115
  127.0 9.0 %all_to_all.92.refs_1_ = f32[32,1,256]{2,1,0:T(1,128)S(1)} all-to-all(f32[32,1,256]{2,1,0:T(1,128)S(1)} %get-tuple-element.167), channel_id=1, replica_groups=mesh['grp'=4,'blk'=8] {'grp','blk'}, dimensions={0} | all-to-all | bytes 65536 | tf_op jit(solution)/shard_map/all_to_all | solution.py:341
  136.3 8.9 %all_to_all.93.refs_1_ = f32[32,1,256]{2,1,0:T(1,128)S(1)} all-to-all(f32[32,1,256]{2,1,0:T(1,128)S(1)} %shard_map.116), channel_id=1, replica_groups=mesh['grp'=4,'blk'=8] {'grp','blk'}, dimensions={0} | all-to-all | bytes 65536 | tf_op jit(solution)/shard_map/all_to_all | solution.py:341
  145.5 8.9 %all_to_all.94.refs_1_ = f32[32,1,256]{2,1,0:T(1,128)S(1)} all-to-all(f32[32,1,256]{2,1,0:T(1,128)S(1)} %shard_map.117), channel_id=1, replica_groups=mesh['grp'=4,'blk'=8] {'grp','blk'}, dimensions={0} | all-to-all | bytes 65536 | tf_op jit(solution)/shard_map/all_to_all | solution.py:341
  154.6 8.9 %all_to_all.95.summed = f32[32,1,256]{2,1,0:T(1,128)S(1)} all-to-all(f32[32,1,256]{2,1,0:T(1,128)S(1)} %shard_map.118), channel_id=1, replica_groups=mesh['grp'=4,'blk'=8] {'grp','blk'}, dimensions={0} | all-to-all | bytes 65536 | tf_op jit(solution)/shard_map/all_to_all | solution.py:341
  163.6 1.1 shard_map.119
  (43 shorter events, 9.2 us)
Async XLA Ops:
  3.2 1.8 %collective-permute-start = (bf16[4,336,128]{2,1,0:T(8,128)(2,1)S(1)}, bf16[4,336,128]{2,1,0:T(8,128)(2,1)S(1)}, u32[]{:S(2)}, u32[]{:S(2)}) collective-permute-start(bf16[4,336,128]{2,1,0:T(8,128)(2,1)S(1)} %get-tuple-element.88.swap), channel_id=1, source_target_pairs={{0,1},{1,0},{2,3},{3,2},{4,5},{5,4},{6,7},{7,6},{8,9},{9,8},{10,11... | collective-permute-start | bytes 1032200 | tf_op jit(solution)/shard_map/ppermute | solution.py:397
  5.1 17.8 %collective-permute-start.1 = (bf16[2,336,128]{2,1,0:T(8,128)(2,1)S(1)}, bf16[2,336,128]{2,1,0:T(8,128)(2,1)S(1)}, u32[]{:S(2)}, u32[]{:S(2)}) collective-permute-start(bf16[2,336,128]{2,1,0:T(8,128)(2,1)S(1)} %get-tuple-element.97), channel_id=1, source_target_pairs={{0,2},{1,5},{2,0},{3,7},{4,6},{5,1},{6,4},{7,3},{8,10},{9,13},{10,... | collective-permute-start | bytes 516104 | tf_op jit(solution)/shard_map/ppermute | solution.py:408
  8.0 14.9 %collective-permute-start.2 = (bf16[2,336,128]{2,1,0:T(8,128)(2,1)S(1)}, bf16[2,336,128]{2,1,0:T(8,128)(2,1)S(1)}, u32[]{:S(2)}, u32[]{:S(2)}) collective-permute-start(bf16[2,336,128]{2,1,0:T(8,128)(2,1)S(1)} %get-tuple-element.98), channel_id=1, source_target_pairs={{0,4},{1,3},{2,6},{3,1},{4,0},{5,7},{6,2},{7,5},{8,12},{9,11},{10,... | collective-permute-start | bytes 516104 | tf_op jit(solution)/shard_map/ppermute | solution.py:408
  9.5 13.4 %collective-permute-start.3 = (bf16[2,336,128]{2,1,0:T(8,128)(2,1)S(1)}, bf16[2,336,128]{2,1,0:T(8,128)(2,1)S(1)}, u32[]{:S(2)}, u32[]{:S(2)}) collective-permute-start(bf16[2,336,128]{2,1,0:T(8,128)(2,1)S(1)} %get-tuple-element.99), channel_id=1, source_target_pairs={{0,6},{1,7},{2,4},{3,5},{4,2},{5,3},{6,0},{7,1},{8,14},{9,15},{10,... | collective-permute-start | bytes 516104 | tf_op jit(solution)/shard_map/ppermute | solution.py:408
  23.7 9.6 %collective-permute-start.4 = (f32[256,256]{1,0:T(8,128)S(1)}, f32[256,256]{1,0:T(8,128)S(1)}, u32[]{:S(2)}, u32[]{:S(2)}) collective-permute-start(f32[256,256]{1,0:T(8,128)S(1)} %get-tuple-element.115.refs_0_.rest_0_), channel_id=1, source_target_pairs={{0,2},{1,5},{2,0},{3,7},{4,6},{5,1},{6,4},{7,3},{8,10},{9,13},{10,... | collective-permute-start | bytes 786440 | tf_op jit(solution)/shard_map/ppermute | solution.py:408
  33.3 9.8 %collective-permute-start.5 = (f32[2,256,256]{2,1,0:T(8,128)S(1)}, f32[2,256,256]{2,1,0:T(8,128)S(1)}, u32[]{:S(2)}, u32[]{:S(2)}) collective-permute-start(f32[2,256,256]{2,1,0:T(8,128)S(1)} %shard_map.99), channel_id=1, source_target_pairs={{0,4},{1,3},{2,6},{3,1},{4,0},{5,7},{6,2},{7,5},{8,12},{9,11},{10,... | collective-permute-start | bytes 1572872 | tf_op jit(solution)/shard_map/ppermute | solution.py:408
  43.2 8.5 %collective-permute-start.6 = (f32[4,256,256]{2,1,0:T(8,128)S(1)}, f32[4,256,256]{2,1,0:T(8,128)S(1)}, u32[]{:S(2)}, u32[]{:S(2)}) collective-permute-start(f32[4,256,256]{2,1,0:T(8,128)S(1)} %shard_map.101), channel_id=1, source_target_pairs={{0,1},{1,0},{2,3},{3,2},{4,5},{5,4},{6,7},{7,6},{8,9},{9,8},{10,11... | collective-permute-start | bytes 3145736 | tf_op jit(solution)/shard_map/ppermute | solution.py:411
  52.8 9.5 %collective-permute-start.7 = (bf16[640,256]{1,0:T(8,128)(2,1)S(1)}, bf16[640,256]{1,0:T(8,128)(2,1)S(1)}, u32[]{:S(2)}, u32[]{:S(2)}) collective-permute-start(bf16[640,256]{1,0:T(8,128)(2,1)S(1)} %get-tuple-element.139.refs_0_.rest_0_), channel_id=1, source_target_pairs={{0,2},{1,5},{2,0},{3,7},{4,6},{5,1},{6,4},{7,3},{8,10},{9,13},{10,... | collective-permute-start | bytes 983048 | tf_op jit(solution)/shard_map/ppermute | solution.py:408
  62.4 11.0 %collective-permute-start.8 = (bf16[2,640,256]{2,1,0:T(8,128)(2,1)S(1)}, bf16[2,640,256]{2,1,0:T(8,128)(2,1)S(1)}, u32[]{:S(2)}, u32[]{:S(2)}) collective-permute-start(bf16[2,640,256]{2,1,0:T(8,128)(2,1)S(1)} %shard_map.104), channel_id=1, source_target_pairs={{0,4},{1,3},{2,6},{3,1},{4,0},{5,7},{6,2},{7,5},{8,12},{9,11},{10,... | collective-permute-start | bytes 1966088 | tf_op jit(solution)/shard_map/ppermute | solution.py:408
  73.6 7.9 %collective-permute-start.9 = (bf16[4,640,256]{2,1,0:T(8,128)(2,1)S(1)}, bf16[4,640,256]{2,1,0:T(8,128)(2,1)S(1)}, u32[]{:S(2)}, u32[]{:S(2)}) collective-permute-start(bf16[4,640,256]{2,1,0:T(8,128)(2,1)S(1)} %shard_map.106), channel_id=1, source_target_pairs={{0,1},{1,0},{2,3},{3,2},{4,5},{5,4},{6,7},{7,6},{8,9},{9,8},{10,11... | collective-permute-start | bytes 3932168 | tf_op jit(solution)/shard_map/ppermute | solution.py:411
  91.6 9.5 %collective-permute-start.10 = (f32[256,256]{1,0:T(8,128)S(1)}, f32[256,256]{1,0:T(8,128)S(1)}, u32[]{:S(2)}, u32[]{:S(2)}) collective-permute-start(f32[256,256]{1,0:T(8,128)S(1)} %get-tuple-element.162.refs_0_.rest_0_.own), channel_id=1, source_target_pairs={{0,2},{1,5},{2,0},{3,7},{4,6},{5,1},{6,4},{7,3},{8,10},{9,13},{10,... | collective-permute-start | bytes 786440 | tf_op jit(solution)/shard_map/ppermute | solution.py:408
  101.2 9.8 %collective-permute-start.11 = (f32[2,256,256]{2,1,0:T(8,128)S(1)}, f32[2,256,256]{2,1,0:T(8,128)S(1)}, u32[]{:S(2)}, u32[]{:S(2)}) collective-permute-start(f32[2,256,256]{2,1,0:T(8,128)S(1)} %shard_map.110), channel_id=1, source_target_pairs={{0,4},{1,3},{2,6},{3,1},{4,0},{5,7},{6,2},{7,5},{8,12},{9,11},{10,... | collective-permute-start | bytes 1572872 | tf_op jit(solution)/shard_map/ppermute | solution.py:408
  111.1 7.6 %collective-permute-start.12 = (f32[4,256,256]{2,1,0:T(8,128)S(1)}, f32[4,256,256]{2,1,0:T(8,128)S(1)}, u32[]{:S(2)}, u32[]{:S(2)}) collective-permute-start(f32[4,256,256]{2,1,0:T(8,128)S(1)} %shard_map.112), channel_id=1, source_target_pairs={{0,1},{1,0},{2,3},{3,2},{4,5},{5,4},{6,7},{7,6},{8,9},{9,8},{10,11... | collective-permute-start | bytes 3145736 | tf_op jit(solution)/shard_map/ppermute | solution.py:411

commit v27 on v25

--- a/solution.py
+++ b/solution.py
@@ -343,7 +343,7 @@
 
 def narrow_exchange(parts, sides, upwards):
     groups, blocks = lax.axis_size("grp"), lax.axis_size("blk")
-    planes = range(groups)
+    planes = [1, 0, *range(2, groups)]
     if not upwards:
         planes = sorted(planes, key=lambda i: abs(2 * i + 1 - groups))
     sets = [

time: 166 us -> 166 us (level)
    all_to_all x5, blocking collectives: 37.4 us -> 35.7 us  [narrow_exchange(): lax.all_to_all(parts, AXES, split_axis=0, concat_axis=0, axis_index_group...]
    all_to_all x11, blocking collectives: 104 us -> 106 us  [exchange(): return lax.all_to_all(parts, AXES, split_axis=0, concat_axis=0, tiled=True)]
where the time goes in v27:
time: 166 us; the launch traced here: 165 us
  blocking collectives  142 us (86%)
  Pallas kernels  12.8 us (8%)
  starting transfers between devices  9.04 us (5%)
    all_to_all x11, blocking collectives, exchange(): return lax.all_to_all(parts, AXES, split_axis=0, concat_axis=0, tiled=True)  106 us
    all_to_all x5, blocking collectives, narrow_exchange(): lax.all_to_all(parts, AXES, split_axis=0, concat_axis=0, axis_index_group...  35.7 us
    ppermute x9, starting transfers between devices, across_pairs(): lax.ppermute(value, 'blk', [(i, i ^ hop) for i, hop in enumerate(hops)])  8.04 us
  transfers between devices with their start and end apart: 13, of which 1 were waited for; matrix products, arithmetic and copies ran while one was open for 0% of the time, Pallas kernels for 2%

profile of v27, /device:TPU:0, one launch (start us, length us, event | category | flops | bytes accessed | tf_op | source)
XLA Modules:
  0.0 165.1 jit_solution(8570572456590148804)
XLA Ops:
  1.3 1.9 %shard_map.95 = (s32[8]{0:T(128)S(1)}, s32[8]{0:T(128)S(1)}, s32[5,128]{1,0:T(8,128)S(1)}, s32[5,128]{1,0:T(8,128)S(1)}, f32[1,256]{1,0:T(1,128)S(1)}, /*index=5...) custom-call(s32[1]{0:T(128)S(6)} %copy.10.tile_count, ...), custom_call_target="tpu_custom_call" | custom-call | tf_op jit(solution)/shard_map/pallas_call | solution.py:389
  3.8 1.1 shard_map.96
  5.1 2.9 %collective-permute-start.1 = (bf16[2,336,128]{2,1,0:T(8,128)(2,1)S(1)}, bf16[2,336,128]{2,1,0:T(8,128)(2,1)S(1)}, u32[]{:S(2)}, u32[]{:S(2)}) collective-permute-start(bf16[2,336,128]{2,1,0:T(8,128)(2,1)S(1)} %get-tuple-element.97), channel_id=1, source_target_pairs={{0,2},{1,5},{2,0},{3,7},{4,6},{5,1},{6,4},{7,3},{8,10},{9,13},{10,... | collective-permute-start | bytes 516104 | tf_op jit(solution)/shard_map/ppermute | solution.py:408
  8.0 1.5 collective-permute-start.2
  9.5 13.4 %all_to_all.80.summed = f32[32,1,256]{2,1,0:T(1,128)S(1)} all-to-all(f32[32,1,256]{2,1,0:T(1,128)S(1)} %shard_map.96), channel_id=1, replica_groups=mesh['grp'=4,'blk'=8] {'grp','blk'}, dimensions={0} | all-to-all | bytes 65536 | tf_op jit(solution)/shard_map/all_to_all | solution.py:341
  24.3 9.0 %all_to_all.81.refs_1_ = f32[32,1,256]{2,1,0:T(1,128)S(1)} all-to-all(f32[32,1,256]{2,1,0:T(1,128)S(1)} %get-tuple-element.101), channel_id=1, replica_groups=mesh['grp'=4,'blk'=8] {'grp','blk'}, dimensions={0} | all-to-all | bytes 65536 | tf_op jit(solution)/shard_map/all_to_all | solution.py:341
  34.2 9.0 %all_to_all.82.refs_3_ = f32[32,1,256]{2,1,0:T(1,128)S(1)} all-to-all(f32[32,1,256]{2,1,0:T(1,128)S(1)} %shard_map.100), channel_id=1, replica_groups=mesh['grp'=4,'blk'=8] {'grp','blk'}, dimensions={0} | all-to-all | bytes 65536 | tf_op jit(solution)/shard_map/all_to_all | solution.py:341
  43.6 7.1 %all_to_all.83.summed = f32[8,1,256]{2,1,0:T(1,128)S(1)} all-to-all(f32[8,1,256]{2,1,0:T(1,128)S(1)} %shard_map.102), channel_id=1, replica_groups={{9,8,1,0,17,16,25,24},{11,10,3,2,19,18,27,26},{13,12,5,4,21,20,29,28},{..., dimensions={0} | all-to-all | bytes 16384 | tf_op jit(solution)/shard_map/all_to_all | solution.py:353
  50.8 1.2 shard_map.103
  52.6 9.8 %all_to_all.84.refs_1_ = f32[32,1,256]{2,1,0:T(1,128)S(1)} all-to-all(f32[32,1,256]{2,1,0:T(1,128)S(1)} %get-tuple-element.121), channel_id=1, replica_groups=mesh['grp'=4,'blk'=8] {'grp','blk'}, dimensions={0} | all-to-all | bytes 65536 | tf_op jit(solution)/shard_map/all_to_all | solution.py:341
  63.3 10.2 %all_to_all.85.refs_3_ = f32[32,1,256]{2,1,0:T(1,128)S(1)} all-to-all(f32[32,1,256]{2,1,0:T(1,128)S(1)} %shard_map.105), channel_id=1, replica_groups=mesh['grp'=4,'blk'=8] {'grp','blk'}, dimensions={0} | all-to-all | bytes 65536 | tf_op jit(solution)/shard_map/all_to_all | solution.py:341
  74.3 7.2 %all_to_all.86.refs_3_ = f32[8,1,256]{2,1,0:T(1,128)S(1)} all-to-all(f32[8,1,256]{2,1,0:T(1,128)S(1)} %shard_map.107), channel_id=1, replica_groups={{9,8,17,16,1,0,25,24},{11,10,19,18,3,2,27,26},{13,12,21,20,5,4,29,28},{..., dimensions={0} | all-to-all | bytes 16384 | tf_op jit(solution)/shard_map/all_to_all | solution.py:353
  82.0 7.0 %all_to_all.87.summed = f32[8,1,256]{2,1,0:T(1,128)S(1)} all-to-all(f32[8,1,256]{2,1,0:T(1,128)S(1)} %shard_map.108), channel_id=1, replica_groups={{9,8,1,0,17,16,25,24},{11,10,3,2,19,18,27,26},{13,12,5,4,21,20,29,28},{..., dimensions={0} | all-to-all | bytes 16384 | tf_op jit(solution)/shard_map/all_to_all | solution.py:353
  89.0 1.7 %shard_map.109 = (f32[256,256]{1,0:T(8,128)S(1)}, f32[32,1,256]{2,1,0:T(1,128)S(1)}) custom-call(f32[8,1,256]{2,1,0:T(1,128)S(1)} %all_to_all.87.summed, f32[1,256]{1,0:T(1,128)S(1)} %get-tuple-element.91.class_prior, f32[1,256]{1,0:T(1,128)S(1)} %get-tuple-element.96.class_target.refs_2_.refs_4_.refs_5_, ...), custom_call_target="tpu_custom_call" | custom-call | tf_op jit(solution)/shard_map/pallas_call | solution.py:485
  91.3 9.8 %all_to_all.88.refs_1_ = f32[32,1,256]{2,1,0:T(1,128)S(1)} all-to-all(f32[32,1,256]{2,1,0:T(1,128)S(1)} %get-tuple-element.144), channel_id=1, replica_groups=mesh['grp'=4,'blk'=8] {'grp','blk'}, dimensions={0} | all-to-all | bytes 65536 | tf_op jit(solution)/shard_map/all_to_all | solution.py:341
  102.0 9.0 %all_to_all.89.refs_3_ = f32[32,1,256]{2,1,0:T(1,128)S(1)} all-to-all(f32[32,1,256]{2,1,0:T(1,128)S(1)} %shard_map.111), channel_id=1, replica_groups=mesh['grp'=4,'blk'=8] {'grp','blk'}, dimensions={0} | all-to-all | bytes 65536 | tf_op jit(solution)/shard_map/all_to_all | solution.py:341
  111.5 7.1 %all_to_all.90.refs_4_ = f32[8,1,256]{2,1,0:T(1,128)S(1)} all-to-all(f32[8,1,256]{2,1,0:T(1,128)S(1)} %shard_map.113), channel_id=1, replica_groups={{9,8,17,16,1,0,25,24},{11,10,19,18,3,2,27,26},{13,12,21,20,5,4,29,28},{..., dimensions={0} | all-to-all | bytes 16384 | tf_op jit(solution)/shard_map/all_to_all | solution.py:353
  119.0 7.2 %all_to_all.91.summed.author_summed = f32[4,1,256]{2,1,0:T(1,128)S(1)} all-to-all(f32[4,1,256]{2,1,0:T(1,128)S(1)} %shard_map.114), channel_id=1, replica_groups={{8,16,0,24},{9,17,1,25},{10,18,2,26},{11,19,3,27},{12,20,4,28},{13,21,5..., dimensions={0} | all-to-all | bytes 8192 | tf_op jit(solution)/shard_map/all_to_all | solution.py:353
  126.3 1.2 shard_map.115
  127.4 9.0 %all_to_all.92.refs_1_ = f32[32,1,256]{2,1,0:T(1,128)S(1)} all-to-all(f32[32,1,256]{2,1,0:T(1,128)S(1)} %get-tuple-element.167), channel_id=1, replica_groups=mesh['grp'=4,'blk'=8] {'grp','blk'}, dimensions={0} | all-to-all | bytes 65536 | tf_op jit(solution)/shard_map/all_to_all | solution.py:341
  136.6 8.9 %all_to_all.93.refs_1_ = f32[32,1,256]{2,1,0:T(1,128)S(1)} all-to-all(f32[32,1,256]{2,1,0:T(1,128)S(1)} %shard_map.116), channel_id=1, replica_groups=mesh['grp'=4,'blk'=8] {'grp','blk'}, dimensions={0} | all-to-all | bytes 65536 | tf_op jit(solution)/shard_map/all_to_all | solution.py:341
  145.8 8.9 %all_to_all.94.refs_1_ = f32[32,1,256]{2,1,0:T(1,128)S(1)} all-to-all(f32[32,1,256]{2,1,0:T(1,128)S(1)} %shard_map.117), channel_id=1, replica_groups=mesh['grp'=4,'blk'=8] {'grp','blk'}, dimensions={0} | all-to-all | bytes 65536 | tf_op jit(solution)/shard_map/all_to_all | solution.py:341
  155.0 8.9 %all_to_all.95.summed = f32[32,1,256]{2,1,0:T(1,128)S(1)} all-to-all(f32[32,1,256]{2,1,0:T(1,128)S(1)} %shard_map.118), channel_id=1, replica_groups=mesh['grp'=4,'blk'=8] {'grp','blk'}, dimensions={0} | all-to-all | bytes 65536 | tf_op jit(solution)/shard_map/all_to_all | solution.py:341
  164.0 1.1 shard_map.119
  (43 shorter events, 9.4 us)
Async XLA Ops:
  3.2 1.8 %collective-permute-start = (bf16[4,336,128]{2,1,0:T(8,128)(2,1)S(1)}, bf16[4,336,128]{2,1,0:T(8,128)(2,1)S(1)}, u32[]{:S(2)}, u32[]{:S(2)}) collective-permute-start(bf16[4,336,128]{2,1,0:T(8,128)(2,1)S(1)} %get-tuple-element.88.swap), channel_id=1, source_target_pairs={{0,1},{1,0},{2,3},{3,2},{4,5},{5,4},{6,7},{7,6},{8,9},{9,8},{10,11... | collective-permute-start | bytes 1032200 | tf_op jit(solution)/shard_map/ppermute | solution.py:397
  5.1 17.8 %collective-permute-start.1 = (bf16[2,336,128]{2,1,0:T(8,128)(2,1)S(1)}, bf16[2,336,128]{2,1,0:T(8,128)(2,1)S(1)}, u32[]{:S(2)}, u32[]{:S(2)}) collective-permute-start(bf16[2,336,128]{2,1,0:T(8,128)(2,1)S(1)} %get-tuple-element.97), channel_id=1, source_target_pairs={{0,2},{1,5},{2,0},{3,7},{4,6},{5,1},{6,4},{7,3},{8,10},{9,13},{10,... | collective-permute-start | bytes 516104 | tf_op jit(solution)/shard_map/ppermute | solution.py:408
  8.0 14.9 %collective-permute-start.2 = (bf16[2,336,128]{2,1,0:T(8,128)(2,1)S(1)}, bf16[2,336,128]{2,1,0:T(8,128)(2,1)S(1)}, u32[]{:S(2)}, u32[]{:S(2)}) collective-permute-start(bf16[2,336,128]{2,1,0:T(8,128)(2,1)S(1)} %get-tuple-element.98), channel_id=1, source_target_pairs={{0,4},{1,3},{2,6},{3,1},{4,0},{5,7},{6,2},{7,5},{8,12},{9,11},{10,... | collective-permute-start | bytes 516104 | tf_op jit(solution)/shard_map/ppermute | solution.py:408
  9.5 13.4 %collective-permute-start.3 = (bf16[2,336,128]{2,1,0:T(8,128)(2,1)S(1)}, bf16[2,336,128]{2,1,0:T(8,128)(2,1)S(1)}, u32[]{:S(2)}, u32[]{:S(2)}) collective-permute-start(bf16[2,336,128]{2,1,0:T(8,128)(2,1)S(1)} %get-tuple-element.99), channel_id=1, source_target_pairs={{0,6},{1,7},{2,4},{3,5},{4,2},{5,3},{6,0},{7,1},{8,14},{9,15},{10,... | collective-permute-start | bytes 516104 | tf_op jit(solution)/shard_map/ppermute | solution.py:408
  23.7 9.6 %collective-permute-start.4 = (f32[256,256]{1,0:T(8,128)S(1)}, f32[256,256]{1,0:T(8,128)S(1)}, u32[]{:S(2)}, u32[]{:S(2)}) collective-permute-start(f32[256,256]{1,0:T(8,128)S(1)} %get-tuple-element.115.refs_0_.rest_0_), channel_id=1, source_target_pairs={{0,2},{1,5},{2,0},{3,7},{4,6},{5,1},{6,4},{7,3},{8,10},{9,13},{10,... | collective-permute-start | bytes 786440 | tf_op jit(solution)/shard_map/ppermute | solution.py:408
  33.3 9.8 %collective-permute-start.5 = (f32[2,256,256]{2,1,0:T(8,128)S(1)}, f32[2,256,256]{2,1,0:T(8,128)S(1)}, u32[]{:S(2)}, u32[]{:S(2)}) collective-permute-start(f32[2,256,256]{2,1,0:T(8,128)S(1)} %shard_map.99), channel_id=1, source_target_pairs={{0,4},{1,3},{2,6},{3,1},{4,0},{5,7},{6,2},{7,5},{8,12},{9,11},{10,... | collective-permute-start | bytes 1572872 | tf_op jit(solution)/shard_map/ppermute | solution.py:408
  43.2 7.6 %collective-permute-start.6 = (f32[4,256,256]{2,1,0:T(8,128)S(1)}, f32[4,256,256]{2,1,0:T(8,128)S(1)}, u32[]{:S(2)}, u32[]{:S(2)}) collective-permute-start(f32[4,256,256]{2,1,0:T(8,128)S(1)} %shard_map.101), channel_id=1, source_target_pairs={{0,1},{1,0},{2,3},{3,2},{4,5},{5,4},{6,7},{7,6},{8,9},{9,8},{10,11... | collective-permute-start | bytes 3145736 | tf_op jit(solution)/shard_map/ppermute | solution.py:411
  52.0 10.4 %collective-permute-start.7 = (bf16[640,256]{1,0:T(8,128)(2,1)S(1)}, bf16[640,256]{1,0:T(8,128)(2,1)S(1)}, u32[]{:S(2)}, u32[]{:S(2)}) collective-permute-start(bf16[640,256]{1,0:T(8,128)(2,1)S(1)} %get-tuple-element.139.refs_0_.rest_0_), channel_id=1, source_target_pairs={{0,2},{1,5},{2,0},{3,7},{4,6},{5,1},{6,4},{7,3},{8,10},{9,13},{10,... | collective-permute-start | bytes 983048 | tf_op jit(solution)/shard_map/ppermute | solution.py:408
  62.4 11.0 %collective-permute-start.8 = (bf16[2,640,256]{2,1,0:T(8,128)(2,1)S(1)}, bf16[2,640,256]{2,1,0:T(8,128)(2,1)S(1)}, u32[]{:S(2)}, u32[]{:S(2)}) collective-permute-start(bf16[2,640,256]{2,1,0:T(8,128)(2,1)S(1)} %shard_map.104), channel_id=1, source_target_pairs={{0,4},{1,3},{2,6},{3,1},{4,0},{5,7},{6,2},{7,5},{8,12},{9,11},{10,... | collective-permute-start | bytes 1966088 | tf_op jit(solution)/shard_map/ppermute | solution.py:408
  73.6 7.9 %collective-permute-start.9 = (bf16[4,640,256]{2,1,0:T(8,128)(2,1)S(1)}, bf16[4,640,256]{2,1,0:T(8,128)(2,1)S(1)}, u32[]{:S(2)}, u32[]{:S(2)}) collective-permute-start(bf16[4,640,256]{2,1,0:T(8,128)(2,1)S(1)} %shard_map.106), channel_id=1, source_target_pairs={{0,1},{1,0},{2,3},{3,2},{4,5},{5,4},{6,7},{7,6},{8,9},{9,8},{10,11... | collective-permute-start | bytes 3932168 | tf_op jit(solution)/shard_map/ppermute | solution.py:411
  90.8 10.4 %collective-permute-start.10 = (f32[256,256]{1,0:T(8,128)S(1)}, f32[256,256]{1,0:T(8,128)S(1)}, u32[]{:S(2)}, u32[]{:S(2)}) collective-permute-start(f32[256,256]{1,0:T(8,128)S(1)} %get-tuple-element.163.refs_0_.rest_0_.own), channel_id=1, source_target_pairs={{0,2},{1,5},{2,0},{3,7},{4,6},{5,1},{6,4},{7,3},{8,10},{9,13},{10,... | collective-permute-start | bytes 786440 | tf_op jit(solution)/shard_map/ppermute | solution.py:408
  101.2 9.8 %collective-permute-start.11 = (f32[2,256,256]{2,1,0:T(8,128)S(1)}, f32[2,256,256]{2,1,0:T(8,128)S(1)}, u32[]{:S(2)}, u32[]{:S(2)}) collective-permute-start(f32[2,256,256]{2,1,0:T(8,128)S(1)} %shard_map.110), channel_id=1, source_target_pairs={{0,4},{1,3},{2,6},{3,1},{4,0},{5,7},{6,2},{7,5},{8,12},{9,11},{10,... | collective-permute-start | bytes 1572872 | tf_op jit(solution)/shard_map/ppermute | solution.py:408
  111.1 7.6 %collective-permute-start.12 = (f32[4,256,256]{2,1,0:T(8,128)S(1)}, f32[4,256,256]{2,1,0:T(8,128)S(1)}, u32[]{:S(2)}, u32[]{:S(2)}) collective-permute-start(f32[4,256,256]{2,1,0:T(8,128)S(1)} %shard_map.112), channel_id=1, source_target_pairs={{0,1},{1,0},{2,3},{3,2},{4,5},{5,4},{6,7},{7,6},{8,9},{9,8},{10,11... | collective-permute-start | bytes 3145736 | tf_op jit(solution)/shard_map/ppermute | solution.py:411
